TPU v7x, 32 devices: a whole 2x2x4 slice. The times are simulated.
32 devices in a mesh: pool: 8 (over z, y), mlp: 4 (over x, core).
Axes of the slice: x: 2, y: 2, z: 4, core: 2. Of those that a mesh axis runs over, the one named last changes fastest.
Arguments:
- residual_in: bfloat16 [16, 3072], P('pool', 'mlp'), may hold values from -6 to 6
- query_new: bfloat16 [16, 3072], P('pool', 'mlp'), may hold values from -6 to 6
- key_new: bfloat16 [16, 3072], P('pool', 'mlp'), may hold values from -6 to 6
- value_new: bfloat16 [16, 3072], P('pool', 'mlp'), may hold values from -6 to 6
- key_cache: bfloat16 [40, 256, 3072], P('pool', None, 'mlp'), may hold values from -240 to 240
- value_cache: bfloat16 [40, 256, 3072], P('pool', None, 'mlp'), may hold values from -6 to 6
- block_table: int32 [16, 8], P('pool'), may hold values from -1 to 39, as said below
- lengths: int32 [16], P('pool'), may hold values from 1 to 2048, as said below
- out_weight: bfloat16 [3072, 3072], P('mlp', 'pool'), may hold values from -0.109375 to 0.109375
- norm_gain: bfloat16 [3072], P('mlp'), may hold values from 0.25 to 1.75
- gate_weight: bfloat16 [3072, 8192], P('mlp', 'pool'), may hold values from -0.109375 to 0.109375
- up_weight: bfloat16 [3072, 8192], P('mlp', 'pool'), may hold values from -0.109375 to 0.109375
- down_weight: bfloat16 [8192, 3072], P('pool', 'mlp'), may hold values from -0.0625 to 0.0625
Outputs:
- layer_out: bfloat16 [16, 3072], P('pool', 'mlp')
Inputs may be any that keep to these rules, and one draw needn't show every extreme that they name: `block_table`: row r lists ceil(lengths[r] / 256) distinct block numbers followed by -1; no block is listed twice in the whole table. `lengths`: some request holds exactly 2048 tokens.
All inputs are finite; a program needn't handle non-finite values.
Results may differ from a plain program's by a relative error of at most 0.012.
Values may be sent and summed in bfloat16 or wider, within the bound.
No kernel may reach another device: no remote copies, remote signals or barrier semaphores. Data moves between devices by JAX's collectives and lax.ppermute only.
A program may use at most 64 MiB of HBM per device.

v0:
```python
import math

import jax
import jax.numpy as jnp
from jax import lax
from jax.sharding import PartitionSpec as P

HD = 96


def rotate(values, positions):
    half_size = values.shape[-1] // 2
    inverse_freq = 10000.0 ** (-(2.0 * jnp.arange(half_size, dtype=jnp.float32)) / values.shape[-1])
    angles = positions.astype(jnp.float32)[:, None, None] * inverse_freq[None, None, :]
    cosine = jnp.cos(angles)
    sine_part = jnp.sin(angles)
    first = values[..., :half_size]
    second = values[..., half_size:]
    return jnp.concatenate(
        [first * cosine - second * sine_part, second * cosine + first * sine_part], -1
    )


def per_device(
    residual_in,
    query_new,
    key_new,
    value_new,
    key_cache,
    value_cache,
    block_table,
    lengths,
    out_weight,
    norm_gain,
    gate_weight,
    up_weight,
    down_weight,
):
    rows_dev, width_dev = residual_in.shape
    head_size = HD
    heads_dev = width_dev // head_size
    blocks_dev, block_len = (key_cache.shape[0], key_cache.shape[1])
    pool_index = lax.axis_index("pool")
    mlp_index = lax.axis_index("mlp")
    requests = rows_dev * lax.axis_size("pool")
    score_scale = 1.0 / math.sqrt(head_size)
    queries = rotate(
        query_new.astype(jnp.float32).reshape(rows_dev, heads_dev, head_size), lengths
    ).astype(jnp.bfloat16)
    new_keys = rotate(
        key_new.astype(jnp.float32).reshape(rows_dev, heads_dev, head_size), lengths
    ).astype(jnp.bfloat16)
    new_values = value_new.reshape(rows_dev, heads_dev, head_size)
    all_queries = lax.all_gather(queries.reshape(rows_dev, width_dev), "pool", axis=0, tiled=True)
    all_tables, all_lengths = (
        lax.all_gather(block_table, "pool", axis=0, tiled=True),
        lax.all_gather(lengths, "pool", axis=0, tiled=True),
    )
    held_ids = pool_index * blocks_dev + jnp.arange(blocks_dev, dtype=jnp.int32)
    matches = all_tables[None, :, :] == held_ids[:, None, None]
    holder = jnp.any(matches, 2)
    block_index = jnp.sum(
        jnp.where(matches, jnp.arange(all_tables.shape[1], dtype=jnp.int32)[None, None, :], 0),
        (1, 2),
    )
    valid_len = jnp.sum(jnp.where(holder, all_lengths[None, :], 0), 1)
    block_query = jnp.dot(
        holder.astype(jnp.bfloat16), all_queries, preferred_element_type=jnp.float32
    ).astype(jnp.bfloat16)
    block_query = block_query.reshape(blocks_dev, heads_dev, head_size)
    key_rows = key_cache.reshape(blocks_dev, block_len, heads_dev, head_size)
    value_rows = value_cache.reshape(blocks_dev, block_len, heads_dev, head_size)
    scores = (
        jnp.einsum("bhd,bthd->bht", block_query, key_rows, preferred_element_type=jnp.float32)
        * score_scale
    )
    token_pos = block_index[:, None] * block_len + jnp.arange(block_len, dtype=jnp.int32)[None, :]
    valid_mask = token_pos < valid_len[:, None]
    scores = jnp.where(valid_mask[:, None, :], scores, -1e30)
    block_max = jnp.max(scores, 2)
    self_score = (
        jnp.sum(queries.astype(jnp.float32) * new_keys.astype(jnp.float32), -1) * score_scale
    )
    request_max = jnp.max(jnp.where(holder[:, :, None], block_max[:, None, :], -1e30), 0)
    lowest = jnp.full((requests, heads_dev), -1e30, jnp.float32)
    own_scores = lax.dynamic_update_slice_in_dim(lowest, self_score, pool_index * rows_dev, 0)
    maxima_all = lax.pmax(jnp.maximum(request_max, own_scores), "pool")
    block_shift = jnp.sum(jnp.where(holder[:, :, None], maxima_all[None, :, :], 0.0), 1)
    weights = jnp.where(valid_mask[:, None, :], jnp.exp(scores - block_shift[:, :, None]), 0.0)
    block_totals = jnp.sum(weights, 2)
    block_numer = jnp.einsum(
        "bht,bthd->bhd",
        weights.astype(jnp.bfloat16),
        value_rows,
        preferred_element_type=jnp.float32,
    )
    block_numer = block_numer.reshape(blocks_dev, width_dev)
    holder_float = holder.astype(jnp.float32)
    numer_rows = jnp.einsum("br,bk->rk", holder_float, block_numer, precision=lax.Precision.HIGHEST)
    total_rows = jnp.einsum(
        "br,bh->rh", holder_float, block_totals, precision=lax.Precision.HIGHEST
    )
    numerator, totals = (
        lax.psum_scatter(numer_rows, "pool", scatter_dimension=0, tiled=True),
        lax.psum_scatter(total_rows, "pool", scatter_dimension=0, tiled=True),
    )
    own_max = lax.dynamic_slice_in_dim(maxima_all, pool_index * rows_dev, rows_dev, 0)
    numerator = numerator.reshape(rows_dev, heads_dev, head_size)
    self_weight = jnp.exp(self_score - own_max)
    totals = totals + self_weight
    self_low = lax.optimization_barrier(self_weight.astype(jnp.bfloat16))
    numerator = numerator + self_low.astype(jnp.float32)[:, :, None] * new_values.astype(
        jnp.float32
    )
    attended = (numerator / totals[:, :, None]).astype(jnp.bfloat16).reshape(rows_dev, width_dev)
    head_part = jnp.dot(
        lax.all_gather(attended, "pool", axis=0, tiled=True),
        out_weight,
        preferred_element_type=jnp.float32,
    )
    head_sum = lax.psum(head_part, "mlp").astype(jnp.bfloat16)
    head_out = lax.all_to_all(head_sum, "pool", split_axis=0, concat_axis=1, tiled=True)
    full_input, full_gain = (
        lax.all_gather(residual_in, "mlp", axis=1, tiled=True),
        lax.all_gather(norm_gain, "mlp", axis=0, tiled=True),
    )
    residual = full_input.astype(jnp.float32) + head_out.astype(jnp.float32)
    mean_square = jnp.mean(residual * residual, -1, keepdims=True)
    normed = (residual * lax.rsqrt(mean_square + 1e-05) * full_gain.astype(jnp.float32)).astype(
        jnp.bfloat16
    )
    own_normed = lax.dynamic_slice_in_dim(normed, mlp_index * width_dev, width_dev, 1)
    ff_dev = gate_weight.shape[1]
    portion = lax.all_gather(own_normed, "pool", axis=0, tiled=True)
    gate_up = jnp.concatenate(
        [
            jnp.dot(portion, gate_weight, preferred_element_type=jnp.float32),
            jnp.dot(portion, up_weight, preferred_element_type=jnp.float32),
        ],
        1,
    )
    summed = lax.psum(gate_up.astype(jnp.bfloat16), "mlp").astype(jnp.float32)
    hidden = (jax.nn.silu(summed[:, :ff_dev]) * summed[:, ff_dev:]).astype(jnp.bfloat16)
    down_out = lax.psum_scatter(
        jnp.dot(hidden, down_weight, preferred_element_type=jnp.float32),
        "pool",
        scatter_dimension=0,
        tiled=True,
    )
    own_residual = lax.dynamic_slice_in_dim(residual, mlp_index * width_dev, width_dev, 1)
    return (own_residual + down_out).astype(jnp.bfloat16)


def solution(mesh):
    in_specs = (
        P("pool", "mlp"),
        P("pool", "mlp"),
        P("pool", "mlp"),
        P("pool", "mlp"),
        P("pool", None, "mlp"),
        P("pool", None, "mlp"),
        P("pool", None),
        P("pool"),
        P("mlp", "pool"),
        P("mlp"),
        P("mlp", "pool"),
        P("mlp", "pool"),
        P("pool", "mlp"),
    )
    out_specs = P("pool", "mlp")
    return jax.shard_map(
        per_device, mesh=mesh, in_specs=in_specs, out_specs=out_specs, check_vma=False
    )
```

profile of v0, /device:TPU:0, one launch (start us, length us, event | category | flops | bytes accessed | tf_op | source)
XLA Modules:
  0.0 313.0 jit_solution(8528777488178820386)
XLA Ops:
  6.6 22.6 %all-gather = s32[8,2,8]{2,1,0:T(2,128)S(1)} all-gather(s32[1,2,8]{2,1,0:T(2,128)} %bitcast.52), channel_id=1, replica_groups=mesh['pool'=8,'mlp'=4] {'pool'}, dimensions={0}, use_global_device_ids=true | all-gather | bytes 576 | tf_op jit(solution)/shard_map/all_gather | solution.py:56
  29.3 0.1 compare_reduce_fusion
  29.4 0.3 fusion.10
  29.6 0.7 convert_element_type.74
  30.3 0.8 reshape.161
  31.1 0.8 reshape.163
  31.8 0.1 multiply_cosine_fusion
  32.1 0.2 multiply_reduce_fusion.1
  32.3 30.3 %all-gather.1 = bf16[8,2,768]{2,1,0:T(2,128)(2,1)S(1)} all-gather(bf16[1,2,768]{2,1,0:T(2,128)(2,1)S(1)} %reshape.170), channel_id=1, replica_groups=mesh['pool'=8,'mlp'=4] {'pool'}, dimensions={0}, use_global_device_ids=true | all-gather | bytes 27648 | tf_op jit(solution)/shard_map/all_gather | solution.py:54
  62.7 0.1 convolution_convert_fusion.2
  62.8 0.7 reshape.187
  63.5 1.3 fusion.20
  65.5 0.9 dynamic-update-slice
  66.4 2.7 copy.25
  69.0 9.0 %all-reduce = s32[16]{0:T(128)} all-reduce(s32[16]{0:T(128)S(1)} %dynamic-update-slice), channel_id=1, replica_groups=mesh['pool'=8,'mlp'=4] {'pool'}, use_global_device_ids=true, to_apply=%add | all-reduce | flops 16 | bytes 128
  78.1 0.7 select_reduce_fusion.2
  78.8 1.1 fusion.21
  80.0 0.5 copy-done.2
  80.5 0.1 fusion.9
  80.8 0.1 dynamic_update_slice.3
  80.9 20.0 %pmax.7 = f32[16,8]{0,1:T(8,128)S(1)} all-reduce(f32[16,8]{0,1:T(8,128)S(1)} %max.5), channel_id=1, replica_groups=mesh['pool'=8,'mlp'=4] {'pool'}, use_global_device_ids=true, to_apply=%region_6.7 | all-reduce | flops 128 | bytes 1024 | tf_op jit(solution)/shard_map/pmax | solution.py:87
  101.0 1.5 fusion.11
  102.5 2.7 copy.27
  105.2 1.9 fusion.2
  107.1 0.9 reshape.159
  108.0 0.2 fusion.22
  108.2 0.2 fusion.23
  108.4 33.4 %all-reduce.4 = (f32[16,8]{1,0:T(8,128)S(1)}, f32[16,768]{1,0:T(8,128)S(1)}) all-reduce(f32[16,8]{1,0:T(8,128)S(1)} %fusion.23, f32[16,768]{1,0:T(8,128)S(1)} %fusion.22), channel_id=3, replica_groups=mesh['pool'=8,'mlp'=4] {'pool'}, use_global_device_ids=true, to_apply=%region_10.11.clone | all-reduce | flops 12416 | bytes 99328
  142.9 0.1 copy.28
  143.2 0.7 fusion.16
  143.9 30.3 %all-gather.2 = bf16[8,2,768]{2,1,0:T(2,128)(2,1)S(1)} all-gather(bf16[1,2,768]{2,1,0:T(2,128)(2,1)S(1)} %fusion.16), channel_id=1, replica_groups=mesh['pool'=8,'mlp'=4] {'pool'}, dimensions={0}, use_global_device_ids=true | all-gather | bytes 27648 | tf_op jit(solution)/shard_map/all_gather | solution.py:117
  174.2 1.2 fusion.24
  175.5 10.3 %psum.14 = bf16[16,384]{1,0:T(8,128)(2,1)S(1)} all-reduce(f32[16,384]{1,0:T(8,128)S(1)} %fusion.24), channel_id=1, replica_groups=mesh['pool'=8,'mlp'=4] {'mlp'}, use_global_device_ids=true, to_apply=%region_11.12 | all-reduce | flops 6144 | bytes 36864 | tf_op jit(solution)/shard_map/psum | solution.py:121
  185.8 0.6 all_to_all.10
  186.4 3.3 %all-to-all-start = ((bf16[8,2,384]{2,1,0:T(2,128)(2,1)}), bf16[8,2,384]{2,1,0:T(2,128)(2,1)S(1)}, u32[]{:S(2)}, u32[]{:S(2)}) async-start(bf16[8,2,384]{2,1,0:T(2,128)(2,1)} %all_to_all.10), calls=%async_computation | async-start | bytes 24576 | tf_op jit(solution)/shard_map/all_to_all | solution.py:122
  189.8 0.7 reshape.174
  190.5 5.1 %all-gather.3 = bf16[4,1,768]{2,1,0:T(2,128)(2,1)S(1)} all-gather(bf16[1,1,768]{2,1,0:T(2,128)(2,1)S(1)} %reshape.174), channel_id=1, replica_groups=mesh['pool'=8,'mlp'=4] {'mlp'}, dimensions={0}, use_global_device_ids=true | all-gather | bytes 7680 | tf_op jit(solution)/shard_map/all_gather | solution.py:125
  195.7 5.3 %all_gather.21 = bf16[2,3072]{1,0:T(2,128)(2,1)S(1)} all-gather(bf16[2,768]{1,0:T(2,128)(2,1)} %param.13), channel_id=1, replica_groups=mesh['pool'=8,'mlp'=4] {'mlp'}, dimensions={1}, use_global_device_ids=true | all-gather | bytes 15360 | tf_op jit(solution)/shard_map/all_gather | solution.py:124
  201.0 0.1 multiply_reduce_fusion
  201.2 30.8 %all-gather.4 = bf16[8,2,768]{2,1,0:T(2,128)(2,1)S(1)} all-gather(bf16[1,2,768]{2,1,0:T(2,128)(2,1)S(1)} %fusion.15), channel_id=1, replica_groups=mesh['pool'=8,'mlp'=4] {'pool'}, dimensions={0}, use_global_device_ids=true | all-gather | bytes 27648 | tf_op jit(solution)/shard_map/all_gather | solution.py:134
  232.0 0.3 convolution_convert_fusion
  232.3 0.3 convolution_convert_fusion.1
  232.7 0.6 pad_maximum_fusion
  233.3 32.1 %all-reduce.7.cloned.1.call-done = bf16[16,2048]{1,0:T(8,128)(2,1)} async-done(((bf16[16,2048]{1,0:T(8,128)(2,1)}), bf16[16,2048]{1,0:T(8,128)(2,1)}) %all-reduce.7.cloned.1.call-update) | async-done | bytes 65552 | tf_op jit(solution)/shard_map/psum | solution.py:142
  265.4 0.8 convert_element_type.91
  266.3 1.7 fusion.6
  268.0 37.5 %all-reduce.3 = f32[16,768]{1,0:T(8,128)S(1)} all-reduce(f32[16,768]{1,0:T(8,128)S(1)} %fusion.6), channel_id=4, replica_groups=mesh['pool'=8,'mlp'=4] {'pool'}, use_global_device_ids=true, to_apply=%region_14.15.clone | all-reduce | flops 12288 | bytes 98304
  305.5 0.6 fusion.12
  (39 shorter events, 1.5 us)
Async XLA Ops:
  6.5 225.5 %copy-start = (bf16[768,1024]{1,0:T(8,128)(2,1)S(1)}, bf16[768,1024]{1,0:T(8,128)(2,1)}, u32[]{:S(2)}) copy-start(bf16[768,1024]{1,0:T(8,128)(2,1)} %param.24) | copy-start | bytes 4718596
  79.9 0.6 copy-start.2
  107.1 125.2 %copy-start.1 = (bf16[768,1024]{1,0:T(8,128)(2,1)S(1)}, bf16[768,1024]{1,0:T(8,128)(2,1)}, u32[]{:S(2)}) copy-start(bf16[768,1024]{1,0:T(8,128)(2,1)} %param.23) | copy-start | bytes 4718596
  186.4 14.6 %all-to-all-start = ((bf16[8,2,384]{2,1,0:T(2,128)(2,1)}), bf16[8,2,384]{2,1,0:T(2,128)(2,1)S(1)}, u32[]{:S(2)}, u32[]{:S(2)}) async-start(bf16[8,2,384]{2,1,0:T(2,128)(2,1)} %all_to_all.10), calls=%async_computation | async-start | bytes 24576 | tf_op jit(solution)/shard_map/all_to_all | solution.py:122
  189.7 75.7 %all-reduce.7.cloned.1.call-start = ((), (), s32[]{:S(2)}) async-start(), calls=%async_computation.1 | async-start | bytes 131072 | tf_op jit(solution)/shard_map/psum | solution.py:142
Sparse Core Ops, SparseCore 0:
  233.4 31.9 all-reduce.6
where the time goes:
time: 314 us; the launch traced here: 313 us
  blocking collectives  235 us (75%)
  waiting for transfers between devices  32.1 us (10%)
  between operations  14.9 us (5%)
  local copies, waits for them, and re-layouts  13.6 us (4%)
  matrix products  7.15 us (2%)
  other arithmetic  7.14 us (2%)
  starting transfers between devices  3.37 us (1%)
    unnamed x3, blocking collectives  80 us
    psum x1, waiting for transfers between devices, per_device(): summed = lax.psum(gate_up.astype(jnp.bfloat16), 'mlp').astype(jnp.float32)  32.1 us
    all_gather x1, blocking collectives, per_device(): portion = lax.all_gather(own_normed, 'pool', axis=0, tiled=True)  30.8 us
    all_gather x1, blocking collectives, per_device(): lax.all_gather(queries.reshape(rows_dev, width_dev), 'pool', axis=0, tile...  30.3 us
    all_gather x1, blocking collectives, per_device(): lax.all_gather(attended, 'pool', axis=0, tiled=True)  30.3 us
    all_gather x1, blocking collectives, per_device(): lax.all_gather(block_table, 'pool', axis=0, tiled=True)  22.6 us
    pmax x1, blocking collectives, per_device(): maxima_all = lax.pmax(jnp.maximum(request_max, own_scores), 'pool')  20 us
    psum x1, blocking collectives, per_device(): head_sum = lax.psum(head_part, 'mlp').astype(jnp.bfloat16)  10.3 us
  transfers between devices with their start and end apart: 2, of which 1 were waited for; matrix products, arithmetic and copies ran while one was open for 0% of the time, Pallas kernels for 0%

commit v1 on v0

v1 whole, which is shorter than its diff:
```python
import math

import jax
import jax.numpy as jnp
from jax import lax
from jax.sharding import PartitionSpec as P

HD = 96
LOW = -1e30
CODE = 128


def rotate(values, positions):
    half_size = values.shape[-1] // 2
    inverse_freq = 10000.0 ** (-(2.0 * jnp.arange(half_size, dtype=jnp.float32)) / values.shape[-1])
    angles = positions.astype(jnp.float32)[:, None, None] * inverse_freq[None, None, :]
    cosine = jnp.cos(angles)
    sine_part = jnp.sin(angles)
    first = values[..., :half_size]
    second = values[..., half_size:]
    return jnp.concatenate(
        [first * cosine - second * sine_part, second * cosine + first * sine_part], -1
    )


def low(values):
    return lax.reduce_precision(values, 8, 7)


def split(values):
    high = low(values)
    return high.astype(jnp.bfloat16), (values - high).astype(jnp.bfloat16)


def encode(ints):
    return (ints // CODE).astype(jnp.bfloat16), (ints % CODE).astype(jnp.bfloat16)


def decode(high, rest):
    return high.astype(jnp.int32) * CODE + rest.astype(jnp.int32)


def gather(values, axis):
    copies = jnp.broadcast_to(values[None], (lax.axis_size(axis),) + values.shape)
    return lax.all_to_all(copies, axis, 0, 0)


def per_device(
    residual_in,
    query_new,
    key_new,
    value_new,
    key_cache,
    value_cache,
    block_table,
    lengths,
    out_weight,
    norm_gain,
    gate_weight,
    up_weight,
    down_weight,
):
    rows, width = residual_in.shape
    heads = width // HD
    blocks, block_len = key_cache.shape[:2]
    most = block_table.shape[1]
    pool, mlp = lax.axis_size("pool"), lax.axis_size("mlp")
    pool_index = lax.axis_index("pool")
    requests = rows * pool
    score_scale = 1.0 / math.sqrt(HD)
    f32, bf16 = jnp.float32, jnp.bfloat16

    queries = rotate(query_new.astype(f32).reshape(rows, heads, HD), lengths).astype(bf16)
    new_keys = rotate(key_new.astype(f32).reshape(rows, heads, HD), lengths).astype(bf16)

    table_high, table_low = encode(block_table + 1)
    len_high, len_low = encode(lengths)
    packed = jnp.concatenate(
        [
            queries.reshape(rows, width),
            residual_in,
            table_high,
            table_low,
            len_high[:, None],
            len_low[:, None],
        ],
        1,
    )
    spare = -packed.shape[1] % 128
    packed = jnp.pad(packed, ((0, 0), (0, spare)))
    got = gather(packed, "pool").reshape(requests, packed.shape[1])
    all_queries = got[:, :width]
    all_input = got[:, width : 2 * width]
    tail = got[:, 2 * width :]
    tables = decode(tail[:, :most], tail[:, most : 2 * most]) - 1
    all_lengths = decode(tail[:, 2 * most], tail[:, 2 * most + 1])

    held_ids = pool_index * blocks + jnp.arange(blocks, dtype=jnp.int32)
    matches = tables[None, :, :] == held_ids[:, None, None]
    holder = jnp.any(matches, 2)
    block_index = jnp.sum(
        jnp.where(matches, jnp.arange(most, dtype=jnp.int32)[None, None, :], 0), (1, 2)
    )
    valid_len = jnp.sum(jnp.where(holder, all_lengths[None, :], 0), 1)
    block_query = jnp.dot(holder.astype(bf16), all_queries, preferred_element_type=f32)
    block_query = block_query.astype(bf16).reshape(blocks, heads, HD)
    key_rows = key_cache.reshape(blocks, block_len, heads, HD)
    value_rows = value_cache.reshape(blocks, block_len, heads, HD)
    scores = (
        jnp.einsum("bhd,bthd->bht", block_query, key_rows, preferred_element_type=f32)
        * score_scale
    )
    token_pos = block_index[:, None] * block_len + jnp.arange(block_len, dtype=jnp.int32)[None, :]
    valid = (token_pos < valid_len[:, None])[:, None, :]
    scores = jnp.where(valid, scores, LOW)
    shift = low(jnp.max(scores, 2))
    weights = jnp.where(valid, jnp.exp(scores - shift[:, :, None]), 0.0)
    totals = jnp.sum(weights, 2)
    numerator = jnp.einsum(
        "bht,bthd->bhd", weights.astype(bf16), value_rows, preferred_element_type=f32
    )
    self_score = jnp.sum(queries.astype(f32) * new_keys.astype(f32), -1) * score_scale
    self_shift = low(self_score)
    self_weight = jnp.exp(self_score - self_shift)
    self_numer = self_weight[:, :, None] * value_new.astype(f32).reshape(rows, heads, HD)

    own_total = jnp.concatenate([totals, self_weight], 0)
    total_high, total_low = split(own_total)
    part = jnp.concatenate(
        [
            jnp.concatenate([numerator, self_numer], 0)
            .astype(bf16)
            .reshape(blocks + rows, width),
            jnp.concatenate([shift, self_shift], 0).astype(bf16),
            total_high,
            total_low,
        ],
        1,
    )
    part = jnp.pad(part, ((0, 0), (0, -part.shape[1] % 128)))
    count = blocks + rows
    parts = gather(part, "pool").reshape(pool * count, part.shape[1])
    all_shift = parts[:, width : width + heads].astype(f32)
    all_total = parts[:, width + heads : width + 2 * heads].astype(f32) + parts[
        :, width + 2 * heads : width + 3 * heads
    ].astype(f32)
    place = jnp.arange(pool * count, dtype=jnp.int32)
    owner, slot = place // count, place % count
    is_block = slot < blocks
    block_id = jnp.where(is_block, owner * blocks + slot, -2)
    self_id = jnp.where(is_block, -2, owner * rows + slot - blocks)
    request_ids = jnp.arange(requests, dtype=jnp.int32)
    belongs = jnp.any(tables[:, None, :] == block_id[None, :, None], 2) | (
        request_ids[:, None] == self_id[None, :]
    )
    top = jnp.max(jnp.where(belongs[:, :, None], all_shift[None], LOW), 1)
    part_top = jnp.sum(jnp.where(belongs[:, :, None], top[:, None, :], 0.0), 0)
    scale = jnp.exp(all_shift - part_top)
    scaled = parts[:, :width].astype(f32).reshape(-1, heads, HD) * scale[:, :, None]
    mix = belongs.astype(f32)
    numer = jnp.dot(mix, scaled.reshape(-1, width), precision=lax.Precision.HIGHEST)
    denom = jnp.dot(mix, all_total * scale, precision=lax.Precision.HIGHEST)
    attended = (numer.reshape(requests, heads, HD) / denom[:, :, None]).astype(bf16)
    attended = attended.reshape(requests, width)

    head_part = jnp.dot(attended, out_weight, preferred_element_type=f32).astype(bf16)
    share = pool // mlp
    route = []
    for p in range(pool):
        for m in range(mlp):
            route.append((p * mlp + m, ((p % share) * mlp + m) * mlp + p // share))
    moved = lax.ppermute(head_part, ("pool", "mlp"), route)
    head_all = gather(moved, "pool").reshape(share, mlp, requests, -1)
    head_out = low(jnp.sum(head_all.astype(f32), 1))
    head_out = jnp.swapaxes(head_out, 0, 1).reshape(requests, width)
    residual = all_input.astype(f32) + head_out
    squares = jnp.sum(residual * residual, -1, keepdims=True)
    portion = (residual * norm_gain.astype(f32)).astype(bf16)

    ff = gate_weight.shape[1]
    square_high, square_low = split(squares)
    sums = jnp.concatenate(
        [
            jnp.dot(portion, gate_weight, preferred_element_type=f32).astype(bf16),
            jnp.dot(portion, up_weight, preferred_element_type=f32).astype(bf16),
            jnp.broadcast_to(square_high, (requests, 64)),
            jnp.broadcast_to(square_low, (requests, 64)),
        ],
        1,
    )
    summed = jnp.sum(gather(sums, "mlp").astype(f32), 0)
    mean_square = (summed[:, 2 * ff : 2 * ff + 1] + summed[:, 2 * ff + 64 : 2 * ff + 65]) / (
        width * mlp
    )
    factor = lax.rsqrt(mean_square + 1e-05)
    gate = summed[:, :ff] * factor
    up = summed[:, ff : 2 * ff] * factor
    hidden = (jax.nn.silu(gate) * up).astype(bf16)

    down = jnp.dot(hidden, down_weight, preferred_element_type=f32)
    down = lax.all_to_all(down.reshape(pool, rows, width), "pool", 0, 0)
    own = lax.dynamic_slice_in_dim(residual, pool_index * rows, rows, 0)
    return (own + jnp.sum(down, 0)).astype(bf16)


def solution(mesh):
    in_specs = (
        P("pool", "mlp"),
        P("pool", "mlp"),
        P("pool", "mlp"),
        P("pool", "mlp"),
        P("pool", None, "mlp"),
        P("pool", None, "mlp"),
        P("pool", None),
        P("pool"),
        P("mlp", "pool"),
        P("mlp"),
        P("mlp", "pool"),
        P("mlp", "pool"),
        P("pool", "mlp"),
    )
    return jax.shard_map(
        per_device, mesh=mesh, in_specs=in_specs, out_specs=P("pool", "mlp"), check_vma=False
    )
```

time: 314 us -> 96.8 us (0.31)
  blocking collectives: 235 us -> 8.57 us
  starting transfers between devices: 3.37 us -> 27.6 us
  between operations: 14.9 us -> 0.2 us
  waiting for transfers between devices: 32.1 us -> 19.7 us
  other arithmetic: 7.14 us -> 14.5 us
  local copies, waits for them, and re-layouts: 13.6 us -> 16.8 us
    all_gather x6 -> x0, blocking collectives: 124 us -> none  [the longest x1 30.8 us: per_device(): portion = lax.all_gather(own_normed, 'pool', axis=0, tiled=True)]
    unnamed x3 -> x0, blocking collectives: 80 us -> none
    psum x1 -> x0, waiting for transfers between devices: 32.1 us -> none  [per_device(): summed = lax.psum(gate_up.astype(jnp.bfloat16), 'mlp').astype(jnp.float32)]
    all_to_all x1 -> x4, starting transfers between devices: 3.33 us -> 27 us  [the longest x3 23.6 us: gather(): return lax.all_to_all(copies, axis, 0, 0)]
    pmax x1 -> x0, blocking collectives: 20 us -> none  [per_device(): maxima_all = lax.pmax(jnp.maximum(request_max, own_scores), 'pool')]
    all_to_all x1 -> x4, waiting for transfers between devices: 0.01 us -> 19.7 us  [the longest x3 13 us: gather(): return lax.all_to_all(copies, axis, 0, 0)]
    psum x1 -> x0, blocking collectives: 10.3 us -> none  [per_device(): head_sum = lax.psum(head_part, 'mlp').astype(jnp.bfloat16)]
    all_to_all x0 -> x1, blocking collectives: none -> 8.57 us  [gather(): return lax.all_to_all(copies, axis, 0, 0)]
  transfers between devices with their start and end apart: 2 -> 5, of which waited for: 1 -> 3; matrix products, arithmetic and copies ran while one was open for 0% -> 12% of each run, Pallas kernels for 0% -> 0%
where the time goes in v1:
time: 96.8 us; the launch traced here: 95.6 us
  starting transfers between devices  27.6 us (29%)
  waiting for transfers between devices  19.7 us (20%)
  local copies, waits for them, and re-layouts  16.8 us (17%)
  other arithmetic  14.5 us (15%)
  blocking collectives  8.57 us (9%)
  matrix products  8.1 us (8%)
    all_to_all x3, starting transfers between devices, gather(): return lax.all_to_all(copies, axis, 0, 0)  23.6 us
    all_to_all x3, waiting for transfers between devices, gather(): return lax.all_to_all(copies, axis, 0, 0)  13 us
    all_to_all x1, blocking collectives, gather(): return lax.all_to_all(copies, axis, 0, 0)  8.57 us
    unnamed x15, local copies, waits for them, and re-layouts  7.47 us
    all_to_all x1, waiting for transfers between devices, per_device(): down = lax.all_to_all(down.reshape(pool, rows, width), 'pool', 0, 0)  6.73 us
    all_to_all x1, starting transfers between devices, per_device(): down = lax.all_to_all(down.reshape(pool, rows, width), 'pool', 0, 0)  3.34 us
    another operation x5, other arithmetic  2.44 us
    broadcast_in_dim x4, local copies, waits for them, and re-layouts, gather(): jnp.broadcast_to(values[None], (lax.axis_size(axis),) + values.shape)  1.96 us
  transfers between devices with their start and end apart: 5, of which 3 were waited for; matrix products, arithmetic and copies ran while one was open for 12% of the time, Pallas kernels for 0%

profile of v1, /device:TPU:0, one launch (start us, length us, event | category | flops | bytes accessed | tf_op | source)
XLA Modules:
  0.0 95.6 jit_solution(12332039464597684890)
XLA Ops:
  0.0 0.8 fusion.51
  0.8 0.8 reshape.278
  1.6 0.8 reshape.280
  3.1 0.7 fusion.47
  3.8 0.8 concatenate.31
  4.6 0.7 broadcast_in_dim.104
  5.2 7.3 %all-to-all-start = ((bf16[8,2,1664]{2,1,0:T(2,128)(2,1)}), bf16[8,2,1664]{2,1,0:T(2,128)(2,1)}, u32[]{:S(2)}, u32[]{:S(2)}) async-start(bf16[8,2,1664]{2,1,0:T(2,128)(2,1)} %broadcast_in_dim.104), calls=%async_computation | async-start | bytes 106496 | tf_op jit(solution)/shard_map/all_to_all | solution.py:45
  12.5 0.6 compare_select_fusion.5
  13.1 0.5 compare_select_fusion.4
  13.6 4.0 %copy.36 = bf16[5,256,768]{1,2,0:T(8,128)(2,1)} copy(bf16[5,256,768]{2,1,0:T(8,128)(2,1)} %param.17) | data formatting | bytes 3932160 | tf_op args[4]
  17.6 2.7 %copy.37 = bf16[5,256,768]{1,2,0:T(8,128)(2,1)S(1)} copy(bf16[5,256,768]{2,1,0:T(8,128)(2,1)} %param.18) | data formatting | bytes 3932160 | tf_op args[5]
  20.2 0.5 reduce-precision_convert_fusion.1
  20.7 0.6 copy-done.3
  21.5 1.3 %multiply_convert_fusion.3 = bf16[2,768]{1,0:T(2,128)(2,1)} fusion(f32[2,768]{1,0:T(2,128)S(1)} %mul.235, bf16[2,768]{1,0:T(2,128)(2,1)} %param.16), kind=kLoop, calls=%fused_computation.72 | loop fusion | flops 4608 | bytes 12288 | tf_op jit(solution)/shard_map/convert.6
  22.7 0.6 iota_add_fusion
  23.3 1.5 %reshape.267 = bf16[16,1664]{1,0:T(8,128)(2,1)} reshape(bf16[8,2,1664]{2,1,0:T(2,128)(2,1)} %all-to-all-done) | data formatting | bytes 106496 | tf_op jit(solution)/shard_map/reshape | solution.py:91
  24.8 0.8 add_add_fusion
  25.6 0.9 add_reduce_fusion
  26.6 0.8 compare_reduce_fusion.1
  27.4 0.9 fusion.27
  28.3 1.5 %convolution_convert_fusion.2 = bf16[5,768]{1,0:T(8,128)(2,1)} fusion(pred[5,16]{1,0:T(8,128)(4,1)S(1)} %compare_reduce_fusion.1, bf16[16,1664]{1,0:T(8,128)(2,1)} %reshape.267), kind=kOutput, calls=%fused_computation.6 | convolution fusion | flops 126720 | bytes 32336 | tf_op jit(solution)/shard_map/dot_general | solution.py:105
  29.9 1.4 %reshape.288 = bf16[5,8,96,1]{2,3,1,0:T(2,128)(2,1)} reshape(bf16[5,768]{1,0:T(8,128)(2,1)} %convolution_convert_fusion.2) | data formatting | bytes 15360 | tf_op jit(solution)/shard_map/reshape | solution.py:106
  31.3 1.9 %fusion.56 = f32[5,8,1,256]{3,2,1,0:T(1,128)S(1)} fusion(bf16[5,8,96,1]{2,3,1,0:T(2,128)(2,1)} %reshape.288, bf16[5,256,8,96]{1,3,2,0:T(8,128)(2,1)} %bitcast.47), kind=kOutput, calls=%fused_computation.124 | convolution fusion | flops 1966080 | bytes 2014720 | tf_op jit(solution)/shard_map/bhd,bthd->bht/dot_general | solution.py:110
  33.4 0.6 reduce-precision_convert_fusion.3
  34.1 0.6 fusion.8
  34.8 0.7 reduce-precision_convert_fusion
  35.5 0.8 fusion.32
  36.3 0.6 broadcast_in_dim.163
  37.0 6.0 %all-to-all-start.1 = ((bf16[8,7,896]{2,1,0:T(8,128)(2,1)}), bf16[8,7,896]{2,1,0:T(8,128)(2,1)S(1)}, u32[]{:S(2)}, u32[]{:S(2)}) async-start(bf16[8,7,896]{2,1,0:T(8,128)(2,1)} %broadcast_in_dim.163), calls=%async_computation.1 | async-start | bytes 229376 | tf_op jit(solution)/shard_map/all_to_all | solution.py:45
  43.0 0.7 compare_reduce_fusion
  43.7 0.6 fusion.38
  44.3 5.9 %all-to-all-done.1 = bf16[8,7,896]{2,1,0:T(8,128)(2,1)S(1)} async-done(((bf16[8,7,896]{2,1,0:T(8,128)(2,1)}), bf16[8,7,896]{2,1,0:T(8,128)(2,1)S(1)}, u32[]{:S(2)}, u32[]{:S(2)}) %all-to-all-start.1) | async-done | bytes 100384 | tf_op jit(solution)/shard_map/all_to_all | solution.py:45
  51.3 0.2 fusion.2
  51.7 1.3 %convolution_convert_fusion.3 = bf16[16,384]{1,0:T(8,128)(2,1)S(1)} fusion(bf16[16,768]{1,0:T(8,128)(2,1)S(1)} %reshape.274, bf16[768,384]{1,0:T(8,128)(2,1)} %param.21), kind=kOutput, calls=%fused_computation.7 | convolution fusion | flops 9443328 | bytes 626688 | tf_op jit(solution)/shard_map/dot_general | solution.py:166
  53.0 0.7 collective-permute-start
  53.7 0.6 broadcast_in_dim.169
  54.4 10.3 %all-to-all-start.2 = ((bf16[8,16,384]{2,1,0:T(8,128)(2,1)}), bf16[8,16,384]{2,1,0:T(8,128)(2,1)S(1)}, u32[]{:S(2)}, u32[]{:S(2)}) async-start(bf16[8,16,384]{2,1,0:T(8,128)(2,1)} %broadcast_in_dim.169), calls=%async_computation.2 | async-start | bytes 196608 | tf_op jit(solution)/shard_map/all_to_all | solution.py:45
  64.7 7.1 %all-to-all-done.2 = bf16[8,16,384]{2,1,0:T(8,128)(2,1)S(1)} async-done(((bf16[8,16,384]{2,1,0:T(8,128)(2,1)}), bf16[8,16,384]{2,1,0:T(8,128)(2,1)S(1)}, u32[]{:S(2)}, u32[]{:S(2)}) %all-to-all-start.2) | async-done | bytes 98336 | tf_op jit(solution)/shard_map/all_to_all | solution.py:45
  71.9 0.9 multiply_reduce_fusion
  72.7 0.3 convolution_convert_fusion
  73.1 0.3 convolution_convert_fusion.1
  73.7 8.6 %all_to_all.25 = bf16[4,16,2176]{2,1,0:T(8,128)(2,1)S(1)} all-to-all(bf16[4,16,2176]{2,1,0:T(8,128)(2,1)S(1)} %broadcast_in_dim.172), channel_id=1, replica_groups=mesh['pool'=8,'mlp'=4] {'mlp'}, dimensions={0} | all-to-all | bytes 557056 | tf_op jit(solution)/shard_map/all_to_all | solution.py:45
  82.3 0.2 fusion.37
  82.5 1.8 %fusion.12 = f32[16,768]{1,0:T(8,128)S(1)} fusion(bf16[1024,768]{1,0:T(8,128)(2,1)} %param.25, f32[16,2176]{1,0:T(8,128)S(1)} %convert_reduce_fusion, f32[16]{0:T(128)S(1)} %fusion.37), kind=kOutput, calls=%fused_computation.30 | convolution fusion | flops 25296896 | bytes 1753600 | tf_op jit(solution)/shard_map/dot_general | solution.py:200
  84.2 0.7 reshape.276
  84.9 3.3 %all-to-all-start.4 = ((f32[8,2,768]{2,1,0:T(2,128)}), f32[8,2,768]{2,1,0:T(2,128)S(1)}, u32[]{:S(2)}, u32[]{:S(2)}) async-start(f32[8,2,768]{2,1,0:T(2,128)} %reshape.276), calls=%async_computation.4 | async-start | bytes 98304 | tf_op jit(solution)/shard_map/all_to_all | solution.py:201
  88.3 6.7 %all-to-all-done.4 = f32[8,2,768]{2,1,0:T(2,128)S(1)} async-done(((f32[8,2,768]{2,1,0:T(2,128)}), f32[8,2,768]{2,1,0:T(2,128)S(1)}, u32[]{:S(2)}, u32[]{:S(2)}) %all-to-all-start.4) | async-done | bytes 49184 | tf_op jit(solution)/shard_map/all_to_all | solution.py:201
  95.0 0.6 add_convert_fusion.1
  (57 shorter events, 3.1 us)
Async XLA Ops:
  0.0 72.7 %copy-start = (bf16[768,1024]{1,0:T(8,128)(2,1)S(1)}, bf16[768,1024]{1,0:T(8,128)(2,1)}, u32[]{:S(2)}) copy-start(bf16[768,1024]{1,0:T(8,128)(2,1)} %param.24) | copy-start | bytes 4718596
  5.2 18.1 %all-to-all-start = ((bf16[8,2,1664]{2,1,0:T(2,128)(2,1)}), bf16[8,2,1664]{2,1,0:T(2,128)(2,1)}, u32[]{:S(2)}, u32[]{:S(2)}) async-start(bf16[8,2,1664]{2,1,0:T(2,128)(2,1)} %broadcast_in_dim.104), calls=%async_computation | async-start | bytes 106496 | tf_op jit(solution)/shard_map/all_to_all | solution.py:45
  20.7 0.6 copy-start.3
  33.3 2.3 %copy-start.2 = (bf16[2,768]{1,0:T(2,128)(2,1)S(1)}, bf16[2,768]{1,0:T(2,128)(2,1)}, u32[]{:S(2)}) copy-start(bf16[2,768]{1,0:T(2,128)(2,1)} %multiply_convert_fusion.3) | copy-start | bytes 9220
  37.0 13.2 %all-to-all-start.1 = ((bf16[8,7,896]{2,1,0:T(8,128)(2,1)}), bf16[8,7,896]{2,1,0:T(8,128)(2,1)S(1)}, u32[]{:S(2)}, u32[]{:S(2)}) async-start(bf16[8,7,896]{2,1,0:T(8,128)(2,1)} %broadcast_in_dim.163), calls=%async_computation.1 | async-start | bytes 229376 | tf_op jit(solution)/shard_map/all_to_all | solution.py:45
  50.2 14.5 %copy-start.4 = (bf16[768]{0:T(1024)(128)(2,1)S(1)}, bf16[768]{0:T(1024)(128)(2,1)}, u32[]{:S(2)}) copy-start(bf16[768]{0:T(1024)(128)(2,1)} %param.22) | copy-start | bytes 4612
  51.6 21.5 %copy-start.1 = (bf16[768,1024]{1,0:T(8,128)(2,1)S(1)}, bf16[768,1024]{1,0:T(8,128)(2,1)}, u32[]{:S(2)}) copy-start(bf16[768,1024]{1,0:T(8,128)(2,1)} %param.23) | copy-start | bytes 4718596
  53.0 0.7 collective-permute-start
  54.4 17.5 %all-to-all-start.2 = ((bf16[8,16,384]{2,1,0:T(8,128)(2,1)}), bf16[8,16,384]{2,1,0:T(8,128)(2,1)S(1)}, u32[]{:S(2)}, u32[]{:S(2)}) async-start(bf16[8,16,384]{2,1,0:T(8,128)(2,1)} %broadcast_in_dim.169), calls=%async_computation.2 | async-start | bytes 196608 | tf_op jit(solution)/shard_map/all_to_all | solution.py:45
  84.9 10.1 %all-to-all-start.4 = ((f32[8,2,768]{2,1,0:T(2,128)}), f32[8,2,768]{2,1,0:T(2,128)S(1)}, u32[]{:S(2)}, u32[]{:S(2)}) async-start(f32[8,2,768]{2,1,0:T(2,128)} %reshape.276), calls=%async_computation.4 | async-start | bytes 98304 | tf_op jit(solution)/shard_map/all_to_all | solution.py:201

commit v2 on v1

--- a/solution.py
+++ b/solution.py
@@ -40,9 +40,62 @@
     return high.astype(jnp.int32) * CODE + rest.astype(jnp.int32)
 
 
+def swap(axis, step):
+    size = lax.axis_size(axis)
+    return [(index, index ^ step) for index in range(size)]
+
+
+def direct(axis):
+    size = lax.axis_size(axis)
+    return size <= 8 and size & (size - 1) == 0
+
+
+def ordered(parts, axis):
+    index = lax.axis_index(axis)
+    bit = 1
+    while bit < len(parts):
+        odd = (index & bit) != 0
+        parts = [jnp.where(odd, parts[s ^ bit], parts[s]) for s in range(len(parts))]
+        bit *= 2
+    return jnp.stack(parts)
+
+
+def exchange(chunks, axis):
+    size = lax.axis_size(axis)
+    if not direct(axis):
+        return lax.all_to_all(chunks, axis, 0, 0)
+    index = lax.axis_index(axis)
+    parts = []
+    for step in range(size):
+        chunk = lax.dynamic_index_in_dim(chunks, index ^ step, 0, keepdims=False)
+        parts.append(lax.ppermute(chunk, axis, swap(axis, step)) if step else chunk)
+    return jnp.stack(parts)
+
+
 def gather(values, axis):
-    copies = jnp.broadcast_to(values[None], (lax.axis_size(axis),) + values.shape)
-    return lax.all_to_all(copies, axis, 0, 0)
+    size = lax.axis_size(axis)
+    if not direct(axis):
+        copies = jnp.broadcast_to(values[None], (size,) + values.shape)
+        return lax.all_to_all(copies, axis, 0, 0)
+    parts = [values]
+    for step in range(1, size):
+        parts.append(lax.ppermute(values, axis, swap(axis, step)))
+    return ordered(parts, axis)
+
+
+def gather_group(values):
+    pool, mlp = lax.axis_size("pool"), lax.axis_size("mlp")
+    share = pool // mlp
+    parts = []
+    for step in range(pool if direct("pool") else 1):
+        route = []
+        for p in range(pool):
+            for m in range(mlp):
+                route.append((p * mlp + m, (((p % share) * mlp + m) ^ step) * mlp + p // share))
+        parts.append(lax.ppermute(values, ("pool", "mlp"), route))
+    if direct("pool"):
+        return ordered(parts, "pool")
+    return gather(parts[0], "pool")
 
 
 def per_device(
@@ -164,13 +217,7 @@
     attended = attended.reshape(requests, width)
 
     head_part = jnp.dot(attended, out_weight, preferred_element_type=f32).astype(bf16)
-    share = pool // mlp
-    route = []
-    for p in range(pool):
-        for m in range(mlp):
-            route.append((p * mlp + m, ((p % share) * mlp + m) * mlp + p // share))
-    moved = lax.ppermute(head_part, ("pool", "mlp"), route)
-    head_all = gather(moved, "pool").reshape(share, mlp, requests, -1)
+    head_all = gather_group(head_part).reshape(pool // mlp, mlp, requests, -1)
     head_out = low(jnp.sum(head_all.astype(f32), 1))
     head_out = jnp.swapaxes(head_out, 0, 1).reshape(requests, width)
     residual = all_input.astype(f32) + head_out
@@ -198,7 +245,7 @@
     hidden = (jax.nn.silu(gate) * up).astype(bf16)
 
     down = jnp.dot(hidden, down_weight, preferred_element_type=f32)
-    down = lax.all_to_all(down.reshape(pool, rows, width), "pool", 0, 0)
+    down = exchange(down.reshape(pool, rows, width), "pool")
     own = lax.dynamic_slice_in_dim(residual, pool_index * rows, rows, 0)
     return (own + jnp.sum(down, 0)).astype(bf16)
 

time: 96.8 us -> 118 us (1.22)
  starting transfers between devices: 27.6 us -> 60.7 us
  blocking collectives: 8.57 us -> 0 us
  other arithmetic: 14.5 us -> 22.9 us
  waiting for transfers between devices: 19.7 us -> 12.3 us
  matrix products: 8.1 us -> 5.52 us
  local copies, waits for them, and re-layouts: 16.8 us -> 14.9 us
    ppermute x1 -> x32, starting transfers between devices: 0.68 us -> 60.7 us  [the longest x17 34 us: gather(): parts.append(lax.ppermute(values, axis, swap(axis, step)))]
    all_to_all x4 -> x0, starting transfers between devices: 27 us -> none  [the longest x3 23.6 us: gather(): return lax.all_to_all(copies, axis, 0, 0)]
    all_to_all x4 -> x0, waiting for transfers between devices: 19.7 us -> none  [the longest x3 13 us: gather(): return lax.all_to_all(copies, axis, 0, 0)]
    ppermute x1 -> x32, waiting for transfers between devices: 0.01 us -> 12.3 us  [the longest x17 8.12 us: gather(): parts.append(lax.ppermute(values, axis, swap(axis, step)))]
    all_to_all x1 -> x0, blocking collectives: 8.57 us -> none  [gather(): return lax.all_to_all(copies, axis, 0, 0)]
    unnamed x1 -> x22, other arithmetic: 0.01 us -> 6.08 us
    broadcast_in_dim x4 -> x0, local copies, waits for them, and re-layouts: 1.96 us -> none  [gather(): jnp.broadcast_to(values[None], (lax.axis_size(axis),) + values.shape)]
    dot_general x1, matrix products: 1.78 us -> 0.37 us  [per_device(): down = jnp.dot(hidden, down_weight, preferred_element_type=f32)]
  transfers between devices with their start and end apart: 5 -> 32, of which waited for: 3 -> 7; matrix products, arithmetic and copies ran while one was open for 12% -> 9% of each run, Pallas kernels for 0% -> 0%
where the time goes in v2:
time: 118 us; the launch traced here: 117 us
  starting transfers between devices  60.7 us (51%)
  other arithmetic  22.9 us (19%)
  local copies, waits for them, and re-layouts  14.9 us (13%)
  waiting for transfers between devices  12.3 us (10%)
  matrix products  5.52 us (5%)
    ppermute x17, starting transfers between devices, gather(): parts.append(lax.ppermute(values, axis, swap(axis, step)))  34 us
    ppermute x8, starting transfers between devices, gather_group(): parts.append(lax.ppermute(values, ('pool', 'mlp'), route))  15.5 us
    ppermute x7, starting transfers between devices, exchange(): parts.append(lax.ppermute(chunk, axis, swap(axis, step)) if step else chunk)  11.2 us
    ppermute x17, waiting for transfers between devices, gather(): parts.append(lax.ppermute(values, axis, swap(axis, step)))  8.12 us
    unnamed x21, local copies, waits for them, and re-layouts  7.48 us
    unnamed x22, other arithmetic  6.08 us
    ppermute x7, waiting for transfers between devices, exchange(): parts.append(lax.ppermute(chunk, axis, swap(axis, step)) if step else chunk)  3.49 us
    another operation x5, other arithmetic  2.44 us
  transfers between devices with their start and end apart: 32, of which 7 were waited for; matrix products, arithmetic and copies ran while one was open for 9% of the time, Pallas kernels for 0%

profile of v2, /device:TPU:0, one launch (start us, length us, event | category | flops | bytes accessed | tf_op | source)
XLA Modules:
  0.0 116.8 jit_solution(13608915109774803115)
XLA Ops:
  0.0 0.8 fusion.65
  0.8 0.8 reshape.282
  1.6 0.8 reshape.284
  3.8 0.8 concatenate.31
  5.2 6.0 %collective-permute-start = (bf16[2,1664]{1,0:T(2,128)(2,1)}, bf16[2,1664]{1,0:T(2,128)(2,1)S(1)}, u32[]{:S(2)}, u32[]{:S(2)}) collective-permute-start(bf16[2,1664]{1,0:T(2,128)(2,1)} %pad.8), channel_id=1, source_target_pairs={{0,28},{4,24},{8,20},{12,16},{16,12},{20,8},{24,4},{28,0},{1,29},{... | collective-permute-start | bytes 19976 | tf_op jit(solution)/shard_map/ppermute | solution.py:82
  11.4 0.7 collective-permute-start.2
  12.1 2.0 %collective-permute-start.3 = (bf16[2,1664]{1,0:T(2,128)(2,1)}, bf16[2,1664]{1,0:T(2,128)(2,1)}, u32[]{:S(2)}, u32[]{:S(2)}) collective-permute-start(bf16[2,1664]{1,0:T(2,128)(2,1)} %pad.8), channel_id=1, source_target_pairs={{0,16},{4,20},{8,24},{12,28},{16,0},{20,4},{24,8},{28,12},{1,17},{... | collective-permute-start | bytes 19976 | tf_op jit(solution)/shard_map/ppermute | solution.py:82
  14.1 2.4 %collective-permute-start.4 = (bf16[2,1664]{1,0:T(2,128)(2,1)}, bf16[2,1664]{1,0:T(2,128)(2,1)}, u32[]{:S(2)}, u32[]{:S(2)}) collective-permute-start(bf16[2,1664]{1,0:T(2,128)(2,1)} %pad.8), channel_id=1, source_target_pairs={{0,12},{4,8},{8,4},{12,0},{16,28},{20,24},{24,20},{28,16},{1,13},{... | collective-permute-start | bytes 19976 | tf_op jit(solution)/shard_map/ppermute | solution.py:82
  17.7 1.3 %multiply_convert_fusion.3 = bf16[2,768]{1,0:T(2,128)(2,1)} fusion(f32[2,768]{1,0:T(2,128)S(1)} %mul.235, bf16[2,768]{1,0:T(2,128)(2,1)} %param.16), kind=kLoop, calls=%fused_computation.182 | loop fusion | flops 4608 | bytes 12288 | tf_op jit(solution)/shard_map/convert.6
  19.5 0.8 collective-permute-start.5
  21.2 4.0 %copy.38 = bf16[5,256,768]{1,2,0:T(8,128)(2,1)} copy(bf16[5,256,768]{2,1,0:T(8,128)(2,1)} %param.17) | data formatting | bytes 3932160 | tf_op args[4]
  25.2 2.7 %copy.39 = bf16[5,256,768]{1,2,0:T(8,128)(2,1)S(1)} copy(bf16[5,256,768]{2,1,0:T(8,128)(2,1)} %param.18) | data formatting | bytes 3932160 | tf_op args[5]
  27.9 1.4 %constant_dynamic-update-slice_fusion.7 = (bf16[8,2,1664]{2,1,0:T(2,128)(2,1)}, bf16[2,1664]{1,0:T(2,128)(2,1)S(1)}, bf16[2,1664]{1,0:T(2,128)(2,1)S(1)}, bf16[2,1664]{1,0:T(2,128)(2,1)S(1)}, bf16[2,1664]{1,0:T(2,128)(2,1)S(1)}) fusion(pred[]{:T(512)S(6)} %ne.105, pred[]{:T(512)S(6)} %ne.106, bf16[2,1664]{1,0:T(2,128)(2,1)} %collective-permute-done.6, ...), kind=kLoop, calls=%fused_computation.34 | loop fusion | flops 23295 | bytes 86091
  29.3 1.4 %constant_dynamic-update-slice_fusion.6 = (bf16[8,2,1664]{2,1,0:T(2,128)(2,1)}, bf16[2,1664]{1,0:T(2,128)(2,1)S(1)}, bf16[2,1664]{1,0:T(2,128)(2,1)S(1)}, bf16[2,1664]{1,0:T(2,128)(2,1)S(1)}, bf16[2,1664]{1,0:T(2,128)(2,1)S(1)}) fusion(bf16[8,2,1664]{2,1,0:T(2,128)(2,1)} %get-tuple-element.32, pred[]{:T(512)S(6)} %ne.105, pred[]{:T(512)S(6)} %ne.106, ...), kind=kLoop, calls=%fused_computation.33 | loop fusion | flops 23296 | bytes 86091
  34.3 1.4 %reshape.271 = bf16[16,1664]{1,0:T(8,128)(2,1)} reshape(bf16[8,2,1664]{2,1,0:T(2,128)(2,1)} %constant_dynamic-update-slice_fusion) | data formatting | bytes 106496 | tf_op jit(solution)/shard_map/reshape | solution.py:144
  35.7 0.8 add_add_fusion
  36.6 1.5 %add_reduce_fusion = s32[16]{0:T(128)} fusion(bf16[16,1664]{1,0:T(8,128)(2,1)} %reshape.271), kind=kLoop, calls=%fused_computation.151 | loop fusion | flops 64 | bytes 128 | tf_op jit(solution)/shard_map/add | solution.py:40
  38.2 0.7 compare_reduce_fusion.1
  38.9 1.4 %fusion.27 = s32[5]{0:T(128)} fusion(s32[16,8]{0,1:T(8,128)S(1)} %copy.37, s32[5]{0:T(128)} %iota_add_fusion), kind=kLoop, calls=%fused_computation.79 | loop fusion | flops 1915 | bytes 552 | tf_op jit(solution)/shard_map/reduce_sum | solution.py:154
  40.3 1.5 %convolution_convert_fusion.2 = bf16[5,768]{1,0:T(8,128)(2,1)} fusion(pred[5,16]{1,0:T(8,128)(4,1)S(1)} %compare_reduce_fusion.1, bf16[16,1664]{1,0:T(8,128)(2,1)} %reshape.271), kind=kOutput, calls=%fused_computation.6 | convolution fusion | flops 126720 | bytes 32336 | tf_op jit(solution)/shard_map/dot_general | solution.py:158
  41.7 1.4 %reshape.292 = bf16[5,8,96,1]{2,3,1,0:T(2,128)(2,1)} reshape(bf16[5,768]{1,0:T(8,128)(2,1)} %convolution_convert_fusion.2) | data formatting | bytes 15360 | tf_op jit(solution)/shard_map/reshape | solution.py:159
  43.1 0.8 select_reduce_fusion.1
  44.5 1.9 %fusion.70 = f32[5,8,1,256]{3,2,1,0:T(1,128)S(1)} fusion(bf16[5,8,96,1]{2,3,1,0:T(2,128)(2,1)} %reshape.292, bf16[5,256,8,96]{1,3,2,0:T(8,128)(2,1)} %bitcast.149), kind=kOutput, calls=%fused_computation.234 | convolution fusion | flops 1966080 | bytes 2014720 | tf_op jit(solution)/shard_map/bhd,bthd->bht/dot_general | solution.py:163
  48.7 0.7 fusion.32
  49.5 2.4 %collective-permute-start.10 = (bf16[7,896]{1,0:T(8,128)(2,1)S(1)}, bf16[7,896]{1,0:T(8,128)(2,1)S(1)}, u32[]{:S(2)}, u32[]{:S(2)}) collective-permute-start(bf16[7,896]{1,0:T(8,128)(2,1)S(1)} %fusion.32), channel_id=1, source_target_pairs={{0,16},{4,20},{8,24},{12,28},{16,0},{20,4},{24,8},{28,12},{1,17},{... | collective-permute-start | bytes 37640 | tf_op jit(solution)/shard_map/ppermute | solution.py:82
  51.9 2.9 %collective-permute-start.11 = (bf16[7,896]{1,0:T(8,128)(2,1)S(1)}, bf16[7,896]{1,0:T(8,128)(2,1)S(1)}, u32[]{:S(2)}, u32[]{:S(2)}) collective-permute-start(bf16[7,896]{1,0:T(8,128)(2,1)S(1)} %fusion.32), channel_id=1, source_target_pairs={{0,12},{4,8},{8,4},{12,0},{16,28},{20,24},{24,20},{28,16},{1,13},{... | collective-permute-start | bytes 37640 | tf_op jit(solution)/shard_map/ppermute | solution.py:82
  55.4 2.4 %collective-permute-start.7 = (bf16[7,896]{1,0:T(8,128)(2,1)S(1)}, bf16[7,896]{1,0:T(8,128)(2,1)S(1)}, u32[]{:S(2)}, u32[]{:S(2)}) collective-permute-start(bf16[7,896]{1,0:T(8,128)(2,1)S(1)} %fusion.32), channel_id=1, source_target_pairs={{0,28},{4,24},{8,20},{12,16},{16,12},{20,8},{24,4},{28,0},{1,29},{... | collective-permute-start | bytes 37640 | tf_op jit(solution)/shard_map/ppermute | solution.py:82
  57.8 0.7 compare_reduce_fusion
  58.5 2.4 %collective-permute-start.8 = (bf16[7,896]{1,0:T(8,128)(2,1)S(1)}, bf16[7,896]{1,0:T(8,128)(2,1)S(1)}, u32[]{:S(2)}, u32[]{:S(2)}) collective-permute-start(bf16[7,896]{1,0:T(8,128)(2,1)S(1)} %fusion.32), channel_id=1, source_target_pairs={{0,24},{4,28},{8,16},{12,20},{16,8},{20,12},{24,0},{28,4},{1,25},{... | collective-permute-start | bytes 37640 | tf_op jit(solution)/shard_map/ppermute | solution.py:82
  61.8 2.3 %collective-permute-done.8 = bf16[7,896]{1,0:T(8,128)(2,1)S(1)} collective-permute-done((bf16[7,896]{1,0:T(8,128)(2,1)S(1)}, bf16[7,896]{1,0:T(8,128)(2,1)S(1)}, u32[]{:S(2)}, u32[]{:S(2)}) %collective-permute-start.8) | collective-permute-done | bytes 12576 | tf_op jit(solution)/shard_map/ppermute | solution.py:82
  64.1 2.4 %collective-permute-done.9 = bf16[7,896]{1,0:T(8,128)(2,1)S(1)} collective-permute-done((bf16[7,896]{1,0:T(8,128)(2,1)S(1)}, bf16[7,896]{1,0:T(8,128)(2,1)S(1)}, u32[]{:S(2)}, u32[]{:S(2)}) %collective-permute-start.9) | collective-permute-done | bytes 12576 | tf_op jit(solution)/shard_map/ppermute | solution.py:82
  68.4 1.5 %collective-permute-start.14 = (bf16[16,384]{1,0:T(8,128)(2,1)S(1)}, bf16[16,384]{1,0:T(8,128)(2,1)S(1)}, u32[]{:S(2)}, u32[]{:S(2)}) collective-permute-start(bf16[16,384]{1,0:T(8,128)(2,1)S(1)} %convolution_convert_fusion.3), channel_id=1, source_target_pairs={{0,28},{1,24},{2,20},{3,16},{4,12},{5,8},{6,4},{7,0},{8,29},{9,25}... | collective-permute-start | bytes 36872 | tf_op jit(solution)/shard_map/ppermute | solution.py:95
  69.8 2.1 %collective-permute-start.15 = (bf16[16,384]{1,0:T(8,128)(2,1)S(1)}, bf16[16,384]{1,0:T(8,128)(2,1)S(1)}, u32[]{:S(2)}, u32[]{:S(2)}) collective-permute-start(bf16[16,384]{1,0:T(8,128)(2,1)S(1)} %convolution_convert_fusion.3), channel_id=1, source_target_pairs={{0,24},{1,28},{2,16},{3,20},{4,8},{5,12},{6,0},{7,4},{8,25},{9,29}... | collective-permute-start | bytes 36872 | tf_op jit(solution)/shard_map/ppermute | solution.py:95
  71.9 3.9 %collective-permute-start.16 = (bf16[16,384]{1,0:T(8,128)(2,1)S(1)}, bf16[16,384]{1,0:T(8,128)(2,1)S(1)}, u32[]{:S(2)}, u32[]{:S(2)}) collective-permute-start(bf16[16,384]{1,0:T(8,128)(2,1)S(1)} %convolution_convert_fusion.3), channel_id=1, source_target_pairs={{0,20},{1,16},{2,28},{3,24},{4,4},{5,0},{6,12},{7,8},{8,21},{9,17}... | collective-permute-start | bytes 36872 | tf_op jit(solution)/shard_map/ppermute | solution.py:95
  75.8 2.0 %collective-permute-start.17 = (bf16[16,384]{1,0:T(8,128)(2,1)S(1)}, bf16[16,384]{1,0:T(8,128)(2,1)S(1)}, u32[]{:S(2)}, u32[]{:S(2)}) collective-permute-start(bf16[16,384]{1,0:T(8,128)(2,1)S(1)} %convolution_convert_fusion.3), channel_id=1, source_target_pairs={{0,16},{1,20},{2,24},{3,28},{4,0},{5,4},{6,8},{7,12},{8,17},{9,21}... | collective-permute-start | bytes 36872 | tf_op jit(solution)/shard_map/ppermute | solution.py:95
  77.9 2.1 %collective-permute-start.18 = (bf16[16,384]{1,0:T(8,128)(2,1)S(1)}, bf16[16,384]{1,0:T(8,128)(2,1)S(1)}, u32[]{:S(2)}, u32[]{:S(2)}) collective-permute-start(bf16[16,384]{1,0:T(8,128)(2,1)S(1)} %convolution_convert_fusion.3), channel_id=1, source_target_pairs={{0,12},{1,8},{2,4},{3,0},{4,28},{5,24},{6,20},{7,16},{8,13},{9,9},... | collective-permute-start | bytes 36872 | tf_op jit(solution)/shard_map/ppermute | solution.py:95
  80.1 3.2 %collective-permute-start.20 = (bf16[16,384]{1,0:T(8,128)(2,1)S(1)}, bf16[16,384]{1,0:T(8,128)(2,1)S(1)}, u32[]{:S(2)}, u32[]{:S(2)}) collective-permute-start(bf16[16,384]{1,0:T(8,128)(2,1)S(1)} %convolution_convert_fusion.3), channel_id=1, source_target_pairs={{0,4},{1,0},{2,12},{3,8},{4,20},{5,16},{6,28},{7,24},{8,5},{9,1},{... | collective-permute-start | bytes 36872 | tf_op jit(solution)/shard_map/ppermute | solution.py:95
  84.9 0.9 multiply_reduce_fusion
  86.6 7.0 %collective-permute-start.22 = (bf16[16,2176]{1,0:T(8,128)(2,1)S(1)}, bf16[16,2176]{1,0:T(8,128)(2,1)S(1)}, u32[]{:S(2)}, u32[]{:S(2)}) collective-permute-start(bf16[16,2176]{1,0:T(8,128)(2,1)S(1)} %concatenate.38), channel_id=1, source_target_pairs={{0,3},{1,2},{2,1},{3,0},{4,7},{5,6},{6,5},{7,4},{8,11},{9,10},{10,... | collective-permute-start | bytes 208904 | tf_op jit(solution)/shard_map/ppermute | solution.py:82
  93.6 3.9 %collective-permute-start.23 = (bf16[16,2176]{1,0:T(8,128)(2,1)S(1)}, bf16[16,2176]{1,0:T(8,128)(2,1)S(1)}, u32[]{:S(2)}, u32[]{:S(2)}) collective-permute-start(bf16[16,2176]{1,0:T(8,128)(2,1)S(1)} %concatenate.38), channel_id=1, source_target_pairs={{0,2},{1,3},{2,0},{3,1},{4,6},{5,7},{6,4},{7,5},{8,10},{9,11},{10,... | collective-permute-start | bytes 208904 | tf_op jit(solution)/shard_map/ppermute | solution.py:82
  97.5 3.2 %collective-permute-done.23 = bf16[16,2176]{1,0:T(8,128)(2,1)S(1)} collective-permute-done((bf16[16,2176]{1,0:T(8,128)(2,1)S(1)}, bf16[16,2176]{1,0:T(8,128)(2,1)S(1)}, u32[]{:S(2)}, u32[]{:S(2)}) %collective-permute-start.23) | collective-permute-done | bytes 69664 | tf_op jit(solution)/shard_map/ppermute | solution.py:82
  101.5 2.0 %collective-permute-start.25 = (f32[2,768]{1,0:T(2,128)S(1)}, f32[2,768]{1,0:T(2,128)S(1)}, u32[]{:S(2)}, u32[]{:S(2)}) collective-permute-start(f32[2,768]{1,0:T(2,128)S(1)} %get-tuple-element.46), channel_id=1, source_target_pairs={{0,4},{4,0},{8,12},{12,8},{16,20},{20,16},{24,28},{28,24},{1,5},{5... | collective-permute-start | bytes 18440 | tf_op jit(solution)/shard_map/ppermute | solution.py:71
  103.6 1.5 %collective-permute-start.27 = (f32[2,768]{1,0:T(2,128)S(1)}, f32[2,768]{1,0:T(2,128)S(1)}, u32[]{:S(2)}, u32[]{:S(2)}) collective-permute-start(f32[2,768]{1,0:T(2,128)S(1)} %get-tuple-element.51), channel_id=1, source_target_pairs={{0,12},{4,8},{8,4},{12,0},{16,28},{20,24},{24,20},{28,16},{1,13},{... | collective-permute-start | bytes 18440 | tf_op jit(solution)/shard_map/ppermute | solution.py:71
  105.1 0.9 collective-permute-start.28
  106.0 3.4 %collective-permute-start.29 = (f32[2,768]{1,0:T(2,128)S(1)}, f32[2,768]{1,0:T(2,128)S(1)}, u32[]{:S(2)}, u32[]{:S(2)}) collective-permute-start(f32[2,768]{1,0:T(2,128)S(1)} %get-tuple-element.49), channel_id=1, source_target_pairs={{0,20},{4,16},{8,28},{12,24},{16,4},{20,0},{24,12},{28,8},{1,21},{... | collective-permute-start | bytes 18440 | tf_op jit(solution)/shard_map/ppermute | solution.py:71
  109.9 2.8 %collective-permute-start.31 = (f32[2,768]{1,0:T(2,128)S(1)}, f32[2,768]{1,0:T(2,128)S(1)}, u32[]{:S(2)}, u32[]{:S(2)}) collective-permute-start(f32[2,768]{1,0:T(2,128)S(1)} %get-tuple-element.47), channel_id=1, source_target_pairs={{0,28},{4,24},{8,20},{12,16},{16,12},{20,8},{24,4},{28,0},{1,29},{... | collective-permute-start | bytes 18440 | tf_op jit(solution)/shard_map/ppermute | solution.py:71
  112.8 2.1 %collective-permute-done.30 = f32[2,768]{1,0:T(2,128)S(1)} collective-permute-done((f32[2,768]{1,0:T(2,128)S(1)}, f32[2,768]{1,0:T(2,128)S(1)}, u32[]{:S(2)}, u32[]{:S(2)}) %collective-permute-start.30) | collective-permute-done | bytes 6176 | tf_op jit(solution)/shard_map/ppermute | solution.py:71
  114.8 1.4 %collective-permute-done.31 = f32[2,768]{1,0:T(2,128)S(1)} collective-permute-done((f32[2,768]{1,0:T(2,128)S(1)}, f32[2,768]{1,0:T(2,128)S(1)}, u32[]{:S(2)}, u32[]{:S(2)}) %collective-permute-start.31) | collective-permute-done | bytes 6176 | tf_op jit(solution)/shard_map/ppermute | solution.py:71
  (136 shorter events, 19.1 us)
Async XLA Ops:
  0.0 85.7 %copy-start = (bf16[768,1024]{1,0:T(8,128)(2,1)S(1)}, bf16[768,1024]{1,0:T(8,128)(2,1)}, u32[]{:S(2)}) copy-start(bf16[768,1024]{1,0:T(8,128)(2,1)} %param.24) | copy-start | bytes 4718596
  5.2 14.4 %collective-permute-start = (bf16[2,1664]{1,0:T(2,128)(2,1)}, bf16[2,1664]{1,0:T(2,128)(2,1)S(1)}, u32[]{:S(2)}, u32[]{:S(2)}) collective-permute-start(bf16[2,1664]{1,0:T(2,128)(2,1)} %pad.8), channel_id=1, source_target_pairs={{0,28},{4,24},{8,20},{12,16},{16,12},{20,8},{24,4},{28,0},{1,29},{... | collective-permute-start | bytes 19976 | tf_op jit(solution)/shard_map/ppermute | solution.py:82
  11.2 9.1 %collective-permute-start.1 = (bf16[2,1664]{1,0:T(2,128)(2,1)}, bf16[2,1664]{1,0:T(2,128)(2,1)S(1)}, u32[]{:S(2)}, u32[]{:S(2)}) collective-permute-start(bf16[2,1664]{1,0:T(2,128)(2,1)} %pad.8), channel_id=1, source_target_pairs={{0,24},{4,28},{8,16},{12,20},{16,8},{20,12},{24,0},{28,4},{1,25},{... | collective-permute-start | bytes 19976 | tf_op jit(solution)/shard_map/ppermute | solution.py:82
  11.4 16.5 %collective-permute-start.2 = (bf16[2,1664]{1,0:T(2,128)(2,1)}, bf16[2,1664]{1,0:T(2,128)(2,1)}, u32[]{:S(2)}, u32[]{:S(2)}) collective-permute-start(bf16[2,1664]{1,0:T(2,128)(2,1)} %pad.8), channel_id=1, source_target_pairs={{0,20},{4,16},{8,28},{12,24},{16,4},{20,0},{24,12},{28,8},{1,21},{... | collective-permute-start | bytes 19976 | tf_op jit(solution)/shard_map/ppermute | solution.py:82
  12.1 15.7 %collective-permute-start.3 = (bf16[2,1664]{1,0:T(2,128)(2,1)}, bf16[2,1664]{1,0:T(2,128)(2,1)}, u32[]{:S(2)}, u32[]{:S(2)}) collective-permute-start(bf16[2,1664]{1,0:T(2,128)(2,1)} %pad.8), channel_id=1, source_target_pairs={{0,16},{4,20},{8,24},{12,28},{16,0},{20,4},{24,8},{28,12},{1,17},{... | collective-permute-start | bytes 19976 | tf_op jit(solution)/shard_map/ppermute | solution.py:82
  14.1 13.8 %collective-permute-start.4 = (bf16[2,1664]{1,0:T(2,128)(2,1)}, bf16[2,1664]{1,0:T(2,128)(2,1)}, u32[]{:S(2)}, u32[]{:S(2)}) collective-permute-start(bf16[2,1664]{1,0:T(2,128)(2,1)} %pad.8), channel_id=1, source_target_pairs={{0,12},{4,8},{8,4},{12,0},{16,28},{20,24},{24,20},{28,16},{1,13},{... | collective-permute-start | bytes 19976 | tf_op jit(solution)/shard_map/ppermute | solution.py:82
  17.0 0.6 copy-start.6
  19.5 8.4 %collective-permute-start.5 = (bf16[2,1664]{1,0:T(2,128)(2,1)}, bf16[2,1664]{1,0:T(2,128)(2,1)}, u32[]{:S(2)}, u32[]{:S(2)}) collective-permute-start(bf16[2,1664]{1,0:T(2,128)(2,1)} %pad.8), channel_id=1, source_target_pairs={{0,8},{4,12},{8,0},{12,4},{16,24},{20,28},{24,16},{28,20},{1,9},{5... | collective-permute-start | bytes 19976 | tf_op jit(solution)/shard_map/ppermute | solution.py:82
  20.3 0.9 copy-start.4
  20.3 7.6 %collective-permute-start.6 = (bf16[2,1664]{1,0:T(2,128)(2,1)}, bf16[2,1664]{1,0:T(2,128)(2,1)}, u32[]{:S(2)}, u32[]{:S(2)}) collective-permute-start(bf16[2,1664]{1,0:T(2,128)(2,1)} %pad.8), channel_id=1, source_target_pairs={{0,4},{4,0},{8,12},{12,8},{16,20},{20,16},{24,28},{28,24},{1,5},{5... | collective-permute-start | bytes 19976 | tf_op jit(solution)/shard_map/ppermute | solution.py:82
  46.4 2.3 %copy-start.5 = (bf16[2,768]{1,0:T(2,128)(2,1)S(1)}, bf16[2,768]{1,0:T(2,128)(2,1)}, u32[]{:S(2)}) copy-start(bf16[2,768]{1,0:T(2,128)(2,1)} %multiply_convert_fusion.3) | copy-start | bytes 9220
  49.5 9.0 %collective-permute-start.10 = (bf16[7,896]{1,0:T(8,128)(2,1)S(1)}, bf16[7,896]{1,0:T(8,128)(2,1)S(1)}, u32[]{:S(2)}, u32[]{:S(2)}) collective-permute-start(bf16[7,896]{1,0:T(8,128)(2,1)S(1)} %fusion.32), channel_id=1, source_target_pairs={{0,16},{4,20},{8,24},{12,28},{16,0},{20,4},{24,8},{28,12},{1,17},{... | collective-permute-start | bytes 37640 | tf_op jit(solution)/shard_map/ppermute | solution.py:82
  51.9 9.1 %collective-permute-start.11 = (bf16[7,896]{1,0:T(8,128)(2,1)S(1)}, bf16[7,896]{1,0:T(8,128)(2,1)S(1)}, u32[]{:S(2)}, u32[]{:S(2)}) collective-permute-start(bf16[7,896]{1,0:T(8,128)(2,1)S(1)} %fusion.32), channel_id=1, source_target_pairs={{0,12},{4,8},{8,4},{12,0},{16,28},{20,24},{24,20},{28,16},{1,13},{... | collective-permute-start | bytes 37640 | tf_op jit(solution)/shard_map/ppermute | solution.py:82
  54.8 6.8 %collective-permute-start.12 = (bf16[7,896]{1,0:T(8,128)(2,1)S(1)}, bf16[7,896]{1,0:T(8,128)(2,1)S(1)}, u32[]{:S(2)}, u32[]{:S(2)}) collective-permute-start(bf16[7,896]{1,0:T(8,128)(2,1)S(1)} %fusion.32), channel_id=1, source_target_pairs={{0,8},{4,12},{8,0},{12,4},{16,24},{20,28},{24,16},{28,20},{1,9},{5... | collective-permute-start | bytes 37640 | tf_op jit(solution)/shard_map/ppermute | solution.py:82
  54.8 6.7 %collective-permute-start.13 = (bf16[7,896]{1,0:T(8,128)(2,1)S(1)}, bf16[7,896]{1,0:T(8,128)(2,1)S(1)}, u32[]{:S(2)}, u32[]{:S(2)}) collective-permute-start(bf16[7,896]{1,0:T(8,128)(2,1)S(1)} %fusion.32), channel_id=1, source_target_pairs={{0,4},{4,0},{8,12},{12,8},{16,20},{20,16},{24,28},{28,24},{1,5},{5... | collective-permute-start | bytes 37640 | tf_op jit(solution)/shard_map/ppermute | solution.py:82
  55.4 6.4 %collective-permute-start.7 = (bf16[7,896]{1,0:T(8,128)(2,1)S(1)}, bf16[7,896]{1,0:T(8,128)(2,1)S(1)}, u32[]{:S(2)}, u32[]{:S(2)}) collective-permute-start(bf16[7,896]{1,0:T(8,128)(2,1)S(1)} %fusion.32), channel_id=1, source_target_pairs={{0,28},{4,24},{8,20},{12,16},{16,12},{20,8},{24,4},{28,0},{1,29},{... | collective-permute-start | bytes 37640 | tf_op jit(solution)/shard_map/ppermute | solution.py:82
  58.5 5.6 %collective-permute-start.8 = (bf16[7,896]{1,0:T(8,128)(2,1)S(1)}, bf16[7,896]{1,0:T(8,128)(2,1)S(1)}, u32[]{:S(2)}, u32[]{:S(2)}) collective-permute-start(bf16[7,896]{1,0:T(8,128)(2,1)S(1)} %fusion.32), channel_id=1, source_target_pairs={{0,24},{4,28},{8,16},{12,20},{16,8},{20,12},{24,0},{28,4},{1,25},{... | collective-permute-start | bytes 37640 | tf_op jit(solution)/shard_map/ppermute | solution.py:82
  60.9 5.5 %collective-permute-start.9 = (bf16[7,896]{1,0:T(8,128)(2,1)S(1)}, bf16[7,896]{1,0:T(8,128)(2,1)S(1)}, u32[]{:S(2)}, u32[]{:S(2)}) collective-permute-start(bf16[7,896]{1,0:T(8,128)(2,1)S(1)} %fusion.32), channel_id=1, source_target_pairs={{0,20},{4,16},{8,28},{12,24},{16,4},{20,0},{24,12},{28,8},{1,21},{... | collective-permute-start | bytes 37640 | tf_op jit(solution)/shard_map/ppermute | solution.py:82
  66.5 1.7 %copy-start.3 = (bf16[768,384]{1,0:T(8,128)(2,1)S(1)}, bf16[768,384]{1,0:T(8,128)(2,1)}, u32[]{:S(2)}) copy-start(bf16[768,384]{1,0:T(8,128)(2,1)} %param.21) | copy-start | bytes 1769476
  66.6 17.3 %copy-start.7 = (bf16[768]{0:T(1024)(128)(2,1)S(1)}, bf16[768]{0:T(1024)(128)(2,1)}, u32[]{:S(2)}) copy-start(bf16[768]{0:T(1024)(128)(2,1)} %param.22) | copy-start | bytes 4612
  68.3 17.7 %copy-start.1 = (bf16[768,1024]{1,0:T(8,128)(2,1)S(1)}, bf16[768,1024]{1,0:T(8,128)(2,1)}, u32[]{:S(2)}) copy-start(bf16[768,1024]{1,0:T(8,128)(2,1)} %param.23) | copy-start | bytes 4718596
  68.4 11.6 %collective-permute-start.14 = (bf16[16,384]{1,0:T(8,128)(2,1)S(1)}, bf16[16,384]{1,0:T(8,128)(2,1)S(1)}, u32[]{:S(2)}, u32[]{:S(2)}) collective-permute-start(bf16[16,384]{1,0:T(8,128)(2,1)S(1)} %convolution_convert_fusion.3), channel_id=1, source_target_pairs={{0,28},{1,24},{2,20},{3,16},{4,12},{5,8},{6,4},{7,0},{8,29},{9,25}... | collective-permute-start | bytes 36872 | tf_op jit(solution)/shard_map/ppermute | solution.py:95
  69.8 10.2 %collective-permute-start.15 = (bf16[16,384]{1,0:T(8,128)(2,1)S(1)}, bf16[16,384]{1,0:T(8,128)(2,1)S(1)}, u32[]{:S(2)}, u32[]{:S(2)}) collective-permute-start(bf16[16,384]{1,0:T(8,128)(2,1)S(1)} %convolution_convert_fusion.3), channel_id=1, source_target_pairs={{0,24},{1,28},{2,16},{3,20},{4,8},{5,12},{6,0},{7,4},{8,25},{9,29}... | collective-permute-start | bytes 36872 | tf_op jit(solution)/shard_map/ppermute | solution.py:95
  71.9 11.3 %collective-permute-start.16 = (bf16[16,384]{1,0:T(8,128)(2,1)S(1)}, bf16[16,384]{1,0:T(8,128)(2,1)S(1)}, u32[]{:S(2)}, u32[]{:S(2)}) collective-permute-start(bf16[16,384]{1,0:T(8,128)(2,1)S(1)} %convolution_convert_fusion.3), channel_id=1, source_target_pairs={{0,20},{1,16},{2,28},{3,24},{4,4},{5,0},{6,12},{7,8},{8,21},{9,17}... | collective-permute-start | bytes 36872 | tf_op jit(solution)/shard_map/ppermute | solution.py:95
  75.8 8.1 %collective-permute-start.17 = (bf16[16,384]{1,0:T(8,128)(2,1)S(1)}, bf16[16,384]{1,0:T(8,128)(2,1)S(1)}, u32[]{:S(2)}, u32[]{:S(2)}) collective-permute-start(bf16[16,384]{1,0:T(8,128)(2,1)S(1)} %convolution_convert_fusion.3), channel_id=1, source_target_pairs={{0,16},{1,20},{2,24},{3,28},{4,0},{5,4},{6,8},{7,12},{8,17},{9,21}... | collective-permute-start | bytes 36872 | tf_op jit(solution)/shard_map/ppermute | solution.py:95
  77.9 6.0 %collective-permute-start.18 = (bf16[16,384]{1,0:T(8,128)(2,1)S(1)}, bf16[16,384]{1,0:T(8,128)(2,1)S(1)}, u32[]{:S(2)}, u32[]{:S(2)}) collective-permute-start(bf16[16,384]{1,0:T(8,128)(2,1)S(1)} %convolution_convert_fusion.3), channel_id=1, source_target_pairs={{0,12},{1,8},{2,4},{3,0},{4,28},{5,24},{6,20},{7,16},{8,13},{9,9},... | collective-permute-start | bytes 36872 | tf_op jit(solution)/shard_map/ppermute | solution.py:95
  80.0 4.0 %collective-permute-start.19 = (bf16[16,384]{1,0:T(8,128)(2,1)S(1)}, bf16[16,384]{1,0:T(8,128)(2,1)S(1)}, u32[]{:S(2)}, u32[]{:S(2)}) collective-permute-start(bf16[16,384]{1,0:T(8,128)(2,1)S(1)} %convolution_convert_fusion.3), channel_id=1, source_target_pairs={{0,8},{1,12},{2,0},{3,4},{4,24},{5,28},{6,16},{7,20},{8,9},{9,13},... | collective-permute-start | bytes 36872 | tf_op jit(solution)/shard_map/ppermute | solution.py:95
  80.1 4.6 %collective-permute-start.20 = (bf16[16,384]{1,0:T(8,128)(2,1)S(1)}, bf16[16,384]{1,0:T(8,128)(2,1)S(1)}, u32[]{:S(2)}, u32[]{:S(2)}) collective-permute-start(bf16[16,384]{1,0:T(8,128)(2,1)S(1)} %convolution_convert_fusion.3), channel_id=1, source_target_pairs={{0,4},{1,0},{2,12},{3,8},{4,20},{5,16},{6,28},{7,24},{8,5},{9,1},{... | collective-permute-start | bytes 36872 | tf_op jit(solution)/shard_map/ppermute | solution.py:95
  83.2 1.4 %collective-permute-start.21 = (bf16[16,384]{1,0:T(8,128)(2,1)S(1)}, bf16[16,384]{1,0:T(8,128)(2,1)S(1)}, u32[]{:S(2)}, u32[]{:S(2)}) collective-permute-start(bf16[16,384]{1,0:T(8,128)(2,1)S(1)} %convolution_convert_fusion.3), channel_id=1, source_target_pairs={{0,0},{1,4},{2,8},{3,12},{4,16},{5,20},{6,24},{7,28},{8,1},{9,5},{... | collective-permute-start | bytes 36872 | tf_op jit(solution)/shard_map/ppermute | solution.py:95
  86.1 15.0 %copy-start.2 = (bf16[1024,768]{1,0:T(8,128)(2,1)S(1)}, bf16[1024,768]{1,0:T(8,128)(2,1)}, u32[]{:S(2)}) copy-start(bf16[1024,768]{1,0:T(8,128)(2,1)} %param.25) | copy-start | bytes 4718596
  86.6 10.9 %collective-permute-start.22 = (bf16[16,2176]{1,0:T(8,128)(2,1)S(1)}, bf16[16,2176]{1,0:T(8,128)(2,1)S(1)}, u32[]{:S(2)}, u32[]{:S(2)}) collective-permute-start(bf16[16,2176]{1,0:T(8,128)(2,1)S(1)} %concatenate.38), channel_id=1, source_target_pairs={{0,3},{1,2},{2,1},{3,0},{4,7},{5,6},{6,5},{7,4},{8,11},{9,10},{10,... | collective-permute-start | bytes 208904 | tf_op jit(solution)/shard_map/ppermute | solution.py:82
  93.6 7.2 %collective-permute-start.23 = (bf16[16,2176]{1,0:T(8,128)(2,1)S(1)}, bf16[16,2176]{1,0:T(8,128)(2,1)S(1)}, u32[]{:S(2)}, u32[]{:S(2)}) collective-permute-start(bf16[16,2176]{1,0:T(8,128)(2,1)S(1)} %concatenate.38), channel_id=1, source_target_pairs={{0,2},{1,3},{2,0},{3,1},{4,6},{5,7},{6,4},{7,5},{8,10},{9,11},{10,... | collective-permute-start | bytes 208904 | tf_op jit(solution)/shard_map/ppermute | solution.py:82
  97.5 3.3 %collective-permute-start.24 = (bf16[16,2176]{1,0:T(8,128)(2,1)S(1)}, bf16[16,2176]{1,0:T(8,128)(2,1)S(1)}, u32[]{:S(2)}, u32[]{:S(2)}) collective-permute-start(bf16[16,2176]{1,0:T(8,128)(2,1)S(1)} %concatenate.38), channel_id=1, source_target_pairs={{0,1},{1,0},{2,3},{3,2},{4,5},{5,4},{6,7},{7,6},{8,9},{9,8},{10,11... | collective-permute-start | bytes 208904 | tf_op jit(solution)/shard_map/ppermute | solution.py:82
  101.5 7.9 %collective-permute-start.25 = (f32[2,768]{1,0:T(2,128)S(1)}, f32[2,768]{1,0:T(2,128)S(1)}, u32[]{:S(2)}, u32[]{:S(2)}) collective-permute-start(f32[2,768]{1,0:T(2,128)S(1)} %get-tuple-element.46), channel_id=1, source_target_pairs={{0,4},{4,0},{8,12},{12,8},{16,20},{20,16},{24,28},{28,24},{1,5},{5... | collective-permute-start | bytes 18440 | tf_op jit(solution)/shard_map/ppermute | solution.py:71
  103.5 6.4 %collective-permute-start.26 = (f32[2,768]{1,0:T(2,128)S(1)}, f32[2,768]{1,0:T(2,128)S(1)}, u32[]{:S(2)}, u32[]{:S(2)}) collective-permute-start(f32[2,768]{1,0:T(2,128)S(1)} %get-tuple-element.52), channel_id=1, source_target_pairs={{0,8},{4,12},{8,0},{12,4},{16,24},{20,28},{24,16},{28,20},{1,9},{5... | collective-permute-start | bytes 18440 | tf_op jit(solution)/shard_map/ppermute | solution.py:71
  103.6 9.2 %collective-permute-start.27 = (f32[2,768]{1,0:T(2,128)S(1)}, f32[2,768]{1,0:T(2,128)S(1)}, u32[]{:S(2)}, u32[]{:S(2)}) collective-permute-start(f32[2,768]{1,0:T(2,128)S(1)} %get-tuple-element.51), channel_id=1, source_target_pairs={{0,12},{4,8},{8,4},{12,0},{16,28},{20,24},{24,20},{28,16},{1,13},{... | collective-permute-start | bytes 18440 | tf_op jit(solution)/shard_map/ppermute | solution.py:71
  105.1 7.7 %collective-permute-start.28 = (f32[2,768]{1,0:T(2,128)S(1)}, f32[2,768]{1,0:T(2,128)S(1)}, u32[]{:S(2)}, u32[]{:S(2)}) collective-permute-start(f32[2,768]{1,0:T(2,128)S(1)} %get-tuple-element.50), channel_id=1, source_target_pairs={{0,16},{4,20},{8,24},{12,28},{16,0},{20,4},{24,8},{28,12},{1,17},{... | collective-permute-start | bytes 18440 | tf_op jit(solution)/shard_map/ppermute | solution.py:71
  106.0 6.7 %collective-permute-start.29 = (f32[2,768]{1,0:T(2,128)S(1)}, f32[2,768]{1,0:T(2,128)S(1)}, u32[]{:S(2)}, u32[]{:S(2)}) collective-permute-start(f32[2,768]{1,0:T(2,128)S(1)} %get-tuple-element.49), channel_id=1, source_target_pairs={{0,20},{4,16},{8,28},{12,24},{16,4},{20,0},{24,12},{28,8},{1,21},{... | collective-permute-start | bytes 18440 | tf_op jit(solution)/shard_map/ppermute | solution.py:71
  109.4 5.4 %collective-permute-start.30 = (f32[2,768]{1,0:T(2,128)S(1)}, f32[2,768]{1,0:T(2,128)S(1)}, u32[]{:S(2)}, u32[]{:S(2)}) collective-permute-start(f32[2,768]{1,0:T(2,128)S(1)} %get-tuple-element.48), channel_id=1, source_target_pairs={{0,24},{4,28},{8,16},{12,20},{16,8},{20,12},{24,0},{28,4},{1,25},{... | collective-permute-start | bytes 18440 | tf_op jit(solution)/shard_map/ppermute | solution.py:71
  109.9 6.3 %collective-permute-start.31 = (f32[2,768]{1,0:T(2,128)S(1)}, f32[2,768]{1,0:T(2,128)S(1)}, u32[]{:S(2)}, u32[]{:S(2)}) collective-permute-start(f32[2,768]{1,0:T(2,128)S(1)} %get-tuple-element.47), channel_id=1, source_target_pairs={{0,28},{4,24},{8,20},{12,16},{16,12},{20,8},{24,4},{28,0},{1,29},{... | collective-permute-start | bytes 18440 | tf_op jit(solution)/shard_map/ppermute | solution.py:71

commit v3 on v1

--- a/solution.py
+++ b/solution.py
@@ -1,8 +1,12 @@
+import functools
 import math
 
 import jax
 import jax.numpy as jnp
+import numpy as np
 from jax import lax
+from jax.experimental import pallas as pl
+from jax.experimental.pallas import tpu as pltpu
 from jax.sharding import PartitionSpec as P
 
 HD = 96
@@ -45,7 +49,7 @@
     return lax.all_to_all(copies, axis, 0, 0)
 
 
-def per_device(
+def per_device_wide(
     residual_in,
     query_new,
     key_new,
@@ -203,6 +207,403 @@
     return (own + jnp.sum(down, 0)).astype(bf16)
 
 
+F32, BF16 = jnp.float32, jnp.bfloat16
+VMEM = pl.BlockSpec(memory_space=pltpu.VMEM)
+SMEM = pl.BlockSpec(memory_space=pltpu.SMEM)
+
+
+def call(kernel, name, outs, args, scratch=(), smem=(), flops=0):
+    size = sum(math.prod(a.shape) * a.dtype.itemsize for a in args)
+    return pl.pallas_call(
+        kernel,
+        out_shape=[jax.ShapeDtypeStruct(shape, dtype) for shape, dtype in outs],
+        in_specs=[SMEM if i in smem else VMEM for i in range(len(args))],
+        out_specs=[VMEM] * len(outs),
+        scratch_shapes=list(scratch),
+        compiler_params=pltpu.CompilerParams(vmem_limit_bytes=16 * 1024 * 1024),
+        cost_estimate=pl.CostEstimate(flops=flops, bytes_accessed=size, transcendentals=0),
+        name=name,
+    )(*args)
+
+
+def lanes(shape):
+    return lax.broadcasted_iota(jnp.int32, shape, len(shape) - 1)
+
+
+def in_order(pieces, index):
+    for bit in (1, 2):
+        odd = (index & bit) != 0
+        pieces = [jnp.where(odd, pieces[s ^ bit], pieces[s]) for s in range(4)]
+    return pieces
+
+
+def rows_of(shape):
+    return lax.broadcasted_iota(jnp.int32, shape, len(shape) - 2)
+
+
+def round_low(values):
+    return values.astype(BF16).astype(F32)
+
+
+def prepare_kernel(table, length, freq, query, key, value, residual, packed, own, scr):
+    rows, width = query.shape
+    heads = width // HD
+    most = table.shape[1]
+    blocks = own.shape[0] - rows - 1
+    scr[...] = jnp.zeros_like(scr)
+    scr[0:rows, :] = query[...].astype(F32)
+    scr[rows : 2 * rows, :] = key[...].astype(F32)
+    values = scr[...]
+    line = rows_of((8, width))
+    where_at = jnp.zeros((8, width), F32)
+    for r in range(rows):
+        here = (line == r) | (line == rows + r)
+        where_at = jnp.where(here, length[r].astype(F32), where_at)
+    angles = where_at * freq[...]
+    lane = lanes((8, width))
+    first = lane % HD < HD // 2
+    ahead = pltpu.roll(values, width - HD // 2, 1)
+    behind = pltpu.roll(values, HD // 2, 1)
+    other = jnp.where(first, -ahead, behind)
+    turned = values * jnp.cos(angles) + other * jnp.sin(angles)
+    scr[...] = round_low(turned)
+    packed[:, :width] = scr[0:rows, :].astype(BF16)
+    packed[:, width : 2 * width] = residual[...]
+    tail = jnp.zeros((rows, 128), F32)
+    at, row = lanes((rows, 128)), rows_of((rows, 128))
+    for r in range(rows):
+        codes = [table[r, k] + 1 for k in range(most)] + [length[r]]
+        spots = [(k, most + k) for k in range(most)] + [(2 * most, 2 * most + 1)]
+        for code, (high, rest) in zip(codes, spots):
+            tail = jnp.where((row == r) & (at == high), (code >> 7).astype(F32), tail)
+            tail = jnp.where((row == r) & (at == rest), (code & 127).astype(F32), tail)
+    packed[:, 2 * width :] = tail.astype(BF16)
+
+    head_mask = lane // HD == line
+    product = scr[0:rows, :] * scr[rows : 2 * rows, :]
+    own[...] = jnp.zeros_like(own)
+    spot = lanes((8, 128))
+    tail = jnp.zeros((8, 128), F32)
+    for r in range(rows):
+        score = jnp.sum(
+            jnp.where(head_mask, jnp.broadcast_to(product[r : r + 1], (8, width)), 0.0),
+            1,
+            keepdims=True,
+        ) * (1.0 / math.sqrt(HD))
+        shift = round_low(score)
+        weight = jnp.exp(score - shift)
+        spread = jnp.sum(jnp.where(head_mask, round_low(weight), 0.0), 0, keepdims=True)
+        own[blocks + r : blocks + r + 1, :width] = spread * value[r : r + 1, :].astype(F32)
+        high = round_low(weight)
+        tail = jnp.where(spot == blocks + r, shift, tail)
+        tail = jnp.where(spot == 8 + blocks + r, high, tail)
+        tail = jnp.where(spot == 16 + blocks + r, weight - high, tail)
+    own[:, width:] = tail
+
+
+def merge_kernel(mine, theirs, both):
+    y = lax.axis_index("pool") % 2
+    both[y] = mine[...]
+    both[1 - y] = theirs[...]
+
+
+def attend_kernel(a0, a1, a2, a3, own, keys, values, part, residual, tables, scr):
+    blocks, block_len, width = keys.shape
+    rows = a0.shape[1]
+    heads = width // HD
+    most = 8
+    me = lax.axis_index("pool")
+    for y in range(2):
+        pieces = [piece[y].astype(F32) for piece in (a0, a1, a2, a3)]
+        for z, piece in enumerate(in_order(pieces, me // 2)):
+            scr[(z * 2 + y) * rows : (z * 2 + y + 1) * rows, :] = piece
+    queries = scr[:, :width]
+    residual[...] = scr[:, width : 2 * width]
+    tail = scr[:, 2 * width :]
+    requests = tail.shape[0]
+    table = tail * CODE + pltpu.roll(tail, 128 - most, 1) - 1.0
+    length = tail[:, 2 * most : 2 * most + 1] * CODE + tail[:, 2 * most + 1 : 2 * most + 2]
+    lane = lanes((requests, 128))
+    table = jnp.where(lane < most, table, -2.0)
+    tables[...] = table
+    head_mask = lanes((heads, width)) // HD == rows_of((heads, width))
+    spot = lanes((heads, 128))
+    token = lanes((heads, block_len)).astype(F32)
+    tail = own[:, width:]
+    part[...] = own[...].astype(BF16)
+    numerators = []
+    for b in range(blocks):
+        match = jnp.where(table == (me * blocks + b).astype(F32), 1.0, 0.0)
+        holder = jnp.sum(match, 1, keepdims=True)
+        place = jnp.sum(jnp.sum(match * lane.astype(F32), 1, keepdims=True), 0, keepdims=True)
+        limit = jnp.sum(holder * length, 0, keepdims=True) - place * block_len
+        query = jnp.sum(holder * queries, 0, keepdims=True)
+        spread = jnp.where(head_mask, query, 0.0).astype(BF16)
+        scores = lax.dot_general(
+            spread, keys[b], (((1,), (1,)), ((), ())), preferred_element_type=F32
+        ) * (1.0 / math.sqrt(HD))
+        valid = token < limit
+        scores = jnp.where(valid, scores, LOW)
+        shift = round_low(jnp.max(scores, 1, keepdims=True))
+        weights = jnp.where(valid, jnp.exp(scores - shift), 0.0)
+        total = jnp.sum(weights, 1, keepdims=True)
+        full = jnp.dot(weights.astype(BF16), values[b], preferred_element_type=F32)
+        numerators.append(jnp.sum(jnp.where(head_mask, full, 0.0), 0, keepdims=True))
+        high = round_low(total)
+        tail = jnp.where(spot == b, shift, tail)
+        tail = jnp.where(spot == 8 + b, high, tail)
+        tail = jnp.where(spot == 16 + b, total - high, tail)
+    line = rows_of((8, width))
+    numer = own[:, :width]
+    for b in range(blocks):
+        numer = jnp.where(line == b, numerators[b], numer)
+    part[:, :width] = numer.astype(BF16)
+    part[:, width:] = tail.astype(BF16)
+
+
+def combine_kernel(b0, b1, b2, b3, tables, weight, head_part, numer, tails, mix):
+    requests = tables.shape[0]
+    slots = b0.shape[1]
+    width = weight.shape[0]
+    heads = width // HD
+    rows, blocks = 2, slots - 3
+    me = lax.axis_index("pool")
+    for step, piece in enumerate((b0, b1, b2, b3)):
+        z = (me // 2) ^ step
+        for y in range(2):
+            owner = z * 2 + y
+            values = piece[y].astype(F32)
+            numer[pl.ds(pl.multiple_of(owner * slots, 8), slots), :] = values[:, :width]
+            tails[owner] = values[:, width:]
+    lane8 = lanes((heads, 128))
+    shifts = jnp.zeros((heads, 128), F32)
+    totals = jnp.zeros((heads, 128), F32)
+    for owner in range(8):
+        tail = tails[owner]
+        total = pltpu.roll(tail, 120, 1) + pltpu.roll(tail, 112, 1)
+        tail, total = jnp.where(lane8 < 8, tail, 0.0), jnp.where(lane8 < 8, total, 0.0)
+        if owner:
+            tail, total = pltpu.roll(tail, 8 * owner, 1), pltpu.roll(total, 8 * owner, 1)
+        shifts, totals = shifts + tail, totals + total
+    lane = lanes((requests, 128))
+    owner, slot = lane // slots, lane % slots
+    block_id = jnp.where((slot < blocks) & (lane < 64), owner * blocks + slot, -5).astype(F32)
+    self_id = jnp.where((slot >= blocks) & (slot < blocks + rows), owner * rows + slot - blocks, -5)
+    table = tables[...]
+    belongs = (self_id == rows_of((requests, 128))) & (lane < 64)
+    for k in range(8):
+        belongs = belongs | (table[:, k : k + 1] == block_id)
+    for h in range(heads):
+        shift = jnp.broadcast_to(shifts[h : h + 1], (requests, 128))
+        top = jnp.max(jnp.where(belongs, shift, LOW), 1, keepdims=True)
+        scale = jnp.where(belongs, jnp.exp(shift - top), 0.0)
+        total = jnp.sum(scale * totals[h : h + 1], 1, keepdims=True)
+        mix[h * requests : (h + 1) * requests, :] = scale / total
+    full = jnp.dot(
+        mix[:, : 8 * slots].astype(BF16), numer[...].astype(BF16), preferred_element_type=F32
+    )
+    head = lanes((requests, width)) // HD
+    attended = jnp.zeros((requests, width), F32)
+    for h in range(heads):
+        attended = jnp.where(head == h, full[h * requests : (h + 1) * requests], attended)
+    head_part[...] = jnp.dot(
+        attended.astype(BF16), weight[...], preferred_element_type=F32
+    ).astype(BF16)
+
+
+def sum_kernel(p0, p1, p2, p3, total):
+    total[...] = (
+        (p0[...].astype(F32) + p1[...].astype(F32)) + (p2[...].astype(F32) + p3[...].astype(F32))
+    ).astype(BF16)
+
+
+def gate_up_kernel(same, flip, all_input, gain, gate, up, sums, own, scr):
+    me = lax.axis_index("pool")
+    odd = me % 2 == 1
+    part = same.shape[1]
+    ff = gate.shape[1]
+    rows = own.shape[0]
+    near, far = same[...].astype(F32), flip[...].astype(F32)
+    scr[:, :part] = all_input[:, :part] + jnp.where(odd, far, near)
+    scr[:, part:] = all_input[:, part:] + jnp.where(odd, near, far)
+    residual = scr[...]
+    mine = scr[0:rows, :]
+    for p in range(1, residual.shape[0] // rows):
+        mine = jnp.where(me == p, scr[p * rows : (p + 1) * rows, :], mine)
+    own[...] = mine
+    square = jnp.sum(residual * residual, 1, keepdims=True)
+    portion = (residual * gain[...].astype(F32)).astype(BF16)
+    sums[:, :ff] = jnp.dot(portion, gate[...], preferred_element_type=F32).astype(BF16)
+    sums[:, ff : 2 * ff] = jnp.dot(portion, up[...], preferred_element_type=F32).astype(BF16)
+    lane = lanes((residual.shape[0], 128))
+    high = round_low(square)
+    tail = jnp.where(lane == 0, high, jnp.where(lane == 1, square - high, 0.0))
+    sums[:, 2 * ff :] = tail.astype(BF16)
+
+
+def core_sum_kernel(mine, theirs, total):
+    ff2 = mine.shape[1] - 128
+    total[:, :ff2] = (mine[:, :ff2].astype(F32) + theirs[:, :ff2].astype(F32)).astype(BF16)
+    tail = mine[:, ff2:].astype(F32) + theirs[:, ff2:].astype(F32)
+    square = jnp.sum(tail, 1, keepdims=True)
+    lane = lanes(tail.shape)
+    high = round_low(square)
+    tail = jnp.where(lane == 0, high, jnp.where(lane == 1, square - high, 0.0))
+    total[:, ff2:] = tail.astype(BF16)
+
+
+def down_kernel(features, mine, theirs, weight, send, keep, scr):
+    y = lax.axis_index("pool") % 2
+    ff = weight.shape[0]
+    tail = mine[:, 2 * ff :].astype(F32) + theirs[:, 2 * ff :].astype(F32)
+    square = jnp.sum(tail, 1, keepdims=True)
+    factor = lax.rsqrt(square * (1.0 / features) + 1e-05)
+    gate = (mine[:, :ff].astype(F32) + theirs[:, :ff].astype(F32)) * factor
+    up = (mine[:, ff : 2 * ff].astype(F32) + theirs[:, ff : 2 * ff].astype(F32)) * factor
+    hidden = (gate / (1.0 + jnp.exp(-gate)) * up).astype(BF16)
+    scr[...] = jnp.dot(hidden, weight[...], preferred_element_type=F32)
+    rows = scr.shape[0] // 8
+    for z in range(4):
+        even = scr[(2 * z) * rows : (2 * z + 1) * rows, :]
+        odd = scr[(2 * z + 1) * rows : (2 * z + 2) * rows, :]
+        keep[z * rows : (z + 1) * rows, :] = jnp.where(y == 0, even, odd)
+        send[z * rows : (z + 1) * rows, :] = jnp.where(y == 0, odd, even)
+
+
+def split_kernel(keep, got, c0, c1, c2, c3, scr):
+    z = lax.axis_index("pool") // 2
+    scr[...] = keep[...] + got[...]
+    rows = c0.shape[0]
+    chunks = in_order([scr[s * rows : (s + 1) * rows, :] for s in range(4)], z)
+    for values, chunk in zip(chunks, (c0, c1, c2, c3)):
+        chunk[...] = values
+
+
+def final_kernel(own, c0, c1, c2, c3, out):
+    out[...] = (own[...] + ((c0[...] + c1[...]) + (c2[...] + c3[...]))).astype(BF16)
+
+
+def flip(values, axis, step):
+    size = lax.axis_size(axis)
+    return lax.ppermute(values, axis, [(index, index ^ step) for index in range(size)])
+
+
+def per_device_small(
+    residual_in,
+    query_new,
+    key_new,
+    value_new,
+    key_cache,
+    value_cache,
+    block_table,
+    lengths,
+    out_weight,
+    norm_gain,
+    gate_weight,
+    up_weight,
+    down_weight,
+):
+    rows, width = residual_in.shape
+    blocks = key_cache.shape[0]
+    pool, mlp = 8, 4
+    requests = rows * pool
+    ff = gate_weight.shape[1]
+    part_cols = out_weight.shape[1]
+    half = HD // 2
+    freq = 10000.0 ** (-2.0 * (np.arange(width) % half) / HD)
+    freq = jnp.asarray(np.broadcast_to(freq.astype(np.float32), (8, width)))
+    packed_width = 2 * width + 128
+    slots = blocks + rows + 1
+    part_width = width + 128
+
+    packed, own = call(
+        prepare_kernel,
+        "rotary",
+        [((rows, packed_width), BF16), ((slots, part_width), F32)],
+        [block_table, lengths, freq, query_new, key_new, value_new, residual_in],
+        [pltpu.VMEM((8, width), F32)],
+        smem=(0, 1),
+    )
+
+    def pool_gather(values):
+        (both,) = call(
+            merge_kernel,
+            "merge",
+            [((2,) + values.shape, values.dtype)],
+            [values, flip(values, "pool", 1)],
+        )
+        return [both] + [flip(both, "pool", step) for step in (2, 4, 6)]
+
+    part, all_input, tables = call(
+        attend_kernel,
+        "attend",
+        [((slots, part_width), BF16), ((requests, width), F32), ((requests, 128), F32)],
+        pool_gather(packed) + [own, key_cache, value_cache],
+        [pltpu.VMEM((requests, packed_width), F32)],
+    )
+    (head_part,) = call(
+        combine_kernel,
+        "combine",
+        [((requests, part_cols), BF16)],
+        pool_gather(part) + [tables, out_weight],
+        [
+            pltpu.VMEM((pool * slots, width), F32),
+            pltpu.VMEM((pool, slots, 128), F32),
+            pltpu.VMEM((requests * width // HD, 128), F32),
+        ],
+    )
+    (head_sum,) = call(
+        sum_kernel,
+        "head_sum",
+        [((requests, part_cols), BF16)],
+        [head_part] + [flip(head_part, "mlp", step) for step in (1, 2, 3)],
+    )
+    share = pool // mlp
+    pieces = []
+    for turn in range(share):
+        route = []
+        for p in range(pool):
+            for m in range(mlp):
+                target = m * share + (p % share ^ turn)
+                route.append((p * mlp + m, target * mlp + p // share))
+        pieces.append(lax.ppermute(head_sum, ("pool", "mlp"), route))
+    sums, own_residual = call(
+        gate_up_kernel,
+        "gate_up",
+        [((requests, 2 * ff + 128), BF16), ((rows, width), F32)],
+        pieces + [all_input, norm_gain.reshape(1, width), gate_weight, up_weight],
+        [pltpu.VMEM((requests, width), F32)],
+    )
+    (core_sums,) = call(
+        core_sum_kernel,
+        "core_sum",
+        [((requests, 2 * ff + 128), BF16)],
+        [sums, flip(sums, "mlp", 1)],
+    )
+    send, keep = call(
+        functools.partial(down_kernel, width * mlp),
+        "down",
+        [((requests // 2, width), F32)] * 2,
+        [core_sums, flip(core_sums, "mlp", 2), down_weight],
+        [pltpu.VMEM((requests, width), F32)],
+    )
+    chunks = call(
+        split_kernel,
+        "pair_sum",
+        [((rows, width), F32)] * 4,
+        [keep, flip(send, "pool", 1)],
+        [pltpu.VMEM((requests // 2, width), F32)],
+    )
+    (out,) = call(
+        final_kernel,
+        "final",
+        [((rows, width), BF16)],
+        [own_residual, chunks[0]]
+        + [flip(chunks[step], "pool", 2 * step) for step in (1, 2, 3)],
+    )
+    return out
+
+
 def solution(mesh):
     in_specs = (
         P("pool", "mlp"),
@@ -219,6 +620,8 @@
         P("mlp", "pool"),
         P("pool", "mlp"),
     )
+    small = mesh.shape["pool"] == 8 and mesh.shape["mlp"] == 4
+    per_device = per_device_small if small else per_device_wide
     return jax.shard_map(
         per_device, mesh=mesh, in_specs=in_specs, out_specs=P("pool", "mlp"), check_vma=False
     )

time: 96.8 us -> 69.6 us (0.72)
  other arithmetic: 14.5 us -> 0 us
  local copies, waits for them, and re-layouts: 16.8 us -> 7.87 us
  blocking collectives: 8.57 us -> 0 us
  matrix products: 8.1 us -> 0 us
  Pallas kernels: 0 us -> 5.73 us
  waiting for transfers between devices: 19.7 us -> 23.8 us
  starting transfers between devices: 27.6 us -> 31.7 us
    ppermute x1 -> x19, starting transfers between devices: 0.68 us -> 31.7 us  [the longest x17 29.5 us: flip(): lax.ppermute(values, axis, [(index, index ^ step) for index in range(size)])]
    all_to_all x4 -> x0, starting transfers between devices: 27 us -> none  [the longest x3 23.6 us: gather(): return lax.all_to_all(copies, axis, 0, 0)]
    ppermute x1 -> x19, waiting for transfers between devices: 0.01 us -> 23.8 us  [the longest x17 22.3 us: flip(): lax.ppermute(values, axis, [(index, index ^ step) for index in range(size)])]
    all_to_all x4 -> x0, waiting for transfers between devices: 19.7 us -> none  [the longest x3 13 us: gather(): return lax.all_to_all(copies, axis, 0, 0)]
    all_to_all x1 -> x0, blocking collectives: 8.57 us -> none  [gather(): return lax.all_to_all(copies, axis, 0, 0)]
    dot_general x9 -> x0, matrix products: 8.1 us -> none  [the longest x1 1.92 us: per_device(): jnp.einsum('bhd,bthd->bht', block_query, key_rows, preferred_element_type...]
    pallas_call x0 -> x11, Pallas kernels: none -> 5.73 us  [call(): pl.pallas_call(kernel, out_shape=[jax.ShapeDtypeStruct(shape, dtype) for...]
    reshape x8 -> x1, local copies, waits for them, and re-layouts: 5.18 us -> 0.01 us  [per_device_small(): norm_gain.reshape(1, width)]
  transfers between devices with their start and end apart: 5 -> 19, of which waited for: 3 -> 15; matrix products, arithmetic and copies ran while one was open for 12% -> 0% of each run, Pallas kernels for 0% -> 0%
where the time goes in v3:
time: 69.6 us; the launch traced here: 69.2 us
  starting transfers between devices  31.7 us (46%)
  waiting for transfers between devices  23.8 us (34%)
  local copies, waits for them, and re-layouts  7.87 us (11%)
  Pallas kernels  5.73 us (8%)
    ppermute x17, starting transfers between devices, flip(): lax.ppermute(values, axis, [(index, index ^ step) for index in range(size)])  29.5 us
    ppermute x17, waiting for transfers between devices, flip(): lax.ppermute(values, axis, [(index, index ^ step) for index in range(size)])  22.3 us
    unnamed x26, local copies, waits for them, and re-layouts  7.18 us
    pallas_call x11, Pallas kernels, call(): pl.pallas_call(kernel, out_shape=[jax.ShapeDtypeStruct(shape, dtype) for...  5.73 us
    ppermute x2, starting transfers between devices, per_device_small(): pieces.append(lax.ppermute(head_sum, ('pool', 'mlp'), route))  2.23 us
    ppermute x2, waiting for transfers between devices, per_device_small(): pieces.append(lax.ppermute(head_sum, ('pool', 'mlp'), route))  1.5 us
  transfers between devices with their start and end apart: 19, of which 15 were waited for; matrix products, arithmetic and copies ran while one was open for 0% of the time, Pallas kernels for 0%

profile of v3, /device:TPU:0, one launch (start us, length us, event | category | flops | bytes accessed | tf_op | source)
XLA Modules:
  0.0 69.2 jit_solution(13793227729866358001)
XLA Ops:
  0.0 0.7 jit_solution_.3.freq
  0.7 0.7 copy-done.6
  1.4 0.7 copy-done.7
  2.1 0.7 copy-done.8
  2.7 0.7 copy-done.9
  3.4 0.7 copy-done.10
  4.1 0.7 copy-done.11
  4.8 0.8 %rotary.1 = (bf16[2,1664]{1,0:T(2,128)(2,1)S(1)}, f32[8,896]{1,0:T(8,128)S(1)}) custom-call(s32[2,8]{1,0:T(2,128)S(1)} %copy-done.10, s32[2]{0:T(128)S(1)} %copy-done.11, f32[8,768]{1,0:T(8,128)S(1)} %jit_solution_.3.freq, bf16[2,768]{1,0:T(2,128)(2,1)S(1)} %copy-done.6, bf16[2,768]{1,0:T(2,128)(2,1)S(1)} %copy-done.7, bf16[2,768]{1,0:T(2,128)(2,1)S(1)} %copy-done.8, ...), custom_call_target="tpu_custom_call" | custom-call | bytes 36936 | tf_op jit(solution)/shard_map/rotary/pallas_call | solution.py:217
  5.6 3.0 %collective-permute-start = (bf16[2,1664]{1,0:T(2,128)(2,1)S(1)}, bf16[2,1664]{1,0:T(2,128)(2,1)S(1)}, u32[]{:S(2)}, u32[]{:S(2)}) collective-permute-start(bf16[2,1664]{1,0:T(2,128)(2,1)S(1)} %get-tuple-element.18.mine), channel_id=1, source_target_pairs={{0,4},{4,0},{8,12},{12,8},{16,20},{20,16},{24,28},{28,24},{1,5},{5... | collective-permute-start | bytes 19976 | tf_op jit(solution)/shard_map/ppermute | solution.py:488
  8.6 1.6 %collective-permute-done.theirs = bf16[2,1664]{1,0:T(2,128)(2,1)S(1)} collective-permute-done((bf16[2,1664]{1,0:T(2,128)(2,1)S(1)}, bf16[2,1664]{1,0:T(2,128)(2,1)S(1)}, u32[]{:S(2)}, u32[]{:S(2)}) %collective-permute-start) | collective-permute-done | bytes 6688 | tf_op jit(solution)/shard_map/ppermute | solution.py:488
  10.2 4.1 %collective-permute-start.3 = (bf16[2,2,1664]{2,1,0:T(2,128)(2,1)S(1)}, bf16[2,2,1664]{2,1,0:T(2,128)(2,1)S(1)}, u32[]{:S(2)}, u32[]{:S(2)}) collective-permute-start(bf16[2,2,1664]{2,1,0:T(2,128)(2,1)S(1)} %merge.2.a0), channel_id=1, source_target_pairs={{0,24},{4,28},{8,16},{12,20},{16,8},{20,12},{24,0},{28,4},{1,25},{... | collective-permute-start | bytes 39944 | tf_op jit(solution)/shard_map/ppermute | solution.py:488
  14.3 0.6 collective-permute-start.1
  14.9 1.1 %collective-permute-done.3.a3 = bf16[2,2,1664]{2,1,0:T(2,128)(2,1)S(1)} collective-permute-done((bf16[2,2,1664]{2,1,0:T(2,128)(2,1)S(1)}, bf16[2,2,1664]{2,1,0:T(2,128)(2,1)S(1)}, u32[]{:S(2)}, u32[]{:S(2)}) %collective-permute-start.3) | collective-permute-done | bytes 13344 | tf_op jit(solution)/shard_map/ppermute | solution.py:488
  16.0 2.9 %collective-permute-done.2.a2 = bf16[2,2,1664]{2,1,0:T(2,128)(2,1)S(1)} collective-permute-done((bf16[2,2,1664]{2,1,0:T(2,128)(2,1)S(1)}, bf16[2,2,1664]{2,1,0:T(2,128)(2,1)S(1)}, u32[]{:S(2)}, u32[]{:S(2)}) %collective-permute-start.2) | collective-permute-done | bytes 13344 | tf_op jit(solution)/shard_map/ppermute | solution.py:488
  18.9 1.5 %copy-done = bf16[5,256,768]{2,1,0:T(8,128)(2,1)S(1)} copy-done((bf16[5,256,768]{2,1,0:T(8,128)(2,1)S(1)}, bf16[5,256,768]{2,1,0:T(8,128)(2,1)}, u32[]{:S(2)}) %copy-start) | copy-done | bytes 1966104
  20.5 1.5 %copy-done.1 = bf16[5,256,768]{2,1,0:T(8,128)(2,1)S(1)} copy-done((bf16[5,256,768]{2,1,0:T(8,128)(2,1)S(1)}, bf16[5,256,768]{2,1,0:T(8,128)(2,1)}, u32[]{:S(2)}) %copy-start.1) | copy-done | bytes 1966104
  22.0 2.6 %attend.1 = (bf16[8,896]{1,0:T(8,128)(2,1)S(1)}, f32[16,768]{1,0:T(8,128)S(1)}, f32[16,128]{1,0:T(8,128)S(1)}) custom-call(bf16[2,2,1664]{2,1,0:T(2,128)(2,1)S(1)} %merge.2.a0, bf16[2,2,1664]{2,1,0:T(2,128)(2,1)S(1)} %collective-permute-done.1.a1, bf16[2,2,1664]{2,1,0:T(2,128)(2,1)S(1)} %collective-permute-done.2.a2, ...), custom_call_target="tpu_custom_call" | custom-call | bytes 4014080 | tf_op jit(solution)/shard_map/attend/pallas_call | solution.py:217
  24.6 1.6 %collective-permute-start.4 = (bf16[8,896]{1,0:T(8,128)(2,1)S(1)}, bf16[8,896]{1,0:T(8,128)(2,1)S(1)}, u32[]{:S(2)}, u32[]{:S(2)}) collective-permute-start(bf16[8,896]{1,0:T(8,128)(2,1)S(1)} %get-tuple-element.20.mine), channel_id=1, source_target_pairs={{0,4},{4,0},{8,12},{12,8},{16,20},{20,16},{24,28},{28,24},{1,5},{5... | collective-permute-start | bytes 43016 | tf_op jit(solution)/shard_map/ppermute | solution.py:488
  26.2 2.2 %collective-permute-done.4.theirs = bf16[8,896]{1,0:T(8,128)(2,1)S(1)} collective-permute-done((bf16[8,896]{1,0:T(8,128)(2,1)S(1)}, bf16[8,896]{1,0:T(8,128)(2,1)S(1)}, u32[]{:S(2)}, u32[]{:S(2)}) %collective-permute-start.4) | collective-permute-done | bytes 14368 | tf_op jit(solution)/shard_map/ppermute | solution.py:488
  28.4 1.5 %collective-permute-start.7 = (bf16[2,8,896]{2,1,0:T(8,128)(2,1)S(1)}, bf16[2,8,896]{2,1,0:T(8,128)(2,1)S(1)}, u32[]{:S(2)}, u32[]{:S(2)}) collective-permute-start(bf16[2,8,896]{2,1,0:T(8,128)(2,1)S(1)} %merge.3.b0), channel_id=1, source_target_pairs={{0,24},{4,28},{8,16},{12,20},{16,8},{20,12},{24,0},{28,4},{1,25},{... | collective-permute-start | bytes 86024 | tf_op jit(solution)/shard_map/ppermute | solution.py:488
  29.9 0.6 collective-permute-start.6
  30.5 2.3 %collective-permute-start.5 = (bf16[2,8,896]{2,1,0:T(8,128)(2,1)S(1)}, bf16[2,8,896]{2,1,0:T(8,128)(2,1)S(1)}, u32[]{:S(2)}, u32[]{:S(2)}) collective-permute-start(bf16[2,8,896]{2,1,0:T(8,128)(2,1)S(1)} %merge.3.b0), channel_id=1, source_target_pairs={{0,8},{4,12},{8,0},{12,4},{16,24},{20,28},{24,16},{28,20},{1,9},{5... | collective-permute-start | bytes 86024 | tf_op jit(solution)/shard_map/ppermute | solution.py:488
  32.8 1.3 %collective-permute-done.7.b3 = bf16[2,8,896]{2,1,0:T(8,128)(2,1)S(1)} collective-permute-done((bf16[2,8,896]{2,1,0:T(8,128)(2,1)S(1)}, bf16[2,8,896]{2,1,0:T(8,128)(2,1)S(1)}, u32[]{:S(2)}, u32[]{:S(2)}) %collective-permute-start.7) | collective-permute-done | bytes 28704 | tf_op jit(solution)/shard_map/ppermute | solution.py:488
  34.1 0.6 collective-permute-done.6.b2
  34.7 0.3 collective-permute-done.5.b1
  35.0 0.7 combine.1.p0
  35.7 1.6 %collective-permute-start.9 = (bf16[16,384]{1,0:T(8,128)(2,1)S(1)}, bf16[16,384]{1,0:T(8,128)(2,1)S(1)}, u32[]{:S(2)}, u32[]{:S(2)}) collective-permute-start(bf16[16,384]{1,0:T(8,128)(2,1)S(1)} %combine.1.p0), channel_id=1, source_target_pairs={{0,2},{1,3},{2,0},{3,1},{4,6},{5,7},{6,4},{7,5},{8,10},{9,11},{10,... | collective-permute-start | bytes 36872 | tf_op jit(solution)/shard_map/ppermute | solution.py:488
  37.3 0.3 collective-permute-start.8
  37.5 1.3 %collective-permute-done.10.p3 = bf16[16,384]{1,0:T(8,128)(2,1)S(1)} collective-permute-done((bf16[16,384]{1,0:T(8,128)(2,1)S(1)}, bf16[16,384]{1,0:T(8,128)(2,1)S(1)}, u32[]{:S(2)}, u32[]{:S(2)}) %collective-permute-start.10) | collective-permute-done | bytes 12320 | tf_op jit(solution)/shard_map/ppermute | solution.py:488
  38.9 0.6 collective-permute-done.9.p2
  39.5 1.6 %collective-permute-start.12 = (bf16[16,384]{1,0:T(8,128)(2,1)S(1)}, bf16[16,384]{1,0:T(8,128)(2,1)S(1)}, u32[]{:S(2)}, u32[]{:S(2)}) collective-permute-start(bf16[16,384]{1,0:T(8,128)(2,1)S(1)} %head_sum.1), channel_id=1, source_target_pairs={{0,4},{1,12},{2,20},{3,28},{4,0},{5,8},{6,16},{7,24},{8,5},{9,13},... | collective-permute-start | bytes 36872 | tf_op jit(solution)/shard_map/ppermute | solution.py:569
  41.1 0.7 collective-permute-start.11
  41.7 1.5 %collective-permute-done.12.flip = bf16[16,384]{1,0:T(8,128)(2,1)S(1)} collective-permute-done((bf16[16,384]{1,0:T(8,128)(2,1)S(1)}, bf16[16,384]{1,0:T(8,128)(2,1)S(1)}, u32[]{:S(2)}, u32[]{:S(2)}) %collective-permute-start.12) | collective-permute-done | bytes 12320 | tf_op jit(solution)/shard_map/ppermute | solution.py:569
  43.3 0.5 gate_up.1
  43.8 4.1 %collective-permute-start.13 = (bf16[16,2176]{1,0:T(8,128)(2,1)S(1)}, bf16[16,2176]{1,0:T(8,128)(2,1)S(1)}, u32[]{:S(2)}, u32[]{:S(2)}) collective-permute-start(bf16[16,2176]{1,0:T(8,128)(2,1)S(1)} %get-tuple-element.24.mine), channel_id=1, source_target_pairs={{0,1},{1,0},{2,3},{3,2},{4,5},{5,4},{6,7},{7,6},{8,9},{9,8},{10,11... | collective-permute-start | bytes 208904 | tf_op jit(solution)/shard_map/ppermute | solution.py:488
  47.9 0.9 %collective-permute-done.13.theirs = bf16[16,2176]{1,0:T(8,128)(2,1)S(1)} collective-permute-done((bf16[16,2176]{1,0:T(8,128)(2,1)S(1)}, bf16[16,2176]{1,0:T(8,128)(2,1)S(1)}, u32[]{:S(2)}, u32[]{:S(2)}) %collective-permute-start.13) | collective-permute-done | bytes 69664 | tf_op jit(solution)/shard_map/ppermute | solution.py:488
  48.8 0.1 core_sum.1.mine
  48.9 4.8 %collective-permute-start.14 = (bf16[16,2176]{1,0:T(8,128)(2,1)S(1)}, bf16[16,2176]{1,0:T(8,128)(2,1)S(1)}, u32[]{:S(2)}, u32[]{:S(2)}) collective-permute-start(bf16[16,2176]{1,0:T(8,128)(2,1)S(1)} %core_sum.1.mine), channel_id=1, source_target_pairs={{0,2},{1,3},{2,0},{3,1},{4,6},{5,7},{6,4},{7,5},{8,10},{9,11},{10,... | collective-permute-start | bytes 208904 | tf_op jit(solution)/shard_map/ppermute | solution.py:488
  53.7 2.7 %collective-permute-done.14.theirs = bf16[16,2176]{1,0:T(8,128)(2,1)S(1)} collective-permute-done((bf16[16,2176]{1,0:T(8,128)(2,1)S(1)}, bf16[16,2176]{1,0:T(8,128)(2,1)S(1)}, u32[]{:S(2)}, u32[]{:S(2)}) %collective-permute-start.14) | collective-permute-done | bytes 69664 | tf_op jit(solution)/shard_map/ppermute | solution.py:488
  56.4 0.4 down.1
  56.8 0.6 collective-permute-start.15
  57.4 3.3 %collective-permute-done.15.got = f32[8,768]{1,0:T(8,128)S(1)} collective-permute-done((f32[8,768]{1,0:T(8,128)S(1)}, f32[8,768]{1,0:T(8,128)S(1)}, u32[]{:S(2)}, u32[]{:S(2)}) %collective-permute-start.15) | collective-permute-done | bytes 24608 | tf_op jit(solution)/shard_map/ppermute | solution.py:488
  60.7 0.1 collective-permute-start.16
  60.8 2.4 %collective-permute-start.17 = (f32[2,768]{1,0:T(2,128)S(1)}, f32[2,768]{1,0:T(2,128)S(1)}, u32[]{:S(2)}, u32[]{:S(2)}) collective-permute-start(f32[2,768]{1,0:T(2,128)S(1)} %get-tuple-element.29), channel_id=1, source_target_pairs={{0,16},{4,20},{8,24},{12,28},{16,0},{20,4},{24,8},{28,12},{1,17},{... | collective-permute-start | bytes 18440 | tf_op jit(solution)/shard_map/ppermute | solution.py:488
  63.2 2.0 %collective-permute-start.18 = (f32[2,768]{1,0:T(2,128)S(1)}, f32[2,768]{1,0:T(2,128)S(1)}, u32[]{:S(2)}, u32[]{:S(2)}) collective-permute-start(f32[2,768]{1,0:T(2,128)S(1)} %get-tuple-element.30), channel_id=1, source_target_pairs={{0,24},{4,28},{8,16},{12,20},{16,8},{20,12},{24,0},{28,4},{1,25},{... | collective-permute-start | bytes 18440 | tf_op jit(solution)/shard_map/ppermute | solution.py:488
  65.2 0.2 collective-permute-done.17.c2
  65.4 3.2 %collective-permute-done.18.c3 = f32[2,768]{1,0:T(2,128)S(1)} collective-permute-done((f32[2,768]{1,0:T(2,128)S(1)}, f32[2,768]{1,0:T(2,128)S(1)}, u32[]{:S(2)}, u32[]{:S(2)}) %collective-permute-start.18) | collective-permute-done | bytes 6176 | tf_op jit(solution)/shard_map/ppermute | solution.py:488
  68.6 0.6 final.1
  (29 shorter events, 0.2 us)
Async XLA Ops:
  0.7 0.7 copy-start.6
  1.4 0.7 copy-start.7
  2.1 0.7 copy-start.8
  2.7 0.7 copy-start.9
  3.4 0.7 copy-start.10
  4.1 0.7 copy-start.11
  5.6 4.6 %collective-permute-start = (bf16[2,1664]{1,0:T(2,128)(2,1)S(1)}, bf16[2,1664]{1,0:T(2,128)(2,1)S(1)}, u32[]{:S(2)}, u32[]{:S(2)}) collective-permute-start(bf16[2,1664]{1,0:T(2,128)(2,1)S(1)} %get-tuple-element.18.mine), channel_id=1, source_target_pairs={{0,4},{4,0},{8,12},{12,8},{16,20},{20,16},{24,28},{28,24},{1,5},{5... | collective-permute-start | bytes 19976 | tf_op jit(solution)/shard_map/ppermute | solution.py:488
  10.2 5.8 %collective-permute-start.3 = (bf16[2,2,1664]{2,1,0:T(2,128)(2,1)S(1)}, bf16[2,2,1664]{2,1,0:T(2,128)(2,1)S(1)}, u32[]{:S(2)}, u32[]{:S(2)}) collective-permute-start(bf16[2,2,1664]{2,1,0:T(2,128)(2,1)S(1)} %merge.2.a0), channel_id=1, source_target_pairs={{0,24},{4,28},{8,16},{12,20},{16,8},{20,12},{24,0},{28,4},{1,25},{... | collective-permute-start | bytes 39944 | tf_op jit(solution)/shard_map/ppermute | solution.py:488
  14.3 4.6 %collective-permute-start.2 = (bf16[2,2,1664]{2,1,0:T(2,128)(2,1)S(1)}, bf16[2,2,1664]{2,1,0:T(2,128)(2,1)S(1)}, u32[]{:S(2)}, u32[]{:S(2)}) collective-permute-start(bf16[2,2,1664]{2,1,0:T(2,128)(2,1)S(1)} %merge.2.a0), channel_id=1, source_target_pairs={{0,16},{4,20},{8,24},{12,28},{16,0},{20,4},{24,8},{28,12},{1,17},{... | collective-permute-start | bytes 39944 | tf_op jit(solution)/shard_map/ppermute | solution.py:488
  14.3 4.6 %collective-permute-start.1 = (bf16[2,2,1664]{2,1,0:T(2,128)(2,1)S(1)}, bf16[2,2,1664]{2,1,0:T(2,128)(2,1)S(1)}, u32[]{:S(2)}, u32[]{:S(2)}) collective-permute-start(bf16[2,2,1664]{2,1,0:T(2,128)(2,1)S(1)} %merge.2.a0), channel_id=1, source_target_pairs={{0,8},{4,12},{8,0},{12,4},{16,24},{20,28},{24,16},{28,20},{1,9},{5... | collective-permute-start | bytes 39944 | tf_op jit(solution)/shard_map/ppermute | solution.py:488
  18.9 1.5 %copy-start = (bf16[5,256,768]{2,1,0:T(8,128)(2,1)S(1)}, bf16[5,256,768]{2,1,0:T(8,128)(2,1)}, u32[]{:S(2)}) copy-start(bf16[5,256,768]{2,1,0:T(8,128)(2,1)} %keys.1) | copy-start | bytes 5898244
  20.5 1.5 %copy-start.1 = (bf16[5,256,768]{2,1,0:T(8,128)(2,1)S(1)}, bf16[5,256,768]{2,1,0:T(8,128)(2,1)}, u32[]{:S(2)}) copy-start(bf16[5,256,768]{2,1,0:T(8,128)(2,1)} %values.1) | copy-start | bytes 5898244
  22.0 12.9 %copy-start.5 = (bf16[768,384]{1,0:T(8,128)(2,1)S(1)}, bf16[768,384]{1,0:T(8,128)(2,1)}, u32[]{:S(2)}) copy-start(bf16[768,384]{1,0:T(8,128)(2,1)} %weight.2) | copy-start | bytes 1769476
  22.0 19.7 %copy-start.12 = (bf16[768]{0:T(1024)(128)(2,1)S(1)}, bf16[768]{0:T(1024)(128)(2,1)}, u32[]{:S(2)}) copy-start(bf16[768]{0:T(1024)(128)(2,1)} %param.23) | copy-start | bytes 4612
  22.0 21.2 %copy-start.3 = (bf16[768,1024]{1,0:T(8,128)(2,1)S(1)}, bf16[768,1024]{1,0:T(8,128)(2,1)}, u32[]{:S(2)}) copy-start(bf16[768,1024]{1,0:T(8,128)(2,1)} %gate.1) | copy-start | bytes 4718596
  22.0 21.2 %copy-start.4 = (bf16[768,1024]{1,0:T(8,128)(2,1)S(1)}, bf16[768,1024]{1,0:T(8,128)(2,1)}, u32[]{:S(2)}) copy-start(bf16[768,1024]{1,0:T(8,128)(2,1)} %up.1) | copy-start | bytes 4718596
  24.6 3.8 %collective-permute-start.4 = (bf16[8,896]{1,0:T(8,128)(2,1)S(1)}, bf16[8,896]{1,0:T(8,128)(2,1)S(1)}, u32[]{:S(2)}, u32[]{:S(2)}) collective-permute-start(bf16[8,896]{1,0:T(8,128)(2,1)S(1)} %get-tuple-element.20.mine), channel_id=1, source_target_pairs={{0,4},{4,0},{8,12},{12,8},{16,20},{20,16},{24,28},{28,24},{1,5},{5... | collective-permute-start | bytes 43016 | tf_op jit(solution)/shard_map/ppermute | solution.py:488
  28.4 5.7 %collective-permute-start.7 = (bf16[2,8,896]{2,1,0:T(8,128)(2,1)S(1)}, bf16[2,8,896]{2,1,0:T(8,128)(2,1)S(1)}, u32[]{:S(2)}, u32[]{:S(2)}) collective-permute-start(bf16[2,8,896]{2,1,0:T(8,128)(2,1)S(1)} %merge.3.b0), channel_id=1, source_target_pairs={{0,24},{4,28},{8,16},{12,20},{16,8},{20,12},{24,0},{28,4},{1,25},{... | collective-permute-start | bytes 86024 | tf_op jit(solution)/shard_map/ppermute | solution.py:488
  29.9 4.8 %collective-permute-start.6 = (bf16[2,8,896]{2,1,0:T(8,128)(2,1)S(1)}, bf16[2,8,896]{2,1,0:T(8,128)(2,1)S(1)}, u32[]{:S(2)}, u32[]{:S(2)}) collective-permute-start(bf16[2,8,896]{2,1,0:T(8,128)(2,1)S(1)} %merge.3.b0), channel_id=1, source_target_pairs={{0,16},{4,20},{8,24},{12,28},{16,0},{20,4},{24,8},{28,12},{1,17},{... | collective-permute-start | bytes 86024 | tf_op jit(solution)/shard_map/ppermute | solution.py:488
  30.5 4.4 %collective-permute-start.5 = (bf16[2,8,896]{2,1,0:T(8,128)(2,1)S(1)}, bf16[2,8,896]{2,1,0:T(8,128)(2,1)S(1)}, u32[]{:S(2)}, u32[]{:S(2)}) collective-permute-start(bf16[2,8,896]{2,1,0:T(8,128)(2,1)S(1)} %merge.3.b0), channel_id=1, source_target_pairs={{0,8},{4,12},{8,0},{12,4},{16,24},{20,28},{24,16},{28,20},{1,9},{5... | collective-permute-start | bytes 86024 | tf_op jit(solution)/shard_map/ppermute | solution.py:488
  35.6 3.2 %collective-permute-start.10 = (bf16[16,384]{1,0:T(8,128)(2,1)S(1)}, bf16[16,384]{1,0:T(8,128)(2,1)S(1)}, u32[]{:S(2)}, u32[]{:S(2)}) collective-permute-start(bf16[16,384]{1,0:T(8,128)(2,1)S(1)} %combine.1.p0), channel_id=1, source_target_pairs={{0,3},{1,2},{2,1},{3,0},{4,7},{5,6},{6,5},{7,4},{8,11},{9,10},{10,... | collective-permute-start | bytes 36872 | tf_op jit(solution)/shard_map/ppermute | solution.py:488
  35.7 3.8 %collective-permute-start.9 = (bf16[16,384]{1,0:T(8,128)(2,1)S(1)}, bf16[16,384]{1,0:T(8,128)(2,1)S(1)}, u32[]{:S(2)}, u32[]{:S(2)}) collective-permute-start(bf16[16,384]{1,0:T(8,128)(2,1)S(1)} %combine.1.p0), channel_id=1, source_target_pairs={{0,2},{1,3},{2,0},{3,1},{4,6},{5,7},{6,4},{7,5},{8,10},{9,11},{10,... | collective-permute-start | bytes 36872 | tf_op jit(solution)/shard_map/ppermute | solution.py:488
  37.3 2.2 %collective-permute-start.8 = (bf16[16,384]{1,0:T(8,128)(2,1)S(1)}, bf16[16,384]{1,0:T(8,128)(2,1)S(1)}, u32[]{:S(2)}, u32[]{:S(2)}) collective-permute-start(bf16[16,384]{1,0:T(8,128)(2,1)S(1)} %combine.1.p0), channel_id=1, source_target_pairs={{0,1},{1,0},{2,3},{3,2},{4,5},{5,4},{6,7},{7,6},{8,9},{9,8},{10,11... | collective-permute-start | bytes 36872 | tf_op jit(solution)/shard_map/ppermute | solution.py:488
  39.5 3.8 %collective-permute-start.12 = (bf16[16,384]{1,0:T(8,128)(2,1)S(1)}, bf16[16,384]{1,0:T(8,128)(2,1)S(1)}, u32[]{:S(2)}, u32[]{:S(2)}) collective-permute-start(bf16[16,384]{1,0:T(8,128)(2,1)S(1)} %head_sum.1), channel_id=1, source_target_pairs={{0,4},{1,12},{2,20},{3,28},{4,0},{5,8},{6,16},{7,24},{8,5},{9,13},... | collective-permute-start | bytes 36872 | tf_op jit(solution)/shard_map/ppermute | solution.py:569
  41.1 2.2 %collective-permute-start.11 = (bf16[16,384]{1,0:T(8,128)(2,1)S(1)}, bf16[16,384]{1,0:T(8,128)(2,1)S(1)}, u32[]{:S(2)}, u32[]{:S(2)}) collective-permute-start(bf16[16,384]{1,0:T(8,128)(2,1)S(1)} %head_sum.1), channel_id=1, source_target_pairs={{0,0},{1,8},{2,16},{3,24},{4,4},{5,12},{6,20},{7,28},{8,1},{9,9},{... | collective-permute-start | bytes 36872 | tf_op jit(solution)/shard_map/ppermute | solution.py:569
  43.2 13.1 %copy-start.2 = (bf16[1024,768]{1,0:T(8,128)(2,1)S(1)}, bf16[1024,768]{1,0:T(8,128)(2,1)}, u32[]{:S(2)}) copy-start(bf16[1024,768]{1,0:T(8,128)(2,1)} %weight.3) | copy-start | bytes 4718596
  43.8 5.0 %collective-permute-start.13 = (bf16[16,2176]{1,0:T(8,128)(2,1)S(1)}, bf16[16,2176]{1,0:T(8,128)(2,1)S(1)}, u32[]{:S(2)}, u32[]{:S(2)}) collective-permute-start(bf16[16,2176]{1,0:T(8,128)(2,1)S(1)} %get-tuple-element.24.mine), channel_id=1, source_target_pairs={{0,1},{1,0},{2,3},{3,2},{4,5},{5,4},{6,7},{7,6},{8,9},{9,8},{10,11... | collective-permute-start | bytes 208904 | tf_op jit(solution)/shard_map/ppermute | solution.py:488
  48.9 7.5 %collective-permute-start.14 = (bf16[16,2176]{1,0:T(8,128)(2,1)S(1)}, bf16[16,2176]{1,0:T(8,128)(2,1)S(1)}, u32[]{:S(2)}, u32[]{:S(2)}) collective-permute-start(bf16[16,2176]{1,0:T(8,128)(2,1)S(1)} %core_sum.1.mine), channel_id=1, source_target_pairs={{0,2},{1,3},{2,0},{3,1},{4,6},{5,7},{6,4},{7,5},{8,10},{9,11},{10,... | collective-permute-start | bytes 208904 | tf_op jit(solution)/shard_map/ppermute | solution.py:488
  56.8 3.9 %collective-permute-start.15 = (f32[8,768]{1,0:T(8,128)S(1)}, f32[8,768]{1,0:T(8,128)S(1)}, u32[]{:S(2)}, u32[]{:S(2)}) collective-permute-start(f32[8,768]{1,0:T(8,128)S(1)} %get-tuple-element.26), channel_id=1, source_target_pairs={{0,4},{4,0},{8,12},{12,8},{16,20},{20,16},{24,28},{28,24},{1,5},{5... | collective-permute-start | bytes 73736 | tf_op jit(solution)/shard_map/ppermute | solution.py:488
  60.7 4.5 %collective-permute-start.16 = (f32[2,768]{1,0:T(2,128)S(1)}, f32[2,768]{1,0:T(2,128)S(1)}, u32[]{:S(2)}, u32[]{:S(2)}) collective-permute-start(f32[2,768]{1,0:T(2,128)S(1)} %get-tuple-element.28), channel_id=1, source_target_pairs={{0,8},{4,12},{8,0},{12,4},{16,24},{20,28},{24,16},{28,20},{1,9},{5... | collective-permute-start | bytes 18440 | tf_op jit(solution)/shard_map/ppermute | solution.py:488
  60.8 4.6 %collective-permute-start.17 = (f32[2,768]{1,0:T(2,128)S(1)}, f32[2,768]{1,0:T(2,128)S(1)}, u32[]{:S(2)}, u32[]{:S(2)}) collective-permute-start(f32[2,768]{1,0:T(2,128)S(1)} %get-tuple-element.29), channel_id=1, source_target_pairs={{0,16},{4,20},{8,24},{12,28},{16,0},{20,4},{24,8},{28,12},{1,17},{... | collective-permute-start | bytes 18440 | tf_op jit(solution)/shard_map/ppermute | solution.py:488
  63.2 5.4 %collective-permute-start.18 = (f32[2,768]{1,0:T(2,128)S(1)}, f32[2,768]{1,0:T(2,128)S(1)}, u32[]{:S(2)}, u32[]{:S(2)}) collective-permute-start(f32[2,768]{1,0:T(2,128)S(1)} %get-tuple-element.30), channel_id=1, source_target_pairs={{0,24},{4,28},{8,16},{12,20},{16,8},{20,12},{24,0},{28,4},{1,25},{... | collective-permute-start | bytes 18440 | tf_op jit(solution)/shard_map/ppermute | solution.py:488

commit v4 on v3

--- a/solution.py
+++ b/solution.py
@@ -209,19 +209,19 @@
 
 F32, BF16 = jnp.float32, jnp.bfloat16
 VMEM = pl.BlockSpec(memory_space=pltpu.VMEM)
-SMEM = pl.BlockSpec(memory_space=pltpu.SMEM)
-
-
-def call(kernel, name, outs, args, scratch=(), smem=(), flops=0):
+HBM = pl.BlockSpec(memory_space=pl.ANY)
+
+
+def call(kernel, name, outs, args, scratch=(), hbm=(), limit=16 * 2**20):
     size = sum(math.prod(a.shape) * a.dtype.itemsize for a in args)
     return pl.pallas_call(
         kernel,
         out_shape=[jax.ShapeDtypeStruct(shape, dtype) for shape, dtype in outs],
-        in_specs=[SMEM if i in smem else VMEM for i in range(len(args))],
+        in_specs=[HBM if i in hbm else VMEM for i in range(len(args))],
         out_specs=[VMEM] * len(outs),
         scratch_shapes=list(scratch),
-        compiler_params=pltpu.CompilerParams(vmem_limit_bytes=16 * 1024 * 1024),
-        cost_estimate=pl.CostEstimate(flops=flops, bytes_accessed=size, transcendentals=0),
+        compiler_params=pltpu.CompilerParams(vmem_limit_bytes=limit),
+        cost_estimate=pl.CostEstimate(flops=0, bytes_accessed=size, transcendentals=0),
         name=name,
     )(*args)
 
@@ -245,7 +245,18 @@
     return values.astype(BF16).astype(F32)
 
 
-def prepare_kernel(table, length, freq, query, key, value, residual, packed, own, scr):
+def prepare_kernel(*refs):
+    sources, (packed, own), held = refs[:6], refs[6:8], refs[8:14]
+    scr, sems = refs[14:]
+    copies = [
+        pltpu.make_async_copy(source, target, sems.at[i])
+        for i, (source, target) in enumerate(zip(sources, held))
+    ]
+    for copy in copies:
+        copy.start()
+    for copy in copies:
+        copy.wait()
+    table, length, query, key, value, residual = held
     rows, width = query.shape
     heads = width // HD
     most = table.shape[1]
@@ -259,8 +270,12 @@
     for r in range(rows):
         here = (line == r) | (line == rows + r)
         where_at = jnp.where(here, length[r].astype(F32), where_at)
-    angles = where_at * freq[...]
     lane = lanes((8, width))
+    turn = lanes((8, 384)) % (HD // 2)
+    freq = jnp.zeros((8, 384), F32)
+    for i in range(HD // 2):
+        freq = jnp.where(turn == i, float(np.float32(10000.0 ** (-2.0 * i / HD))), freq)
+    angles = where_at * jnp.concatenate([freq] * (width // 384), 1)
     first = lane % HD < HD // 2
     ahead = pltpu.roll(values, width - HD // 2, 1)
     behind = pltpu.roll(values, HD // 2, 1)
@@ -307,8 +322,17 @@
     both[1 - y] = theirs[...]
 
 
-def attend_kernel(a0, a1, a2, a3, own, keys, values, part, residual, tables, scr):
+def attend_kernel(
+    a0, a1, a2, a3, own, far_keys, far_values, part, residual, tables, scr, keys, values, sems
+):
     blocks, block_len, width = keys.shape
+    copies = [
+        pltpu.make_async_copy(far.at[b], near.at[b], sems.at[i, b])
+        for i, (far, near) in enumerate(((far_keys, keys), (far_values, values)))
+        for b in range(blocks)
+    ]
+    for copy in copies:
+        copy.start()
     rows = a0.shape[1]
     heads = width // HD
     most = 8
@@ -328,31 +352,41 @@
     tables[...] = table
     head_mask = lanes((heads, width)) // HD == rows_of((heads, width))
     spot = lanes((heads, 128))
-    token = lanes((heads, block_len)).astype(F32)
     tail = own[:, width:]
     part[...] = own[...].astype(BF16)
-    numerators = []
+    scores, limits = [], []
     for b in range(blocks):
         match = jnp.where(table == (me * blocks + b).astype(F32), 1.0, 0.0)
         holder = jnp.sum(match, 1, keepdims=True)
         place = jnp.sum(jnp.sum(match * lane.astype(F32), 1, keepdims=True), 0, keepdims=True)
         limit = jnp.sum(holder * length, 0, keepdims=True) - place * block_len
+        limits.append(jnp.broadcast_to(limit, (heads, block_len)))
         query = jnp.sum(holder * queries, 0, keepdims=True)
         spread = jnp.where(head_mask, query, 0.0).astype(BF16)
-        scores = lax.dot_general(
-            spread, keys[b], (((1,), (1,)), ((), ())), preferred_element_type=F32
-        ) * (1.0 / math.sqrt(HD))
-        valid = token < limit
-        scores = jnp.where(valid, scores, LOW)
-        shift = round_low(jnp.max(scores, 1, keepdims=True))
-        weights = jnp.where(valid, jnp.exp(scores - shift), 0.0)
-        total = jnp.sum(weights, 1, keepdims=True)
-        full = jnp.dot(weights.astype(BF16), values[b], preferred_element_type=F32)
+        copies[b].wait()
+        scores.append(
+            lax.dot_general(
+                spread, keys[b], (((1,), (1,)), ((), ())), preferred_element_type=F32
+            )
+        )
+    scores = jnp.concatenate(scores, 0) * (1.0 / math.sqrt(HD))
+    token = lanes((blocks * heads, block_len)).astype(F32)
+    valid = token < jnp.concatenate(limits, 0)
+    scores = jnp.where(valid, scores, LOW)
+    shift = round_low(jnp.max(scores, 1, keepdims=True))
+    weights = jnp.where(valid, jnp.exp(scores - shift), 0.0)
+    total = jnp.sum(weights, 1, keepdims=True)
+    high = round_low(total)
+    rest = total - high
+    numerators = []
+    for b in range(blocks):
+        mine = slice(b * heads, (b + 1) * heads)
+        copies[blocks + b].wait()
+        full = jnp.dot(weights[mine].astype(BF16), values[b], preferred_element_type=F32)
         numerators.append(jnp.sum(jnp.where(head_mask, full, 0.0), 0, keepdims=True))
-        high = round_low(total)
-        tail = jnp.where(spot == b, shift, tail)
-        tail = jnp.where(spot == 8 + b, high, tail)
-        tail = jnp.where(spot == 16 + b, total - high, tail)
+        tail = jnp.where(spot == b, shift[mine], tail)
+        tail = jnp.where(spot == 8 + b, high[mine], tail)
+        tail = jnp.where(spot == 16 + b, rest[mine], tail)
     line = rows_of((8, width))
     numer = own[:, :width]
     for b in range(blocks):
@@ -509,9 +543,6 @@
     requests = rows * pool
     ff = gate_weight.shape[1]
     part_cols = out_weight.shape[1]
-    half = HD // 2
-    freq = 10000.0 ** (-2.0 * (np.arange(width) % half) / HD)
-    freq = jnp.asarray(np.broadcast_to(freq.astype(np.float32), (8, width)))
     packed_width = 2 * width + 128
     slots = blocks + rows + 1
     part_width = width + 128
@@ -520,9 +551,12 @@
         prepare_kernel,
         "rotary",
         [((rows, packed_width), BF16), ((slots, part_width), F32)],
-        [block_table, lengths, freq, query_new, key_new, value_new, residual_in],
-        [pltpu.VMEM((8, width), F32)],
-        smem=(0, 1),
+        [block_table, lengths, query_new, key_new, value_new, residual_in],
+        [pltpu.SMEM(block_table.shape, jnp.int32), pltpu.SMEM(lengths.shape, jnp.int32)]
+        + [pltpu.VMEM((rows, width), BF16)] * 4
+        + [pltpu.VMEM((8, width), F32), pltpu.SemaphoreType.DMA((6,))],
+        hbm=range(6),
+        limit=52 * 2**20,
     )
 
     def pool_gather(values):
@@ -539,7 +573,14 @@
         "attend",
         [((slots, part_width), BF16), ((requests, width), F32), ((requests, 128), F32)],
         pool_gather(packed) + [own, key_cache, value_cache],
-        [pltpu.VMEM((requests, packed_width), F32)],
+        [
+            pltpu.VMEM((requests, packed_width), F32),
+            pltpu.VMEM(key_cache.shape, BF16),
+            pltpu.VMEM(value_cache.shape, BF16),
+            pltpu.SemaphoreType.DMA((2, blocks)),
+        ],
+        hbm=(5, 6),
+        limit=52 * 2**20,
     )
     (head_part,) = call(
         combine_kernel,
@@ -558,14 +599,15 @@
         [((requests, part_cols), BF16)],
         [head_part] + [flip(head_part, "mlp", step) for step in (1, 2, 3)],
     )
-    share = pool // mlp
     pieces = []
-    for turn in range(share):
+    for turn in range(2):
         route = []
-        for p in range(pool):
-            for m in range(mlp):
-                target = m * share + (p % share ^ turn)
-                route.append((p * mlp + m, target * mlp + p // share))
+        for m in range(mlp):
+            by_distance = sorted(range(4), key=lambda z: (-abs(z - m), z))
+            for z, step in zip(by_distance, (0, 1, 2, 3)):
+                for y in range(2):
+                    source = (m * 2 + y) * mlp + (m ^ step)
+                    route.append((source, (z * 2 + (y ^ turn)) * mlp + m))
         pieces.append(lax.ppermute(head_sum, ("pool", "mlp"), route))
     sums, own_residual = call(
         gate_up_kernel,
@@ -598,8 +640,7 @@
         final_kernel,
         "final",
         [((rows, width), BF16)],
-        [own_residual, chunks[0]]
-        + [flip(chunks[step], "pool", 2 * step) for step in (1, 2, 3)],
+        [own_residual, chunks[0]] + [flip(chunks[s], "pool", 2 * s) for s in (3, 2, 1)],
     )
     return out
 

time: 69.6 us -> 62.7 us (0.901)
  starting transfers between devices: 31.7 us -> 26.9 us
  local copies, waits for them, and re-layouts: 7.87 us -> 4.09 us
  Pallas kernels: 5.73 us -> 7.24 us
    ppermute x17, starting transfers between devices: 29.5 us -> 22.9 us  [flip(): lax.ppermute(values, axis, [(index, index ^ step) for index in range(size)])]
    unnamed x26 -> x22, local copies, waits for them, and re-layouts: 7.18 us -> 4.09 us
    ppermute x2, starting transfers between devices: 2.23 us -> 3.95 us  [per_device_small(): pieces.append(lax.ppermute(head_sum, ('pool', 'mlp'), route))]
    pallas_call x11, Pallas kernels: 5.73 us -> 7.24 us  [call(): pl.pallas_call(kernel, out_shape=[jax.ShapeDtypeStruct(shape, dtype) for...]
    ppermute x2, waiting for transfers between devices: 1.5 us -> 2.55 us  [per_device_small(): pieces.append(lax.ppermute(head_sum, ('pool', 'mlp'), route))]
    ppermute x17, waiting for transfers between devices: 22.3 us -> 21.6 us  [flip(): lax.ppermute(values, axis, [(index, index ^ step) for index in range(size)])]
  transfers between devices with their start and end apart: 19 -> 19, of which waited for: 15 -> 16; matrix products, arithmetic and copies ran while one was open for 0% -> 0% of each run, Pallas kernels for 0% -> 0%
where the time goes in v4:
time: 62.7 us; the launch traced here: 62.4 us
  starting transfers between devices  26.9 us (43%)
  waiting for transfers between devices  24.1 us (38%)
  Pallas kernels  7.24 us (12%)
  local copies, waits for them, and re-layouts  4.09 us (7%)
    ppermute x17, starting transfers between devices, flip(): lax.ppermute(values, axis, [(index, index ^ step) for index in range(size)])  22.9 us
    ppermute x17, waiting for transfers between devices, flip(): lax.ppermute(values, axis, [(index, index ^ step) for index in range(size)])  21.6 us
    pallas_call x11, Pallas kernels, call(): pl.pallas_call(kernel, out_shape=[jax.ShapeDtypeStruct(shape, dtype) for...  7.24 us
    unnamed x22, local copies, waits for them, and re-layouts  4.09 us
    ppermute x2, starting transfers between devices, per_device_small(): pieces.append(lax.ppermute(head_sum, ('pool', 'mlp'), route))  3.95 us
    ppermute x2, waiting for transfers between devices, per_device_small(): pieces.append(lax.ppermute(head_sum, ('pool', 'mlp'), route))  2.55 us
  transfers between devices with their start and end apart: 19, of which 16 were waited for; matrix products, arithmetic and copies ran while one was open for 0% of the time, Pallas kernels for 0%

profile of v4, /device:TPU:0, one launch (start us, length us, event | category | flops | bytes accessed | tf_op | source)
XLA Modules:
  0.0 62.4 jit_solution(561445556322824425)
XLA Ops:
  0.0 0.7 %copy-done.4 = bf16[2,768]{1,0:T(2,128)(2,1)S(1)} copy-done((bf16[2,768]{1,0:T(2,128)(2,1)S(1)}, bf16[2,768]{1,0:T(2,128)(2,1)}, u32[]{:S(2)}) %copy-start.4) | copy-done | bytes 3096
  0.7 0.7 %copy-done.5 = bf16[2,768]{1,0:T(2,128)(2,1)S(1)} copy-done((bf16[2,768]{1,0:T(2,128)(2,1)S(1)}, bf16[2,768]{1,0:T(2,128)(2,1)}, u32[]{:S(2)}) %copy-start.5) | copy-done | bytes 3096
  1.4 0.7 %copy-done.6 = bf16[2,768]{1,0:T(2,128)(2,1)S(1)} copy-done((bf16[2,768]{1,0:T(2,128)(2,1)S(1)}, bf16[2,768]{1,0:T(2,128)(2,1)}, u32[]{:S(2)}) %copy-start.6) | copy-done | bytes 3096
  2.1 0.7 %copy-done.7 = bf16[2,768]{1,0:T(2,128)(2,1)S(1)} copy-done((bf16[2,768]{1,0:T(2,128)(2,1)S(1)}, bf16[2,768]{1,0:T(2,128)(2,1)}, u32[]{:S(2)}) %copy-start.7) | copy-done | bytes 3096
  2.7 0.7 %copy-done.8 = s32[2,8]{1,0:T(2,128)S(1)} copy-done((s32[2,8]{1,0:T(2,128)S(1)}, s32[2,8]{1,0:T(2,128)}, u32[]{:S(2)}) %copy-start.8) | copy-done | bytes 88
  3.4 0.7 %copy-done.9 = s32[2]{0:T(128)S(1)} copy-done((s32[2]{0:T(128)S(1)}, s32[2]{0:T(128)}, u32[]{:S(2)}) %copy-start.9) | copy-done | bytes 32
  4.1 0.9 %rotary.1 = (bf16[2,1664]{1,0:T(2,128)(2,1)S(1)}, f32[8,896]{1,0:T(8,128)S(1)}) custom-call(s32[2,8]{1,0:T(2,128)S(1)} %copy-done.8, s32[2]{0:T(128)S(1)} %copy-done.9, bf16[2,768]{1,0:T(2,128)(2,1)S(1)} %copy-done.4, bf16[2,768]{1,0:T(2,128)(2,1)S(1)} %copy-done.5, bf16[2,768]{1,0:T(2,128)(2,1)S(1)} %copy-done.6, bf16[2,768]{1,0:T(2,128)(2,1)S(1)} %copy-done.7), custom_call_target="tpu_custom_call" | custom-call | bytes 12360 | tf_op jit(solution)/shard_map/rotary/pallas_call | solution.py:217
  5.0 3.0 %collective-permute-start = (bf16[2,1664]{1,0:T(2,128)(2,1)S(1)}, bf16[2,1664]{1,0:T(2,128)(2,1)S(1)}, u32[]{:S(2)}, u32[]{:S(2)}) collective-permute-start(bf16[2,1664]{1,0:T(2,128)(2,1)S(1)} %get-tuple-element.18.mine), channel_id=1, source_target_pairs={{0,4},{4,0},{8,12},{12,8},{16,20},{20,16},{24,28},{28,24},{1,5},{5... | collective-permute-start | bytes 19976 | tf_op jit(solution)/shard_map/ppermute | solution.py:522
  8.0 1.6 %collective-permute-done.theirs = bf16[2,1664]{1,0:T(2,128)(2,1)S(1)} collective-permute-done((bf16[2,1664]{1,0:T(2,128)(2,1)S(1)}, bf16[2,1664]{1,0:T(2,128)(2,1)S(1)}, u32[]{:S(2)}, u32[]{:S(2)}) %collective-permute-start) | collective-permute-done | bytes 6688 | tf_op jit(solution)/shard_map/ppermute | solution.py:522
  9.6 4.1 %collective-permute-start.3 = (bf16[2,2,1664]{2,1,0:T(2,128)(2,1)S(1)}, bf16[2,2,1664]{2,1,0:T(2,128)(2,1)S(1)}, u32[]{:S(2)}, u32[]{:S(2)}) collective-permute-start(bf16[2,2,1664]{2,1,0:T(2,128)(2,1)S(1)} %merge.2.a0), channel_id=1, source_target_pairs={{0,24},{4,28},{8,16},{12,20},{16,8},{20,12},{24,0},{28,4},{1,25},{... | collective-permute-start | bytes 39944 | tf_op jit(solution)/shard_map/ppermute | solution.py:522
  13.7 0.0 collective-permute-start.2
  13.7 0.6 collective-permute-start.1
  14.3 1.1 %collective-permute-done.3.a3 = bf16[2,2,1664]{2,1,0:T(2,128)(2,1)S(1)} collective-permute-done((bf16[2,2,1664]{2,1,0:T(2,128)(2,1)S(1)}, bf16[2,2,1664]{2,1,0:T(2,128)(2,1)S(1)}, u32[]{:S(2)}, u32[]{:S(2)}) %collective-permute-start.3) | collective-permute-done | bytes 13344 | tf_op jit(solution)/shard_map/ppermute | solution.py:522
  15.4 2.9 %collective-permute-done.2.a2 = bf16[2,2,1664]{2,1,0:T(2,128)(2,1)S(1)} collective-permute-done((bf16[2,2,1664]{2,1,0:T(2,128)(2,1)S(1)}, bf16[2,2,1664]{2,1,0:T(2,128)(2,1)S(1)}, u32[]{:S(2)}, u32[]{:S(2)}) %collective-permute-start.2) | collective-permute-done | bytes 13344 | tf_op jit(solution)/shard_map/ppermute | solution.py:522
  18.3 0.0 collective-permute-done.1.a1
  18.3 0.0 copy-start.2
  18.3 4.0 %attend.1 = (bf16[8,896]{1,0:T(8,128)(2,1)S(1)}, f32[16,768]{1,0:T(8,128)S(1)}, f32[16,128]{1,0:T(8,128)S(1)}) custom-call(bf16[2,2,1664]{2,1,0:T(2,128)(2,1)S(1)} %merge.2.a0, bf16[2,2,1664]{2,1,0:T(2,128)(2,1)S(1)} %collective-permute-done.1.a1, bf16[2,2,1664]{2,1,0:T(2,128)(2,1)S(1)} %collective-permute-done.2.a2, ...), custom_call_target="tpu_custom_call" | custom-call | bytes 4014080 | tf_op jit(solution)/shard_map/attend/pallas_call | solution.py:217
  22.4 1.6 %collective-permute-start.4 = (bf16[8,896]{1,0:T(8,128)(2,1)S(1)}, bf16[8,896]{1,0:T(8,128)(2,1)S(1)}, u32[]{:S(2)}, u32[]{:S(2)}) collective-permute-start(bf16[8,896]{1,0:T(8,128)(2,1)S(1)} %get-tuple-element.20.mine), channel_id=1, source_target_pairs={{0,4},{4,0},{8,12},{12,8},{16,20},{20,16},{24,28},{28,24},{1,5},{5... | collective-permute-start | bytes 43016 | tf_op jit(solution)/shard_map/ppermute | solution.py:522
  24.0 2.2 %collective-permute-done.4.theirs = bf16[8,896]{1,0:T(8,128)(2,1)S(1)} collective-permute-done((bf16[8,896]{1,0:T(8,128)(2,1)S(1)}, bf16[8,896]{1,0:T(8,128)(2,1)S(1)}, u32[]{:S(2)}, u32[]{:S(2)}) %collective-permute-start.4) | collective-permute-done | bytes 14368 | tf_op jit(solution)/shard_map/ppermute | solution.py:522
  26.2 1.4 %collective-permute-start.7 = (bf16[2,8,896]{2,1,0:T(8,128)(2,1)S(1)}, bf16[2,8,896]{2,1,0:T(8,128)(2,1)S(1)}, u32[]{:S(2)}, u32[]{:S(2)}) collective-permute-start(bf16[2,8,896]{2,1,0:T(8,128)(2,1)S(1)} %merge.3.b0), channel_id=1, source_target_pairs={{0,24},{4,28},{8,16},{12,20},{16,8},{20,12},{24,0},{28,4},{1,25},{... | collective-permute-start | bytes 86024 | tf_op jit(solution)/shard_map/ppermute | solution.py:522
  27.6 0.6 %collective-permute-start.6 = (bf16[2,8,896]{2,1,0:T(8,128)(2,1)S(1)}, bf16[2,8,896]{2,1,0:T(8,128)(2,1)S(1)}, u32[]{:S(2)}, u32[]{:S(2)}) collective-permute-start(bf16[2,8,896]{2,1,0:T(8,128)(2,1)S(1)} %merge.3.b0), channel_id=1, source_target_pairs={{0,16},{4,20},{8,24},{12,28},{16,0},{20,4},{24,8},{28,12},{1,17},{... | collective-permute-start | bytes 86024 | tf_op jit(solution)/shard_map/ppermute | solution.py:522
  28.3 2.3 %collective-permute-start.5 = (bf16[2,8,896]{2,1,0:T(8,128)(2,1)S(1)}, bf16[2,8,896]{2,1,0:T(8,128)(2,1)S(1)}, u32[]{:S(2)}, u32[]{:S(2)}) collective-permute-start(bf16[2,8,896]{2,1,0:T(8,128)(2,1)S(1)} %merge.3.b0), channel_id=1, source_target_pairs={{0,8},{4,12},{8,0},{12,4},{16,24},{20,28},{24,16},{28,20},{1,9},{5... | collective-permute-start | bytes 86024 | tf_op jit(solution)/shard_map/ppermute | solution.py:522
  30.6 1.3 %collective-permute-done.7.b3 = bf16[2,8,896]{2,1,0:T(8,128)(2,1)S(1)} collective-permute-done((bf16[2,8,896]{2,1,0:T(8,128)(2,1)S(1)}, bf16[2,8,896]{2,1,0:T(8,128)(2,1)S(1)}, u32[]{:S(2)}, u32[]{:S(2)}) %collective-permute-start.7) | collective-permute-done | bytes 28704 | tf_op jit(solution)/shard_map/ppermute | solution.py:522
  31.8 0.6 collective-permute-done.6.b2
  32.4 0.3 collective-permute-done.5.b1
  32.7 0.7 %combine.1.p0 = bf16[16,384]{1,0:T(8,128)(2,1)S(1)} custom-call(bf16[2,8,896]{2,1,0:T(8,128)(2,1)S(1)} %merge.3.b0, bf16[2,8,896]{2,1,0:T(8,128)(2,1)S(1)} %collective-permute-done.5.b1, bf16[2,8,896]{2,1,0:T(8,128)(2,1)S(1)} %collective-permute-done.6.b2, bf16[2,8,896]{2,1,0:T(8,128)(2,1)S(1)} %collective-permute-done.7.b3, ...), custom_call_target="tpu_custom_call" | custom-call | bytes 712704 | tf_op jit(solution)/shard_map/combine/pallas_call | solution.py:217
  33.4 0.1 collective-permute-start.10
  33.4 1.6 %collective-permute-start.9 = (bf16[16,384]{1,0:T(8,128)(2,1)S(1)}, bf16[16,384]{1,0:T(8,128)(2,1)S(1)}, u32[]{:S(2)}, u32[]{:S(2)}) collective-permute-start(bf16[16,384]{1,0:T(8,128)(2,1)S(1)} %combine.1.p0), channel_id=1, source_target_pairs={{0,2},{1,3},{2,0},{3,1},{4,6},{5,7},{6,4},{7,5},{8,10},{9,11},{10,... | collective-permute-start | bytes 36872 | tf_op jit(solution)/shard_map/ppermute | solution.py:522
  35.0 0.3 collective-permute-start.8
  35.3 1.3 %collective-permute-done.10.p3 = bf16[16,384]{1,0:T(8,128)(2,1)S(1)} collective-permute-done((bf16[16,384]{1,0:T(8,128)(2,1)S(1)}, bf16[16,384]{1,0:T(8,128)(2,1)S(1)}, u32[]{:S(2)}, u32[]{:S(2)}) %collective-permute-start.10) | collective-permute-done | bytes 12320 | tf_op jit(solution)/shard_map/ppermute | solution.py:522
  36.6 0.6 collective-permute-done.9.p2
  37.2 3.4 %collective-permute-start.12 = (bf16[16,384]{1,0:T(8,128)(2,1)S(1)}, bf16[16,384]{1,0:T(8,128)(2,1)S(1)}, u32[]{:S(2)}, u32[]{:S(2)}) collective-permute-start(bf16[16,384]{1,0:T(8,128)(2,1)S(1)} %head_sum.1), channel_id=1, source_target_pairs={{0,28},{4,24},{1,20},{5,16},{2,12},{6,8},{3,4},{7,0},{9,29},{13,25... | collective-permute-start | bytes 36872 | tf_op jit(solution)/shard_map/ppermute | solution.py:611
  40.6 0.6 collective-permute-start.11
  41.2 0.8 %collective-permute-done.12.flip = bf16[16,384]{1,0:T(8,128)(2,1)S(1)} collective-permute-done((bf16[16,384]{1,0:T(8,128)(2,1)S(1)}, bf16[16,384]{1,0:T(8,128)(2,1)S(1)}, u32[]{:S(2)}, u32[]{:S(2)}) %collective-permute-start.12) | collective-permute-done | bytes 12320 | tf_op jit(solution)/shard_map/ppermute | solution.py:611
  42.0 1.7 %collective-permute-done.11.same = bf16[16,384]{1,0:T(8,128)(2,1)S(1)} collective-permute-done((bf16[16,384]{1,0:T(8,128)(2,1)S(1)}, bf16[16,384]{1,0:T(8,128)(2,1)S(1)}, u32[]{:S(2)}, u32[]{:S(2)}) %collective-permute-start.11) | collective-permute-done | bytes 12320 | tf_op jit(solution)/shard_map/ppermute | solution.py:611
  43.7 0.5 gate_up.1
  44.3 1.3 %collective-permute-done.13.theirs = bf16[16,2176]{1,0:T(8,128)(2,1)S(1)} collective-permute-done((bf16[16,2176]{1,0:T(8,128)(2,1)S(1)}, bf16[16,2176]{1,0:T(8,128)(2,1)S(1)}, u32[]{:S(2)}, u32[]{:S(2)}) %collective-permute-start.13) | collective-permute-done | bytes 69664 | tf_op jit(solution)/shard_map/ppermute | solution.py:522
  45.5 0.1 core_sum.1.mine
  45.6 2.3 %collective-permute-start.14 = (bf16[16,2176]{1,0:T(8,128)(2,1)S(1)}, bf16[16,2176]{1,0:T(8,128)(2,1)S(1)}, u32[]{:S(2)}, u32[]{:S(2)}) collective-permute-start(bf16[16,2176]{1,0:T(8,128)(2,1)S(1)} %core_sum.1.mine), channel_id=1, source_target_pairs={{0,2},{1,3},{2,0},{3,1},{4,6},{5,7},{6,4},{7,5},{8,10},{9,11},{10,... | collective-permute-start | bytes 208904 | tf_op jit(solution)/shard_map/ppermute | solution.py:522
  47.9 2.5 %collective-permute-done.14.theirs = bf16[16,2176]{1,0:T(8,128)(2,1)S(1)} collective-permute-done((bf16[16,2176]{1,0:T(8,128)(2,1)S(1)}, bf16[16,2176]{1,0:T(8,128)(2,1)S(1)}, u32[]{:S(2)}, u32[]{:S(2)}) %collective-permute-start.14) | collective-permute-done | bytes 69664 | tf_op jit(solution)/shard_map/ppermute | solution.py:522
  50.4 0.4 down.1
  50.8 0.6 collective-permute-start.15
  51.4 3.3 %collective-permute-done.15.got = f32[8,768]{1,0:T(8,128)S(1)} collective-permute-done((f32[8,768]{1,0:T(8,128)S(1)}, f32[8,768]{1,0:T(8,128)S(1)}, u32[]{:S(2)}, u32[]{:S(2)}) %collective-permute-start.15) | collective-permute-done | bytes 24608 | tf_op jit(solution)/shard_map/ppermute | solution.py:522
  54.8 2.5 %collective-permute-start.16 = (f32[2,768]{1,0:T(2,128)S(1)}, f32[2,768]{1,0:T(2,128)S(1)}, u32[]{:S(2)}, u32[]{:S(2)}) collective-permute-start(f32[2,768]{1,0:T(2,128)S(1)} %get-tuple-element.28), channel_id=1, source_target_pairs={{0,24},{4,28},{8,16},{12,20},{16,8},{20,12},{24,0},{28,4},{1,25},{... | collective-permute-start | bytes 18440 | tf_op jit(solution)/shard_map/ppermute | solution.py:522
  57.3 1.9 %collective-permute-start.18 = (f32[2,768]{1,0:T(2,128)S(1)}, f32[2,768]{1,0:T(2,128)S(1)}, u32[]{:S(2)}, u32[]{:S(2)}) collective-permute-start(f32[2,768]{1,0:T(2,128)S(1)} %get-tuple-element.30), channel_id=1, source_target_pairs={{0,8},{4,12},{8,0},{12,4},{16,24},{20,28},{24,16},{28,20},{1,9},{5... | collective-permute-start | bytes 18440 | tf_op jit(solution)/shard_map/ppermute | solution.py:522
  59.2 1.0 %collective-permute-done.16.c1 = f32[2,768]{1,0:T(2,128)S(1)} collective-permute-done((f32[2,768]{1,0:T(2,128)S(1)}, f32[2,768]{1,0:T(2,128)S(1)}, u32[]{:S(2)}, u32[]{:S(2)}) %collective-permute-start.16) | collective-permute-done | bytes 6176 | tf_op jit(solution)/shard_map/ppermute | solution.py:522
  60.3 1.6 %collective-permute-done.17.c2 = f32[2,768]{1,0:T(2,128)S(1)} collective-permute-done((f32[2,768]{1,0:T(2,128)S(1)}, f32[2,768]{1,0:T(2,128)S(1)}, u32[]{:S(2)}, u32[]{:S(2)}) %collective-permute-start.17) | collective-permute-done | bytes 6176 | tf_op jit(solution)/shard_map/ppermute | solution.py:522
  61.8 0.6 final.1
  (24 shorter events, 0.1 us)
Async XLA Ops:
  0.0 0.7 %copy-start.4 = (bf16[2,768]{1,0:T(2,128)(2,1)S(1)}, bf16[2,768]{1,0:T(2,128)(2,1)}, u32[]{:S(2)}) copy-start(bf16[2,768]{1,0:T(2,128)(2,1)} %refs_2_.1) | copy-start | bytes 9220
  0.7 0.7 %copy-start.5 = (bf16[2,768]{1,0:T(2,128)(2,1)S(1)}, bf16[2,768]{1,0:T(2,128)(2,1)}, u32[]{:S(2)}) copy-start(bf16[2,768]{1,0:T(2,128)(2,1)} %refs_3_.1) | copy-start | bytes 9220
  1.4 0.7 %copy-start.6 = (bf16[2,768]{1,0:T(2,128)(2,1)S(1)}, bf16[2,768]{1,0:T(2,128)(2,1)}, u32[]{:S(2)}) copy-start(bf16[2,768]{1,0:T(2,128)(2,1)} %refs_4_.1) | copy-start | bytes 9220
  2.1 0.7 %copy-start.7 = (bf16[2,768]{1,0:T(2,128)(2,1)S(1)}, bf16[2,768]{1,0:T(2,128)(2,1)}, u32[]{:S(2)}) copy-start(bf16[2,768]{1,0:T(2,128)(2,1)} %refs_5_.1) | copy-start | bytes 9220
  2.7 0.7 %copy-start.8 = (s32[2,8]{1,0:T(2,128)S(1)}, s32[2,8]{1,0:T(2,128)}, u32[]{:S(2)}) copy-start(s32[2,8]{1,0:T(2,128)} %refs_0_.1) | copy-start | bytes 196
  3.4 0.7 %copy-start.9 = (s32[2]{0:T(128)S(1)}, s32[2]{0:T(128)}, u32[]{:S(2)}) copy-start(s32[2]{0:T(128)} %refs_1_.1) | copy-start | bytes 28
  5.0 4.6 %collective-permute-start = (bf16[2,1664]{1,0:T(2,128)(2,1)S(1)}, bf16[2,1664]{1,0:T(2,128)(2,1)S(1)}, u32[]{:S(2)}, u32[]{:S(2)}) collective-permute-start(bf16[2,1664]{1,0:T(2,128)(2,1)S(1)} %get-tuple-element.18.mine), channel_id=1, source_target_pairs={{0,4},{4,0},{8,12},{12,8},{16,20},{20,16},{24,28},{28,24},{1,5},{5... | collective-permute-start | bytes 19976 | tf_op jit(solution)/shard_map/ppermute | solution.py:522
  9.6 5.8 %collective-permute-start.3 = (bf16[2,2,1664]{2,1,0:T(2,128)(2,1)S(1)}, bf16[2,2,1664]{2,1,0:T(2,128)(2,1)S(1)}, u32[]{:S(2)}, u32[]{:S(2)}) collective-permute-start(bf16[2,2,1664]{2,1,0:T(2,128)(2,1)S(1)} %merge.2.a0), channel_id=1, source_target_pairs={{0,24},{4,28},{8,16},{12,20},{16,8},{20,12},{24,0},{28,4},{1,25},{... | collective-permute-start | bytes 39944 | tf_op jit(solution)/shard_map/ppermute | solution.py:522
  13.7 4.6 %collective-permute-start.2 = (bf16[2,2,1664]{2,1,0:T(2,128)(2,1)S(1)}, bf16[2,2,1664]{2,1,0:T(2,128)(2,1)S(1)}, u32[]{:S(2)}, u32[]{:S(2)}) collective-permute-start(bf16[2,2,1664]{2,1,0:T(2,128)(2,1)S(1)} %merge.2.a0), channel_id=1, source_target_pairs={{0,16},{4,20},{8,24},{12,28},{16,0},{20,4},{24,8},{28,12},{1,17},{... | collective-permute-start | bytes 39944 | tf_op jit(solution)/shard_map/ppermute | solution.py:522
  13.7 4.6 %collective-permute-start.1 = (bf16[2,2,1664]{2,1,0:T(2,128)(2,1)S(1)}, bf16[2,2,1664]{2,1,0:T(2,128)(2,1)S(1)}, u32[]{:S(2)}, u32[]{:S(2)}) collective-permute-start(bf16[2,2,1664]{2,1,0:T(2,128)(2,1)S(1)} %merge.2.a0), channel_id=1, source_target_pairs={{0,8},{4,12},{8,0},{12,4},{16,24},{20,28},{24,16},{28,20},{1,9},{5... | collective-permute-start | bytes 39944 | tf_op jit(solution)/shard_map/ppermute | solution.py:522
  18.3 14.4 %copy-start.3 = (bf16[768,384]{1,0:T(8,128)(2,1)S(1)}, bf16[768,384]{1,0:T(8,128)(2,1)}, u32[]{:S(2)}) copy-start(bf16[768,384]{1,0:T(8,128)(2,1)} %weight.2) | copy-start | bytes 1769476
  18.3 22.8 %copy-start.10 = (bf16[768]{0:T(1024)(128)(2,1)S(1)}, bf16[768]{0:T(1024)(128)(2,1)}, u32[]{:S(2)}) copy-start(bf16[768]{0:T(1024)(128)(2,1)} %param.22) | copy-start | bytes 4612
  18.3 25.4 %copy-start.1 = (bf16[768,1024]{1,0:T(8,128)(2,1)S(1)}, bf16[768,1024]{1,0:T(8,128)(2,1)}, u32[]{:S(2)}) copy-start(bf16[768,1024]{1,0:T(8,128)(2,1)} %gate.1) | copy-start | bytes 4718596
  18.3 25.4 %copy-start.2 = (bf16[768,1024]{1,0:T(8,128)(2,1)S(1)}, bf16[768,1024]{1,0:T(8,128)(2,1)}, u32[]{:S(2)}) copy-start(bf16[768,1024]{1,0:T(8,128)(2,1)} %up.1) | copy-start | bytes 4718596
  22.4 3.8 %collective-permute-start.4 = (bf16[8,896]{1,0:T(8,128)(2,1)S(1)}, bf16[8,896]{1,0:T(8,128)(2,1)S(1)}, u32[]{:S(2)}, u32[]{:S(2)}) collective-permute-start(bf16[8,896]{1,0:T(8,128)(2,1)S(1)} %get-tuple-element.20.mine), channel_id=1, source_target_pairs={{0,4},{4,0},{8,12},{12,8},{16,20},{20,16},{24,28},{28,24},{1,5},{5... | collective-permute-start | bytes 43016 | tf_op jit(solution)/shard_map/ppermute | solution.py:522
  26.2 5.7 %collective-permute-start.7 = (bf16[2,8,896]{2,1,0:T(8,128)(2,1)S(1)}, bf16[2,8,896]{2,1,0:T(8,128)(2,1)S(1)}, u32[]{:S(2)}, u32[]{:S(2)}) collective-permute-start(bf16[2,8,896]{2,1,0:T(8,128)(2,1)S(1)} %merge.3.b0), channel_id=1, source_target_pairs={{0,24},{4,28},{8,16},{12,20},{16,8},{20,12},{24,0},{28,4},{1,25},{... | collective-permute-start | bytes 86024 | tf_op jit(solution)/shard_map/ppermute | solution.py:522
  27.6 4.8 %collective-permute-start.6 = (bf16[2,8,896]{2,1,0:T(8,128)(2,1)S(1)}, bf16[2,8,896]{2,1,0:T(8,128)(2,1)S(1)}, u32[]{:S(2)}, u32[]{:S(2)}) collective-permute-start(bf16[2,8,896]{2,1,0:T(8,128)(2,1)S(1)} %merge.3.b0), channel_id=1, source_target_pairs={{0,16},{4,20},{8,24},{12,28},{16,0},{20,4},{24,8},{28,12},{1,17},{... | collective-permute-start | bytes 86024 | tf_op jit(solution)/shard_map/ppermute | solution.py:522
  28.3 4.4 %collective-permute-start.5 = (bf16[2,8,896]{2,1,0:T(8,128)(2,1)S(1)}, bf16[2,8,896]{2,1,0:T(8,128)(2,1)S(1)}, u32[]{:S(2)}, u32[]{:S(2)}) collective-permute-start(bf16[2,8,896]{2,1,0:T(8,128)(2,1)S(1)} %merge.3.b0), channel_id=1, source_target_pairs={{0,8},{4,12},{8,0},{12,4},{16,24},{20,28},{24,16},{28,20},{1,9},{5... | collective-permute-start | bytes 86024 | tf_op jit(solution)/shard_map/ppermute | solution.py:522
  33.4 3.2 %collective-permute-start.10 = (bf16[16,384]{1,0:T(8,128)(2,1)S(1)}, bf16[16,384]{1,0:T(8,128)(2,1)S(1)}, u32[]{:S(2)}, u32[]{:S(2)}) collective-permute-start(bf16[16,384]{1,0:T(8,128)(2,1)S(1)} %combine.1.p0), channel_id=1, source_target_pairs={{0,3},{1,2},{2,1},{3,0},{4,7},{5,6},{6,5},{7,4},{8,11},{9,10},{10,... | collective-permute-start | bytes 36872 | tf_op jit(solution)/shard_map/ppermute | solution.py:522
  33.4 3.8 %collective-permute-start.9 = (bf16[16,384]{1,0:T(8,128)(2,1)S(1)}, bf16[16,384]{1,0:T(8,128)(2,1)S(1)}, u32[]{:S(2)}, u32[]{:S(2)}) collective-permute-start(bf16[16,384]{1,0:T(8,128)(2,1)S(1)} %combine.1.p0), channel_id=1, source_target_pairs={{0,2},{1,3},{2,0},{3,1},{4,6},{5,7},{6,4},{7,5},{8,10},{9,11},{10,... | collective-permute-start | bytes 36872 | tf_op jit(solution)/shard_map/ppermute | solution.py:522
  35.0 2.2 %collective-permute-start.8 = (bf16[16,384]{1,0:T(8,128)(2,1)S(1)}, bf16[16,384]{1,0:T(8,128)(2,1)S(1)}, u32[]{:S(2)}, u32[]{:S(2)}) collective-permute-start(bf16[16,384]{1,0:T(8,128)(2,1)S(1)} %combine.1.p0), channel_id=1, source_target_pairs={{0,1},{1,0},{2,3},{3,2},{4,5},{5,4},{6,7},{7,6},{8,9},{9,8},{10,11... | collective-permute-start | bytes 36872 | tf_op jit(solution)/shard_map/ppermute | solution.py:522
  37.2 4.8 %collective-permute-start.12 = (bf16[16,384]{1,0:T(8,128)(2,1)S(1)}, bf16[16,384]{1,0:T(8,128)(2,1)S(1)}, u32[]{:S(2)}, u32[]{:S(2)}) collective-permute-start(bf16[16,384]{1,0:T(8,128)(2,1)S(1)} %head_sum.1), channel_id=1, source_target_pairs={{0,28},{4,24},{1,20},{5,16},{2,12},{6,8},{3,4},{7,0},{9,29},{13,25... | collective-permute-start | bytes 36872 | tf_op jit(solution)/shard_map/ppermute | solution.py:611
  40.6 3.1 %collective-permute-start.11 = (bf16[16,384]{1,0:T(8,128)(2,1)S(1)}, bf16[16,384]{1,0:T(8,128)(2,1)S(1)}, u32[]{:S(2)}, u32[]{:S(2)}) collective-permute-start(bf16[16,384]{1,0:T(8,128)(2,1)S(1)} %head_sum.1), channel_id=1, source_target_pairs={{0,24},{4,28},{1,16},{5,20},{2,8},{6,12},{3,0},{7,4},{9,25},{13,29... | collective-permute-start | bytes 36872 | tf_op jit(solution)/shard_map/ppermute | solution.py:611
  43.7 6.7 %copy-start = (bf16[1024,768]{1,0:T(8,128)(2,1)S(1)}, bf16[1024,768]{1,0:T(8,128)(2,1)}, u32[]{:S(2)}) copy-start(bf16[1024,768]{1,0:T(8,128)(2,1)} %weight.3) | copy-start | bytes 4718596
  44.3 1.3 %collective-permute-start.13 = (bf16[16,2176]{1,0:T(8,128)(2,1)S(1)}, bf16[16,2176]{1,0:T(8,128)(2,1)S(1)}, u32[]{:S(2)}, u32[]{:S(2)}) collective-permute-start(bf16[16,2176]{1,0:T(8,128)(2,1)S(1)} %get-tuple-element.24.mine), channel_id=1, source_target_pairs={{0,1},{1,0},{2,3},{3,2},{4,5},{5,4},{6,7},{7,6},{8,9},{9,8},{10,11... | collective-permute-start | bytes 208904 | tf_op jit(solution)/shard_map/ppermute | solution.py:522
  45.6 4.8 %collective-permute-start.14 = (bf16[16,2176]{1,0:T(8,128)(2,1)S(1)}, bf16[16,2176]{1,0:T(8,128)(2,1)S(1)}, u32[]{:S(2)}, u32[]{:S(2)}) collective-permute-start(bf16[16,2176]{1,0:T(8,128)(2,1)S(1)} %core_sum.1.mine), channel_id=1, source_target_pairs={{0,2},{1,3},{2,0},{3,1},{4,6},{5,7},{6,4},{7,5},{8,10},{9,11},{10,... | collective-permute-start | bytes 208904 | tf_op jit(solution)/shard_map/ppermute | solution.py:522
  50.8 3.9 %collective-permute-start.15 = (f32[8,768]{1,0:T(8,128)S(1)}, f32[8,768]{1,0:T(8,128)S(1)}, u32[]{:S(2)}, u32[]{:S(2)}) collective-permute-start(f32[8,768]{1,0:T(8,128)S(1)} %get-tuple-element.26), channel_id=1, source_target_pairs={{0,4},{4,0},{8,12},{12,8},{16,20},{20,16},{24,28},{28,24},{1,5},{5... | collective-permute-start | bytes 73736 | tf_op jit(solution)/shard_map/ppermute | solution.py:522
  54.8 5.5 %collective-permute-start.16 = (f32[2,768]{1,0:T(2,128)S(1)}, f32[2,768]{1,0:T(2,128)S(1)}, u32[]{:S(2)}, u32[]{:S(2)}) collective-permute-start(f32[2,768]{1,0:T(2,128)S(1)} %get-tuple-element.28), channel_id=1, source_target_pairs={{0,24},{4,28},{8,16},{12,20},{16,8},{20,12},{24,0},{28,4},{1,25},{... | collective-permute-start | bytes 18440 | tf_op jit(solution)/shard_map/ppermute | solution.py:522
  57.3 4.5 %collective-permute-start.17 = (f32[2,768]{1,0:T(2,128)S(1)}, f32[2,768]{1,0:T(2,128)S(1)}, u32[]{:S(2)}, u32[]{:S(2)}) collective-permute-start(f32[2,768]{1,0:T(2,128)S(1)} %get-tuple-element.29), channel_id=1, source_target_pairs={{0,16},{4,20},{8,24},{12,28},{16,0},{20,4},{24,8},{28,12},{1,17},{... | collective-permute-start | bytes 18440 | tf_op jit(solution)/shard_map/ppermute | solution.py:522
  57.3 4.5 %collective-permute-start.18 = (f32[2,768]{1,0:T(2,128)S(1)}, f32[2,768]{1,0:T(2,128)S(1)}, u32[]{:S(2)}, u32[]{:S(2)}) collective-permute-start(f32[2,768]{1,0:T(2,128)S(1)} %get-tuple-element.30), channel_id=1, source_target_pairs={{0,8},{4,12},{8,0},{12,4},{16,24},{20,28},{24,16},{28,20},{1,9},{5... | collective-permute-start | bytes 18440 | tf_op jit(solution)/shard_map/ppermute | solution.py:522

commit v5 on v4

--- a/solution.py
+++ b/solution.py
@@ -246,8 +246,8 @@
 
 
 def prepare_kernel(*refs):
-    sources, (packed, own), held = refs[:6], refs[6:8], refs[8:14]
-    scr, sems = refs[14:]
+    sources, (packed, own), held = refs[:6], refs[8:10], refs[10:16]
+    scr, sems = refs[16:]
     copies = [
         pltpu.make_async_copy(source, target, sems.at[i])
         for i, (source, target) in enumerate(zip(sources, held))
@@ -322,17 +322,8 @@
     both[1 - y] = theirs[...]
 
 
-def attend_kernel(
-    a0, a1, a2, a3, own, far_keys, far_values, part, residual, tables, scr, keys, values, sems
-):
+def attend_kernel(a0, a1, a2, a3, own, keys, values, part, residual, tables, scr):
     blocks, block_len, width = keys.shape
-    copies = [
-        pltpu.make_async_copy(far.at[b], near.at[b], sems.at[i, b])
-        for i, (far, near) in enumerate(((far_keys, keys), (far_values, values)))
-        for b in range(blocks)
-    ]
-    for copy in copies:
-        copy.start()
     rows = a0.shape[1]
     heads = width // HD
     most = 8
@@ -363,7 +354,6 @@
         limits.append(jnp.broadcast_to(limit, (heads, block_len)))
         query = jnp.sum(holder * queries, 0, keepdims=True)
         spread = jnp.where(head_mask, query, 0.0).astype(BF16)
-        copies[b].wait()
         scores.append(
             lax.dot_general(
                 spread, keys[b], (((1,), (1,)), ((), ())), preferred_element_type=F32
@@ -381,7 +371,6 @@
     numerators = []
     for b in range(blocks):
         mine = slice(b * heads, (b + 1) * heads)
-        copies[blocks + b].wait()
         full = jnp.dot(weights[mine].astype(BF16), values[b], preferred_element_type=F32)
         numerators.append(jnp.sum(jnp.where(head_mask, full, 0.0), 0, keepdims=True))
         tail = jnp.where(spot == b, shift[mine], tail)
@@ -551,12 +540,12 @@
         prepare_kernel,
         "rotary",
         [((rows, packed_width), BF16), ((slots, part_width), F32)],
-        [block_table, lengths, query_new, key_new, value_new, residual_in],
+        [block_table, lengths, query_new, key_new, value_new, residual_in, key_cache, value_cache],
         [pltpu.SMEM(block_table.shape, jnp.int32), pltpu.SMEM(lengths.shape, jnp.int32)]
         + [pltpu.VMEM((rows, width), BF16)] * 4
         + [pltpu.VMEM((8, width), F32), pltpu.SemaphoreType.DMA((6,))],
-        hbm=range(6),
-        limit=52 * 2**20,
+        hbm=range(8),
+        limit=54 * 2**20,
     )
 
     def pool_gather(values):
@@ -573,14 +562,7 @@
         "attend",
         [((slots, part_width), BF16), ((requests, width), F32), ((requests, 128), F32)],
         pool_gather(packed) + [own, key_cache, value_cache],
-        [
-            pltpu.VMEM((requests, packed_width), F32),
-            pltpu.VMEM(key_cache.shape, BF16),
-            pltpu.VMEM(value_cache.shape, BF16),
-            pltpu.SemaphoreType.DMA((2, blocks)),
-        ],
-        hbm=(5, 6),
-        limit=52 * 2**20,
+        [pltpu.VMEM((requests, packed_width), F32)],
     )
     (head_part,) = call(
         combine_kernel,

time: 62.7 us -> 58.2 us (0.928)
  local copies, waits for them, and re-layouts: 4.09 us -> 1.46 us
  Pallas kernels: 7.24 us -> 5.27 us
    unnamed x22 -> x18, local copies, waits for them, and re-layouts: 4.09 us -> 1.46 us
    pallas_call x11, Pallas kernels: 7.24 us -> 5.27 us  [call(): pl.pallas_call(kernel, out_shape=[jax.ShapeDtypeStruct(shape, dtype) for...]
where the time goes in v5:
time: 58.2 us; the launch traced here: 58 us
  starting transfers between devices  26.8 us (46%)
  waiting for transfers between devices  24.4 us (42%)
  Pallas kernels  5.27 us (9%)
  local copies, waits for them, and re-layouts  1.46 us (3%)
    ppermute x17, starting transfers between devices, flip(): lax.ppermute(values, axis, [(index, index ^ step) for index in range(size)])  22.9 us
    ppermute x17, waiting for transfers between devices, flip(): lax.ppermute(values, axis, [(index, index ^ step) for index in range(size)])  21.8 us
    pallas_call x11, Pallas kernels, call(): pl.pallas_call(kernel, out_shape=[jax.ShapeDtypeStruct(shape, dtype) for...  5.27 us
    ppermute x2, starting transfers between devices, per_device_small(): pieces.append(lax.ppermute(head_sum, ('pool', 'mlp'), route))  3.94 us
    ppermute x2, waiting for transfers between devices, per_device_small(): pieces.append(lax.ppermute(head_sum, ('pool', 'mlp'), route))  2.55 us
    unnamed x18, local copies, waits for them, and re-layouts  1.46 us
  transfers between devices with their start and end apart: 19, of which 16 were waited for; matrix products, arithmetic and copies ran while one was open for 0% of the time, Pallas kernels for 0%

profile of v5, /device:TPU:0, one launch (start us, length us, event | category | flops | bytes accessed | tf_op | source)
XLA Modules:
  0.0 58.0 jit_solution(4295305248343101670)
XLA Ops:
  0.0 1.8 %rotary.1 = (bf16[2,1664]{1,0:T(2,128)(2,1)}, f32[8,896]{1,0:T(8,128)}) custom-call(s32[2,8]{1,0:T(2,128)} %refs_0_.1, s32[2]{0:T(128)} %refs_1_.1, bf16[2,768]{1,0:T(2,128)(2,1)} %refs_2_.1, bf16[2,768]{1,0:T(2,128)(2,1)} %refs_3_.1, bf16[2,768]{1,0:T(2,128)(2,1)} %refs_4_.1, bf16[2,768]{1,0:T(2,128)(2,1)} %refs_5_.1, bf16[5,256,768]{2,1,0:T(8,128)(2,1)} %keys.1, ...), custom_call_target="tpu_custom_call" | custom-call | bytes 3944520 | tf_op jit(solution)/shard_map/rotary/pallas_call | solution.py:217
  1.8 3.0 %collective-permute-start = (bf16[2,1664]{1,0:T(2,128)(2,1)}, bf16[2,1664]{1,0:T(2,128)(2,1)S(1)}, u32[]{:S(2)}, u32[]{:S(2)}) collective-permute-start(bf16[2,1664]{1,0:T(2,128)(2,1)} %get-tuple-element.18.mine), channel_id=1, source_target_pairs={{0,4},{4,0},{8,12},{12,8},{16,20},{20,16},{24,28},{28,24},{1,5},{5... | collective-permute-start | bytes 19976 | tf_op jit(solution)/shard_map/ppermute | solution.py:511
  4.9 1.8 %collective-permute-done.theirs = bf16[2,1664]{1,0:T(2,128)(2,1)S(1)} collective-permute-done((bf16[2,1664]{1,0:T(2,128)(2,1)}, bf16[2,1664]{1,0:T(2,128)(2,1)S(1)}, u32[]{:S(2)}, u32[]{:S(2)}) %collective-permute-start) | collective-permute-done | bytes 6688 | tf_op jit(solution)/shard_map/ppermute | solution.py:511
  6.7 0.7 %copy-done.7 = bf16[2,1664]{1,0:T(2,128)(2,1)S(1)} copy-done((bf16[2,1664]{1,0:T(2,128)(2,1)S(1)}, bf16[2,1664]{1,0:T(2,128)(2,1)}, u32[]{:S(2)}) %copy-start.7) | copy-done | bytes 6680
  7.4 4.1 %collective-permute-start.3 = (bf16[2,2,1664]{2,1,0:T(2,128)(2,1)S(1)}, bf16[2,2,1664]{2,1,0:T(2,128)(2,1)S(1)}, u32[]{:S(2)}, u32[]{:S(2)}) collective-permute-start(bf16[2,2,1664]{2,1,0:T(2,128)(2,1)S(1)} %merge.2.a0), channel_id=1, source_target_pairs={{0,24},{4,28},{8,16},{12,20},{16,8},{20,12},{24,0},{28,4},{1,25},{... | collective-permute-start | bytes 39944 | tf_op jit(solution)/shard_map/ppermute | solution.py:511
  11.5 0.0 collective-permute-start.2
  11.5 0.6 collective-permute-start.1
  12.0 1.1 %collective-permute-done.3.a3 = bf16[2,2,1664]{2,1,0:T(2,128)(2,1)S(1)} collective-permute-done((bf16[2,2,1664]{2,1,0:T(2,128)(2,1)S(1)}, bf16[2,2,1664]{2,1,0:T(2,128)(2,1)S(1)}, u32[]{:S(2)}, u32[]{:S(2)}) %collective-permute-start.3) | collective-permute-done | bytes 13344 | tf_op jit(solution)/shard_map/ppermute | solution.py:511
  13.2 2.9 %collective-permute-done.2.a2 = bf16[2,2,1664]{2,1,0:T(2,128)(2,1)S(1)} collective-permute-done((bf16[2,2,1664]{2,1,0:T(2,128)(2,1)S(1)}, bf16[2,2,1664]{2,1,0:T(2,128)(2,1)S(1)}, u32[]{:S(2)}, u32[]{:S(2)}) %collective-permute-start.2) | collective-permute-done | bytes 13344 | tf_op jit(solution)/shard_map/ppermute | solution.py:511
  16.1 0.0 collective-permute-done.1.a1
  16.1 0.0 copy-done.1
  16.1 0.7 %copy-done.6 = f32[8,896]{1,0:T(8,128)S(1)} copy-done((f32[8,896]{1,0:T(8,128)S(1)}, f32[8,896]{1,0:T(8,128)}, u32[]{:S(2)}) %copy-start.6) | copy-done | bytes 28696
  16.9 1.1 %attend.1 = (bf16[8,896]{1,0:T(8,128)(2,1)S(1)}, f32[16,768]{1,0:T(8,128)S(1)}, f32[16,128]{1,0:T(8,128)S(1)}) custom-call(bf16[2,2,1664]{2,1,0:T(2,128)(2,1)S(1)} %merge.2.a0, bf16[2,2,1664]{2,1,0:T(2,128)(2,1)S(1)} %collective-permute-done.1.a1, bf16[2,2,1664]{2,1,0:T(2,128)(2,1)S(1)} %collective-permute-done.2.a2, ...), custom_call_target="tpu_custom_call" | custom-call | bytes 4014080 | tf_op jit(solution)/shard_map/attend/pallas_call | solution.py:217
  18.0 1.6 %collective-permute-start.4 = (bf16[8,896]{1,0:T(8,128)(2,1)S(1)}, bf16[8,896]{1,0:T(8,128)(2,1)S(1)}, u32[]{:S(2)}, u32[]{:S(2)}) collective-permute-start(bf16[8,896]{1,0:T(8,128)(2,1)S(1)} %get-tuple-element.20.mine), channel_id=1, source_target_pairs={{0,4},{4,0},{8,12},{12,8},{16,20},{20,16},{24,28},{28,24},{1,5},{5... | collective-permute-start | bytes 43016 | tf_op jit(solution)/shard_map/ppermute | solution.py:511
  19.6 2.2 %collective-permute-done.4.theirs = bf16[8,896]{1,0:T(8,128)(2,1)S(1)} collective-permute-done((bf16[8,896]{1,0:T(8,128)(2,1)S(1)}, bf16[8,896]{1,0:T(8,128)(2,1)S(1)}, u32[]{:S(2)}, u32[]{:S(2)}) %collective-permute-start.4) | collective-permute-done | bytes 14368 | tf_op jit(solution)/shard_map/ppermute | solution.py:511
  21.8 1.5 %collective-permute-start.7 = (bf16[2,8,896]{2,1,0:T(8,128)(2,1)S(1)}, bf16[2,8,896]{2,1,0:T(8,128)(2,1)S(1)}, u32[]{:S(2)}, u32[]{:S(2)}) collective-permute-start(bf16[2,8,896]{2,1,0:T(8,128)(2,1)S(1)} %merge.3.b0), channel_id=1, source_target_pairs={{0,24},{4,28},{8,16},{12,20},{16,8},{20,12},{24,0},{28,4},{1,25},{... | collective-permute-start | bytes 86024 | tf_op jit(solution)/shard_map/ppermute | solution.py:511
  23.2 0.6 %collective-permute-start.6 = (bf16[2,8,896]{2,1,0:T(8,128)(2,1)S(1)}, bf16[2,8,896]{2,1,0:T(8,128)(2,1)S(1)}, u32[]{:S(2)}, u32[]{:S(2)}) collective-permute-start(bf16[2,8,896]{2,1,0:T(8,128)(2,1)S(1)} %merge.3.b0), channel_id=1, source_target_pairs={{0,16},{4,20},{8,24},{12,28},{16,0},{20,4},{24,8},{28,12},{1,17},{... | collective-permute-start | bytes 86024 | tf_op jit(solution)/shard_map/ppermute | solution.py:511
  23.9 2.3 %collective-permute-start.5 = (bf16[2,8,896]{2,1,0:T(8,128)(2,1)S(1)}, bf16[2,8,896]{2,1,0:T(8,128)(2,1)S(1)}, u32[]{:S(2)}, u32[]{:S(2)}) collective-permute-start(bf16[2,8,896]{2,1,0:T(8,128)(2,1)S(1)} %merge.3.b0), channel_id=1, source_target_pairs={{0,8},{4,12},{8,0},{12,4},{16,24},{20,28},{24,16},{28,20},{1,9},{5... | collective-permute-start | bytes 86024 | tf_op jit(solution)/shard_map/ppermute | solution.py:511
  26.2 1.3 %collective-permute-done.7.b3 = bf16[2,8,896]{2,1,0:T(8,128)(2,1)S(1)} collective-permute-done((bf16[2,8,896]{2,1,0:T(8,128)(2,1)S(1)}, bf16[2,8,896]{2,1,0:T(8,128)(2,1)S(1)}, u32[]{:S(2)}, u32[]{:S(2)}) %collective-permute-start.7) | collective-permute-done | bytes 28704 | tf_op jit(solution)/shard_map/ppermute | solution.py:511
  27.4 0.6 %collective-permute-done.6.b2 = bf16[2,8,896]{2,1,0:T(8,128)(2,1)S(1)} collective-permute-done((bf16[2,8,896]{2,1,0:T(8,128)(2,1)S(1)}, bf16[2,8,896]{2,1,0:T(8,128)(2,1)S(1)}, u32[]{:S(2)}, u32[]{:S(2)}) %collective-permute-start.6) | collective-permute-done | bytes 28704 | tf_op jit(solution)/shard_map/ppermute | solution.py:511
  28.0 0.3 collective-permute-done.5.b1
  28.3 0.7 %combine.1.p0 = bf16[16,384]{1,0:T(8,128)(2,1)S(1)} custom-call(bf16[2,8,896]{2,1,0:T(8,128)(2,1)S(1)} %merge.3.b0, bf16[2,8,896]{2,1,0:T(8,128)(2,1)S(1)} %collective-permute-done.5.b1, bf16[2,8,896]{2,1,0:T(8,128)(2,1)S(1)} %collective-permute-done.6.b2, bf16[2,8,896]{2,1,0:T(8,128)(2,1)S(1)} %collective-permute-done.7.b3, ...), custom_call_target="tpu_custom_call" | custom-call | bytes 712704 | tf_op jit(solution)/shard_map/combine/pallas_call | solution.py:217
  29.0 0.1 collective-permute-start.10
  29.0 1.6 %collective-permute-start.9 = (bf16[16,384]{1,0:T(8,128)(2,1)S(1)}, bf16[16,384]{1,0:T(8,128)(2,1)S(1)}, u32[]{:S(2)}, u32[]{:S(2)}) collective-permute-start(bf16[16,384]{1,0:T(8,128)(2,1)S(1)} %combine.1.p0), channel_id=1, source_target_pairs={{0,2},{1,3},{2,0},{3,1},{4,6},{5,7},{6,4},{7,5},{8,10},{9,11},{10,... | collective-permute-start | bytes 36872 | tf_op jit(solution)/shard_map/ppermute | solution.py:511
  30.6 0.3 collective-permute-start.8
  30.9 1.3 %collective-permute-done.10.p3 = bf16[16,384]{1,0:T(8,128)(2,1)S(1)} collective-permute-done((bf16[16,384]{1,0:T(8,128)(2,1)S(1)}, bf16[16,384]{1,0:T(8,128)(2,1)S(1)}, u32[]{:S(2)}, u32[]{:S(2)}) %collective-permute-start.10) | collective-permute-done | bytes 12320 | tf_op jit(solution)/shard_map/ppermute | solution.py:511
  32.2 0.6 collective-permute-done.9.p2
  32.8 0.0 collective-permute-done.8.p1
  32.8 3.4 %collective-permute-start.12 = (bf16[16,384]{1,0:T(8,128)(2,1)S(1)}, bf16[16,384]{1,0:T(8,128)(2,1)S(1)}, u32[]{:S(2)}, u32[]{:S(2)}) collective-permute-start(bf16[16,384]{1,0:T(8,128)(2,1)S(1)} %head_sum.1), channel_id=1, source_target_pairs={{0,28},{4,24},{1,20},{5,16},{2,12},{6,8},{3,4},{7,0},{9,29},{13,25... | collective-permute-start | bytes 36872 | tf_op jit(solution)/shard_map/ppermute | solution.py:593
  36.2 0.6 collective-permute-start.11
  36.8 0.8 %collective-permute-done.12.flip = bf16[16,384]{1,0:T(8,128)(2,1)S(1)} collective-permute-done((bf16[16,384]{1,0:T(8,128)(2,1)S(1)}, bf16[16,384]{1,0:T(8,128)(2,1)S(1)}, u32[]{:S(2)}, u32[]{:S(2)}) %collective-permute-start.12) | collective-permute-done | bytes 12320 | tf_op jit(solution)/shard_map/ppermute | solution.py:593
  37.6 1.7 %collective-permute-done.11.same = bf16[16,384]{1,0:T(8,128)(2,1)S(1)} collective-permute-done((bf16[16,384]{1,0:T(8,128)(2,1)S(1)}, bf16[16,384]{1,0:T(8,128)(2,1)S(1)}, u32[]{:S(2)}, u32[]{:S(2)}) %collective-permute-start.11) | collective-permute-done | bytes 12320 | tf_op jit(solution)/shard_map/ppermute | solution.py:593
  39.3 0.5 gate_up.1
  39.9 0.0 collective-permute-start.13
  39.9 1.3 %collective-permute-done.13.theirs = bf16[16,2176]{1,0:T(8,128)(2,1)S(1)} collective-permute-done((bf16[16,2176]{1,0:T(8,128)(2,1)S(1)}, bf16[16,2176]{1,0:T(8,128)(2,1)S(1)}, u32[]{:S(2)}, u32[]{:S(2)}) %collective-permute-start.13) | collective-permute-done | bytes 69664 | tf_op jit(solution)/shard_map/ppermute | solution.py:511
  41.1 0.1 core_sum.1.mine
  41.2 2.3 %collective-permute-start.14 = (bf16[16,2176]{1,0:T(8,128)(2,1)S(1)}, bf16[16,2176]{1,0:T(8,128)(2,1)S(1)}, u32[]{:S(2)}, u32[]{:S(2)}) collective-permute-start(bf16[16,2176]{1,0:T(8,128)(2,1)S(1)} %core_sum.1.mine), channel_id=1, source_target_pairs={{0,2},{1,3},{2,0},{3,1},{4,6},{5,7},{6,4},{7,5},{8,10},{9,11},{10,... | collective-permute-start | bytes 208904 | tf_op jit(solution)/shard_map/ppermute | solution.py:511
  43.5 2.5 %collective-permute-done.14.theirs = bf16[16,2176]{1,0:T(8,128)(2,1)S(1)} collective-permute-done((bf16[16,2176]{1,0:T(8,128)(2,1)S(1)}, bf16[16,2176]{1,0:T(8,128)(2,1)S(1)}, u32[]{:S(2)}, u32[]{:S(2)}) %collective-permute-start.14) | collective-permute-done | bytes 69664 | tf_op jit(solution)/shard_map/ppermute | solution.py:511
  46.0 0.4 down.1
  46.4 0.6 collective-permute-start.15
  47.0 3.3 %collective-permute-done.15.got = f32[8,768]{1,0:T(8,128)S(1)} collective-permute-done((f32[8,768]{1,0:T(8,128)S(1)}, f32[8,768]{1,0:T(8,128)S(1)}, u32[]{:S(2)}, u32[]{:S(2)}) %collective-permute-start.15) | collective-permute-done | bytes 24608 | tf_op jit(solution)/shard_map/ppermute | solution.py:511
  50.4 2.5 %collective-permute-start.16 = (f32[2,768]{1,0:T(2,128)S(1)}, f32[2,768]{1,0:T(2,128)S(1)}, u32[]{:S(2)}, u32[]{:S(2)}) collective-permute-start(f32[2,768]{1,0:T(2,128)S(1)} %get-tuple-element.28), channel_id=1, source_target_pairs={{0,24},{4,28},{8,16},{12,20},{16,8},{20,12},{24,0},{28,4},{1,25},{... | collective-permute-start | bytes 18440 | tf_op jit(solution)/shard_map/ppermute | solution.py:511
  52.9 0.0 collective-permute-start.17
  52.9 1.9 %collective-permute-start.18 = (f32[2,768]{1,0:T(2,128)S(1)}, f32[2,768]{1,0:T(2,128)S(1)}, u32[]{:S(2)}, u32[]{:S(2)}) collective-permute-start(f32[2,768]{1,0:T(2,128)S(1)} %get-tuple-element.30), channel_id=1, source_target_pairs={{0,8},{4,12},{8,0},{12,4},{16,24},{20,28},{24,16},{28,20},{1,9},{5... | collective-permute-start | bytes 18440 | tf_op jit(solution)/shard_map/ppermute | solution.py:511
  54.8 1.0 %collective-permute-done.16.c1 = f32[2,768]{1,0:T(2,128)S(1)} collective-permute-done((f32[2,768]{1,0:T(2,128)S(1)}, f32[2,768]{1,0:T(2,128)S(1)}, u32[]{:S(2)}, u32[]{:S(2)}) %collective-permute-start.16) | collective-permute-done | bytes 6176 | tf_op jit(solution)/shard_map/ppermute | solution.py:511
  55.9 1.6 %collective-permute-done.17.c2 = f32[2,768]{1,0:T(2,128)S(1)} collective-permute-done((f32[2,768]{1,0:T(2,128)S(1)}, f32[2,768]{1,0:T(2,128)S(1)}, u32[]{:S(2)}, u32[]{:S(2)}) %collective-permute-start.17) | collective-permute-done | bytes 6176 | tf_op jit(solution)/shard_map/ppermute | solution.py:511
  57.4 0.0 collective-permute-done.18.c3
  57.4 0.6 %final.1 = bf16[2,768]{1,0:T(2,128)(2,1)} custom-call(f32[2,768]{1,0:T(2,128)S(1)} %get-tuple-element.23.own, f32[2,768]{1,0:T(2,128)S(1)} %get-tuple-element.27.c0, f32[2,768]{1,0:T(2,128)S(1)} %collective-permute-done.16.c1, f32[2,768]{1,0:T(2,128)S(1)} %collective-permute-done.17.c2, f32[2,768]{1,0:T(2,128)S(1)} %collective-permute-done.18.c3), custom_call_target="tpu_custom_call" | custom-call | bytes 30720 | tf_op jit(solution)/shard_map/final/pallas_call | solution.py:217
  (20 shorter events, 0.1 us)
Async XLA Ops:
  0.0 16.1 %copy-start.1 = (bf16[5,256,768]{2,1,0:T(8,128)(2,1)S(1)}, bf16[5,256,768]{2,1,0:T(8,128)(2,1)}, u32[]{:S(2)}) copy-start(bf16[5,256,768]{2,1,0:T(8,128)(2,1)} %values.1) | copy-start | bytes 5898244
  0.0 16.1 %copy-start = (bf16[5,256,768]{2,1,0:T(8,128)(2,1)S(1)}, bf16[5,256,768]{2,1,0:T(8,128)(2,1)}, u32[]{:S(2)}) copy-start(bf16[5,256,768]{2,1,0:T(8,128)(2,1)} %keys.1) | copy-start | bytes 5898244
  1.8 4.9 %collective-permute-start = (bf16[2,1664]{1,0:T(2,128)(2,1)}, bf16[2,1664]{1,0:T(2,128)(2,1)S(1)}, u32[]{:S(2)}, u32[]{:S(2)}) collective-permute-start(bf16[2,1664]{1,0:T(2,128)(2,1)} %get-tuple-element.18.mine), channel_id=1, source_target_pairs={{0,4},{4,0},{8,12},{12,8},{16,20},{20,16},{24,28},{28,24},{1,5},{5... | collective-permute-start | bytes 19976 | tf_op jit(solution)/shard_map/ppermute | solution.py:511
  6.7 0.7 %copy-start.7 = (bf16[2,1664]{1,0:T(2,128)(2,1)S(1)}, bf16[2,1664]{1,0:T(2,128)(2,1)}, u32[]{:S(2)}) copy-start(bf16[2,1664]{1,0:T(2,128)(2,1)} %get-tuple-element.18.mine) | copy-start | bytes 19972
  7.4 5.8 %collective-permute-start.3 = (bf16[2,2,1664]{2,1,0:T(2,128)(2,1)S(1)}, bf16[2,2,1664]{2,1,0:T(2,128)(2,1)S(1)}, u32[]{:S(2)}, u32[]{:S(2)}) collective-permute-start(bf16[2,2,1664]{2,1,0:T(2,128)(2,1)S(1)} %merge.2.a0), channel_id=1, source_target_pairs={{0,24},{4,28},{8,16},{12,20},{16,8},{20,12},{24,0},{28,4},{1,25},{... | collective-permute-start | bytes 39944 | tf_op jit(solution)/shard_map/ppermute | solution.py:511
  11.5 4.6 %collective-permute-start.2 = (bf16[2,2,1664]{2,1,0:T(2,128)(2,1)S(1)}, bf16[2,2,1664]{2,1,0:T(2,128)(2,1)S(1)}, u32[]{:S(2)}, u32[]{:S(2)}) collective-permute-start(bf16[2,2,1664]{2,1,0:T(2,128)(2,1)S(1)} %merge.2.a0), channel_id=1, source_target_pairs={{0,16},{4,20},{8,24},{12,28},{16,0},{20,4},{24,8},{28,12},{1,17},{... | collective-permute-start | bytes 39944 | tf_op jit(solution)/shard_map/ppermute | solution.py:511
  11.5 4.6 %collective-permute-start.1 = (bf16[2,2,1664]{2,1,0:T(2,128)(2,1)S(1)}, bf16[2,2,1664]{2,1,0:T(2,128)(2,1)S(1)}, u32[]{:S(2)}, u32[]{:S(2)}) collective-permute-start(bf16[2,2,1664]{2,1,0:T(2,128)(2,1)S(1)} %merge.2.a0), channel_id=1, source_target_pairs={{0,8},{4,12},{8,0},{12,4},{16,24},{20,28},{24,16},{28,20},{1,9},{5... | collective-permute-start | bytes 39944 | tf_op jit(solution)/shard_map/ppermute | solution.py:511
  16.1 0.7 %copy-start.6 = (f32[8,896]{1,0:T(8,128)S(1)}, f32[8,896]{1,0:T(8,128)}, u32[]{:S(2)}) copy-start(f32[8,896]{1,0:T(8,128)} %get-tuple-element.19.own) | copy-start | bytes 86020
  16.8 11.5 %copy-start.5 = (bf16[768,384]{1,0:T(8,128)(2,1)S(1)}, bf16[768,384]{1,0:T(8,128)(2,1)}, u32[]{:S(2)}) copy-start(bf16[768,384]{1,0:T(8,128)(2,1)} %weight.2) | copy-start | bytes 1769476
  16.8 19.9 %copy-start.8 = (bf16[768]{0:T(1024)(128)(2,1)S(1)}, bf16[768]{0:T(1024)(128)(2,1)}, u32[]{:S(2)}) copy-start(bf16[768]{0:T(1024)(128)(2,1)} %param.22) | copy-start | bytes 4612
  16.8 22.5 %copy-start.3 = (bf16[768,1024]{1,0:T(8,128)(2,1)S(1)}, bf16[768,1024]{1,0:T(8,128)(2,1)}, u32[]{:S(2)}) copy-start(bf16[768,1024]{1,0:T(8,128)(2,1)} %gate.1) | copy-start | bytes 4718596
  16.9 22.5 %copy-start.4 = (bf16[768,1024]{1,0:T(8,128)(2,1)S(1)}, bf16[768,1024]{1,0:T(8,128)(2,1)}, u32[]{:S(2)}) copy-start(bf16[768,1024]{1,0:T(8,128)(2,1)} %up.1) | copy-start | bytes 4718596
  18.0 3.8 %collective-permute-start.4 = (bf16[8,896]{1,0:T(8,128)(2,1)S(1)}, bf16[8,896]{1,0:T(8,128)(2,1)S(1)}, u32[]{:S(2)}, u32[]{:S(2)}) collective-permute-start(bf16[8,896]{1,0:T(8,128)(2,1)S(1)} %get-tuple-element.20.mine), channel_id=1, source_target_pairs={{0,4},{4,0},{8,12},{12,8},{16,20},{20,16},{24,28},{28,24},{1,5},{5... | collective-permute-start | bytes 43016 | tf_op jit(solution)/shard_map/ppermute | solution.py:511
  21.8 5.7 %collective-permute-start.7 = (bf16[2,8,896]{2,1,0:T(8,128)(2,1)S(1)}, bf16[2,8,896]{2,1,0:T(8,128)(2,1)S(1)}, u32[]{:S(2)}, u32[]{:S(2)}) collective-permute-start(bf16[2,8,896]{2,1,0:T(8,128)(2,1)S(1)} %merge.3.b0), channel_id=1, source_target_pairs={{0,24},{4,28},{8,16},{12,20},{16,8},{20,12},{24,0},{28,4},{1,25},{... | collective-permute-start | bytes 86024 | tf_op jit(solution)/shard_map/ppermute | solution.py:511
  23.2 4.8 %collective-permute-start.6 = (bf16[2,8,896]{2,1,0:T(8,128)(2,1)S(1)}, bf16[2,8,896]{2,1,0:T(8,128)(2,1)S(1)}, u32[]{:S(2)}, u32[]{:S(2)}) collective-permute-start(bf16[2,8,896]{2,1,0:T(8,128)(2,1)S(1)} %merge.3.b0), channel_id=1, source_target_pairs={{0,16},{4,20},{8,24},{12,28},{16,0},{20,4},{24,8},{28,12},{1,17},{... | collective-permute-start | bytes 86024 | tf_op jit(solution)/shard_map/ppermute | solution.py:511
  23.9 4.4 %collective-permute-start.5 = (bf16[2,8,896]{2,1,0:T(8,128)(2,1)S(1)}, bf16[2,8,896]{2,1,0:T(8,128)(2,1)S(1)}, u32[]{:S(2)}, u32[]{:S(2)}) collective-permute-start(bf16[2,8,896]{2,1,0:T(8,128)(2,1)S(1)} %merge.3.b0), channel_id=1, source_target_pairs={{0,8},{4,12},{8,0},{12,4},{16,24},{20,28},{24,16},{28,20},{1,9},{5... | collective-permute-start | bytes 86024 | tf_op jit(solution)/shard_map/ppermute | solution.py:511
  29.0 3.3 %collective-permute-start.10 = (bf16[16,384]{1,0:T(8,128)(2,1)S(1)}, bf16[16,384]{1,0:T(8,128)(2,1)S(1)}, u32[]{:S(2)}, u32[]{:S(2)}) collective-permute-start(bf16[16,384]{1,0:T(8,128)(2,1)S(1)} %combine.1.p0), channel_id=1, source_target_pairs={{0,3},{1,2},{2,1},{3,0},{4,7},{5,6},{6,5},{7,4},{8,11},{9,10},{10,... | collective-permute-start | bytes 36872 | tf_op jit(solution)/shard_map/ppermute | solution.py:511
  29.0 3.8 %collective-permute-start.9 = (bf16[16,384]{1,0:T(8,128)(2,1)S(1)}, bf16[16,384]{1,0:T(8,128)(2,1)S(1)}, u32[]{:S(2)}, u32[]{:S(2)}) collective-permute-start(bf16[16,384]{1,0:T(8,128)(2,1)S(1)} %combine.1.p0), channel_id=1, source_target_pairs={{0,2},{1,3},{2,0},{3,1},{4,6},{5,7},{6,4},{7,5},{8,10},{9,11},{10,... | collective-permute-start | bytes 36872 | tf_op jit(solution)/shard_map/ppermute | solution.py:511
  30.6 2.2 %collective-permute-start.8 = (bf16[16,384]{1,0:T(8,128)(2,1)S(1)}, bf16[16,384]{1,0:T(8,128)(2,1)S(1)}, u32[]{:S(2)}, u32[]{:S(2)}) collective-permute-start(bf16[16,384]{1,0:T(8,128)(2,1)S(1)} %combine.1.p0), channel_id=1, source_target_pairs={{0,1},{1,0},{2,3},{3,2},{4,5},{5,4},{6,7},{7,6},{8,9},{9,8},{10,11... | collective-permute-start | bytes 36872 | tf_op jit(solution)/shard_map/ppermute | solution.py:511
  32.8 4.8 %collective-permute-start.12 = (bf16[16,384]{1,0:T(8,128)(2,1)S(1)}, bf16[16,384]{1,0:T(8,128)(2,1)S(1)}, u32[]{:S(2)}, u32[]{:S(2)}) collective-permute-start(bf16[16,384]{1,0:T(8,128)(2,1)S(1)} %head_sum.1), channel_id=1, source_target_pairs={{0,28},{4,24},{1,20},{5,16},{2,12},{6,8},{3,4},{7,0},{9,29},{13,25... | collective-permute-start | bytes 36872 | tf_op jit(solution)/shard_map/ppermute | solution.py:593
  36.2 3.1 %collective-permute-start.11 = (bf16[16,384]{1,0:T(8,128)(2,1)S(1)}, bf16[16,384]{1,0:T(8,128)(2,1)S(1)}, u32[]{:S(2)}, u32[]{:S(2)}) collective-permute-start(bf16[16,384]{1,0:T(8,128)(2,1)S(1)} %head_sum.1), channel_id=1, source_target_pairs={{0,24},{4,28},{1,16},{5,20},{2,8},{6,12},{3,0},{7,4},{9,25},{13,29... | collective-permute-start | bytes 36872 | tf_op jit(solution)/shard_map/ppermute | solution.py:593
  39.3 6.7 %copy-start.2 = (bf16[1024,768]{1,0:T(8,128)(2,1)S(1)}, bf16[1024,768]{1,0:T(8,128)(2,1)}, u32[]{:S(2)}) copy-start(bf16[1024,768]{1,0:T(8,128)(2,1)} %weight.3) | copy-start | bytes 4718596
  39.9 1.3 %collective-permute-start.13 = (bf16[16,2176]{1,0:T(8,128)(2,1)S(1)}, bf16[16,2176]{1,0:T(8,128)(2,1)S(1)}, u32[]{:S(2)}, u32[]{:S(2)}) collective-permute-start(bf16[16,2176]{1,0:T(8,128)(2,1)S(1)} %get-tuple-element.24.mine), channel_id=1, source_target_pairs={{0,1},{1,0},{2,3},{3,2},{4,5},{5,4},{6,7},{7,6},{8,9},{9,8},{10,11... | collective-permute-start | bytes 208904 | tf_op jit(solution)/shard_map/ppermute | solution.py:511
  41.2 4.8 %collective-permute-start.14 = (bf16[16,2176]{1,0:T(8,128)(2,1)S(1)}, bf16[16,2176]{1,0:T(8,128)(2,1)S(1)}, u32[]{:S(2)}, u32[]{:S(2)}) collective-permute-start(bf16[16,2176]{1,0:T(8,128)(2,1)S(1)} %core_sum.1.mine), channel_id=1, source_target_pairs={{0,2},{1,3},{2,0},{3,1},{4,6},{5,7},{6,4},{7,5},{8,10},{9,11},{10,... | collective-permute-start | bytes 208904 | tf_op jit(solution)/shard_map/ppermute | solution.py:511
  46.4 3.9 %collective-permute-start.15 = (f32[8,768]{1,0:T(8,128)S(1)}, f32[8,768]{1,0:T(8,128)S(1)}, u32[]{:S(2)}, u32[]{:S(2)}) collective-permute-start(f32[8,768]{1,0:T(8,128)S(1)} %get-tuple-element.26), channel_id=1, source_target_pairs={{0,4},{4,0},{8,12},{12,8},{16,20},{20,16},{24,28},{28,24},{1,5},{5... | collective-permute-start | bytes 73736 | tf_op jit(solution)/shard_map/ppermute | solution.py:511
  50.4 5.5 %collective-permute-start.16 = (f32[2,768]{1,0:T(2,128)S(1)}, f32[2,768]{1,0:T(2,128)S(1)}, u32[]{:S(2)}, u32[]{:S(2)}) collective-permute-start(f32[2,768]{1,0:T(2,128)S(1)} %get-tuple-element.28), channel_id=1, source_target_pairs={{0,24},{4,28},{8,16},{12,20},{16,8},{20,12},{24,0},{28,4},{1,25},{... | collective-permute-start | bytes 18440 | tf_op jit(solution)/shard_map/ppermute | solution.py:511
  52.9 4.5 %collective-permute-start.17 = (f32[2,768]{1,0:T(2,128)S(1)}, f32[2,768]{1,0:T(2,128)S(1)}, u32[]{:S(2)}, u32[]{:S(2)}) collective-permute-start(f32[2,768]{1,0:T(2,128)S(1)} %get-tuple-element.29), channel_id=1, source_target_pairs={{0,16},{4,20},{8,24},{12,28},{16,0},{20,4},{24,8},{28,12},{1,17},{... | collective-permute-start | bytes 18440 | tf_op jit(solution)/shard_map/ppermute | solution.py:511
  52.9 4.5 %collective-permute-start.18 = (f32[2,768]{1,0:T(2,128)S(1)}, f32[2,768]{1,0:T(2,128)S(1)}, u32[]{:S(2)}, u32[]{:S(2)}) collective-permute-start(f32[2,768]{1,0:T(2,128)S(1)} %get-tuple-element.30), channel_id=1, source_target_pairs={{0,8},{4,12},{8,0},{12,4},{16,24},{20,28},{24,16},{28,20},{1,9},{5... | collective-permute-start | bytes 18440 | tf_op jit(solution)/shard_map/ppermute | solution.py:511

commit v6 on v5

--- a/solution.py
+++ b/solution.py
@@ -475,8 +475,7 @@
     total[:, ff2:] = tail.astype(BF16)
 
 
-def down_kernel(features, mine, theirs, weight, send, keep, scr):
-    y = lax.axis_index("pool") % 2
+def down_kernel(features, mine, theirs, weight, parts, scr):
     ff = weight.shape[0]
     tail = mine[:, 2 * ff :].astype(F32) + theirs[:, 2 * ff :].astype(F32)
     square = jnp.sum(tail, 1, keepdims=True)
@@ -485,25 +484,16 @@
     up = (mine[:, ff : 2 * ff].astype(F32) + theirs[:, ff : 2 * ff].astype(F32)) * factor
     hidden = (gate / (1.0 + jnp.exp(-gate)) * up).astype(BF16)
     scr[...] = jnp.dot(hidden, weight[...], preferred_element_type=F32)
-    rows = scr.shape[0] // 8
-    for z in range(4):
-        even = scr[(2 * z) * rows : (2 * z + 1) * rows, :]
-        odd = scr[(2 * z + 1) * rows : (2 * z + 2) * rows, :]
-        keep[z * rows : (z + 1) * rows, :] = jnp.where(y == 0, even, odd)
-        send[z * rows : (z + 1) * rows, :] = jnp.where(y == 0, odd, even)
-
-
-def split_kernel(keep, got, c0, c1, c2, c3, scr):
-    z = lax.axis_index("pool") // 2
-    scr[...] = keep[...] + got[...]
-    rows = c0.shape[0]
-    chunks = in_order([scr[s * rows : (s + 1) * rows, :] for s in range(4)], z)
-    for values, chunk in zip(chunks, (c0, c1, c2, c3)):
-        chunk[...] = values
-
-
-def final_kernel(own, c0, c1, c2, c3, out):
-    out[...] = (own[...] + ((c0[...] + c1[...]) + (c2[...] + c3[...]))).astype(BF16)
+    rows = parts.shape[1]
+    for p in range(parts.shape[0]):
+        parts[p] = scr[p * rows : (p + 1) * rows, :].astype(BF16)
+
+
+def final_kernel(own, parts, out):
+    total = own[...]
+    for p in range(parts.shape[0]):
+        total = total + parts[p].astype(F32)
+    out[...] = total.astype(BF16)
 
 
 def flip(values, axis, step):
@@ -604,25 +594,18 @@
         [((requests, 2 * ff + 128), BF16)],
         [sums, flip(sums, "mlp", 1)],
     )
-    send, keep = call(
+    (down,) = call(
         functools.partial(down_kernel, width * mlp),
         "down",
-        [((requests // 2, width), F32)] * 2,
+        [((pool, rows, width), BF16)],
         [core_sums, flip(core_sums, "mlp", 2), down_weight],
         [pltpu.VMEM((requests, width), F32)],
-    )
-    chunks = call(
-        split_kernel,
-        "pair_sum",
-        [((rows, width), F32)] * 4,
-        [keep, flip(send, "pool", 1)],
-        [pltpu.VMEM((requests // 2, width), F32)],
     )
     (out,) = call(
         final_kernel,
         "final",
         [((rows, width), BF16)],
-        [own_residual, chunks[0]] + [flip(chunks[s], "pool", 2 * s) for s in (3, 2, 1)],
+        [own_residual, lax.all_to_all(down, "pool", 0, 0)],
     )
     return out
 

time: 58.2 us -> 57.8 us (level)
  blocking collectives: 0 us -> 10.6 us
  waiting for transfers between devices: 24.4 us -> 18.4 us
  starting transfers between devices: 26.8 us -> 21.8 us
    all_to_all x0 -> x1, blocking collectives: none -> 10.6 us  [per_device_small(): lax.all_to_all(down, 'pool', 0, 0)]
    ppermute x17 -> x13, waiting for transfers between devices: 21.8 us -> 15.9 us  [flip(): lax.ppermute(values, axis, [(index, index ^ step) for index in range(size)])]
    ppermute x17 -> x13, starting transfers between devices: 22.9 us -> 17.9 us  [flip(): lax.ppermute(values, axis, [(index, index ^ step) for index in range(size)])]
    pallas_call x11 -> x10, Pallas kernels: 5.27 us -> 5.24 us  [call(): pl.pallas_call(kernel, out_shape=[jax.ShapeDtypeStruct(shape, dtype) for...]
  transfers between devices with their start and end apart: 19 -> 15, of which waited for: 16 -> 13; matrix products, arithmetic and copies ran while one was open for 0% -> 0% of each run, Pallas kernels for 0% -> 0%
where the time goes in v6:
time: 57.8 us; the launch traced here: 57.6 us
  starting transfers between devices  21.8 us (38%)
  waiting for transfers between devices  18.4 us (32%)
  blocking collectives  10.6 us (18%)
  Pallas kernels  5.24 us (9%)
  local copies, waits for them, and re-layouts  1.46 us (3%)
    ppermute x13, starting transfers between devices, flip(): lax.ppermute(values, axis, [(index, index ^ step) for index in range(size)])  17.9 us
    ppermute x13, waiting for transfers between devices, flip(): lax.ppermute(values, axis, [(index, index ^ step) for index in range(size)])  15.9 us
    all_to_all x1, blocking collectives, per_device_small(): lax.all_to_all(down, 'pool', 0, 0)  10.6 us
    pallas_call x10, Pallas kernels, call(): pl.pallas_call(kernel, out_shape=[jax.ShapeDtypeStruct(shape, dtype) for...  5.24 us
    ppermute x2, starting transfers between devices, per_device_small(): pieces.append(lax.ppermute(head_sum, ('pool', 'mlp'), route))  3.94 us
    ppermute x2, waiting for transfers between devices, per_device_small(): pieces.append(lax.ppermute(head_sum, ('pool', 'mlp'), route))  2.55 us
    unnamed x18, local copies, waits for them, and re-layouts  1.46 us
  transfers between devices with their start and end apart: 15, of which 13 were waited for; matrix products, arithmetic and copies ran while one was open for 0% of the time, Pallas kernels for 0%

profile of v6, /device:TPU:0, one launch (start us, length us, event | category | flops | bytes accessed | tf_op | source)
XLA Modules:
  0.0 57.6 jit_solution(1001135497499509313)
XLA Ops:
  0.0 1.8 %rotary.1 = (bf16[2,1664]{1,0:T(2,128)(2,1)}, f32[8,896]{1,0:T(8,128)}) custom-call(s32[2,8]{1,0:T(2,128)} %refs_0_.1, s32[2]{0:T(128)} %refs_1_.1, bf16[2,768]{1,0:T(2,128)(2,1)} %refs_2_.1, bf16[2,768]{1,0:T(2,128)(2,1)} %refs_3_.1, bf16[2,768]{1,0:T(2,128)(2,1)} %refs_4_.1, bf16[2,768]{1,0:T(2,128)(2,1)} %refs_5_.1, bf16[5,256,768]{2,1,0:T(8,128)(2,1)} %keys.1, ...), custom_call_target="tpu_custom_call" | custom-call | bytes 3944520 | tf_op jit(solution)/shard_map/rotary/pallas_call | solution.py:217
  1.8 3.0 %collective-permute-start = (bf16[2,1664]{1,0:T(2,128)(2,1)}, bf16[2,1664]{1,0:T(2,128)(2,1)S(1)}, u32[]{:S(2)}, u32[]{:S(2)}) collective-permute-start(bf16[2,1664]{1,0:T(2,128)(2,1)} %get-tuple-element.12.mine), channel_id=1, source_target_pairs={{0,4},{4,0},{8,12},{12,8},{16,20},{20,16},{24,28},{28,24},{1,5},{5... | collective-permute-start | bytes 19976 | tf_op jit(solution)/shard_map/ppermute | solution.py:501
  4.9 1.8 %collective-permute-done.theirs = bf16[2,1664]{1,0:T(2,128)(2,1)S(1)} collective-permute-done((bf16[2,1664]{1,0:T(2,128)(2,1)}, bf16[2,1664]{1,0:T(2,128)(2,1)S(1)}, u32[]{:S(2)}, u32[]{:S(2)}) %collective-permute-start) | collective-permute-done | bytes 6688 | tf_op jit(solution)/shard_map/ppermute | solution.py:501
  6.7 0.7 %copy-done.7 = bf16[2,1664]{1,0:T(2,128)(2,1)S(1)} copy-done((bf16[2,1664]{1,0:T(2,128)(2,1)S(1)}, bf16[2,1664]{1,0:T(2,128)(2,1)}, u32[]{:S(2)}) %copy-start.7) | copy-done | bytes 6680
  7.4 4.1 %collective-permute-start.3 = (bf16[2,2,1664]{2,1,0:T(2,128)(2,1)S(1)}, bf16[2,2,1664]{2,1,0:T(2,128)(2,1)S(1)}, u32[]{:S(2)}, u32[]{:S(2)}) collective-permute-start(bf16[2,2,1664]{2,1,0:T(2,128)(2,1)S(1)} %merge.2.a0), channel_id=1, source_target_pairs={{0,24},{4,28},{8,16},{12,20},{16,8},{20,12},{24,0},{28,4},{1,25},{... | collective-permute-start | bytes 39944 | tf_op jit(solution)/shard_map/ppermute | solution.py:501
  11.5 0.0 collective-permute-start.2
  11.5 0.6 collective-permute-start.1
  12.0 1.1 %collective-permute-done.3.a3 = bf16[2,2,1664]{2,1,0:T(2,128)(2,1)S(1)} collective-permute-done((bf16[2,2,1664]{2,1,0:T(2,128)(2,1)S(1)}, bf16[2,2,1664]{2,1,0:T(2,128)(2,1)S(1)}, u32[]{:S(2)}, u32[]{:S(2)}) %collective-permute-start.3) | collective-permute-done | bytes 13344 | tf_op jit(solution)/shard_map/ppermute | solution.py:501
  13.2 2.9 %collective-permute-done.2.a2 = bf16[2,2,1664]{2,1,0:T(2,128)(2,1)S(1)} collective-permute-done((bf16[2,2,1664]{2,1,0:T(2,128)(2,1)S(1)}, bf16[2,2,1664]{2,1,0:T(2,128)(2,1)S(1)}, u32[]{:S(2)}, u32[]{:S(2)}) %collective-permute-start.2) | collective-permute-done | bytes 13344 | tf_op jit(solution)/shard_map/ppermute | solution.py:501
  16.1 0.0 collective-permute-done.1.a1
  16.1 0.0 copy-done.1
  16.1 0.0 copy-done
  16.1 0.0 copy-start.6
  16.1 0.7 %copy-done.6 = f32[8,896]{1,0:T(8,128)S(1)} copy-done((f32[8,896]{1,0:T(8,128)S(1)}, f32[8,896]{1,0:T(8,128)}, u32[]{:S(2)}) %copy-start.6) | copy-done | bytes 28696
  16.9 1.1 %attend.1 = (bf16[8,896]{1,0:T(8,128)(2,1)S(1)}, f32[16,768]{1,0:T(8,128)S(1)}, f32[16,128]{1,0:T(8,128)S(1)}) custom-call(bf16[2,2,1664]{2,1,0:T(2,128)(2,1)S(1)} %merge.2.a0, bf16[2,2,1664]{2,1,0:T(2,128)(2,1)S(1)} %collective-permute-done.1.a1, bf16[2,2,1664]{2,1,0:T(2,128)(2,1)S(1)} %collective-permute-done.2.a2, ...), custom_call_target="tpu_custom_call" | custom-call | bytes 4014080 | tf_op jit(solution)/shard_map/attend/pallas_call | solution.py:217
  18.0 1.6 %collective-permute-start.4 = (bf16[8,896]{1,0:T(8,128)(2,1)S(1)}, bf16[8,896]{1,0:T(8,128)(2,1)S(1)}, u32[]{:S(2)}, u32[]{:S(2)}) collective-permute-start(bf16[8,896]{1,0:T(8,128)(2,1)S(1)} %get-tuple-element.14.mine), channel_id=1, source_target_pairs={{0,4},{4,0},{8,12},{12,8},{16,20},{20,16},{24,28},{28,24},{1,5},{5... | collective-permute-start | bytes 43016 | tf_op jit(solution)/shard_map/ppermute | solution.py:501
  19.6 2.2 %collective-permute-done.4.theirs = bf16[8,896]{1,0:T(8,128)(2,1)S(1)} collective-permute-done((bf16[8,896]{1,0:T(8,128)(2,1)S(1)}, bf16[8,896]{1,0:T(8,128)(2,1)S(1)}, u32[]{:S(2)}, u32[]{:S(2)}) %collective-permute-start.4) | collective-permute-done | bytes 14368 | tf_op jit(solution)/shard_map/ppermute | solution.py:501
  21.8 1.5 %collective-permute-start.7 = (bf16[2,8,896]{2,1,0:T(8,128)(2,1)S(1)}, bf16[2,8,896]{2,1,0:T(8,128)(2,1)S(1)}, u32[]{:S(2)}, u32[]{:S(2)}) collective-permute-start(bf16[2,8,896]{2,1,0:T(8,128)(2,1)S(1)} %merge.3.b0), channel_id=1, source_target_pairs={{0,24},{4,28},{8,16},{12,20},{16,8},{20,12},{24,0},{28,4},{1,25},{... | collective-permute-start | bytes 86024 | tf_op jit(solution)/shard_map/ppermute | solution.py:501
  23.2 0.6 %collective-permute-start.6 = (bf16[2,8,896]{2,1,0:T(8,128)(2,1)S(1)}, bf16[2,8,896]{2,1,0:T(8,128)(2,1)S(1)}, u32[]{:S(2)}, u32[]{:S(2)}) collective-permute-start(bf16[2,8,896]{2,1,0:T(8,128)(2,1)S(1)} %merge.3.b0), channel_id=1, source_target_pairs={{0,16},{4,20},{8,24},{12,28},{16,0},{20,4},{24,8},{28,12},{1,17},{... | collective-permute-start | bytes 86024 | tf_op jit(solution)/shard_map/ppermute | solution.py:501
  23.9 2.3 %collective-permute-start.5 = (bf16[2,8,896]{2,1,0:T(8,128)(2,1)S(1)}, bf16[2,8,896]{2,1,0:T(8,128)(2,1)S(1)}, u32[]{:S(2)}, u32[]{:S(2)}) collective-permute-start(bf16[2,8,896]{2,1,0:T(8,128)(2,1)S(1)} %merge.3.b0), channel_id=1, source_target_pairs={{0,8},{4,12},{8,0},{12,4},{16,24},{20,28},{24,16},{28,20},{1,9},{5... | collective-permute-start | bytes 86024 | tf_op jit(solution)/shard_map/ppermute | solution.py:501
  26.2 1.3 %collective-permute-done.7.b3 = bf16[2,8,896]{2,1,0:T(8,128)(2,1)S(1)} collective-permute-done((bf16[2,8,896]{2,1,0:T(8,128)(2,1)S(1)}, bf16[2,8,896]{2,1,0:T(8,128)(2,1)S(1)}, u32[]{:S(2)}, u32[]{:S(2)}) %collective-permute-start.7) | collective-permute-done | bytes 28704 | tf_op jit(solution)/shard_map/ppermute | solution.py:501
  27.4 0.6 %collective-permute-done.6.b2 = bf16[2,8,896]{2,1,0:T(8,128)(2,1)S(1)} collective-permute-done((bf16[2,8,896]{2,1,0:T(8,128)(2,1)S(1)}, bf16[2,8,896]{2,1,0:T(8,128)(2,1)S(1)}, u32[]{:S(2)}, u32[]{:S(2)}) %collective-permute-start.6) | collective-permute-done | bytes 28704 | tf_op jit(solution)/shard_map/ppermute | solution.py:501
  28.0 0.3 collective-permute-done.5.b1
  28.3 0.0 copy-done.5
  28.3 0.7 %combine.1.p0 = bf16[16,384]{1,0:T(8,128)(2,1)S(1)} custom-call(bf16[2,8,896]{2,1,0:T(8,128)(2,1)S(1)} %merge.3.b0, bf16[2,8,896]{2,1,0:T(8,128)(2,1)S(1)} %collective-permute-done.5.b1, bf16[2,8,896]{2,1,0:T(8,128)(2,1)S(1)} %collective-permute-done.6.b2, bf16[2,8,896]{2,1,0:T(8,128)(2,1)S(1)} %collective-permute-done.7.b3, ...), custom_call_target="tpu_custom_call" | custom-call | bytes 712704 | tf_op jit(solution)/shard_map/combine/pallas_call | solution.py:217
  29.0 0.1 collective-permute-start.10
  29.0 1.6 %collective-permute-start.9 = (bf16[16,384]{1,0:T(8,128)(2,1)S(1)}, bf16[16,384]{1,0:T(8,128)(2,1)S(1)}, u32[]{:S(2)}, u32[]{:S(2)}) collective-permute-start(bf16[16,384]{1,0:T(8,128)(2,1)S(1)} %combine.1.p0), channel_id=1, source_target_pairs={{0,2},{1,3},{2,0},{3,1},{4,6},{5,7},{6,4},{7,5},{8,10},{9,11},{10,... | collective-permute-start | bytes 36872 | tf_op jit(solution)/shard_map/ppermute | solution.py:501
  30.6 0.3 collective-permute-start.8
  30.9 1.3 %collective-permute-done.10.p3 = bf16[16,384]{1,0:T(8,128)(2,1)S(1)} collective-permute-done((bf16[16,384]{1,0:T(8,128)(2,1)S(1)}, bf16[16,384]{1,0:T(8,128)(2,1)S(1)}, u32[]{:S(2)}, u32[]{:S(2)}) %collective-permute-start.10) | collective-permute-done | bytes 12320 | tf_op jit(solution)/shard_map/ppermute | solution.py:501
  32.2 0.6 collective-permute-done.9.p2
  32.8 0.0 collective-permute-done.8.p1
  32.8 3.4 %collective-permute-start.12 = (bf16[16,384]{1,0:T(8,128)(2,1)S(1)}, bf16[16,384]{1,0:T(8,128)(2,1)S(1)}, u32[]{:S(2)}, u32[]{:S(2)}) collective-permute-start(bf16[16,384]{1,0:T(8,128)(2,1)S(1)} %head_sum.1), channel_id=1, source_target_pairs={{0,28},{4,24},{1,20},{5,16},{2,12},{6,8},{3,4},{7,0},{9,29},{13,25... | collective-permute-start | bytes 36872 | tf_op jit(solution)/shard_map/ppermute | solution.py:583
  36.2 0.6 collective-permute-start.11
  36.8 0.0 copy-done.8
  36.8 0.8 %collective-permute-done.12.flip = bf16[16,384]{1,0:T(8,128)(2,1)S(1)} collective-permute-done((bf16[16,384]{1,0:T(8,128)(2,1)S(1)}, bf16[16,384]{1,0:T(8,128)(2,1)S(1)}, u32[]{:S(2)}, u32[]{:S(2)}) %collective-permute-start.12) | collective-permute-done | bytes 12320 | tf_op jit(solution)/shard_map/ppermute | solution.py:583
  37.6 1.7 %collective-permute-done.11.same = bf16[16,384]{1,0:T(8,128)(2,1)S(1)} collective-permute-done((bf16[16,384]{1,0:T(8,128)(2,1)S(1)}, bf16[16,384]{1,0:T(8,128)(2,1)S(1)}, u32[]{:S(2)}, u32[]{:S(2)}) %collective-permute-start.11) | collective-permute-done | bytes 12320 | tf_op jit(solution)/shard_map/ppermute | solution.py:583
  39.3 0.0 copy-done.3
  39.3 0.0 copy-done.4
  39.3 0.5 gate_up.1
  39.9 0.0 collective-permute-start.13
  39.9 1.3 %collective-permute-done.13.theirs = bf16[16,2176]{1,0:T(8,128)(2,1)S(1)} collective-permute-done((bf16[16,2176]{1,0:T(8,128)(2,1)S(1)}, bf16[16,2176]{1,0:T(8,128)(2,1)S(1)}, u32[]{:S(2)}, u32[]{:S(2)}) %collective-permute-start.13) | collective-permute-done | bytes 69664 | tf_op jit(solution)/shard_map/ppermute | solution.py:501
  41.1 0.1 core_sum.1.mine
  41.2 2.3 %collective-permute-start.14 = (bf16[16,2176]{1,0:T(8,128)(2,1)S(1)}, bf16[16,2176]{1,0:T(8,128)(2,1)S(1)}, u32[]{:S(2)}, u32[]{:S(2)}) collective-permute-start(bf16[16,2176]{1,0:T(8,128)(2,1)S(1)} %core_sum.1.mine), channel_id=1, source_target_pairs={{0,2},{1,3},{2,0},{3,1},{4,6},{5,7},{6,4},{7,5},{8,10},{9,11},{10,... | collective-permute-start | bytes 208904 | tf_op jit(solution)/shard_map/ppermute | solution.py:501
  43.5 2.5 %collective-permute-done.14.theirs = bf16[16,2176]{1,0:T(8,128)(2,1)S(1)} collective-permute-done((bf16[16,2176]{1,0:T(8,128)(2,1)S(1)}, bf16[16,2176]{1,0:T(8,128)(2,1)S(1)}, u32[]{:S(2)}, u32[]{:S(2)}) %collective-permute-start.14) | collective-permute-done | bytes 69664 | tf_op jit(solution)/shard_map/ppermute | solution.py:501
  46.0 0.0 copy-done.2
  46.0 0.4 down.1
  46.4 10.6 %all_to_all.5.parts = bf16[8,2,768]{2,1,0:T(2,128)(2,1)S(1)} all-to-all(bf16[8,2,768]{2,1,0:T(2,128)(2,1)S(1)} %down.1), channel_id=1, replica_groups=mesh['pool'=8,'mlp'=4] {'pool'}, dimensions={0} | all-to-all | bytes 49152 | tf_op jit(solution)/shard_map/all_to_all | solution.py:608
  57.0 0.6 %final.1 = bf16[2,768]{1,0:T(2,128)(2,1)} custom-call(f32[2,768]{1,0:T(2,128)S(1)} %get-tuple-element.17.own, bf16[8,2,768]{2,1,0:T(2,128)(2,1)S(1)} %all_to_all.5.parts), custom_call_target="tpu_custom_call" | custom-call | bytes 30720 | tf_op jit(solution)/shard_map/final/pallas_call | solution.py:217
  (12 shorter events, 0.0 us)
Async XLA Ops:
  0.0 16.1 %copy-start.1 = (bf16[5,256,768]{2,1,0:T(8,128)(2,1)S(1)}, bf16[5,256,768]{2,1,0:T(8,128)(2,1)}, u32[]{:S(2)}) copy-start(bf16[5,256,768]{2,1,0:T(8,128)(2,1)} %values.1) | copy-start | bytes 5898244
  0.0 16.1 %copy-start = (bf16[5,256,768]{2,1,0:T(8,128)(2,1)S(1)}, bf16[5,256,768]{2,1,0:T(8,128)(2,1)}, u32[]{:S(2)}) copy-start(bf16[5,256,768]{2,1,0:T(8,128)(2,1)} %keys.1) | copy-start | bytes 5898244
  1.8 4.9 %collective-permute-start = (bf16[2,1664]{1,0:T(2,128)(2,1)}, bf16[2,1664]{1,0:T(2,128)(2,1)S(1)}, u32[]{:S(2)}, u32[]{:S(2)}) collective-permute-start(bf16[2,1664]{1,0:T(2,128)(2,1)} %get-tuple-element.12.mine), channel_id=1, source_target_pairs={{0,4},{4,0},{8,12},{12,8},{16,20},{20,16},{24,28},{28,24},{1,5},{5... | collective-permute-start | bytes 19976 | tf_op jit(solution)/shard_map/ppermute | solution.py:501
  6.7 0.7 %copy-start.7 = (bf16[2,1664]{1,0:T(2,128)(2,1)S(1)}, bf16[2,1664]{1,0:T(2,128)(2,1)}, u32[]{:S(2)}) copy-start(bf16[2,1664]{1,0:T(2,128)(2,1)} %get-tuple-element.12.mine) | copy-start | bytes 19972
  7.4 5.8 %collective-permute-start.3 = (bf16[2,2,1664]{2,1,0:T(2,128)(2,1)S(1)}, bf16[2,2,1664]{2,1,0:T(2,128)(2,1)S(1)}, u32[]{:S(2)}, u32[]{:S(2)}) collective-permute-start(bf16[2,2,1664]{2,1,0:T(2,128)(2,1)S(1)} %merge.2.a0), channel_id=1, source_target_pairs={{0,24},{4,28},{8,16},{12,20},{16,8},{20,12},{24,0},{28,4},{1,25},{... | collective-permute-start | bytes 39944 | tf_op jit(solution)/shard_map/ppermute | solution.py:501
  11.5 4.6 %collective-permute-start.2 = (bf16[2,2,1664]{2,1,0:T(2,128)(2,1)S(1)}, bf16[2,2,1664]{2,1,0:T(2,128)(2,1)S(1)}, u32[]{:S(2)}, u32[]{:S(2)}) collective-permute-start(bf16[2,2,1664]{2,1,0:T(2,128)(2,1)S(1)} %merge.2.a0), channel_id=1, source_target_pairs={{0,16},{4,20},{8,24},{12,28},{16,0},{20,4},{24,8},{28,12},{1,17},{... | collective-permute-start | bytes 39944 | tf_op jit(solution)/shard_map/ppermute | solution.py:501
  11.5 4.6 %collective-permute-start.1 = (bf16[2,2,1664]{2,1,0:T(2,128)(2,1)S(1)}, bf16[2,2,1664]{2,1,0:T(2,128)(2,1)S(1)}, u32[]{:S(2)}, u32[]{:S(2)}) collective-permute-start(bf16[2,2,1664]{2,1,0:T(2,128)(2,1)S(1)} %merge.2.a0), channel_id=1, source_target_pairs={{0,8},{4,12},{8,0},{12,4},{16,24},{20,28},{24,16},{28,20},{1,9},{5... | collective-permute-start | bytes 39944 | tf_op jit(solution)/shard_map/ppermute | solution.py:501
  16.1 0.7 %copy-start.6 = (f32[8,896]{1,0:T(8,128)S(1)}, f32[8,896]{1,0:T(8,128)}, u32[]{:S(2)}) copy-start(f32[8,896]{1,0:T(8,128)} %get-tuple-element.13.own) | copy-start | bytes 86020
  16.8 11.5 %copy-start.5 = (bf16[768,384]{1,0:T(8,128)(2,1)S(1)}, bf16[768,384]{1,0:T(8,128)(2,1)}, u32[]{:S(2)}) copy-start(bf16[768,384]{1,0:T(8,128)(2,1)} %weight.2) | copy-start | bytes 1769476
  16.8 19.9 %copy-start.8 = (bf16[768]{0:T(1024)(128)(2,1)S(1)}, bf16[768]{0:T(1024)(128)(2,1)}, u32[]{:S(2)}) copy-start(bf16[768]{0:T(1024)(128)(2,1)} %param.22) | copy-start | bytes 4612
  16.8 22.5 %copy-start.3 = (bf16[768,1024]{1,0:T(8,128)(2,1)S(1)}, bf16[768,1024]{1,0:T(8,128)(2,1)}, u32[]{:S(2)}) copy-start(bf16[768,1024]{1,0:T(8,128)(2,1)} %gate.1) | copy-start | bytes 4718596
  16.9 22.5 %copy-start.4 = (bf16[768,1024]{1,0:T(8,128)(2,1)S(1)}, bf16[768,1024]{1,0:T(8,128)(2,1)}, u32[]{:S(2)}) copy-start(bf16[768,1024]{1,0:T(8,128)(2,1)} %up.1) | copy-start | bytes 4718596
  18.0 3.8 %collective-permute-start.4 = (bf16[8,896]{1,0:T(8,128)(2,1)S(1)}, bf16[8,896]{1,0:T(8,128)(2,1)S(1)}, u32[]{:S(2)}, u32[]{:S(2)}) collective-permute-start(bf16[8,896]{1,0:T(8,128)(2,1)S(1)} %get-tuple-element.14.mine), channel_id=1, source_target_pairs={{0,4},{4,0},{8,12},{12,8},{16,20},{20,16},{24,28},{28,24},{1,5},{5... | collective-permute-start | bytes 43016 | tf_op jit(solution)/shard_map/ppermute | solution.py:501
  21.8 5.7 %collective-permute-start.7 = (bf16[2,8,896]{2,1,0:T(8,128)(2,1)S(1)}, bf16[2,8,896]{2,1,0:T(8,128)(2,1)S(1)}, u32[]{:S(2)}, u32[]{:S(2)}) collective-permute-start(bf16[2,8,896]{2,1,0:T(8,128)(2,1)S(1)} %merge.3.b0), channel_id=1, source_target_pairs={{0,24},{4,28},{8,16},{12,20},{16,8},{20,12},{24,0},{28,4},{1,25},{... | collective-permute-start | bytes 86024 | tf_op jit(solution)/shard_map/ppermute | solution.py:501
  23.2 4.8 %collective-permute-start.6 = (bf16[2,8,896]{2,1,0:T(8,128)(2,1)S(1)}, bf16[2,8,896]{2,1,0:T(8,128)(2,1)S(1)}, u32[]{:S(2)}, u32[]{:S(2)}) collective-permute-start(bf16[2,8,896]{2,1,0:T(8,128)(2,1)S(1)} %merge.3.b0), channel_id=1, source_target_pairs={{0,16},{4,20},{8,24},{12,28},{16,0},{20,4},{24,8},{28,12},{1,17},{... | collective-permute-start | bytes 86024 | tf_op jit(solution)/shard_map/ppermute | solution.py:501
  23.9 4.4 %collective-permute-start.5 = (bf16[2,8,896]{2,1,0:T(8,128)(2,1)S(1)}, bf16[2,8,896]{2,1,0:T(8,128)(2,1)S(1)}, u32[]{:S(2)}, u32[]{:S(2)}) collective-permute-start(bf16[2,8,896]{2,1,0:T(8,128)(2,1)S(1)} %merge.3.b0), channel_id=1, source_target_pairs={{0,8},{4,12},{8,0},{12,4},{16,24},{20,28},{24,16},{28,20},{1,9},{5... | collective-permute-start | bytes 86024 | tf_op jit(solution)/shard_map/ppermute | solution.py:501
  29.0 3.3 %collective-permute-start.10 = (bf16[16,384]{1,0:T(8,128)(2,1)S(1)}, bf16[16,384]{1,0:T(8,128)(2,1)S(1)}, u32[]{:S(2)}, u32[]{:S(2)}) collective-permute-start(bf16[16,384]{1,0:T(8,128)(2,1)S(1)} %combine.1.p0), channel_id=1, source_target_pairs={{0,3},{1,2},{2,1},{3,0},{4,7},{5,6},{6,5},{7,4},{8,11},{9,10},{10,... | collective-permute-start | bytes 36872 | tf_op jit(solution)/shard_map/ppermute | solution.py:501
  29.0 3.8 %collective-permute-start.9 = (bf16[16,384]{1,0:T(8,128)(2,1)S(1)}, bf16[16,384]{1,0:T(8,128)(2,1)S(1)}, u32[]{:S(2)}, u32[]{:S(2)}) collective-permute-start(bf16[16,384]{1,0:T(8,128)(2,1)S(1)} %combine.1.p0), channel_id=1, source_target_pairs={{0,2},{1,3},{2,0},{3,1},{4,6},{5,7},{6,4},{7,5},{8,10},{9,11},{10,... | collective-permute-start | bytes 36872 | tf_op jit(solution)/shard_map/ppermute | solution.py:501
  30.6 2.2 %collective-permute-start.8 = (bf16[16,384]{1,0:T(8,128)(2,1)S(1)}, bf16[16,384]{1,0:T(8,128)(2,1)S(1)}, u32[]{:S(2)}, u32[]{:S(2)}) collective-permute-start(bf16[16,384]{1,0:T(8,128)(2,1)S(1)} %combine.1.p0), channel_id=1, source_target_pairs={{0,1},{1,0},{2,3},{3,2},{4,5},{5,4},{6,7},{7,6},{8,9},{9,8},{10,11... | collective-permute-start | bytes 36872 | tf_op jit(solution)/shard_map/ppermute | solution.py:501
  32.8 4.8 %collective-permute-start.12 = (bf16[16,384]{1,0:T(8,128)(2,1)S(1)}, bf16[16,384]{1,0:T(8,128)(2,1)S(1)}, u32[]{:S(2)}, u32[]{:S(2)}) collective-permute-start(bf16[16,384]{1,0:T(8,128)(2,1)S(1)} %head_sum.1), channel_id=1, source_target_pairs={{0,28},{4,24},{1,20},{5,16},{2,12},{6,8},{3,4},{7,0},{9,29},{13,25... | collective-permute-start | bytes 36872 | tf_op jit(solution)/shard_map/ppermute | solution.py:583
  36.2 3.1 %collective-permute-start.11 = (bf16[16,384]{1,0:T(8,128)(2,1)S(1)}, bf16[16,384]{1,0:T(8,128)(2,1)S(1)}, u32[]{:S(2)}, u32[]{:S(2)}) collective-permute-start(bf16[16,384]{1,0:T(8,128)(2,1)S(1)} %head_sum.1), channel_id=1, source_target_pairs={{0,24},{4,28},{1,16},{5,20},{2,8},{6,12},{3,0},{7,4},{9,25},{13,29... | collective-permute-start | bytes 36872 | tf_op jit(solution)/shard_map/ppermute | solution.py:583
  39.3 6.7 %copy-start.2 = (bf16[1024,768]{1,0:T(8,128)(2,1)S(1)}, bf16[1024,768]{1,0:T(8,128)(2,1)}, u32[]{:S(2)}) copy-start(bf16[1024,768]{1,0:T(8,128)(2,1)} %weight.3) | copy-start | bytes 4718596
  39.9 1.3 %collective-permute-start.13 = (bf16[16,2176]{1,0:T(8,128)(2,1)S(1)}, bf16[16,2176]{1,0:T(8,128)(2,1)S(1)}, u32[]{:S(2)}, u32[]{:S(2)}) collective-permute-start(bf16[16,2176]{1,0:T(8,128)(2,1)S(1)} %get-tuple-element.18.mine), channel_id=1, source_target_pairs={{0,1},{1,0},{2,3},{3,2},{4,5},{5,4},{6,7},{7,6},{8,9},{9,8},{10,11... | collective-permute-start | bytes 208904 | tf_op jit(solution)/shard_map/ppermute | solution.py:501
  41.2 4.8 %collective-permute-start.14 = (bf16[16,2176]{1,0:T(8,128)(2,1)S(1)}, bf16[16,2176]{1,0:T(8,128)(2,1)S(1)}, u32[]{:S(2)}, u32[]{:S(2)}) collective-permute-start(bf16[16,2176]{1,0:T(8,128)(2,1)S(1)} %core_sum.1.mine), channel_id=1, source_target_pairs={{0,2},{1,3},{2,0},{3,1},{4,6},{5,7},{6,4},{7,5},{8,10},{9,11},{10,... | collective-permute-start | bytes 208904 | tf_op jit(solution)/shard_map/ppermute | solution.py:501

commit v7 on v6

--- a/solution.py
+++ b/solution.py
@@ -243,6 +243,37 @@
 
 def round_low(values):
     return values.astype(BF16).astype(F32)
+
+
+def head_start(shape):
+    return rows_of(shape) * HD % 128
+
+
+def flatten(tail, width):
+    heads = tail.shape[0]
+    spread = jnp.zeros((heads, width), F32)
+    start = head_start((heads, width))
+    for k in (0, 32, 64, 96):
+        moved = pltpu.roll(tail, k, 1) if k else tail
+        spread = jnp.where(start == k, jnp.concatenate([moved] * (width // 128), 1), spread)
+    lane = lanes((heads, width))
+    used = (lane // HD == rows_of((heads, width))) & (lane % HD < 24)
+    return jnp.sum(jnp.where(used, spread, 0.0), 0, keepdims=True)
+
+
+def unflatten(row, heads):
+    width = row.shape[1]
+    lane = lanes((heads, width))
+    used = (lane // HD == rows_of((heads, width))) & (lane % HD < 24)
+    spread = jnp.where(used, jnp.broadcast_to(row, (heads, width)), 0.0)
+    folded = spread[:, :128]
+    for at in range(128, width, 128):
+        folded = folded + spread[:, at : at + 128]
+    start = head_start((heads, 128))
+    tail = jnp.where(start == 0, folded, 0.0)
+    for k in (32, 64, 96):
+        tail = jnp.where(start == k, pltpu.roll(folded, 128 - k, 1), tail)
+    return tail
 
 
 def prepare_kernel(*refs):
@@ -316,6 +347,11 @@
     own[:, width:] = tail
 
 
+def carry_kernel(packed, own, packed_near, own_near):
+    packed_near[...] = packed[...]
+    own_near[...] = own[...]
+
+
 def merge_kernel(mine, theirs, both):
     y = lax.axis_index("pool") % 2
     both[y] = mine[...]
@@ -344,7 +380,6 @@
     head_mask = lanes((heads, width)) // HD == rows_of((heads, width))
     spot = lanes((heads, 128))
     tail = own[:, width:]
-    part[...] = own[...].astype(BF16)
     scores, limits = [], []
     for b in range(blocks):
         match = jnp.where(table == (me * blocks + b).astype(F32), 1.0, 0.0)
@@ -380,8 +415,8 @@
     numer = own[:, :width]
     for b in range(blocks):
         numer = jnp.where(line == b, numerators[b], numer)
-    part[:, :width] = numer.astype(BF16)
-    part[:, width:] = tail.astype(BF16)
+    numer = jnp.where(line == 7, flatten(tail, width), numer)
+    part[...] = numer.astype(BF16)
 
 
 def combine_kernel(b0, b1, b2, b3, tables, weight, head_part, numer, tails, mix):
@@ -396,8 +431,8 @@
         for y in range(2):
             owner = z * 2 + y
             values = piece[y].astype(F32)
-            numer[pl.ds(pl.multiple_of(owner * slots, 8), slots), :] = values[:, :width]
-            tails[owner] = values[:, width:]
+            numer[pl.ds(pl.multiple_of(owner * slots, 8), slots), :] = values
+            tails[owner] = unflatten(values[slots - 1 : slots], heads)
     lane8 = lanes((heads, 128))
     shifts = jnp.zeros((heads, 128), F32)
     totals = jnp.zeros((heads, 128), F32)
@@ -538,27 +573,34 @@
         limit=54 * 2**20,
     )
 
-    def pool_gather(values):
+    packed_near, own = call(
+        carry_kernel,
+        "carry",
+        [(packed.shape, BF16), (own.shape, F32)],
+        [packed, own],
+    )
+
+    def pool_gather(values, near):
         (both,) = call(
             merge_kernel,
             "merge",
             [((2,) + values.shape, values.dtype)],
-            [values, flip(values, "pool", 1)],
+            [near, flip(values, "pool", 1)],
         )
         return [both] + [flip(both, "pool", step) for step in (2, 4, 6)]
 
     part, all_input, tables = call(
         attend_kernel,
         "attend",
-        [((slots, part_width), BF16), ((requests, width), F32), ((requests, 128), F32)],
-        pool_gather(packed) + [own, key_cache, value_cache],
+        [((slots, width), BF16), ((requests, width), F32), ((requests, 128), F32)],
+        pool_gather(packed, packed_near) + [own, key_cache, value_cache],
         [pltpu.VMEM((requests, packed_width), F32)],
     )
     (head_part,) = call(
         combine_kernel,
         "combine",
         [((requests, part_cols), BF16)],
-        pool_gather(part) + [tables, out_weight],
+        pool_gather(part, part) + [tables, out_weight],
         [
             pltpu.VMEM((pool * slots, width), F32),
             pltpu.VMEM((pool, slots, 128), F32),

time: 57.8 us -> 56.4 us (0.976)
  waiting for transfers between devices: 18.4 us -> 16.9 us
    ppermute x13, waiting for transfers between devices: 15.9 us -> 14.3 us  [flip(): lax.ppermute(values, axis, [(index, index ^ step) for index in range(size)])]
    pallas_call x10 -> x11, Pallas kernels: 5.24 us -> 5.3 us  [call(): pl.pallas_call(kernel, out_shape=[jax.ShapeDtypeStruct(shape, dtype) for...]
where the time goes in v7:
time: 56.4 us; the launch traced here: 56.2 us
  starting transfers between devices  21.9 us (39%)
  waiting for transfers between devices  16.9 us (30%)
  blocking collectives  10.6 us (19%)
  Pallas kernels  5.3 us (9%)
  local copies, waits for them, and re-layouts  1.48 us (3%)
    ppermute x13, starting transfers between devices, flip(): lax.ppermute(values, axis, [(index, index ^ step) for index in range(size)])  17.9 us
    ppermute x13, waiting for transfers between devices, flip(): lax.ppermute(values, axis, [(index, index ^ step) for index in range(size)])  14.3 us
    all_to_all x1, blocking collectives, per_device_small(): lax.all_to_all(down, 'pool', 0, 0)  10.6 us
    pallas_call x11, Pallas kernels, call(): pl.pallas_call(kernel, out_shape=[jax.ShapeDtypeStruct(shape, dtype) for...  5.3 us
    ppermute x2, starting transfers between devices, per_device_small(): pieces.append(lax.ppermute(head_sum, ('pool', 'mlp'), route))  3.95 us
    ppermute x2, waiting for transfers between devices, per_device_small(): pieces.append(lax.ppermute(head_sum, ('pool', 'mlp'), route))  2.56 us
    unnamed x18, local copies, waits for them, and re-layouts  1.48 us
  transfers between devices with their start and end apart: 15, of which 13 were waited for; matrix products, arithmetic and copies ran while one was open for 0% of the time, Pallas kernels for 0%

profile of v7, /device:TPU:0, one launch (start us, length us, event | category | flops | bytes accessed | tf_op | source)
XLA Modules:
  0.0 56.2 jit_solution(14995009785958537887)
XLA Ops:
  0.0 1.8 %rotary.1 = (bf16[2,1664]{1,0:T(2,128)(2,1)}, f32[8,896]{1,0:T(8,128)}) custom-call(s32[2,8]{1,0:T(2,128)} %refs_0_.1, s32[2]{0:T(128)} %refs_1_.1, bf16[2,768]{1,0:T(2,128)(2,1)} %refs_2_.1, bf16[2,768]{1,0:T(2,128)(2,1)} %refs_3_.1, bf16[2,768]{1,0:T(2,128)(2,1)} %refs_4_.1, bf16[2,768]{1,0:T(2,128)(2,1)} %refs_5_.1, bf16[5,256,768]{2,1,0:T(8,128)(2,1)} %keys.1, ...), custom_call_target="tpu_custom_call" | custom-call | bytes 3944520 | tf_op jit(solution)/shard_map/rotary/pallas_call | solution.py:217
  1.8 3.0 %collective-permute-start = (bf16[2,1664]{1,0:T(2,128)(2,1)}, bf16[2,1664]{1,0:T(2,128)(2,1)S(1)}, u32[]{:S(2)}, u32[]{:S(2)}) collective-permute-start(bf16[2,1664]{1,0:T(2,128)(2,1)} %get-tuple-element.14.packed), channel_id=1, source_target_pairs={{0,4},{4,0},{8,12},{12,8},{16,20},{20,16},{24,28},{28,24},{1,5},{5... | collective-permute-start | bytes 19976 | tf_op jit(solution)/shard_map/ppermute | solution.py:536
  4.8 0.7 %copy-done.6 = f32[8,896]{1,0:T(8,128)S(1)} copy-done((f32[8,896]{1,0:T(8,128)S(1)}, f32[8,896]{1,0:T(8,128)}, u32[]{:S(2)}) %copy-start.6) | copy-done | bytes 28696
  5.6 0.7 %copy-done.7 = bf16[2,1664]{1,0:T(2,128)(2,1)S(1)} copy-done((bf16[2,1664]{1,0:T(2,128)(2,1)S(1)}, bf16[2,1664]{1,0:T(2,128)(2,1)}, u32[]{:S(2)}) %copy-start.7) | copy-done | bytes 6680
  6.3 0.4 collective-permute-done.theirs
  6.7 4.1 %collective-permute-start.3 = (bf16[2,2,1664]{2,1,0:T(2,128)(2,1)S(1)}, bf16[2,2,1664]{2,1,0:T(2,128)(2,1)S(1)}, u32[]{:S(2)}, u32[]{:S(2)}) collective-permute-start(bf16[2,2,1664]{2,1,0:T(2,128)(2,1)S(1)} %merge.2.a0), channel_id=1, source_target_pairs={{0,24},{4,28},{8,16},{12,20},{16,8},{20,12},{24,0},{28,4},{1,25},{... | collective-permute-start | bytes 39944 | tf_op jit(solution)/shard_map/ppermute | solution.py:536
  10.8 0.0 collective-permute-start.2
  10.8 0.6 %collective-permute-start.1 = (bf16[2,2,1664]{2,1,0:T(2,128)(2,1)S(1)}, bf16[2,2,1664]{2,1,0:T(2,128)(2,1)S(1)}, u32[]{:S(2)}, u32[]{:S(2)}) collective-permute-start(bf16[2,2,1664]{2,1,0:T(2,128)(2,1)S(1)} %merge.2.a0), channel_id=1, source_target_pairs={{0,8},{4,12},{8,0},{12,4},{16,24},{20,28},{24,16},{28,20},{1,9},{5... | collective-permute-start | bytes 39944 | tf_op jit(solution)/shard_map/ppermute | solution.py:536
  11.3 1.1 %collective-permute-done.3.a3 = bf16[2,2,1664]{2,1,0:T(2,128)(2,1)S(1)} collective-permute-done((bf16[2,2,1664]{2,1,0:T(2,128)(2,1)S(1)}, bf16[2,2,1664]{2,1,0:T(2,128)(2,1)S(1)}, u32[]{:S(2)}, u32[]{:S(2)}) %collective-permute-start.3) | collective-permute-done | bytes 13344 | tf_op jit(solution)/shard_map/ppermute | solution.py:536
  12.5 2.9 %collective-permute-done.2.a2 = bf16[2,2,1664]{2,1,0:T(2,128)(2,1)S(1)} collective-permute-done((bf16[2,2,1664]{2,1,0:T(2,128)(2,1)S(1)}, bf16[2,2,1664]{2,1,0:T(2,128)(2,1)S(1)}, u32[]{:S(2)}, u32[]{:S(2)}) %collective-permute-start.2) | collective-permute-done | bytes 13344 | tf_op jit(solution)/shard_map/ppermute | solution.py:536
  15.4 0.0 collective-permute-done.1.a1
  15.4 0.0 copy-done.1
  15.4 0.0 copy-done
  15.4 0.0 copy-start.5
  15.4 0.0 copy-start.8
  15.4 0.0 copy-start.3
  15.4 0.0 copy-start.4
  15.4 1.1 %attend.1 = (bf16[8,768]{1,0:T(8,128)(2,1)S(1)}, f32[16,768]{1,0:T(8,128)S(1)}, f32[16,128]{1,0:T(8,128)S(1)}) custom-call(bf16[2,2,1664]{2,1,0:T(2,128)(2,1)S(1)} %merge.2.a0, bf16[2,2,1664]{2,1,0:T(2,128)(2,1)S(1)} %collective-permute-done.1.a1, bf16[2,2,1664]{2,1,0:T(2,128)(2,1)S(1)} %collective-permute-done.2.a2, ...), custom_call_target="tpu_custom_call" | custom-call | bytes 4014080 | tf_op jit(solution)/shard_map/attend/pallas_call | solution.py:217
  16.6 1.6 %collective-permute-start.4 = (bf16[8,768]{1,0:T(8,128)(2,1)S(1)}, bf16[8,768]{1,0:T(8,128)(2,1)S(1)}, u32[]{:S(2)}, u32[]{:S(2)}) collective-permute-start(bf16[8,768]{1,0:T(8,128)(2,1)S(1)} %get-tuple-element.18.mine), channel_id=1, source_target_pairs={{0,4},{4,0},{8,12},{12,8},{16,20},{20,16},{24,28},{28,24},{1,5},{5... | collective-permute-start | bytes 36872 | tf_op jit(solution)/shard_map/ppermute | solution.py:536
  18.2 2.2 %collective-permute-done.4.theirs = bf16[8,768]{1,0:T(8,128)(2,1)S(1)} collective-permute-done((bf16[8,768]{1,0:T(8,128)(2,1)S(1)}, bf16[8,768]{1,0:T(8,128)(2,1)S(1)}, u32[]{:S(2)}, u32[]{:S(2)}) %collective-permute-start.4) | collective-permute-done | bytes 12320 | tf_op jit(solution)/shard_map/ppermute | solution.py:536
  20.4 1.4 %collective-permute-start.7 = (bf16[2,8,768]{2,1,0:T(8,128)(2,1)S(1)}, bf16[2,8,768]{2,1,0:T(8,128)(2,1)S(1)}, u32[]{:S(2)}, u32[]{:S(2)}) collective-permute-start(bf16[2,8,768]{2,1,0:T(8,128)(2,1)S(1)} %merge.3.b0), channel_id=1, source_target_pairs={{0,24},{4,28},{8,16},{12,20},{16,8},{20,12},{24,0},{28,4},{1,25},{... | collective-permute-start | bytes 73736 | tf_op jit(solution)/shard_map/ppermute | solution.py:536
  21.8 0.6 %collective-permute-start.6 = (bf16[2,8,768]{2,1,0:T(8,128)(2,1)S(1)}, bf16[2,8,768]{2,1,0:T(8,128)(2,1)S(1)}, u32[]{:S(2)}, u32[]{:S(2)}) collective-permute-start(bf16[2,8,768]{2,1,0:T(8,128)(2,1)S(1)} %merge.3.b0), channel_id=1, source_target_pairs={{0,16},{4,20},{8,24},{12,28},{16,0},{20,4},{24,8},{28,12},{1,17},{... | collective-permute-start | bytes 73736 | tf_op jit(solution)/shard_map/ppermute | solution.py:536
  22.4 2.3 %collective-permute-start.5 = (bf16[2,8,768]{2,1,0:T(8,128)(2,1)S(1)}, bf16[2,8,768]{2,1,0:T(8,128)(2,1)S(1)}, u32[]{:S(2)}, u32[]{:S(2)}) collective-permute-start(bf16[2,8,768]{2,1,0:T(8,128)(2,1)S(1)} %merge.3.b0), channel_id=1, source_target_pairs={{0,8},{4,12},{8,0},{12,4},{16,24},{20,28},{24,16},{28,20},{1,9},{5... | collective-permute-start | bytes 73736 | tf_op jit(solution)/shard_map/ppermute | solution.py:536
  24.7 1.2 %collective-permute-done.7.b3 = bf16[2,8,768]{2,1,0:T(8,128)(2,1)S(1)} collective-permute-done((bf16[2,8,768]{2,1,0:T(8,128)(2,1)S(1)}, bf16[2,8,768]{2,1,0:T(8,128)(2,1)S(1)}, u32[]{:S(2)}, u32[]{:S(2)}) %collective-permute-start.7) | collective-permute-done | bytes 24608 | tf_op jit(solution)/shard_map/ppermute | solution.py:536
  26.0 0.6 %collective-permute-done.6.b2 = bf16[2,8,768]{2,1,0:T(8,128)(2,1)S(1)} collective-permute-done((bf16[2,8,768]{2,1,0:T(8,128)(2,1)S(1)}, bf16[2,8,768]{2,1,0:T(8,128)(2,1)S(1)}, u32[]{:S(2)}, u32[]{:S(2)}) %collective-permute-start.6) | collective-permute-done | bytes 24608 | tf_op jit(solution)/shard_map/ppermute | solution.py:536
  26.5 0.2 collective-permute-done.5.b1
  26.8 0.0 copy-done.5
  26.8 0.7 %combine.1.p0 = bf16[16,384]{1,0:T(8,128)(2,1)S(1)} custom-call(bf16[2,8,768]{2,1,0:T(8,128)(2,1)S(1)} %merge.3.b0, bf16[2,8,768]{2,1,0:T(8,128)(2,1)S(1)} %collective-permute-done.5.b1, bf16[2,8,768]{2,1,0:T(8,128)(2,1)S(1)} %collective-permute-done.6.b2, bf16[2,8,768]{2,1,0:T(8,128)(2,1)S(1)} %collective-permute-done.7.b3, ...), custom_call_target="tpu_custom_call" | custom-call | bytes 696320 | tf_op jit(solution)/shard_map/combine/pallas_call | solution.py:217
  27.5 0.1 collective-permute-start.10
  27.6 1.6 %collective-permute-start.9 = (bf16[16,384]{1,0:T(8,128)(2,1)S(1)}, bf16[16,384]{1,0:T(8,128)(2,1)S(1)}, u32[]{:S(2)}, u32[]{:S(2)}) collective-permute-start(bf16[16,384]{1,0:T(8,128)(2,1)S(1)} %combine.1.p0), channel_id=1, source_target_pairs={{0,2},{1,3},{2,0},{3,1},{4,6},{5,7},{6,4},{7,5},{8,10},{9,11},{10,... | collective-permute-start | bytes 36872 | tf_op jit(solution)/shard_map/ppermute | solution.py:536
  29.1 0.3 collective-permute-start.8
  29.4 1.3 %collective-permute-done.10.p3 = bf16[16,384]{1,0:T(8,128)(2,1)S(1)} collective-permute-done((bf16[16,384]{1,0:T(8,128)(2,1)S(1)}, bf16[16,384]{1,0:T(8,128)(2,1)S(1)}, u32[]{:S(2)}, u32[]{:S(2)}) %collective-permute-start.10) | collective-permute-done | bytes 12320 | tf_op jit(solution)/shard_map/ppermute | solution.py:536
  30.8 0.6 %collective-permute-done.9.p2 = bf16[16,384]{1,0:T(8,128)(2,1)S(1)} collective-permute-done((bf16[16,384]{1,0:T(8,128)(2,1)S(1)}, bf16[16,384]{1,0:T(8,128)(2,1)S(1)}, u32[]{:S(2)}, u32[]{:S(2)}) %collective-permute-start.9) | collective-permute-done | bytes 12320 | tf_op jit(solution)/shard_map/ppermute | solution.py:536
  31.3 0.0 collective-permute-done.8.p1
  31.4 3.4 %collective-permute-start.12 = (bf16[16,384]{1,0:T(8,128)(2,1)S(1)}, bf16[16,384]{1,0:T(8,128)(2,1)S(1)}, u32[]{:S(2)}, u32[]{:S(2)}) collective-permute-start(bf16[16,384]{1,0:T(8,128)(2,1)S(1)} %head_sum.1), channel_id=1, source_target_pairs={{0,28},{4,24},{1,20},{5,16},{2,12},{6,8},{3,4},{7,0},{9,29},{13,25... | collective-permute-start | bytes 36872 | tf_op jit(solution)/shard_map/ppermute | solution.py:625
  34.8 0.6 collective-permute-start.11
  35.3 0.8 %collective-permute-done.12.flip = bf16[16,384]{1,0:T(8,128)(2,1)S(1)} collective-permute-done((bf16[16,384]{1,0:T(8,128)(2,1)S(1)}, bf16[16,384]{1,0:T(8,128)(2,1)S(1)}, u32[]{:S(2)}, u32[]{:S(2)}) %collective-permute-start.12) | collective-permute-done | bytes 12320 | tf_op jit(solution)/shard_map/ppermute | solution.py:625
  36.2 1.7 %collective-permute-done.11.same = bf16[16,384]{1,0:T(8,128)(2,1)S(1)} collective-permute-done((bf16[16,384]{1,0:T(8,128)(2,1)S(1)}, bf16[16,384]{1,0:T(8,128)(2,1)S(1)}, u32[]{:S(2)}, u32[]{:S(2)}) %collective-permute-start.11) | collective-permute-done | bytes 12320 | tf_op jit(solution)/shard_map/ppermute | solution.py:625
  37.9 0.0 copy-done.4
  37.9 0.5 gate_up.1
  38.4 0.0 collective-permute-start.13
  38.4 1.3 %collective-permute-done.13.theirs = bf16[16,2176]{1,0:T(8,128)(2,1)S(1)} collective-permute-done((bf16[16,2176]{1,0:T(8,128)(2,1)S(1)}, bf16[16,2176]{1,0:T(8,128)(2,1)S(1)}, u32[]{:S(2)}, u32[]{:S(2)}) %collective-permute-start.13) | collective-permute-done | bytes 69664 | tf_op jit(solution)/shard_map/ppermute | solution.py:536
  39.7 0.1 core_sum.1.mine
  39.8 2.4 %collective-permute-start.14 = (bf16[16,2176]{1,0:T(8,128)(2,1)S(1)}, bf16[16,2176]{1,0:T(8,128)(2,1)S(1)}, u32[]{:S(2)}, u32[]{:S(2)}) collective-permute-start(bf16[16,2176]{1,0:T(8,128)(2,1)S(1)} %core_sum.1.mine), channel_id=1, source_target_pairs={{0,2},{1,3},{2,0},{3,1},{4,6},{5,7},{6,4},{7,5},{8,10},{9,11},{10,... | collective-permute-start | bytes 208904 | tf_op jit(solution)/shard_map/ppermute | solution.py:536
  42.1 2.5 %collective-permute-done.14.theirs = bf16[16,2176]{1,0:T(8,128)(2,1)S(1)} collective-permute-done((bf16[16,2176]{1,0:T(8,128)(2,1)S(1)}, bf16[16,2176]{1,0:T(8,128)(2,1)S(1)}, u32[]{:S(2)}, u32[]{:S(2)}) %collective-permute-start.14) | collective-permute-done | bytes 69664 | tf_op jit(solution)/shard_map/ppermute | solution.py:536
  44.6 0.4 down.1
  45.0 10.6 %all_to_all.5.parts = bf16[8,2,768]{2,1,0:T(2,128)(2,1)S(1)} all-to-all(bf16[8,2,768]{2,1,0:T(2,128)(2,1)S(1)} %down.1), channel_id=1, replica_groups=mesh['pool'=8,'mlp'=4] {'pool'}, dimensions={0} | all-to-all | bytes 49152 | tf_op jit(solution)/shard_map/all_to_all | solution.py:650
  55.6 0.6 %final.1 = bf16[2,768]{1,0:T(2,128)(2,1)} custom-call(f32[2,768]{1,0:T(2,128)S(1)} %get-tuple-element.21.own, bf16[8,2,768]{2,1,0:T(2,128)(2,1)S(1)} %all_to_all.5.parts), custom_call_target="tpu_custom_call" | custom-call | bytes 30720 | tf_op jit(solution)/shard_map/final/pallas_call | solution.py:217
  (13 shorter events, 0.0 us)
Async XLA Ops:
  0.0 15.4 %copy-start.1 = (bf16[5,256,768]{2,1,0:T(8,128)(2,1)S(1)}, bf16[5,256,768]{2,1,0:T(8,128)(2,1)}, u32[]{:S(2)}) copy-start(bf16[5,256,768]{2,1,0:T(8,128)(2,1)} %values.1) | copy-start | bytes 5898244
  0.0 15.4 %copy-start = (bf16[5,256,768]{2,1,0:T(8,128)(2,1)S(1)}, bf16[5,256,768]{2,1,0:T(8,128)(2,1)}, u32[]{:S(2)}) copy-start(bf16[5,256,768]{2,1,0:T(8,128)(2,1)} %keys.1) | copy-start | bytes 5898244
  1.8 4.9 %collective-permute-start = (bf16[2,1664]{1,0:T(2,128)(2,1)}, bf16[2,1664]{1,0:T(2,128)(2,1)S(1)}, u32[]{:S(2)}, u32[]{:S(2)}) collective-permute-start(bf16[2,1664]{1,0:T(2,128)(2,1)} %get-tuple-element.14.packed), channel_id=1, source_target_pairs={{0,4},{4,0},{8,12},{12,8},{16,20},{20,16},{24,28},{28,24},{1,5},{5... | collective-permute-start | bytes 19976 | tf_op jit(solution)/shard_map/ppermute | solution.py:536
  4.8 0.7 %copy-start.6 = (f32[8,896]{1,0:T(8,128)S(1)}, f32[8,896]{1,0:T(8,128)}, u32[]{:S(2)}) copy-start(f32[8,896]{1,0:T(8,128)} %get-tuple-element.15.own) | copy-start | bytes 86020
  5.6 0.7 %copy-start.7 = (bf16[2,1664]{1,0:T(2,128)(2,1)S(1)}, bf16[2,1664]{1,0:T(2,128)(2,1)}, u32[]{:S(2)}) copy-start(bf16[2,1664]{1,0:T(2,128)(2,1)} %get-tuple-element.14.packed) | copy-start | bytes 19972
  6.7 5.8 %collective-permute-start.3 = (bf16[2,2,1664]{2,1,0:T(2,128)(2,1)S(1)}, bf16[2,2,1664]{2,1,0:T(2,128)(2,1)S(1)}, u32[]{:S(2)}, u32[]{:S(2)}) collective-permute-start(bf16[2,2,1664]{2,1,0:T(2,128)(2,1)S(1)} %merge.2.a0), channel_id=1, source_target_pairs={{0,24},{4,28},{8,16},{12,20},{16,8},{20,12},{24,0},{28,4},{1,25},{... | collective-permute-start | bytes 39944 | tf_op jit(solution)/shard_map/ppermute | solution.py:536
  10.8 4.6 %collective-permute-start.2 = (bf16[2,2,1664]{2,1,0:T(2,128)(2,1)S(1)}, bf16[2,2,1664]{2,1,0:T(2,128)(2,1)S(1)}, u32[]{:S(2)}, u32[]{:S(2)}) collective-permute-start(bf16[2,2,1664]{2,1,0:T(2,128)(2,1)S(1)} %merge.2.a0), channel_id=1, source_target_pairs={{0,16},{4,20},{8,24},{12,28},{16,0},{20,4},{24,8},{28,12},{1,17},{... | collective-permute-start | bytes 39944 | tf_op jit(solution)/shard_map/ppermute | solution.py:536
  10.8 4.6 %collective-permute-start.1 = (bf16[2,2,1664]{2,1,0:T(2,128)(2,1)S(1)}, bf16[2,2,1664]{2,1,0:T(2,128)(2,1)S(1)}, u32[]{:S(2)}, u32[]{:S(2)}) collective-permute-start(bf16[2,2,1664]{2,1,0:T(2,128)(2,1)S(1)} %merge.2.a0), channel_id=1, source_target_pairs={{0,8},{4,12},{8,0},{12,4},{16,24},{20,28},{24,16},{28,20},{1,9},{5... | collective-permute-start | bytes 39944 | tf_op jit(solution)/shard_map/ppermute | solution.py:536
  15.4 11.4 %copy-start.5 = (bf16[768,384]{1,0:T(8,128)(2,1)S(1)}, bf16[768,384]{1,0:T(8,128)(2,1)}, u32[]{:S(2)}) copy-start(bf16[768,384]{1,0:T(8,128)(2,1)} %weight.2) | copy-start | bytes 1769476
  15.4 19.9 %copy-start.8 = (bf16[768]{0:T(1024)(128)(2,1)S(1)}, bf16[768]{0:T(1024)(128)(2,1)}, u32[]{:S(2)}) copy-start(bf16[768]{0:T(1024)(128)(2,1)} %param.22) | copy-start | bytes 4612
  15.4 22.5 %copy-start.3 = (bf16[768,1024]{1,0:T(8,128)(2,1)S(1)}, bf16[768,1024]{1,0:T(8,128)(2,1)}, u32[]{:S(2)}) copy-start(bf16[768,1024]{1,0:T(8,128)(2,1)} %gate.1) | copy-start | bytes 4718596
  15.4 22.4 %copy-start.4 = (bf16[768,1024]{1,0:T(8,128)(2,1)S(1)}, bf16[768,1024]{1,0:T(8,128)(2,1)}, u32[]{:S(2)}) copy-start(bf16[768,1024]{1,0:T(8,128)(2,1)} %up.1) | copy-start | bytes 4718596
  16.6 3.8 %collective-permute-start.4 = (bf16[8,768]{1,0:T(8,128)(2,1)S(1)}, bf16[8,768]{1,0:T(8,128)(2,1)S(1)}, u32[]{:S(2)}, u32[]{:S(2)}) collective-permute-start(bf16[8,768]{1,0:T(8,128)(2,1)S(1)} %get-tuple-element.18.mine), channel_id=1, source_target_pairs={{0,4},{4,0},{8,12},{12,8},{16,20},{20,16},{24,28},{28,24},{1,5},{5... | collective-permute-start | bytes 36872 | tf_op jit(solution)/shard_map/ppermute | solution.py:536
  20.4 5.6 %collective-permute-start.7 = (bf16[2,8,768]{2,1,0:T(8,128)(2,1)S(1)}, bf16[2,8,768]{2,1,0:T(8,128)(2,1)S(1)}, u32[]{:S(2)}, u32[]{:S(2)}) collective-permute-start(bf16[2,8,768]{2,1,0:T(8,128)(2,1)S(1)} %merge.3.b0), channel_id=1, source_target_pairs={{0,24},{4,28},{8,16},{12,20},{16,8},{20,12},{24,0},{28,4},{1,25},{... | collective-permute-start | bytes 73736 | tf_op jit(solution)/shard_map/ppermute | solution.py:536
  21.8 4.7 %collective-permute-start.6 = (bf16[2,8,768]{2,1,0:T(8,128)(2,1)S(1)}, bf16[2,8,768]{2,1,0:T(8,128)(2,1)S(1)}, u32[]{:S(2)}, u32[]{:S(2)}) collective-permute-start(bf16[2,8,768]{2,1,0:T(8,128)(2,1)S(1)} %merge.3.b0), channel_id=1, source_target_pairs={{0,16},{4,20},{8,24},{12,28},{16,0},{20,4},{24,8},{28,12},{1,17},{... | collective-permute-start | bytes 73736 | tf_op jit(solution)/shard_map/ppermute | solution.py:536
  22.4 4.4 %collective-permute-start.5 = (bf16[2,8,768]{2,1,0:T(8,128)(2,1)S(1)}, bf16[2,8,768]{2,1,0:T(8,128)(2,1)S(1)}, u32[]{:S(2)}, u32[]{:S(2)}) collective-permute-start(bf16[2,8,768]{2,1,0:T(8,128)(2,1)S(1)} %merge.3.b0), channel_id=1, source_target_pairs={{0,8},{4,12},{8,0},{12,4},{16,24},{20,28},{24,16},{28,20},{1,9},{5... | collective-permute-start | bytes 73736 | tf_op jit(solution)/shard_map/ppermute | solution.py:536
  27.5 3.2 %collective-permute-start.10 = (bf16[16,384]{1,0:T(8,128)(2,1)S(1)}, bf16[16,384]{1,0:T(8,128)(2,1)S(1)}, u32[]{:S(2)}, u32[]{:S(2)}) collective-permute-start(bf16[16,384]{1,0:T(8,128)(2,1)S(1)} %combine.1.p0), channel_id=1, source_target_pairs={{0,3},{1,2},{2,1},{3,0},{4,7},{5,6},{6,5},{7,4},{8,11},{9,10},{10,... | collective-permute-start | bytes 36872 | tf_op jit(solution)/shard_map/ppermute | solution.py:536
  27.6 3.8 %collective-permute-start.9 = (bf16[16,384]{1,0:T(8,128)(2,1)S(1)}, bf16[16,384]{1,0:T(8,128)(2,1)S(1)}, u32[]{:S(2)}, u32[]{:S(2)}) collective-permute-start(bf16[16,384]{1,0:T(8,128)(2,1)S(1)} %combine.1.p0), channel_id=1, source_target_pairs={{0,2},{1,3},{2,0},{3,1},{4,6},{5,7},{6,4},{7,5},{8,10},{9,11},{10,... | collective-permute-start | bytes 36872 | tf_op jit(solution)/shard_map/ppermute | solution.py:536
  29.1 2.2 %collective-permute-start.8 = (bf16[16,384]{1,0:T(8,128)(2,1)S(1)}, bf16[16,384]{1,0:T(8,128)(2,1)S(1)}, u32[]{:S(2)}, u32[]{:S(2)}) collective-permute-start(bf16[16,384]{1,0:T(8,128)(2,1)S(1)} %combine.1.p0), channel_id=1, source_target_pairs={{0,1},{1,0},{2,3},{3,2},{4,5},{5,4},{6,7},{7,6},{8,9},{9,8},{10,11... | collective-permute-start | bytes 36872 | tf_op jit(solution)/shard_map/ppermute | solution.py:536
  31.4 4.8 %collective-permute-start.12 = (bf16[16,384]{1,0:T(8,128)(2,1)S(1)}, bf16[16,384]{1,0:T(8,128)(2,1)S(1)}, u32[]{:S(2)}, u32[]{:S(2)}) collective-permute-start(bf16[16,384]{1,0:T(8,128)(2,1)S(1)} %head_sum.1), channel_id=1, source_target_pairs={{0,28},{4,24},{1,20},{5,16},{2,12},{6,8},{3,4},{7,0},{9,29},{13,25... | collective-permute-start | bytes 36872 | tf_op jit(solution)/shard_map/ppermute | solution.py:625
  34.8 3.1 %collective-permute-start.11 = (bf16[16,384]{1,0:T(8,128)(2,1)S(1)}, bf16[16,384]{1,0:T(8,128)(2,1)S(1)}, u32[]{:S(2)}, u32[]{:S(2)}) collective-permute-start(bf16[16,384]{1,0:T(8,128)(2,1)S(1)} %head_sum.1), channel_id=1, source_target_pairs={{0,24},{4,28},{1,16},{5,20},{2,8},{6,12},{3,0},{7,4},{9,25},{13,29... | collective-permute-start | bytes 36872 | tf_op jit(solution)/shard_map/ppermute | solution.py:625
  37.9 6.7 %copy-start.2 = (bf16[1024,768]{1,0:T(8,128)(2,1)S(1)}, bf16[1024,768]{1,0:T(8,128)(2,1)}, u32[]{:S(2)}) copy-start(bf16[1024,768]{1,0:T(8,128)(2,1)} %weight.3) | copy-start | bytes 4718596
  38.4 1.3 %collective-permute-start.13 = (bf16[16,2176]{1,0:T(8,128)(2,1)S(1)}, bf16[16,2176]{1,0:T(8,128)(2,1)S(1)}, u32[]{:S(2)}, u32[]{:S(2)}) collective-permute-start(bf16[16,2176]{1,0:T(8,128)(2,1)S(1)} %get-tuple-element.22.mine), channel_id=1, source_target_pairs={{0,1},{1,0},{2,3},{3,2},{4,5},{5,4},{6,7},{7,6},{8,9},{9,8},{10,11... | collective-permute-start | bytes 208904 | tf_op jit(solution)/shard_map/ppermute | solution.py:536
  39.8 4.8 %collective-permute-start.14 = (bf16[16,2176]{1,0:T(8,128)(2,1)S(1)}, bf16[16,2176]{1,0:T(8,128)(2,1)S(1)}, u32[]{:S(2)}, u32[]{:S(2)}) collective-permute-start(bf16[16,2176]{1,0:T(8,128)(2,1)S(1)} %core_sum.1.mine), channel_id=1, source_target_pairs={{0,2},{1,3},{2,0},{3,1},{4,6},{5,7},{6,4},{7,5},{8,10},{9,11},{10,... | collective-permute-start | bytes 208904 | tf_op jit(solution)/shard_map/ppermute | solution.py:536

commit v8 on v7

--- a/solution.py
+++ b/solution.py
@@ -520,8 +520,9 @@
     hidden = (gate / (1.0 + jnp.exp(-gate)) * up).astype(BF16)
     scr[...] = jnp.dot(hidden, weight[...], preferred_element_type=F32)
     rows = parts.shape[1]
-    for p in range(parts.shape[0]):
-        parts[p] = scr[p * rows : (p + 1) * rows, :].astype(BF16)
+    pool = parts.shape[0]
+    for p in range(pool):
+        parts[pool - 1 - p] = scr[p * rows : (p + 1) * rows, :].astype(BF16)
 
 
 def final_kernel(own, parts, out):
@@ -643,11 +644,12 @@
         [core_sums, flip(core_sums, "mlp", 2), down_weight],
         [pltpu.VMEM((requests, width), F32)],
     )
+    backwards = list(range(pool))[::-1]
     (out,) = call(
         final_kernel,
         "final",
         [((rows, width), BF16)],
-        [own_residual, lax.all_to_all(down, "pool", 0, 0)],
+        [own_residual, lax.all_to_all(down, "pool", 0, 0, axis_index_groups=[backwards])],
     )
     return out
 

time: 56.4 us -> 54.2 us (0.961)
  blocking collectives: 10.6 us -> 8.36 us
    all_to_all x1, blocking collectives: 10.6 us -> 8.36 us  [per_device_small(): lax.all_to_all(down, 'pool', 0, 0, axis_index_groups=[backwards])]
where the time goes in v8:
time: 54.2 us; the launch traced here: 54 us
  starting transfers between devices  21.9 us (40%)
  waiting for transfers between devices  16.9 us (31%)
  blocking collectives  8.36 us (15%)
  Pallas kernels  5.3 us (10%)
  local copies, waits for them, and re-layouts  1.48 us (3%)
    ppermute x13, starting transfers between devices, flip(): lax.ppermute(values, axis, [(index, index ^ step) for index in range(size)])  17.9 us
    ppermute x13, waiting for transfers between devices, flip(): lax.ppermute(values, axis, [(index, index ^ step) for index in range(size)])  14.3 us
    all_to_all x1, blocking collectives, per_device_small(): lax.all_to_all(down, 'pool', 0, 0, axis_index_groups=[backwards])  8.36 us
    pallas_call x11, Pallas kernels, call(): pl.pallas_call(kernel, out_shape=[jax.ShapeDtypeStruct(shape, dtype) for...  5.3 us
    ppermute x2, starting transfers between devices, per_device_small(): pieces.append(lax.ppermute(head_sum, ('pool', 'mlp'), route))  3.95 us
    ppermute x2, waiting for transfers between devices, per_device_small(): pieces.append(lax.ppermute(head_sum, ('pool', 'mlp'), route))  2.56 us
    unnamed x18, local copies, waits for them, and re-layouts  1.48 us
  transfers between devices with their start and end apart: 15, of which 13 were waited for; matrix products, arithmetic and copies ran while one was open for 0% of the time, Pallas kernels for 0%

profile of v8, /device:TPU:0, one launch (start us, length us, event | category | flops | bytes accessed | tf_op | source)
XLA Modules:
  0.0 54.0 jit_solution(14267980334279056209)
XLA Ops:
  0.0 1.8 %rotary.1 = (bf16[2,1664]{1,0:T(2,128)(2,1)}, f32[8,896]{1,0:T(8,128)}) custom-call(s32[2,8]{1,0:T(2,128)} %refs_0_.1, s32[2]{0:T(128)} %refs_1_.1, bf16[2,768]{1,0:T(2,128)(2,1)} %refs_2_.1, bf16[2,768]{1,0:T(2,128)(2,1)} %refs_3_.1, bf16[2,768]{1,0:T(2,128)(2,1)} %refs_4_.1, bf16[2,768]{1,0:T(2,128)(2,1)} %refs_5_.1, bf16[5,256,768]{2,1,0:T(8,128)(2,1)} %keys.1, ...), custom_call_target="tpu_custom_call" | custom-call | bytes 3944520 | tf_op jit(solution)/shard_map/rotary/pallas_call | solution.py:217
  1.8 3.0 %collective-permute-start = (bf16[2,1664]{1,0:T(2,128)(2,1)}, bf16[2,1664]{1,0:T(2,128)(2,1)S(1)}, u32[]{:S(2)}, u32[]{:S(2)}) collective-permute-start(bf16[2,1664]{1,0:T(2,128)(2,1)} %get-tuple-element.14.packed), channel_id=1, source_target_pairs={{0,4},{4,0},{8,12},{12,8},{16,20},{20,16},{24,28},{28,24},{1,5},{5... | collective-permute-start | bytes 19976 | tf_op jit(solution)/shard_map/ppermute | solution.py:537
  4.8 0.7 %copy-done.6 = f32[8,896]{1,0:T(8,128)S(1)} copy-done((f32[8,896]{1,0:T(8,128)S(1)}, f32[8,896]{1,0:T(8,128)}, u32[]{:S(2)}) %copy-start.6) | copy-done | bytes 28696
  5.6 0.7 %copy-done.7 = bf16[2,1664]{1,0:T(2,128)(2,1)S(1)} copy-done((bf16[2,1664]{1,0:T(2,128)(2,1)S(1)}, bf16[2,1664]{1,0:T(2,128)(2,1)}, u32[]{:S(2)}) %copy-start.7) | copy-done | bytes 6680
  6.3 0.4 collective-permute-done.theirs
  6.7 4.1 %collective-permute-start.3 = (bf16[2,2,1664]{2,1,0:T(2,128)(2,1)S(1)}, bf16[2,2,1664]{2,1,0:T(2,128)(2,1)S(1)}, u32[]{:S(2)}, u32[]{:S(2)}) collective-permute-start(bf16[2,2,1664]{2,1,0:T(2,128)(2,1)S(1)} %merge.2.a0), channel_id=1, source_target_pairs={{0,24},{4,28},{8,16},{12,20},{16,8},{20,12},{24,0},{28,4},{1,25},{... | collective-permute-start | bytes 39944 | tf_op jit(solution)/shard_map/ppermute | solution.py:537
  10.8 0.0 collective-permute-start.2
  10.8 0.6 %collective-permute-start.1 = (bf16[2,2,1664]{2,1,0:T(2,128)(2,1)S(1)}, bf16[2,2,1664]{2,1,0:T(2,128)(2,1)S(1)}, u32[]{:S(2)}, u32[]{:S(2)}) collective-permute-start(bf16[2,2,1664]{2,1,0:T(2,128)(2,1)S(1)} %merge.2.a0), channel_id=1, source_target_pairs={{0,8},{4,12},{8,0},{12,4},{16,24},{20,28},{24,16},{28,20},{1,9},{5... | collective-permute-start | bytes 39944 | tf_op jit(solution)/shard_map/ppermute | solution.py:537
  11.3 1.1 %collective-permute-done.3.a3 = bf16[2,2,1664]{2,1,0:T(2,128)(2,1)S(1)} collective-permute-done((bf16[2,2,1664]{2,1,0:T(2,128)(2,1)S(1)}, bf16[2,2,1664]{2,1,0:T(2,128)(2,1)S(1)}, u32[]{:S(2)}, u32[]{:S(2)}) %collective-permute-start.3) | collective-permute-done | bytes 13344 | tf_op jit(solution)/shard_map/ppermute | solution.py:537
  12.5 2.9 %collective-permute-done.2.a2 = bf16[2,2,1664]{2,1,0:T(2,128)(2,1)S(1)} collective-permute-done((bf16[2,2,1664]{2,1,0:T(2,128)(2,1)S(1)}, bf16[2,2,1664]{2,1,0:T(2,128)(2,1)S(1)}, u32[]{:S(2)}, u32[]{:S(2)}) %collective-permute-start.2) | collective-permute-done | bytes 13344 | tf_op jit(solution)/shard_map/ppermute | solution.py:537
  15.4 0.0 collective-permute-done.1.a1
  15.4 0.0 copy-done.1
  15.4 0.0 copy-done
  15.4 0.0 copy-start.5
  15.4 0.0 copy-start.8
  15.4 0.0 copy-start.3
  15.4 0.0 copy-start.4
  15.4 1.1 %attend.1 = (bf16[8,768]{1,0:T(8,128)(2,1)S(1)}, f32[16,768]{1,0:T(8,128)S(1)}, f32[16,128]{1,0:T(8,128)S(1)}) custom-call(bf16[2,2,1664]{2,1,0:T(2,128)(2,1)S(1)} %merge.2.a0, bf16[2,2,1664]{2,1,0:T(2,128)(2,1)S(1)} %collective-permute-done.1.a1, bf16[2,2,1664]{2,1,0:T(2,128)(2,1)S(1)} %collective-permute-done.2.a2, ...), custom_call_target="tpu_custom_call" | custom-call | bytes 4014080 | tf_op jit(solution)/shard_map/attend/pallas_call | solution.py:217
  16.6 1.6 %collective-permute-start.4 = (bf16[8,768]{1,0:T(8,128)(2,1)S(1)}, bf16[8,768]{1,0:T(8,128)(2,1)S(1)}, u32[]{:S(2)}, u32[]{:S(2)}) collective-permute-start(bf16[8,768]{1,0:T(8,128)(2,1)S(1)} %get-tuple-element.18.mine), channel_id=1, source_target_pairs={{0,4},{4,0},{8,12},{12,8},{16,20},{20,16},{24,28},{28,24},{1,5},{5... | collective-permute-start | bytes 36872 | tf_op jit(solution)/shard_map/ppermute | solution.py:537
  18.2 2.2 %collective-permute-done.4.theirs = bf16[8,768]{1,0:T(8,128)(2,1)S(1)} collective-permute-done((bf16[8,768]{1,0:T(8,128)(2,1)S(1)}, bf16[8,768]{1,0:T(8,128)(2,1)S(1)}, u32[]{:S(2)}, u32[]{:S(2)}) %collective-permute-start.4) | collective-permute-done | bytes 12320 | tf_op jit(solution)/shard_map/ppermute | solution.py:537
  20.4 1.4 %collective-permute-start.7 = (bf16[2,8,768]{2,1,0:T(8,128)(2,1)S(1)}, bf16[2,8,768]{2,1,0:T(8,128)(2,1)S(1)}, u32[]{:S(2)}, u32[]{:S(2)}) collective-permute-start(bf16[2,8,768]{2,1,0:T(8,128)(2,1)S(1)} %merge.3.b0), channel_id=1, source_target_pairs={{0,24},{4,28},{8,16},{12,20},{16,8},{20,12},{24,0},{28,4},{1,25},{... | collective-permute-start | bytes 73736 | tf_op jit(solution)/shard_map/ppermute | solution.py:537
  21.8 0.6 %collective-permute-start.6 = (bf16[2,8,768]{2,1,0:T(8,128)(2,1)S(1)}, bf16[2,8,768]{2,1,0:T(8,128)(2,1)S(1)}, u32[]{:S(2)}, u32[]{:S(2)}) collective-permute-start(bf16[2,8,768]{2,1,0:T(8,128)(2,1)S(1)} %merge.3.b0), channel_id=1, source_target_pairs={{0,16},{4,20},{8,24},{12,28},{16,0},{20,4},{24,8},{28,12},{1,17},{... | collective-permute-start | bytes 73736 | tf_op jit(solution)/shard_map/ppermute | solution.py:537
  22.4 2.3 %collective-permute-start.5 = (bf16[2,8,768]{2,1,0:T(8,128)(2,1)S(1)}, bf16[2,8,768]{2,1,0:T(8,128)(2,1)S(1)}, u32[]{:S(2)}, u32[]{:S(2)}) collective-permute-start(bf16[2,8,768]{2,1,0:T(8,128)(2,1)S(1)} %merge.3.b0), channel_id=1, source_target_pairs={{0,8},{4,12},{8,0},{12,4},{16,24},{20,28},{24,16},{28,20},{1,9},{5... | collective-permute-start | bytes 73736 | tf_op jit(solution)/shard_map/ppermute | solution.py:537
  24.7 1.2 %collective-permute-done.7.b3 = bf16[2,8,768]{2,1,0:T(8,128)(2,1)S(1)} collective-permute-done((bf16[2,8,768]{2,1,0:T(8,128)(2,1)S(1)}, bf16[2,8,768]{2,1,0:T(8,128)(2,1)S(1)}, u32[]{:S(2)}, u32[]{:S(2)}) %collective-permute-start.7) | collective-permute-done | bytes 24608 | tf_op jit(solution)/shard_map/ppermute | solution.py:537
  26.0 0.6 %collective-permute-done.6.b2 = bf16[2,8,768]{2,1,0:T(8,128)(2,1)S(1)} collective-permute-done((bf16[2,8,768]{2,1,0:T(8,128)(2,1)S(1)}, bf16[2,8,768]{2,1,0:T(8,128)(2,1)S(1)}, u32[]{:S(2)}, u32[]{:S(2)}) %collective-permute-start.6) | collective-permute-done | bytes 24608 | tf_op jit(solution)/shard_map/ppermute | solution.py:537
  26.5 0.2 collective-permute-done.5.b1
  26.8 0.7 %combine.1.p0 = bf16[16,384]{1,0:T(8,128)(2,1)S(1)} custom-call(bf16[2,8,768]{2,1,0:T(8,128)(2,1)S(1)} %merge.3.b0, bf16[2,8,768]{2,1,0:T(8,128)(2,1)S(1)} %collective-permute-done.5.b1, bf16[2,8,768]{2,1,0:T(8,128)(2,1)S(1)} %collective-permute-done.6.b2, bf16[2,8,768]{2,1,0:T(8,128)(2,1)S(1)} %collective-permute-done.7.b3, ...), custom_call_target="tpu_custom_call" | custom-call | bytes 696320 | tf_op jit(solution)/shard_map/combine/pallas_call | solution.py:217
  27.5 0.1 collective-permute-start.10
  27.6 1.6 %collective-permute-start.9 = (bf16[16,384]{1,0:T(8,128)(2,1)S(1)}, bf16[16,384]{1,0:T(8,128)(2,1)S(1)}, u32[]{:S(2)}, u32[]{:S(2)}) collective-permute-start(bf16[16,384]{1,0:T(8,128)(2,1)S(1)} %combine.1.p0), channel_id=1, source_target_pairs={{0,2},{1,3},{2,0},{3,1},{4,6},{5,7},{6,4},{7,5},{8,10},{9,11},{10,... | collective-permute-start | bytes 36872 | tf_op jit(solution)/shard_map/ppermute | solution.py:537
  29.1 0.3 collective-permute-start.8
  29.4 1.3 %collective-permute-done.10.p3 = bf16[16,384]{1,0:T(8,128)(2,1)S(1)} collective-permute-done((bf16[16,384]{1,0:T(8,128)(2,1)S(1)}, bf16[16,384]{1,0:T(8,128)(2,1)S(1)}, u32[]{:S(2)}, u32[]{:S(2)}) %collective-permute-start.10) | collective-permute-done | bytes 12320 | tf_op jit(solution)/shard_map/ppermute | solution.py:537
  30.8 0.6 %collective-permute-done.9.p2 = bf16[16,384]{1,0:T(8,128)(2,1)S(1)} collective-permute-done((bf16[16,384]{1,0:T(8,128)(2,1)S(1)}, bf16[16,384]{1,0:T(8,128)(2,1)S(1)}, u32[]{:S(2)}, u32[]{:S(2)}) %collective-permute-start.9) | collective-permute-done | bytes 12320 | tf_op jit(solution)/shard_map/ppermute | solution.py:537
  31.3 0.0 collective-permute-done.8.p1
  31.4 3.4 %collective-permute-start.12 = (bf16[16,384]{1,0:T(8,128)(2,1)S(1)}, bf16[16,384]{1,0:T(8,128)(2,1)S(1)}, u32[]{:S(2)}, u32[]{:S(2)}) collective-permute-start(bf16[16,384]{1,0:T(8,128)(2,1)S(1)} %head_sum.1), channel_id=1, source_target_pairs={{0,28},{4,24},{1,20},{5,16},{2,12},{6,8},{3,4},{7,0},{9,29},{13,25... | collective-permute-start | bytes 36872 | tf_op jit(solution)/shard_map/ppermute | solution.py:626
  34.8 0.6 %collective-permute-start.11 = (bf16[16,384]{1,0:T(8,128)(2,1)S(1)}, bf16[16,384]{1,0:T(8,128)(2,1)S(1)}, u32[]{:S(2)}, u32[]{:S(2)}) collective-permute-start(bf16[16,384]{1,0:T(8,128)(2,1)S(1)} %head_sum.1), channel_id=1, source_target_pairs={{0,24},{4,28},{1,16},{5,20},{2,8},{6,12},{3,0},{7,4},{9,25},{13,29... | collective-permute-start | bytes 36872 | tf_op jit(solution)/shard_map/ppermute | solution.py:626
  35.3 0.0 copy-done.8
  35.3 0.8 %collective-permute-done.12.flip = bf16[16,384]{1,0:T(8,128)(2,1)S(1)} collective-permute-done((bf16[16,384]{1,0:T(8,128)(2,1)S(1)}, bf16[16,384]{1,0:T(8,128)(2,1)S(1)}, u32[]{:S(2)}, u32[]{:S(2)}) %collective-permute-start.12) | collective-permute-done | bytes 12320 | tf_op jit(solution)/shard_map/ppermute | solution.py:626
  36.2 1.7 %collective-permute-done.11.same = bf16[16,384]{1,0:T(8,128)(2,1)S(1)} collective-permute-done((bf16[16,384]{1,0:T(8,128)(2,1)S(1)}, bf16[16,384]{1,0:T(8,128)(2,1)S(1)}, u32[]{:S(2)}, u32[]{:S(2)}) %collective-permute-start.11) | collective-permute-done | bytes 12320 | tf_op jit(solution)/shard_map/ppermute | solution.py:626
  37.9 0.5 gate_up.1
  38.4 0.0 collective-permute-start.13
  38.4 1.3 %collective-permute-done.13.theirs = bf16[16,2176]{1,0:T(8,128)(2,1)S(1)} collective-permute-done((bf16[16,2176]{1,0:T(8,128)(2,1)S(1)}, bf16[16,2176]{1,0:T(8,128)(2,1)S(1)}, u32[]{:S(2)}, u32[]{:S(2)}) %collective-permute-start.13) | collective-permute-done | bytes 69664 | tf_op jit(solution)/shard_map/ppermute | solution.py:537
  39.7 0.1 core_sum.1.mine
  39.8 2.4 %collective-permute-start.14 = (bf16[16,2176]{1,0:T(8,128)(2,1)S(1)}, bf16[16,2176]{1,0:T(8,128)(2,1)S(1)}, u32[]{:S(2)}, u32[]{:S(2)}) collective-permute-start(bf16[16,2176]{1,0:T(8,128)(2,1)S(1)} %core_sum.1.mine), channel_id=1, source_target_pairs={{0,2},{1,3},{2,0},{3,1},{4,6},{5,7},{6,4},{7,5},{8,10},{9,11},{10,... | collective-permute-start | bytes 208904 | tf_op jit(solution)/shard_map/ppermute | solution.py:537
  42.1 2.5 %collective-permute-done.14.theirs = bf16[16,2176]{1,0:T(8,128)(2,1)S(1)} collective-permute-done((bf16[16,2176]{1,0:T(8,128)(2,1)S(1)}, bf16[16,2176]{1,0:T(8,128)(2,1)S(1)}, u32[]{:S(2)}, u32[]{:S(2)}) %collective-permute-start.14) | collective-permute-done | bytes 69664 | tf_op jit(solution)/shard_map/ppermute | solution.py:537
  44.6 0.0 copy-done.2
  44.6 0.4 down.1
  45.0 8.4 %all_to_all.5.parts = bf16[8,2,768]{2,1,0:T(2,128)(2,1)S(1)} all-to-all(bf16[8,2,768]{2,1,0:T(2,128)(2,1)S(1)} %down.1), channel_id=1, replica_groups={{28,24,20,16,12,8,4,0},{29,25,21,17,13,9,5,1},{30,26,22,18,14,10,6,2},{..., dimensions={0} | all-to-all | bytes 49152 | tf_op jit(solution)/shard_map/all_to_all | solution.py:652
  53.4 0.6 %final.1 = bf16[2,768]{1,0:T(2,128)(2,1)} custom-call(f32[2,768]{1,0:T(2,128)S(1)} %get-tuple-element.21.own, bf16[8,2,768]{2,1,0:T(2,128)(2,1)S(1)} %all_to_all.5.parts), custom_call_target="tpu_custom_call" | custom-call | bytes 30720 | tf_op jit(solution)/shard_map/final/pallas_call | solution.py:217
  (13 shorter events, 0.0 us)
Async XLA Ops:
  0.0 15.4 %copy-start.1 = (bf16[5,256,768]{2,1,0:T(8,128)(2,1)S(1)}, bf16[5,256,768]{2,1,0:T(8,128)(2,1)}, u32[]{:S(2)}) copy-start(bf16[5,256,768]{2,1,0:T(8,128)(2,1)} %values.1) | copy-start | bytes 5898244
  0.0 15.4 %copy-start = (bf16[5,256,768]{2,1,0:T(8,128)(2,1)S(1)}, bf16[5,256,768]{2,1,0:T(8,128)(2,1)}, u32[]{:S(2)}) copy-start(bf16[5,256,768]{2,1,0:T(8,128)(2,1)} %keys.1) | copy-start | bytes 5898244
  1.8 4.9 %collective-permute-start = (bf16[2,1664]{1,0:T(2,128)(2,1)}, bf16[2,1664]{1,0:T(2,128)(2,1)S(1)}, u32[]{:S(2)}, u32[]{:S(2)}) collective-permute-start(bf16[2,1664]{1,0:T(2,128)(2,1)} %get-tuple-element.14.packed), channel_id=1, source_target_pairs={{0,4},{4,0},{8,12},{12,8},{16,20},{20,16},{24,28},{28,24},{1,5},{5... | collective-permute-start | bytes 19976 | tf_op jit(solution)/shard_map/ppermute | solution.py:537
  4.8 0.7 %copy-start.6 = (f32[8,896]{1,0:T(8,128)S(1)}, f32[8,896]{1,0:T(8,128)}, u32[]{:S(2)}) copy-start(f32[8,896]{1,0:T(8,128)} %get-tuple-element.15.own) | copy-start | bytes 86020
  5.6 0.7 %copy-start.7 = (bf16[2,1664]{1,0:T(2,128)(2,1)S(1)}, bf16[2,1664]{1,0:T(2,128)(2,1)}, u32[]{:S(2)}) copy-start(bf16[2,1664]{1,0:T(2,128)(2,1)} %get-tuple-element.14.packed) | copy-start | bytes 19972
  6.7 5.8 %collective-permute-start.3 = (bf16[2,2,1664]{2,1,0:T(2,128)(2,1)S(1)}, bf16[2,2,1664]{2,1,0:T(2,128)(2,1)S(1)}, u32[]{:S(2)}, u32[]{:S(2)}) collective-permute-start(bf16[2,2,1664]{2,1,0:T(2,128)(2,1)S(1)} %merge.2.a0), channel_id=1, source_target_pairs={{0,24},{4,28},{8,16},{12,20},{16,8},{20,12},{24,0},{28,4},{1,25},{... | collective-permute-start | bytes 39944 | tf_op jit(solution)/shard_map/ppermute | solution.py:537
  10.8 4.6 %collective-permute-start.2 = (bf16[2,2,1664]{2,1,0:T(2,128)(2,1)S(1)}, bf16[2,2,1664]{2,1,0:T(2,128)(2,1)S(1)}, u32[]{:S(2)}, u32[]{:S(2)}) collective-permute-start(bf16[2,2,1664]{2,1,0:T(2,128)(2,1)S(1)} %merge.2.a0), channel_id=1, source_target_pairs={{0,16},{4,20},{8,24},{12,28},{16,0},{20,4},{24,8},{28,12},{1,17},{... | collective-permute-start | bytes 39944 | tf_op jit(solution)/shard_map/ppermute | solution.py:537
  10.8 4.6 %collective-permute-start.1 = (bf16[2,2,1664]{2,1,0:T(2,128)(2,1)S(1)}, bf16[2,2,1664]{2,1,0:T(2,128)(2,1)S(1)}, u32[]{:S(2)}, u32[]{:S(2)}) collective-permute-start(bf16[2,2,1664]{2,1,0:T(2,128)(2,1)S(1)} %merge.2.a0), channel_id=1, source_target_pairs={{0,8},{4,12},{8,0},{12,4},{16,24},{20,28},{24,16},{28,20},{1,9},{5... | collective-permute-start | bytes 39944 | tf_op jit(solution)/shard_map/ppermute | solution.py:537
  15.4 11.4 %copy-start.5 = (bf16[768,384]{1,0:T(8,128)(2,1)S(1)}, bf16[768,384]{1,0:T(8,128)(2,1)}, u32[]{:S(2)}) copy-start(bf16[768,384]{1,0:T(8,128)(2,1)} %weight.2) | copy-start | bytes 1769476
  15.4 19.9 %copy-start.8 = (bf16[768]{0:T(1024)(128)(2,1)S(1)}, bf16[768]{0:T(1024)(128)(2,1)}, u32[]{:S(2)}) copy-start(bf16[768]{0:T(1024)(128)(2,1)} %param.22) | copy-start | bytes 4612
  15.4 22.5 %copy-start.3 = (bf16[768,1024]{1,0:T(8,128)(2,1)S(1)}, bf16[768,1024]{1,0:T(8,128)(2,1)}, u32[]{:S(2)}) copy-start(bf16[768,1024]{1,0:T(8,128)(2,1)} %gate.1) | copy-start | bytes 4718596
  15.4 22.4 %copy-start.4 = (bf16[768,1024]{1,0:T(8,128)(2,1)S(1)}, bf16[768,1024]{1,0:T(8,128)(2,1)}, u32[]{:S(2)}) copy-start(bf16[768,1024]{1,0:T(8,128)(2,1)} %up.1) | copy-start | bytes 4718596
  16.6 3.8 %collective-permute-start.4 = (bf16[8,768]{1,0:T(8,128)(2,1)S(1)}, bf16[8,768]{1,0:T(8,128)(2,1)S(1)}, u32[]{:S(2)}, u32[]{:S(2)}) collective-permute-start(bf16[8,768]{1,0:T(8,128)(2,1)S(1)} %get-tuple-element.18.mine), channel_id=1, source_target_pairs={{0,4},{4,0},{8,12},{12,8},{16,20},{20,16},{24,28},{28,24},{1,5},{5... | collective-permute-start | bytes 36872 | tf_op jit(solution)/shard_map/ppermute | solution.py:537
  20.4 5.6 %collective-permute-start.7 = (bf16[2,8,768]{2,1,0:T(8,128)(2,1)S(1)}, bf16[2,8,768]{2,1,0:T(8,128)(2,1)S(1)}, u32[]{:S(2)}, u32[]{:S(2)}) collective-permute-start(bf16[2,8,768]{2,1,0:T(8,128)(2,1)S(1)} %merge.3.b0), channel_id=1, source_target_pairs={{0,24},{4,28},{8,16},{12,20},{16,8},{20,12},{24,0},{28,4},{1,25},{... | collective-permute-start | bytes 73736 | tf_op jit(solution)/shard_map/ppermute | solution.py:537
  21.8 4.7 %collective-permute-start.6 = (bf16[2,8,768]{2,1,0:T(8,128)(2,1)S(1)}, bf16[2,8,768]{2,1,0:T(8,128)(2,1)S(1)}, u32[]{:S(2)}, u32[]{:S(2)}) collective-permute-start(bf16[2,8,768]{2,1,0:T(8,128)(2,1)S(1)} %merge.3.b0), channel_id=1, source_target_pairs={{0,16},{4,20},{8,24},{12,28},{16,0},{20,4},{24,8},{28,12},{1,17},{... | collective-permute-start | bytes 73736 | tf_op jit(solution)/shard_map/ppermute | solution.py:537
  22.4 4.4 %collective-permute-start.5 = (bf16[2,8,768]{2,1,0:T(8,128)(2,1)S(1)}, bf16[2,8,768]{2,1,0:T(8,128)(2,1)S(1)}, u32[]{:S(2)}, u32[]{:S(2)}) collective-permute-start(bf16[2,8,768]{2,1,0:T(8,128)(2,1)S(1)} %merge.3.b0), channel_id=1, source_target_pairs={{0,8},{4,12},{8,0},{12,4},{16,24},{20,28},{24,16},{28,20},{1,9},{5... | collective-permute-start | bytes 73736 | tf_op jit(solution)/shard_map/ppermute | solution.py:537
  27.5 3.2 %collective-permute-start.10 = (bf16[16,384]{1,0:T(8,128)(2,1)S(1)}, bf16[16,384]{1,0:T(8,128)(2,1)S(1)}, u32[]{:S(2)}, u32[]{:S(2)}) collective-permute-start(bf16[16,384]{1,0:T(8,128)(2,1)S(1)} %combine.1.p0), channel_id=1, source_target_pairs={{0,3},{1,2},{2,1},{3,0},{4,7},{5,6},{6,5},{7,4},{8,11},{9,10},{10,... | collective-permute-start | bytes 36872 | tf_op jit(solution)/shard_map/ppermute | solution.py:537
  27.6 3.8 %collective-permute-start.9 = (bf16[16,384]{1,0:T(8,128)(2,1)S(1)}, bf16[16,384]{1,0:T(8,128)(2,1)S(1)}, u32[]{:S(2)}, u32[]{:S(2)}) collective-permute-start(bf16[16,384]{1,0:T(8,128)(2,1)S(1)} %combine.1.p0), channel_id=1, source_target_pairs={{0,2},{1,3},{2,0},{3,1},{4,6},{5,7},{6,4},{7,5},{8,10},{9,11},{10,... | collective-permute-start | bytes 36872 | tf_op jit(solution)/shard_map/ppermute | solution.py:537
  29.1 2.2 %collective-permute-start.8 = (bf16[16,384]{1,0:T(8,128)(2,1)S(1)}, bf16[16,384]{1,0:T(8,128)(2,1)S(1)}, u32[]{:S(2)}, u32[]{:S(2)}) collective-permute-start(bf16[16,384]{1,0:T(8,128)(2,1)S(1)} %combine.1.p0), channel_id=1, source_target_pairs={{0,1},{1,0},{2,3},{3,2},{4,5},{5,4},{6,7},{7,6},{8,9},{9,8},{10,11... | collective-permute-start | bytes 36872 | tf_op jit(solution)/shard_map/ppermute | solution.py:537
  31.4 4.8 %collective-permute-start.12 = (bf16[16,384]{1,0:T(8,128)(2,1)S(1)}, bf16[16,384]{1,0:T(8,128)(2,1)S(1)}, u32[]{:S(2)}, u32[]{:S(2)}) collective-permute-start(bf16[16,384]{1,0:T(8,128)(2,1)S(1)} %head_sum.1), channel_id=1, source_target_pairs={{0,28},{4,24},{1,20},{5,16},{2,12},{6,8},{3,4},{7,0},{9,29},{13,25... | collective-permute-start | bytes 36872 | tf_op jit(solution)/shard_map/ppermute | solution.py:626
  34.8 3.1 %collective-permute-start.11 = (bf16[16,384]{1,0:T(8,128)(2,1)S(1)}, bf16[16,384]{1,0:T(8,128)(2,1)S(1)}, u32[]{:S(2)}, u32[]{:S(2)}) collective-permute-start(bf16[16,384]{1,0:T(8,128)(2,1)S(1)} %head_sum.1), channel_id=1, source_target_pairs={{0,24},{4,28},{1,16},{5,20},{2,8},{6,12},{3,0},{7,4},{9,25},{13,29... | collective-permute-start | bytes 36872 | tf_op jit(solution)/shard_map/ppermute | solution.py:626
  37.9 6.7 %copy-start.2 = (bf16[1024,768]{1,0:T(8,128)(2,1)S(1)}, bf16[1024,768]{1,0:T(8,128)(2,1)}, u32[]{:S(2)}) copy-start(bf16[1024,768]{1,0:T(8,128)(2,1)} %weight.3) | copy-start | bytes 4718596
  38.4 1.3 %collective-permute-start.13 = (bf16[16,2176]{1,0:T(8,128)(2,1)S(1)}, bf16[16,2176]{1,0:T(8,128)(2,1)S(1)}, u32[]{:S(2)}, u32[]{:S(2)}) collective-permute-start(bf16[16,2176]{1,0:T(8,128)(2,1)S(1)} %get-tuple-element.22.mine), channel_id=1, source_target_pairs={{0,1},{1,0},{2,3},{3,2},{4,5},{5,4},{6,7},{7,6},{8,9},{9,8},{10,11... | collective-permute-start | bytes 208904 | tf_op jit(solution)/shard_map/ppermute | solution.py:537
  39.8 4.8 %collective-permute-start.14 = (bf16[16,2176]{1,0:T(8,128)(2,1)S(1)}, bf16[16,2176]{1,0:T(8,128)(2,1)S(1)}, u32[]{:S(2)}, u32[]{:S(2)}) collective-permute-start(bf16[16,2176]{1,0:T(8,128)(2,1)S(1)} %core_sum.1.mine), channel_id=1, source_target_pairs={{0,2},{1,3},{2,0},{3,1},{4,6},{5,7},{6,4},{7,5},{8,10},{9,11},{10,... | collective-permute-start | bytes 208904 | tf_op jit(solution)/shard_map/ppermute | solution.py:537

commit v9 on v8

--- a/solution.py
+++ b/solution.py
@@ -475,11 +475,12 @@
     ).astype(BF16)
 
 
-def gate_up_kernel(same, flip, all_input, gain, gate, up, sums, own, scr):
+def gate_up_kernel(same, flip, all_input, gain, gate, up, send, keep, own, scr):
     me = lax.axis_index("pool")
+    core = lax.axis_index("mlp") % 2
     odd = me % 2 == 1
     part = same.shape[1]
-    ff = gate.shape[1]
+    half = gate.shape[1] // 2
     rows = own.shape[0]
     near, far = same[...].astype(F32), flip[...].astype(F32)
     scr[:, :part] = all_input[:, :part] + jnp.where(odd, far, near)
@@ -491,34 +492,48 @@
     own[...] = mine
     square = jnp.sum(residual * residual, 1, keepdims=True)
     portion = (residual * gain[...].astype(F32)).astype(BF16)
-    sums[:, :ff] = jnp.dot(portion, gate[...], preferred_element_type=F32).astype(BF16)
-    sums[:, ff : 2 * ff] = jnp.dot(portion, up[...], preferred_element_type=F32).astype(BF16)
-    lane = lanes((residual.shape[0], 128))
+    for at, weight in ((0, gate), (half, up)):
+        low_half = jnp.dot(portion, weight[:, :half], preferred_element_type=F32)
+        high_half = jnp.dot(portion, weight[:, half:], preferred_element_type=F32)
+        keep[:, at : at + half] = jnp.where(core == 0, low_half, high_half).astype(BF16)
+        send[:, at : at + half] = jnp.where(core == 0, high_half, low_half).astype(BF16)
+    tail = square_tail(square)
+    keep[:, 2 * half :] = tail
+    send[:, 2 * half :] = tail
+
+
+def square_tail(square):
+    lane = lanes((square.shape[0], 128))
     high = round_low(square)
-    tail = jnp.where(lane == 0, high, jnp.where(lane == 1, square - high, 0.0))
-    sums[:, 2 * ff :] = tail.astype(BF16)
+    return jnp.where(lane == 0, high, jnp.where(lane == 1, square - high, 0.0)).astype(BF16)
 
 
 def core_sum_kernel(mine, theirs, total):
-    ff2 = mine.shape[1] - 128
-    total[:, :ff2] = (mine[:, :ff2].astype(F32) + theirs[:, :ff2].astype(F32)).astype(BF16)
-    tail = mine[:, ff2:].astype(F32) + theirs[:, ff2:].astype(F32)
-    square = jnp.sum(tail, 1, keepdims=True)
-    lane = lanes(tail.shape)
-    high = round_low(square)
-    tail = jnp.where(lane == 0, high, jnp.where(lane == 1, square - high, 0.0))
-    total[:, ff2:] = tail.astype(BF16)
-
-
-def down_kernel(features, mine, theirs, weight, parts, scr):
-    ff = weight.shape[0]
-    tail = mine[:, 2 * ff :].astype(F32) + theirs[:, 2 * ff :].astype(F32)
+    ff = mine.shape[1] - 128
+    total[:, :ff] = (mine[:, :ff].astype(F32) + theirs[:, :ff].astype(F32)).astype(BF16)
+    tail = mine[:, ff:].astype(F32) + theirs[:, ff:].astype(F32)
+    total[:, ff:] = square_tail(jnp.sum(tail, 1, keepdims=True))
+
+
+def hidden_kernel(features, mine, theirs, hidden):
+    half = hidden.shape[1]
+    tail = mine[:, 2 * half :].astype(F32) + theirs[:, 2 * half :].astype(F32)
     square = jnp.sum(tail, 1, keepdims=True)
     factor = lax.rsqrt(square * (1.0 / features) + 1e-05)
-    gate = (mine[:, :ff].astype(F32) + theirs[:, :ff].astype(F32)) * factor
-    up = (mine[:, ff : 2 * ff].astype(F32) + theirs[:, ff : 2 * ff].astype(F32)) * factor
-    hidden = (gate / (1.0 + jnp.exp(-gate)) * up).astype(BF16)
-    scr[...] = jnp.dot(hidden, weight[...], preferred_element_type=F32)
+    gate = (mine[:, :half].astype(F32) + theirs[:, :half].astype(F32)) * factor
+    up = (mine[:, half : 2 * half].astype(F32) + theirs[:, half : 2 * half].astype(F32)) * factor
+    hidden[...] = (gate / (1.0 + jnp.exp(-gate)) * up).astype(BF16)
+
+
+def down_kernel(mine, theirs, weight, parts, scr):
+    half = weight.shape[0] // 2
+    first = lax.axis_index("mlp") % 2 == 0
+    mine, theirs = mine[...].astype(F32), theirs[...].astype(F32)
+    low_half = jnp.where(first, mine, theirs).astype(BF16)
+    high_half = jnp.where(first, theirs, mine).astype(BF16)
+    scr[...] = jnp.dot(low_half, weight[:half], preferred_element_type=F32) + jnp.dot(
+        high_half, weight[half:], preferred_element_type=F32
+    )
     rows = parts.shape[1]
     pool = parts.shape[0]
     for p in range(pool):
@@ -624,24 +639,30 @@
                     source = (m * 2 + y) * mlp + (m ^ step)
                     route.append((source, (z * 2 + (y ^ turn)) * mlp + m))
         pieces.append(lax.ppermute(head_sum, ("pool", "mlp"), route))
-    sums, own_residual = call(
+    send, keep, own_residual = call(
         gate_up_kernel,
         "gate_up",
-        [((requests, 2 * ff + 128), BF16), ((rows, width), F32)],
+        [((requests, ff + 128), BF16)] * 2 + [((rows, width), F32)],
         pieces + [all_input, norm_gain.reshape(1, width), gate_weight, up_weight],
         [pltpu.VMEM((requests, width), F32)],
     )
     (core_sums,) = call(
         core_sum_kernel,
         "core_sum",
-        [((requests, 2 * ff + 128), BF16)],
-        [sums, flip(sums, "mlp", 1)],
+        [((requests, ff + 128), BF16)],
+        [keep, flip(send, "mlp", 1)],
+    )
+    (hidden,) = call(
+        functools.partial(hidden_kernel, width * mlp),
+        "hidden",
+        [((requests, ff // 2), BF16)],
+        [core_sums, flip(core_sums, "mlp", 2)],
     )
     (down,) = call(
-        functools.partial(down_kernel, width * mlp),
+        down_kernel,
         "down",
         [((pool, rows, width), BF16)],
-        [core_sums, flip(core_sums, "mlp", 2), down_weight],
+        [hidden, flip(hidden, "mlp", 1), down_weight],
         [pltpu.VMEM((requests, width), F32)],
     )
     backwards = list(range(pool))[::-1]

time: 54.2 us -> 58.8 us (1.085)
  waiting for transfers between devices: 16.9 us -> 22.6 us
  starting transfers between devices: 21.9 us -> 20.6 us
    ppermute x13 -> x14, waiting for transfers between devices: 14.3 us -> 19.6 us  [flip(): lax.ppermute(values, axis, [(index, index ^ step) for index in range(size)])]
    ppermute x13 -> x14, starting transfers between devices: 17.9 us -> 15.9 us  [flip(): lax.ppermute(values, axis, [(index, index ^ step) for index in range(size)])]
    ppermute x2, starting transfers between devices: 3.95 us -> 4.65 us  [per_device_small(): pieces.append(lax.ppermute(head_sum, ('pool', 'mlp'), route))]
    pallas_call x11 -> x12, Pallas kernels: 5.3 us -> 5.33 us  [call(): pl.pallas_call(kernel, out_shape=[jax.ShapeDtypeStruct(shape, dtype) for...]
  transfers between devices with their start and end apart: 15 -> 16, of which waited for: 13 -> 13; matrix products, arithmetic and copies ran while one was open for 0% -> 0% of each run, Pallas kernels for 0% -> 0%
where the time goes in v9:
time: 58.8 us; the launch traced here: 58.5 us
  waiting for transfers between devices  22.6 us (38%)
  starting transfers between devices  20.6 us (35%)
  blocking collectives  8.42 us (14%)
  Pallas kernels  5.33 us (9%)
  local copies, waits for them, and re-layouts  1.48 us (3%)
    ppermute x14, waiting for transfers between devices, flip(): lax.ppermute(values, axis, [(index, index ^ step) for index in range(size)])  19.6 us
    ppermute x14, starting transfers between devices, flip(): lax.ppermute(values, axis, [(index, index ^ step) for index in range(size)])  15.9 us
    all_to_all x1, blocking collectives, per_device_small(): lax.all_to_all(down, 'pool', 0, 0, axis_index_groups=[backwards])  8.42 us
    pallas_call x12, Pallas kernels, call(): pl.pallas_call(kernel, out_shape=[jax.ShapeDtypeStruct(shape, dtype) for...  5.33 us
    ppermute x2, starting transfers between devices, per_device_small(): pieces.append(lax.ppermute(head_sum, ('pool', 'mlp'), route))  4.65 us
    ppermute x2, waiting for transfers between devices, per_device_small(): pieces.append(lax.ppermute(head_sum, ('pool', 'mlp'), route))  2.98 us
    unnamed x18, local copies, waits for them, and re-layouts  1.47 us
  transfers between devices with their start and end apart: 16, of which 13 were waited for; matrix products, arithmetic and copies ran while one was open for 0% of the time, Pallas kernels for 0%

profile of v9, /device:TPU:0, one launch (start us, length us, event | category | flops | bytes accessed | tf_op | source)
XLA Modules:
  0.0 58.5 jit_solution(13380832787911531633)
XLA Ops:
  0.0 1.8 %rotary.1 = (bf16[2,1664]{1,0:T(2,128)(2,1)}, f32[8,896]{1,0:T(8,128)}) custom-call(s32[2,8]{1,0:T(2,128)} %refs_0_.1, s32[2]{0:T(128)} %refs_1_.1, bf16[2,768]{1,0:T(2,128)(2,1)} %refs_2_.1, bf16[2,768]{1,0:T(2,128)(2,1)} %refs_3_.1, bf16[2,768]{1,0:T(2,128)(2,1)} %refs_4_.1, bf16[2,768]{1,0:T(2,128)(2,1)} %refs_5_.1, bf16[5,256,768]{2,1,0:T(8,128)(2,1)} %keys.1, ...), custom_call_target="tpu_custom_call" | custom-call | bytes 3944520 | tf_op jit(solution)/shard_map/rotary/pallas_call | solution.py:217
  1.8 3.0 %collective-permute-start = (bf16[2,1664]{1,0:T(2,128)(2,1)}, bf16[2,1664]{1,0:T(2,128)(2,1)S(1)}, u32[]{:S(2)}, u32[]{:S(2)}) collective-permute-start(bf16[2,1664]{1,0:T(2,128)(2,1)} %get-tuple-element.15.packed), channel_id=1, source_target_pairs={{0,4},{4,0},{8,12},{12,8},{16,20},{20,16},{24,28},{28,24},{1,5},{5... | collective-permute-start | bytes 19976 | tf_op jit(solution)/shard_map/ppermute | solution.py:552
  4.8 0.7 %copy-done.6 = f32[8,896]{1,0:T(8,128)S(1)} copy-done((f32[8,896]{1,0:T(8,128)S(1)}, f32[8,896]{1,0:T(8,128)}, u32[]{:S(2)}) %copy-start.6) | copy-done | bytes 28696
  5.6 0.7 %copy-done.7 = bf16[2,1664]{1,0:T(2,128)(2,1)S(1)} copy-done((bf16[2,1664]{1,0:T(2,128)(2,1)S(1)}, bf16[2,1664]{1,0:T(2,128)(2,1)}, u32[]{:S(2)}) %copy-start.7) | copy-done | bytes 6680
  6.3 0.4 collective-permute-done.theirs
  6.7 2.1 %collective-permute-start.1 = (bf16[2,2,1664]{2,1,0:T(2,128)(2,1)S(1)}, bf16[2,2,1664]{2,1,0:T(2,128)(2,1)S(1)}, u32[]{:S(2)}, u32[]{:S(2)}) collective-permute-start(bf16[2,2,1664]{2,1,0:T(2,128)(2,1)S(1)} %merge.2.a0), channel_id=1, source_target_pairs={{0,8},{4,12},{8,0},{12,4},{16,24},{20,28},{24,16},{28,20},{1,9},{5... | collective-permute-start | bytes 39944 | tf_op jit(solution)/shard_map/ppermute | solution.py:552
  8.8 2.6 %collective-permute-start.2 = (bf16[2,2,1664]{2,1,0:T(2,128)(2,1)S(1)}, bf16[2,2,1664]{2,1,0:T(2,128)(2,1)S(1)}, u32[]{:S(2)}, u32[]{:S(2)}) collective-permute-start(bf16[2,2,1664]{2,1,0:T(2,128)(2,1)S(1)} %merge.2.a0), channel_id=1, source_target_pairs={{0,16},{4,20},{8,24},{12,28},{16,0},{20,4},{24,8},{28,12},{1,17},{... | collective-permute-start | bytes 39944 | tf_op jit(solution)/shard_map/ppermute | solution.py:552
  11.3 0.0 collective-permute-start.3
  11.3 0.0 collective-permute-done.1.a1
  11.3 2.0 %collective-permute-done.2.a2 = bf16[2,2,1664]{2,1,0:T(2,128)(2,1)S(1)} collective-permute-done((bf16[2,2,1664]{2,1,0:T(2,128)(2,1)S(1)}, bf16[2,2,1664]{2,1,0:T(2,128)(2,1)S(1)}, u32[]{:S(2)}, u32[]{:S(2)}) %collective-permute-start.2) | collective-permute-done | bytes 13344 | tf_op jit(solution)/shard_map/ppermute | solution.py:552
  13.4 3.5 %collective-permute-done.3.a3 = bf16[2,2,1664]{2,1,0:T(2,128)(2,1)S(1)} collective-permute-done((bf16[2,2,1664]{2,1,0:T(2,128)(2,1)S(1)}, bf16[2,2,1664]{2,1,0:T(2,128)(2,1)S(1)}, u32[]{:S(2)}, u32[]{:S(2)}) %collective-permute-start.3) | collective-permute-done | bytes 13344 | tf_op jit(solution)/shard_map/ppermute | solution.py:552
  16.8 0.0 copy-done
  16.8 0.0 copy-done.1
  16.9 0.0 copy-start.3
  16.9 0.0 copy-start.4
  16.9 1.1 %attend.1 = (bf16[8,768]{1,0:T(8,128)(2,1)S(1)}, f32[16,768]{1,0:T(8,128)S(1)}, f32[16,128]{1,0:T(8,128)S(1)}) custom-call(bf16[2,2,1664]{2,1,0:T(2,128)(2,1)S(1)} %merge.2.a0, bf16[2,2,1664]{2,1,0:T(2,128)(2,1)S(1)} %collective-permute-done.1.a1, bf16[2,2,1664]{2,1,0:T(2,128)(2,1)S(1)} %collective-permute-done.2.a2, ...), custom_call_target="tpu_custom_call" | custom-call | bytes 4014080 | tf_op jit(solution)/shard_map/attend/pallas_call | solution.py:217
  18.0 1.6 %collective-permute-start.4 = (bf16[8,768]{1,0:T(8,128)(2,1)S(1)}, bf16[8,768]{1,0:T(8,128)(2,1)S(1)}, u32[]{:S(2)}, u32[]{:S(2)}) collective-permute-start(bf16[8,768]{1,0:T(8,128)(2,1)S(1)} %get-tuple-element.19.mine), channel_id=1, source_target_pairs={{0,4},{4,0},{8,12},{12,8},{16,20},{20,16},{24,28},{28,24},{1,5},{5... | collective-permute-start | bytes 36872 | tf_op jit(solution)/shard_map/ppermute | solution.py:552
  19.6 2.2 %collective-permute-done.4.theirs = bf16[8,768]{1,0:T(8,128)(2,1)S(1)} collective-permute-done((bf16[8,768]{1,0:T(8,128)(2,1)S(1)}, bf16[8,768]{1,0:T(8,128)(2,1)S(1)}, u32[]{:S(2)}, u32[]{:S(2)}) %collective-permute-start.4) | collective-permute-done | bytes 12320 | tf_op jit(solution)/shard_map/ppermute | solution.py:552
  21.8 0.0 collective-permute-start.5
  21.8 0.7 %collective-permute-start.6 = (bf16[2,8,768]{2,1,0:T(8,128)(2,1)S(1)}, bf16[2,8,768]{2,1,0:T(8,128)(2,1)S(1)}, u32[]{:S(2)}, u32[]{:S(2)}) collective-permute-start(bf16[2,8,768]{2,1,0:T(8,128)(2,1)S(1)} %merge.3.b0), channel_id=1, source_target_pairs={{0,16},{4,20},{8,24},{12,28},{16,0},{20,4},{24,8},{28,12},{1,17},{... | collective-permute-start | bytes 73736 | tf_op jit(solution)/shard_map/ppermute | solution.py:552
  22.5 3.7 %collective-permute-start.7 = (bf16[2,8,768]{2,1,0:T(8,128)(2,1)S(1)}, bf16[2,8,768]{2,1,0:T(8,128)(2,1)S(1)}, u32[]{:S(2)}, u32[]{:S(2)}) collective-permute-start(bf16[2,8,768]{2,1,0:T(8,128)(2,1)S(1)} %merge.3.b0), channel_id=1, source_target_pairs={{0,24},{4,28},{8,16},{12,20},{16,8},{20,12},{24,0},{28,4},{1,25},{... | collective-permute-start | bytes 73736 | tf_op jit(solution)/shard_map/ppermute | solution.py:552
  26.2 0.0 collective-permute-done.5.b1
  26.2 0.4 collective-permute-done.6.b2
  26.6 1.7 %collective-permute-done.7.b3 = bf16[2,8,768]{2,1,0:T(8,128)(2,1)S(1)} collective-permute-done((bf16[2,8,768]{2,1,0:T(8,128)(2,1)S(1)}, bf16[2,8,768]{2,1,0:T(8,128)(2,1)S(1)}, u32[]{:S(2)}, u32[]{:S(2)}) %collective-permute-start.7) | collective-permute-done | bytes 24608 | tf_op jit(solution)/shard_map/ppermute | solution.py:552
  28.2 0.0 copy-done.5
  28.3 0.7 %combine.1.p0 = bf16[16,384]{1,0:T(8,128)(2,1)S(1)} custom-call(bf16[2,8,768]{2,1,0:T(8,128)(2,1)S(1)} %merge.3.b0, bf16[2,8,768]{2,1,0:T(8,128)(2,1)S(1)} %collective-permute-done.5.b1, bf16[2,8,768]{2,1,0:T(8,128)(2,1)S(1)} %collective-permute-done.6.b2, bf16[2,8,768]{2,1,0:T(8,128)(2,1)S(1)} %collective-permute-done.7.b3, ...), custom_call_target="tpu_custom_call" | custom-call | bytes 696320 | tf_op jit(solution)/shard_map/combine/pallas_call | solution.py:217
  29.0 0.1 collective-permute-start.10
  29.0 1.6 %collective-permute-start.8 = (bf16[16,384]{1,0:T(8,128)(2,1)S(1)}, bf16[16,384]{1,0:T(8,128)(2,1)S(1)}, u32[]{:S(2)}, u32[]{:S(2)}) collective-permute-start(bf16[16,384]{1,0:T(8,128)(2,1)S(1)} %combine.1.p0), channel_id=1, source_target_pairs={{0,1},{1,0},{2,3},{3,2},{4,5},{5,4},{6,7},{7,6},{8,9},{9,8},{10,11... | collective-permute-start | bytes 36872 | tf_op jit(solution)/shard_map/ppermute | solution.py:552
  30.6 0.5 collective-permute-start.9
  31.2 1.1 %collective-permute-done.10.p3 = bf16[16,384]{1,0:T(8,128)(2,1)S(1)} collective-permute-done((bf16[16,384]{1,0:T(8,128)(2,1)S(1)}, bf16[16,384]{1,0:T(8,128)(2,1)S(1)}, u32[]{:S(2)}, u32[]{:S(2)}) %collective-permute-start.10) | collective-permute-done | bytes 12320 | tf_op jit(solution)/shard_map/ppermute | solution.py:552
  32.2 0.0 collective-permute-done.8.p1
  32.2 2.1 %collective-permute-done.9.p2 = bf16[16,384]{1,0:T(8,128)(2,1)S(1)} collective-permute-done((bf16[16,384]{1,0:T(8,128)(2,1)S(1)}, bf16[16,384]{1,0:T(8,128)(2,1)S(1)}, u32[]{:S(2)}, u32[]{:S(2)}) %collective-permute-start.9) | collective-permute-done | bytes 12320 | tf_op jit(solution)/shard_map/ppermute | solution.py:552
  34.3 3.6 %collective-permute-start.11 = (bf16[16,384]{1,0:T(8,128)(2,1)S(1)}, bf16[16,384]{1,0:T(8,128)(2,1)S(1)}, u32[]{:S(2)}, u32[]{:S(2)}) collective-permute-start(bf16[16,384]{1,0:T(8,128)(2,1)S(1)} %head_sum.1), channel_id=1, source_target_pairs={{0,24},{4,28},{1,16},{5,20},{2,8},{6,12},{3,0},{7,4},{9,25},{13,29... | collective-permute-start | bytes 36872 | tf_op jit(solution)/shard_map/ppermute | solution.py:641
  38.0 1.0 %collective-permute-start.12 = (bf16[16,384]{1,0:T(8,128)(2,1)S(1)}, bf16[16,384]{1,0:T(8,128)(2,1)S(1)}, u32[]{:S(2)}, u32[]{:S(2)}) collective-permute-start(bf16[16,384]{1,0:T(8,128)(2,1)S(1)} %head_sum.1), channel_id=1, source_target_pairs={{0,28},{4,24},{1,20},{5,16},{2,12},{6,8},{3,4},{7,0},{9,29},{13,25... | collective-permute-start | bytes 36872 | tf_op jit(solution)/shard_map/ppermute | solution.py:641
  39.0 0.4 collective-permute-done.11.same
  39.4 2.6 %collective-permute-done.12.flip = bf16[16,384]{1,0:T(8,128)(2,1)S(1)} collective-permute-done((bf16[16,384]{1,0:T(8,128)(2,1)S(1)}, bf16[16,384]{1,0:T(8,128)(2,1)S(1)}, u32[]{:S(2)}, u32[]{:S(2)}) %collective-permute-start.12) | collective-permute-done | bytes 12320 | tf_op jit(solution)/shard_map/ppermute | solution.py:641
  42.0 0.5 gate_up.1
  42.5 0.0 collective-permute-start.13
  42.5 1.2 %collective-permute-done.13.theirs = bf16[16,1152]{1,0:T(8,128)(2,1)S(1)} collective-permute-done((bf16[16,1152]{1,0:T(8,128)(2,1)S(1)}, bf16[16,1152]{1,0:T(8,128)(2,1)S(1)}, u32[]{:S(2)}, u32[]{:S(2)}) %collective-permute-start.13) | collective-permute-done | bytes 36896 | tf_op jit(solution)/shard_map/ppermute | solution.py:552
  43.7 0.1 core_sum.1.mine
  43.8 0.0 collective-permute-start.14
  43.8 4.0 %collective-permute-done.14.theirs = bf16[16,1152]{1,0:T(8,128)(2,1)S(1)} collective-permute-done((bf16[16,1152]{1,0:T(8,128)(2,1)S(1)}, bf16[16,1152]{1,0:T(8,128)(2,1)S(1)}, u32[]{:S(2)}, u32[]{:S(2)}) %collective-permute-start.14) | collective-permute-done | bytes 36896 | tf_op jit(solution)/shard_map/ppermute | solution.py:552
  47.8 0.1 hidden.1.mine
  47.9 0.1 collective-permute-start.15
  48.0 1.2 %collective-permute-done.15.theirs = bf16[16,512]{1,0:T(8,128)(2,1)S(1)} collective-permute-done((bf16[16,512]{1,0:T(8,128)(2,1)S(1)}, bf16[16,512]{1,0:T(8,128)(2,1)S(1)}, u32[]{:S(2)}, u32[]{:S(2)}) %collective-permute-start.15) | collective-permute-done | bytes 16416 | tf_op jit(solution)/shard_map/ppermute | solution.py:552
  49.2 0.3 down.1
  49.5 8.4 %all_to_all.5.parts = bf16[8,2,768]{2,1,0:T(2,128)(2,1)S(1)} all-to-all(bf16[8,2,768]{2,1,0:T(2,128)(2,1)S(1)} %down.1), channel_id=1, replica_groups={{28,24,20,16,12,8,4,0},{29,25,21,17,13,9,5,1},{30,26,22,18,14,10,6,2},{..., dimensions={0} | all-to-all | bytes 49152 | tf_op jit(solution)/shard_map/all_to_all | solution.py:673
  57.9 0.6 %final.1 = bf16[2,768]{1,0:T(2,128)(2,1)} custom-call(f32[2,768]{1,0:T(2,128)S(1)} %get-tuple-element.22.own, bf16[8,2,768]{2,1,0:T(2,128)(2,1)S(1)} %all_to_all.5.parts), custom_call_target="tpu_custom_call" | custom-call | bytes 30720 | tf_op jit(solution)/shard_map/final/pallas_call | solution.py:217
  (16 shorter events, 0.0 us)
Async XLA Ops:
  0.0 16.8 %copy-start = (bf16[5,256,768]{2,1,0:T(8,128)(2,1)S(1)}, bf16[5,256,768]{2,1,0:T(8,128)(2,1)}, u32[]{:S(2)}) copy-start(bf16[5,256,768]{2,1,0:T(8,128)(2,1)} %keys.1) | copy-start | bytes 5898244
  0.0 16.8 %copy-start.1 = (bf16[5,256,768]{2,1,0:T(8,128)(2,1)S(1)}, bf16[5,256,768]{2,1,0:T(8,128)(2,1)}, u32[]{:S(2)}) copy-start(bf16[5,256,768]{2,1,0:T(8,128)(2,1)} %values.1) | copy-start | bytes 5898244
  1.8 4.9 %collective-permute-start = (bf16[2,1664]{1,0:T(2,128)(2,1)}, bf16[2,1664]{1,0:T(2,128)(2,1)S(1)}, u32[]{:S(2)}, u32[]{:S(2)}) collective-permute-start(bf16[2,1664]{1,0:T(2,128)(2,1)} %get-tuple-element.15.packed), channel_id=1, source_target_pairs={{0,4},{4,0},{8,12},{12,8},{16,20},{20,16},{24,28},{28,24},{1,5},{5... | collective-permute-start | bytes 19976 | tf_op jit(solution)/shard_map/ppermute | solution.py:552
  4.8 0.7 %copy-start.6 = (f32[8,896]{1,0:T(8,128)S(1)}, f32[8,896]{1,0:T(8,128)}, u32[]{:S(2)}) copy-start(f32[8,896]{1,0:T(8,128)} %get-tuple-element.16.own) | copy-start | bytes 86020
  5.6 0.7 %copy-start.7 = (bf16[2,1664]{1,0:T(2,128)(2,1)S(1)}, bf16[2,1664]{1,0:T(2,128)(2,1)}, u32[]{:S(2)}) copy-start(bf16[2,1664]{1,0:T(2,128)(2,1)} %get-tuple-element.15.packed) | copy-start | bytes 19972
  6.7 4.7 %collective-permute-start.1 = (bf16[2,2,1664]{2,1,0:T(2,128)(2,1)S(1)}, bf16[2,2,1664]{2,1,0:T(2,128)(2,1)S(1)}, u32[]{:S(2)}, u32[]{:S(2)}) collective-permute-start(bf16[2,2,1664]{2,1,0:T(2,128)(2,1)S(1)} %merge.2.a0), channel_id=1, source_target_pairs={{0,8},{4,12},{8,0},{12,4},{16,24},{20,28},{24,16},{28,20},{1,9},{5... | collective-permute-start | bytes 39944 | tf_op jit(solution)/shard_map/ppermute | solution.py:552
  8.8 4.6 %collective-permute-start.2 = (bf16[2,2,1664]{2,1,0:T(2,128)(2,1)S(1)}, bf16[2,2,1664]{2,1,0:T(2,128)(2,1)S(1)}, u32[]{:S(2)}, u32[]{:S(2)}) collective-permute-start(bf16[2,2,1664]{2,1,0:T(2,128)(2,1)S(1)} %merge.2.a0), channel_id=1, source_target_pairs={{0,16},{4,20},{8,24},{12,28},{16,0},{20,4},{24,8},{28,12},{1,17},{... | collective-permute-start | bytes 39944 | tf_op jit(solution)/shard_map/ppermute | solution.py:552
  11.3 5.5 %collective-permute-start.3 = (bf16[2,2,1664]{2,1,0:T(2,128)(2,1)S(1)}, bf16[2,2,1664]{2,1,0:T(2,128)(2,1)S(1)}, u32[]{:S(2)}, u32[]{:S(2)}) collective-permute-start(bf16[2,2,1664]{2,1,0:T(2,128)(2,1)S(1)} %merge.2.a0), channel_id=1, source_target_pairs={{0,24},{4,28},{8,16},{12,20},{16,8},{20,12},{24,0},{28,4},{1,25},{... | collective-permute-start | bytes 39944 | tf_op jit(solution)/shard_map/ppermute | solution.py:552
  16.9 11.4 %copy-start.5 = (bf16[768,384]{1,0:T(8,128)(2,1)S(1)}, bf16[768,384]{1,0:T(8,128)(2,1)}, u32[]{:S(2)}) copy-start(bf16[768,384]{1,0:T(8,128)(2,1)} %weight.2) | copy-start | bytes 1769476
  16.9 22.1 %copy-start.8 = (bf16[768]{0:T(1024)(128)(2,1)S(1)}, bf16[768]{0:T(1024)(128)(2,1)}, u32[]{:S(2)}) copy-start(bf16[768]{0:T(1024)(128)(2,1)} %param.22) | copy-start | bytes 4612
  16.9 25.1 %copy-start.3 = (bf16[768,1024]{1,0:T(8,128)(2,1)S(1)}, bf16[768,1024]{1,0:T(8,128)(2,1)}, u32[]{:S(2)}) copy-start(bf16[768,1024]{1,0:T(8,128)(2,1)} %gate.1) | copy-start | bytes 4718596
  16.9 25.1 %copy-start.4 = (bf16[768,1024]{1,0:T(8,128)(2,1)S(1)}, bf16[768,1024]{1,0:T(8,128)(2,1)}, u32[]{:S(2)}) copy-start(bf16[768,1024]{1,0:T(8,128)(2,1)} %up.1) | copy-start | bytes 4718596
  18.0 3.8 %collective-permute-start.4 = (bf16[8,768]{1,0:T(8,128)(2,1)S(1)}, bf16[8,768]{1,0:T(8,128)(2,1)S(1)}, u32[]{:S(2)}, u32[]{:S(2)}) collective-permute-start(bf16[8,768]{1,0:T(8,128)(2,1)S(1)} %get-tuple-element.19.mine), channel_id=1, source_target_pairs={{0,4},{4,0},{8,12},{12,8},{16,20},{20,16},{24,28},{28,24},{1,5},{5... | collective-permute-start | bytes 36872 | tf_op jit(solution)/shard_map/ppermute | solution.py:552
  21.8 4.4 %collective-permute-start.5 = (bf16[2,8,768]{2,1,0:T(8,128)(2,1)S(1)}, bf16[2,8,768]{2,1,0:T(8,128)(2,1)S(1)}, u32[]{:S(2)}, u32[]{:S(2)}) collective-permute-start(bf16[2,8,768]{2,1,0:T(8,128)(2,1)S(1)} %merge.3.b0), channel_id=1, source_target_pairs={{0,8},{4,12},{8,0},{12,4},{16,24},{20,28},{24,16},{28,20},{1,9},{5... | collective-permute-start | bytes 73736 | tf_op jit(solution)/shard_map/ppermute | solution.py:552
  21.8 4.8 %collective-permute-start.6 = (bf16[2,8,768]{2,1,0:T(8,128)(2,1)S(1)}, bf16[2,8,768]{2,1,0:T(8,128)(2,1)S(1)}, u32[]{:S(2)}, u32[]{:S(2)}) collective-permute-start(bf16[2,8,768]{2,1,0:T(8,128)(2,1)S(1)} %merge.3.b0), channel_id=1, source_target_pairs={{0,16},{4,20},{8,24},{12,28},{16,0},{20,4},{24,8},{28,12},{1,17},{... | collective-permute-start | bytes 73736 | tf_op jit(solution)/shard_map/ppermute | solution.py:552
  22.5 5.7 %collective-permute-start.7 = (bf16[2,8,768]{2,1,0:T(8,128)(2,1)S(1)}, bf16[2,8,768]{2,1,0:T(8,128)(2,1)S(1)}, u32[]{:S(2)}, u32[]{:S(2)}) collective-permute-start(bf16[2,8,768]{2,1,0:T(8,128)(2,1)S(1)} %merge.3.b0), channel_id=1, source_target_pairs={{0,24},{4,28},{8,16},{12,20},{16,8},{20,12},{24,0},{28,4},{1,25},{... | collective-permute-start | bytes 73736 | tf_op jit(solution)/shard_map/ppermute | solution.py:552
  29.0 3.2 %collective-permute-start.10 = (bf16[16,384]{1,0:T(8,128)(2,1)S(1)}, bf16[16,384]{1,0:T(8,128)(2,1)S(1)}, u32[]{:S(2)}, u32[]{:S(2)}) collective-permute-start(bf16[16,384]{1,0:T(8,128)(2,1)S(1)} %combine.1.p0), channel_id=1, source_target_pairs={{0,3},{1,2},{2,1},{3,0},{4,7},{5,6},{6,5},{7,4},{8,11},{9,10},{10,... | collective-permute-start | bytes 36872 | tf_op jit(solution)/shard_map/ppermute | solution.py:552
  29.0 3.2 %collective-permute-start.8 = (bf16[16,384]{1,0:T(8,128)(2,1)S(1)}, bf16[16,384]{1,0:T(8,128)(2,1)S(1)}, u32[]{:S(2)}, u32[]{:S(2)}) collective-permute-start(bf16[16,384]{1,0:T(8,128)(2,1)S(1)} %combine.1.p0), channel_id=1, source_target_pairs={{0,1},{1,0},{2,3},{3,2},{4,5},{5,4},{6,7},{7,6},{8,9},{9,8},{10,11... | collective-permute-start | bytes 36872 | tf_op jit(solution)/shard_map/ppermute | solution.py:552
  30.6 3.7 %collective-permute-start.9 = (bf16[16,384]{1,0:T(8,128)(2,1)S(1)}, bf16[16,384]{1,0:T(8,128)(2,1)S(1)}, u32[]{:S(2)}, u32[]{:S(2)}) collective-permute-start(bf16[16,384]{1,0:T(8,128)(2,1)S(1)} %combine.1.p0), channel_id=1, source_target_pairs={{0,2},{1,3},{2,0},{3,1},{4,6},{5,7},{6,4},{7,5},{8,10},{9,11},{10,... | collective-permute-start | bytes 36872 | tf_op jit(solution)/shard_map/ppermute | solution.py:552
  34.3 5.0 %collective-permute-start.11 = (bf16[16,384]{1,0:T(8,128)(2,1)S(1)}, bf16[16,384]{1,0:T(8,128)(2,1)S(1)}, u32[]{:S(2)}, u32[]{:S(2)}) collective-permute-start(bf16[16,384]{1,0:T(8,128)(2,1)S(1)} %head_sum.1), channel_id=1, source_target_pairs={{0,24},{4,28},{1,16},{5,20},{2,8},{6,12},{3,0},{7,4},{9,25},{13,29... | collective-permute-start | bytes 36872 | tf_op jit(solution)/shard_map/ppermute | solution.py:641
  38.0 4.0 %collective-permute-start.12 = (bf16[16,384]{1,0:T(8,128)(2,1)S(1)}, bf16[16,384]{1,0:T(8,128)(2,1)S(1)}, u32[]{:S(2)}, u32[]{:S(2)}) collective-permute-start(bf16[16,384]{1,0:T(8,128)(2,1)S(1)} %head_sum.1), channel_id=1, source_target_pairs={{0,28},{4,24},{1,20},{5,16},{2,12},{6,8},{3,4},{7,0},{9,29},{13,25... | collective-permute-start | bytes 36872 | tf_op jit(solution)/shard_map/ppermute | solution.py:641
  42.0 7.2 %copy-start.2 = (bf16[1024,768]{1,0:T(8,128)(2,1)S(1)}, bf16[1024,768]{1,0:T(8,128)(2,1)}, u32[]{:S(2)}) copy-start(bf16[1024,768]{1,0:T(8,128)(2,1)} %weight.3) | copy-start | bytes 4718596
  42.5 1.2 %collective-permute-start.13 = (bf16[16,1152]{1,0:T(8,128)(2,1)S(1)}, bf16[16,1152]{1,0:T(8,128)(2,1)S(1)}, u32[]{:S(2)}, u32[]{:S(2)}) collective-permute-start(bf16[16,1152]{1,0:T(8,128)(2,1)S(1)} %get-tuple-element.24), channel_id=1, source_target_pairs={{0,1},{1,0},{2,3},{3,2},{4,5},{5,4},{6,7},{7,6},{8,9},{9,8},{10,11... | collective-permute-start | bytes 110600 | tf_op jit(solution)/shard_map/ppermute | solution.py:552
  43.8 4.0 %collective-permute-start.14 = (bf16[16,1152]{1,0:T(8,128)(2,1)S(1)}, bf16[16,1152]{1,0:T(8,128)(2,1)S(1)}, u32[]{:S(2)}, u32[]{:S(2)}) collective-permute-start(bf16[16,1152]{1,0:T(8,128)(2,1)S(1)} %core_sum.1.mine), channel_id=1, source_target_pairs={{0,2},{1,3},{2,0},{3,1},{4,6},{5,7},{6,4},{7,5},{8,10},{9,11},{10,... | collective-permute-start | bytes 110600 | tf_op jit(solution)/shard_map/ppermute | solution.py:552
  47.9 1.2 %collective-permute-start.15 = (bf16[16,512]{1,0:T(8,128)(2,1)S(1)}, bf16[16,512]{1,0:T(8,128)(2,1)S(1)}, u32[]{:S(2)}, u32[]{:S(2)}) collective-permute-start(bf16[16,512]{1,0:T(8,128)(2,1)S(1)} %hidden.1.mine), channel_id=1, source_target_pairs={{0,1},{1,0},{2,3},{3,2},{4,5},{5,4},{6,7},{7,6},{8,9},{9,8},{10,11... | collective-permute-start | bytes 49160 | tf_op jit(solution)/shard_map/ppermute | solution.py:552

commit v10 on v8

--- a/solution.py
+++ b/solution.py
@@ -277,7 +277,7 @@
 
 
 def prepare_kernel(*refs):
-    sources, (packed, own), held = refs[:6], refs[8:10], refs[10:16]
+    sources, (packed, new), held = refs[:6], refs[8:10], refs[10:16]
     scr, sems = refs[16:]
     copies = [
         pltpu.make_async_copy(source, target, sems.at[i])
@@ -285,34 +285,32 @@
     ]
     for copy in copies:
         copy.start()
+    table, length, query, key, value, residual = held
+    rows, width = query.shape
+    most = table.shape[1]
+    period = 384
+    turn = lanes((8, period)) % (HD // 2)
+    freq = jnp.zeros((8, period), F32)
+    for i in range(HD // 2):
+        freq = jnp.where(turn == i, float(np.float32(10000.0 ** (-2.0 * i / HD))), freq)
     for copy in copies:
         copy.wait()
-    table, length, query, key, value, residual = held
-    rows, width = query.shape
-    heads = width // HD
-    most = table.shape[1]
-    blocks = own.shape[0] - rows - 1
     scr[...] = jnp.zeros_like(scr)
     scr[0:rows, :] = query[...].astype(F32)
     scr[rows : 2 * rows, :] = key[...].astype(F32)
     values = scr[...]
-    line = rows_of((8, width))
-    where_at = jnp.zeros((8, width), F32)
+    line = rows_of((8, period))
+    where_at = jnp.zeros((8, period), F32)
     for r in range(rows):
         here = (line == r) | (line == rows + r)
         where_at = jnp.where(here, length[r].astype(F32), where_at)
-    lane = lanes((8, width))
-    turn = lanes((8, 384)) % (HD // 2)
-    freq = jnp.zeros((8, 384), F32)
-    for i in range(HD // 2):
-        freq = jnp.where(turn == i, float(np.float32(10000.0 ** (-2.0 * i / HD))), freq)
-    angles = where_at * jnp.concatenate([freq] * (width // 384), 1)
-    first = lane % HD < HD // 2
+    angles = where_at * freq
+    cosine = jnp.concatenate([jnp.cos(angles)] * (width // period), 1)
+    sine = jnp.concatenate([jnp.sin(angles)] * (width // period), 1)
+    first = lanes((8, width)) % HD < HD // 2
     ahead = pltpu.roll(values, width - HD // 2, 1)
     behind = pltpu.roll(values, HD // 2, 1)
-    other = jnp.where(first, -ahead, behind)
-    turned = values * jnp.cos(angles) + other * jnp.sin(angles)
-    scr[...] = round_low(turned)
+    scr[...] = values * cosine + jnp.where(first, -ahead, behind) * sine
     packed[:, :width] = scr[0:rows, :].astype(BF16)
     packed[:, width : 2 * width] = residual[...]
     tail = jnp.zeros((rows, 128), F32)
@@ -324,32 +322,35 @@
             tail = jnp.where((row == r) & (at == high), (code >> 7).astype(F32), tail)
             tail = jnp.where((row == r) & (at == rest), (code & 127).astype(F32), tail)
     packed[:, 2 * width :] = tail.astype(BF16)
-
-    head_mask = lane // HD == line
-    product = scr[0:rows, :] * scr[rows : 2 * rows, :]
+    new[:, :width] = scr[rows : 2 * rows, :].astype(BF16)
+    new[:, width:] = value[...]
+
+
+def carry_kernel(packed, new, packed_near, own):
+    packed_near[...] = packed[...]
+    rows, width = new.shape[0], new.shape[1] // 2
+    blocks = own.shape[0] - rows - 1
+    heads = width // HD
+    head_mask = lanes((heads, width)) // HD == rows_of((heads, width))
+    product = packed[:, :width].astype(F32) * new[:, :width].astype(F32)
     own[...] = jnp.zeros_like(own)
-    spot = lanes((8, 128))
-    tail = jnp.zeros((8, 128), F32)
+    spot = lanes((heads, 128))
+    tail = jnp.zeros((heads, 128), F32)
     for r in range(rows):
         score = jnp.sum(
-            jnp.where(head_mask, jnp.broadcast_to(product[r : r + 1], (8, width)), 0.0),
+            jnp.where(head_mask, jnp.broadcast_to(product[r : r + 1], (heads, width)), 0.0),
             1,
             keepdims=True,
         ) * (1.0 / math.sqrt(HD))
         shift = round_low(score)
         weight = jnp.exp(score - shift)
         spread = jnp.sum(jnp.where(head_mask, round_low(weight), 0.0), 0, keepdims=True)
-        own[blocks + r : blocks + r + 1, :width] = spread * value[r : r + 1, :].astype(F32)
+        own[blocks + r : blocks + r + 1, :width] = spread * new[r : r + 1, width:].astype(F32)
         high = round_low(weight)
         tail = jnp.where(spot == blocks + r, shift, tail)
         tail = jnp.where(spot == 8 + blocks + r, high, tail)
         tail = jnp.where(spot == 16 + blocks + r, weight - high, tail)
     own[:, width:] = tail
-
-
-def carry_kernel(packed, own, packed_near, own_near):
-    packed_near[...] = packed[...]
-    own_near[...] = own[...]
 
 
 def merge_kernel(mine, theirs, both):
@@ -562,10 +563,10 @@
     slots = blocks + rows + 1
     part_width = width + 128
 
-    packed, own = call(
+    packed, new = call(
         prepare_kernel,
         "rotary",
-        [((rows, packed_width), BF16), ((slots, part_width), F32)],
+        [((rows, packed_width), BF16), ((rows, 2 * width), BF16)],
         [block_table, lengths, query_new, key_new, value_new, residual_in, key_cache, value_cache],
         [pltpu.SMEM(block_table.shape, jnp.int32), pltpu.SMEM(lengths.shape, jnp.int32)]
         + [pltpu.VMEM((rows, width), BF16)] * 4
@@ -577,8 +578,8 @@
     packed_near, own = call(
         carry_kernel,
         "carry",
-        [(packed.shape, BF16), (own.shape, F32)],
-        [packed, own],
+        [(packed.shape, BF16), ((slots, part_width), F32)],
+        [packed, new],
     )
 
     def pool_gather(values, near):
@@ -612,14 +613,14 @@
         sum_kernel,
         "head_sum",
         [((requests, part_cols), BF16)],
-        [head_part] + [flip(head_part, "mlp", step) for step in (1, 2, 3)],
+        [head_part] + [flip(head_part, "mlp", step) for step in (1, 3, 2)],
     )
     pieces = []
     for turn in range(2):
         route = []
         for m in range(mlp):
             by_distance = sorted(range(4), key=lambda z: (-abs(z - m), z))
-            for z, step in zip(by_distance, (0, 1, 2, 3)):
+            for z, step in zip(by_distance, (1, 0, 3, 2) if m % 2 == 0 else (0, 1, 2, 3)):
                 for y in range(2):
                     source = (m * 2 + y) * mlp + (m ^ step)
                     route.append((source, (z * 2 + (y ^ turn)) * mlp + m))

time: 54.2 us -> 54.7 us (level)
  waiting for transfers between devices: 16.9 us -> 17.8 us
where the time goes in v10:
time: 54.7 us; the launch traced here: 54.4 us
  starting transfers between devices  21.4 us (39%)
  waiting for transfers between devices  17.8 us (33%)
  blocking collectives  8.36 us (15%)
  Pallas kernels  5.26 us (10%)
  local copies, waits for them, and re-layouts  1.46 us (3%)
    ppermute x13, starting transfers between devices, flip(): lax.ppermute(values, axis, [(index, index ^ step) for index in range(size)])  17.9 us
    ppermute x13, waiting for transfers between devices, flip(): lax.ppermute(values, axis, [(index, index ^ step) for index in range(size)])  14.8 us
    all_to_all x1, blocking collectives, per_device_small(): lax.all_to_all(down, 'pool', 0, 0, axis_index_groups=[backwards])  8.36 us
    pallas_call x11, Pallas kernels, call(): pl.pallas_call(kernel, out_shape=[jax.ShapeDtypeStruct(shape, dtype) for...  5.26 us
    ppermute x2, starting transfers between devices, per_device_small(): pieces.append(lax.ppermute(head_sum, ('pool', 'mlp'), route))  3.45 us
    ppermute x2, waiting for transfers between devices, per_device_small(): pieces.append(lax.ppermute(head_sum, ('pool', 'mlp'), route))  3.02 us
    unnamed x18, local copies, waits for them, and re-layouts  1.45 us
  transfers between devices with their start and end apart: 15, of which 13 were waited for; matrix products, arithmetic and copies ran while one was open for 0% of the time, Pallas kernels for 0%

profile of v10, /device:TPU:0, one launch (start us, length us, event | category | flops | bytes accessed | tf_op | source)
XLA Modules:
  0.0 54.4 jit_solution(12825894147791045569)
XLA Ops:
  0.0 1.6 %rotary.1 = (bf16[2,1664]{1,0:T(2,128)(2,1)}, bf16[2,1536]{1,0:T(2,128)(2,1)}) custom-call(s32[2,8]{1,0:T(2,128)} %refs_0_.1, s32[2]{0:T(128)} %refs_1_.1, bf16[2,768]{1,0:T(2,128)(2,1)} %refs_2_.1, bf16[2,768]{1,0:T(2,128)(2,1)} %refs_3_.1, bf16[2,768]{1,0:T(2,128)(2,1)} %refs_4_.1, bf16[2,768]{1,0:T(2,128)(2,1)} %refs_5_.1, bf16[5,256,768]{2,1,0:T(8,128)(2,1)} %keys.1, ...), custom_call_target="tpu_custom_call" | custom-call | bytes 3944520 | tf_op jit(solution)/shard_map/rotary/pallas_call | solution.py:217
  1.6 3.0 %collective-permute-start = (bf16[2,1664]{1,0:T(2,128)(2,1)}, bf16[2,1664]{1,0:T(2,128)(2,1)S(1)}, u32[]{:S(2)}, u32[]{:S(2)}) collective-permute-start(bf16[2,1664]{1,0:T(2,128)(2,1)} %get-tuple-element.14.packed), channel_id=1, source_target_pairs={{0,4},{4,0},{8,12},{12,8},{16,20},{20,16},{24,28},{28,24},{1,5},{5... | collective-permute-start | bytes 19976 | tf_op jit(solution)/shard_map/ppermute | solution.py:538
  4.7 0.7 %copy-done.6 = bf16[2,1664]{1,0:T(2,128)(2,1)S(1)} copy-done((bf16[2,1664]{1,0:T(2,128)(2,1)S(1)}, bf16[2,1664]{1,0:T(2,128)(2,1)}, u32[]{:S(2)}) %copy-start.6) | copy-done | bytes 6680
  5.4 0.7 %copy-done.7 = bf16[2,1536]{1,0:T(2,128)(2,1)S(1)} copy-done((bf16[2,1536]{1,0:T(2,128)(2,1)S(1)}, bf16[2,1536]{1,0:T(2,128)(2,1)}, u32[]{:S(2)}) %copy-start.7) | copy-done | bytes 6168
  6.1 0.1 carry.1
  6.2 0.3 collective-permute-done.theirs
  6.5 4.1 %collective-permute-start.3 = (bf16[2,2,1664]{2,1,0:T(2,128)(2,1)S(1)}, bf16[2,2,1664]{2,1,0:T(2,128)(2,1)S(1)}, u32[]{:S(2)}, u32[]{:S(2)}) collective-permute-start(bf16[2,2,1664]{2,1,0:T(2,128)(2,1)S(1)} %merge.2.a0), channel_id=1, source_target_pairs={{0,24},{4,28},{8,16},{12,20},{16,8},{20,12},{24,0},{28,4},{1,25},{... | collective-permute-start | bytes 39944 | tf_op jit(solution)/shard_map/ppermute | solution.py:538
  10.6 0.0 collective-permute-start.2
  10.6 0.6 %collective-permute-start.1 = (bf16[2,2,1664]{2,1,0:T(2,128)(2,1)S(1)}, bf16[2,2,1664]{2,1,0:T(2,128)(2,1)S(1)}, u32[]{:S(2)}, u32[]{:S(2)}) collective-permute-start(bf16[2,2,1664]{2,1,0:T(2,128)(2,1)S(1)} %merge.2.a0), channel_id=1, source_target_pairs={{0,8},{4,12},{8,0},{12,4},{16,24},{20,28},{24,16},{28,20},{1,9},{5... | collective-permute-start | bytes 39944 | tf_op jit(solution)/shard_map/ppermute | solution.py:538
  11.2 1.1 %collective-permute-done.3.a3 = bf16[2,2,1664]{2,1,0:T(2,128)(2,1)S(1)} collective-permute-done((bf16[2,2,1664]{2,1,0:T(2,128)(2,1)S(1)}, bf16[2,2,1664]{2,1,0:T(2,128)(2,1)S(1)}, u32[]{:S(2)}, u32[]{:S(2)}) %collective-permute-start.3) | collective-permute-done | bytes 13344 | tf_op jit(solution)/shard_map/ppermute | solution.py:538
  12.3 2.9 %collective-permute-done.2.a2 = bf16[2,2,1664]{2,1,0:T(2,128)(2,1)S(1)} collective-permute-done((bf16[2,2,1664]{2,1,0:T(2,128)(2,1)S(1)}, bf16[2,2,1664]{2,1,0:T(2,128)(2,1)S(1)}, u32[]{:S(2)}, u32[]{:S(2)}) %collective-permute-start.2) | collective-permute-done | bytes 13344 | tf_op jit(solution)/shard_map/ppermute | solution.py:538
  15.2 0.0 collective-permute-done.1.a1
  15.2 0.0 copy-done.1
  15.2 0.0 copy-done
  15.2 0.0 copy-start.5
  15.2 0.0 copy-start.8
  15.3 0.0 copy-start.3
  15.3 0.0 copy-start.4
  15.3 1.1 %attend.1 = (bf16[8,768]{1,0:T(8,128)(2,1)S(1)}, f32[16,768]{1,0:T(8,128)S(1)}, f32[16,128]{1,0:T(8,128)S(1)}) custom-call(bf16[2,2,1664]{2,1,0:T(2,128)(2,1)S(1)} %merge.2.a0, bf16[2,2,1664]{2,1,0:T(2,128)(2,1)S(1)} %collective-permute-done.1.a1, bf16[2,2,1664]{2,1,0:T(2,128)(2,1)S(1)} %collective-permute-done.2.a2, ...), custom_call_target="tpu_custom_call" | custom-call | bytes 4014080 | tf_op jit(solution)/shard_map/attend/pallas_call | solution.py:217
  16.4 1.6 %collective-permute-start.4 = (bf16[8,768]{1,0:T(8,128)(2,1)S(1)}, bf16[8,768]{1,0:T(8,128)(2,1)S(1)}, u32[]{:S(2)}, u32[]{:S(2)}) collective-permute-start(bf16[8,768]{1,0:T(8,128)(2,1)S(1)} %get-tuple-element.18.mine), channel_id=1, source_target_pairs={{0,4},{4,0},{8,12},{12,8},{16,20},{20,16},{24,28},{28,24},{1,5},{5... | collective-permute-start | bytes 36872 | tf_op jit(solution)/shard_map/ppermute | solution.py:538
  18.0 2.2 %collective-permute-done.4.theirs = bf16[8,768]{1,0:T(8,128)(2,1)S(1)} collective-permute-done((bf16[8,768]{1,0:T(8,128)(2,1)S(1)}, bf16[8,768]{1,0:T(8,128)(2,1)S(1)}, u32[]{:S(2)}, u32[]{:S(2)}) %collective-permute-start.4) | collective-permute-done | bytes 12320 | tf_op jit(solution)/shard_map/ppermute | solution.py:538
  20.2 1.4 %collective-permute-start.7 = (bf16[2,8,768]{2,1,0:T(8,128)(2,1)S(1)}, bf16[2,8,768]{2,1,0:T(8,128)(2,1)S(1)}, u32[]{:S(2)}, u32[]{:S(2)}) collective-permute-start(bf16[2,8,768]{2,1,0:T(8,128)(2,1)S(1)} %merge.3.b0), channel_id=1, source_target_pairs={{0,24},{4,28},{8,16},{12,20},{16,8},{20,12},{24,0},{28,4},{1,25},{... | collective-permute-start | bytes 73736 | tf_op jit(solution)/shard_map/ppermute | solution.py:538
  21.6 0.6 %collective-permute-start.6 = (bf16[2,8,768]{2,1,0:T(8,128)(2,1)S(1)}, bf16[2,8,768]{2,1,0:T(8,128)(2,1)S(1)}, u32[]{:S(2)}, u32[]{:S(2)}) collective-permute-start(bf16[2,8,768]{2,1,0:T(8,128)(2,1)S(1)} %merge.3.b0), channel_id=1, source_target_pairs={{0,16},{4,20},{8,24},{12,28},{16,0},{20,4},{24,8},{28,12},{1,17},{... | collective-permute-start | bytes 73736 | tf_op jit(solution)/shard_map/ppermute | solution.py:538
  22.3 2.3 %collective-permute-start.5 = (bf16[2,8,768]{2,1,0:T(8,128)(2,1)S(1)}, bf16[2,8,768]{2,1,0:T(8,128)(2,1)S(1)}, u32[]{:S(2)}, u32[]{:S(2)}) collective-permute-start(bf16[2,8,768]{2,1,0:T(8,128)(2,1)S(1)} %merge.3.b0), channel_id=1, source_target_pairs={{0,8},{4,12},{8,0},{12,4},{16,24},{20,28},{24,16},{28,20},{1,9},{5... | collective-permute-start | bytes 73736 | tf_op jit(solution)/shard_map/ppermute | solution.py:538
  24.6 1.2 %collective-permute-done.7.b3 = bf16[2,8,768]{2,1,0:T(8,128)(2,1)S(1)} collective-permute-done((bf16[2,8,768]{2,1,0:T(8,128)(2,1)S(1)}, bf16[2,8,768]{2,1,0:T(8,128)(2,1)S(1)}, u32[]{:S(2)}, u32[]{:S(2)}) %collective-permute-start.7) | collective-permute-done | bytes 24608 | tf_op jit(solution)/shard_map/ppermute | solution.py:538
  25.8 0.6 %collective-permute-done.6.b2 = bf16[2,8,768]{2,1,0:T(8,128)(2,1)S(1)} collective-permute-done((bf16[2,8,768]{2,1,0:T(8,128)(2,1)S(1)}, bf16[2,8,768]{2,1,0:T(8,128)(2,1)S(1)}, u32[]{:S(2)}, u32[]{:S(2)}) %collective-permute-start.6) | collective-permute-done | bytes 24608 | tf_op jit(solution)/shard_map/ppermute | solution.py:538
  26.4 0.2 collective-permute-done.5.b1
  26.6 0.7 %combine.1.p0 = bf16[16,384]{1,0:T(8,128)(2,1)S(1)} custom-call(bf16[2,8,768]{2,1,0:T(8,128)(2,1)S(1)} %merge.3.b0, bf16[2,8,768]{2,1,0:T(8,128)(2,1)S(1)} %collective-permute-done.5.b1, bf16[2,8,768]{2,1,0:T(8,128)(2,1)S(1)} %collective-permute-done.6.b2, bf16[2,8,768]{2,1,0:T(8,128)(2,1)S(1)} %collective-permute-done.7.b3, ...), custom_call_target="tpu_custom_call" | custom-call | bytes 696320 | tf_op jit(solution)/shard_map/combine/pallas_call | solution.py:217
  27.4 1.5 %collective-permute-start.10 = (bf16[16,384]{1,0:T(8,128)(2,1)S(1)}, bf16[16,384]{1,0:T(8,128)(2,1)S(1)}, u32[]{:S(2)}, u32[]{:S(2)}) collective-permute-start(bf16[16,384]{1,0:T(8,128)(2,1)S(1)} %combine.1.p0), channel_id=1, source_target_pairs={{0,2},{1,3},{2,0},{3,1},{4,6},{5,7},{6,4},{7,5},{8,10},{9,11},{10,... | collective-permute-start | bytes 36872 | tf_op jit(solution)/shard_map/ppermute | solution.py:538
  28.9 0.0 collective-permute-start.9
  28.9 0.7 %collective-permute-start.8 = (bf16[16,384]{1,0:T(8,128)(2,1)S(1)}, bf16[16,384]{1,0:T(8,128)(2,1)S(1)}, u32[]{:S(2)}, u32[]{:S(2)}) collective-permute-start(bf16[16,384]{1,0:T(8,128)(2,1)S(1)} %combine.1.p0), channel_id=1, source_target_pairs={{0,1},{1,0},{2,3},{3,2},{4,5},{5,4},{6,7},{7,6},{8,9},{9,8},{10,11... | collective-permute-start | bytes 36872 | tf_op jit(solution)/shard_map/ppermute | solution.py:538
  29.5 1.6 %collective-permute-done.10.p3 = bf16[16,384]{1,0:T(8,128)(2,1)S(1)} collective-permute-done((bf16[16,384]{1,0:T(8,128)(2,1)S(1)}, bf16[16,384]{1,0:T(8,128)(2,1)S(1)}, u32[]{:S(2)}, u32[]{:S(2)}) %collective-permute-start.10) | collective-permute-done | bytes 12320 | tf_op jit(solution)/shard_map/ppermute | solution.py:538
  31.1 0.9 %collective-permute-done.9.p2 = bf16[16,384]{1,0:T(8,128)(2,1)S(1)} collective-permute-done((bf16[16,384]{1,0:T(8,128)(2,1)S(1)}, bf16[16,384]{1,0:T(8,128)(2,1)S(1)}, u32[]{:S(2)}, u32[]{:S(2)}) %collective-permute-start.9) | collective-permute-done | bytes 12320 | tf_op jit(solution)/shard_map/ppermute | solution.py:538
  32.0 0.0 collective-permute-done.8.p1
  32.0 2.8 %collective-permute-start.12 = (bf16[16,384]{1,0:T(8,128)(2,1)S(1)}, bf16[16,384]{1,0:T(8,128)(2,1)S(1)}, u32[]{:S(2)}, u32[]{:S(2)}) collective-permute-start(bf16[16,384]{1,0:T(8,128)(2,1)S(1)} %head_sum.1), channel_id=1, source_target_pairs={{1,28},{5,24},{0,20},{4,16},{3,12},{7,8},{2,4},{6,0},{9,29},{13,25... | collective-permute-start | bytes 36872 | tf_op jit(solution)/shard_map/ppermute | solution.py:627
  34.8 0.7 %collective-permute-start.11 = (bf16[16,384]{1,0:T(8,128)(2,1)S(1)}, bf16[16,384]{1,0:T(8,128)(2,1)S(1)}, u32[]{:S(2)}, u32[]{:S(2)}) collective-permute-start(bf16[16,384]{1,0:T(8,128)(2,1)S(1)} %head_sum.1), channel_id=1, source_target_pairs={{1,24},{5,28},{0,16},{4,20},{3,8},{7,12},{2,0},{6,4},{9,25},{13,29... | collective-permute-start | bytes 36872 | tf_op jit(solution)/shard_map/ppermute | solution.py:627
  35.5 1.2 %collective-permute-done.12.flip = bf16[16,384]{1,0:T(8,128)(2,1)S(1)} collective-permute-done((bf16[16,384]{1,0:T(8,128)(2,1)S(1)}, bf16[16,384]{1,0:T(8,128)(2,1)S(1)}, u32[]{:S(2)}, u32[]{:S(2)}) %collective-permute-start.12) | collective-permute-done | bytes 12320 | tf_op jit(solution)/shard_map/ppermute | solution.py:627
  36.7 1.8 %collective-permute-done.11.same = bf16[16,384]{1,0:T(8,128)(2,1)S(1)} collective-permute-done((bf16[16,384]{1,0:T(8,128)(2,1)S(1)}, bf16[16,384]{1,0:T(8,128)(2,1)S(1)}, u32[]{:S(2)}, u32[]{:S(2)}) %collective-permute-start.11) | collective-permute-done | bytes 12320 | tf_op jit(solution)/shard_map/ppermute | solution.py:627
  38.5 0.5 gate_up.1
  39.0 0.2 collective-permute-start.13
  39.2 1.1 %collective-permute-done.13.theirs = bf16[16,2176]{1,0:T(8,128)(2,1)S(1)} collective-permute-done((bf16[16,2176]{1,0:T(8,128)(2,1)S(1)}, bf16[16,2176]{1,0:T(8,128)(2,1)S(1)}, u32[]{:S(2)}, u32[]{:S(2)}) %collective-permute-start.13) | collective-permute-done | bytes 69664 | tf_op jit(solution)/shard_map/ppermute | solution.py:538
  40.3 0.1 core_sum.1.mine
  40.4 1.9 %collective-permute-start.14 = (bf16[16,2176]{1,0:T(8,128)(2,1)S(1)}, bf16[16,2176]{1,0:T(8,128)(2,1)S(1)}, u32[]{:S(2)}, u32[]{:S(2)}) collective-permute-start(bf16[16,2176]{1,0:T(8,128)(2,1)S(1)} %core_sum.1.mine), channel_id=1, source_target_pairs={{0,2},{1,3},{2,0},{3,1},{4,6},{5,7},{6,4},{7,5},{8,10},{9,11},{10,... | collective-permute-start | bytes 208904 | tf_op jit(solution)/shard_map/ppermute | solution.py:538
  42.3 2.7 %collective-permute-done.14.theirs = bf16[16,2176]{1,0:T(8,128)(2,1)S(1)} collective-permute-done((bf16[16,2176]{1,0:T(8,128)(2,1)S(1)}, bf16[16,2176]{1,0:T(8,128)(2,1)S(1)}, u32[]{:S(2)}, u32[]{:S(2)}) %collective-permute-start.14) | collective-permute-done | bytes 69664 | tf_op jit(solution)/shard_map/ppermute | solution.py:538
  45.0 0.0 copy-done.2
  45.0 0.4 down.1
  45.4 8.4 %all_to_all.5.parts = bf16[8,2,768]{2,1,0:T(2,128)(2,1)S(1)} all-to-all(bf16[8,2,768]{2,1,0:T(2,128)(2,1)S(1)} %down.1), channel_id=1, replica_groups={{28,24,20,16,12,8,4,0},{29,25,21,17,13,9,5,1},{30,26,22,18,14,10,6,2},{..., dimensions={0} | all-to-all | bytes 49152 | tf_op jit(solution)/shard_map/all_to_all | solution.py:653
  53.8 0.6 %final.1 = bf16[2,768]{1,0:T(2,128)(2,1)} custom-call(f32[2,768]{1,0:T(2,128)S(1)} %get-tuple-element.21.own, bf16[8,2,768]{2,1,0:T(2,128)(2,1)S(1)} %all_to_all.5.parts), custom_call_target="tpu_custom_call" | custom-call | bytes 30720 | tf_op jit(solution)/shard_map/final/pallas_call | solution.py:217
  (13 shorter events, 0.0 us)
Async XLA Ops:
  0.0 15.2 %copy-start.1 = (bf16[5,256,768]{2,1,0:T(8,128)(2,1)S(1)}, bf16[5,256,768]{2,1,0:T(8,128)(2,1)}, u32[]{:S(2)}) copy-start(bf16[5,256,768]{2,1,0:T(8,128)(2,1)} %values.1) | copy-start | bytes 5898244
  0.0 15.2 %copy-start = (bf16[5,256,768]{2,1,0:T(8,128)(2,1)S(1)}, bf16[5,256,768]{2,1,0:T(8,128)(2,1)}, u32[]{:S(2)}) copy-start(bf16[5,256,768]{2,1,0:T(8,128)(2,1)} %keys.1) | copy-start | bytes 5898244
  1.6 4.9 %collective-permute-start = (bf16[2,1664]{1,0:T(2,128)(2,1)}, bf16[2,1664]{1,0:T(2,128)(2,1)S(1)}, u32[]{:S(2)}, u32[]{:S(2)}) collective-permute-start(bf16[2,1664]{1,0:T(2,128)(2,1)} %get-tuple-element.14.packed), channel_id=1, source_target_pairs={{0,4},{4,0},{8,12},{12,8},{16,20},{20,16},{24,28},{28,24},{1,5},{5... | collective-permute-start | bytes 19976 | tf_op jit(solution)/shard_map/ppermute | solution.py:538
  4.7 0.7 %copy-start.6 = (bf16[2,1664]{1,0:T(2,128)(2,1)S(1)}, bf16[2,1664]{1,0:T(2,128)(2,1)}, u32[]{:S(2)}) copy-start(bf16[2,1664]{1,0:T(2,128)(2,1)} %get-tuple-element.14.packed) | copy-start | bytes 19972
  5.4 0.7 %copy-start.7 = (bf16[2,1536]{1,0:T(2,128)(2,1)S(1)}, bf16[2,1536]{1,0:T(2,128)(2,1)}, u32[]{:S(2)}) copy-start(bf16[2,1536]{1,0:T(2,128)(2,1)} %get-tuple-element.15.new) | copy-start | bytes 18436
  6.5 5.8 %collective-permute-start.3 = (bf16[2,2,1664]{2,1,0:T(2,128)(2,1)S(1)}, bf16[2,2,1664]{2,1,0:T(2,128)(2,1)S(1)}, u32[]{:S(2)}, u32[]{:S(2)}) collective-permute-start(bf16[2,2,1664]{2,1,0:T(2,128)(2,1)S(1)} %merge.2.a0), channel_id=1, source_target_pairs={{0,24},{4,28},{8,16},{12,20},{16,8},{20,12},{24,0},{28,4},{1,25},{... | collective-permute-start | bytes 39944 | tf_op jit(solution)/shard_map/ppermute | solution.py:538
  10.6 4.6 %collective-permute-start.2 = (bf16[2,2,1664]{2,1,0:T(2,128)(2,1)S(1)}, bf16[2,2,1664]{2,1,0:T(2,128)(2,1)S(1)}, u32[]{:S(2)}, u32[]{:S(2)}) collective-permute-start(bf16[2,2,1664]{2,1,0:T(2,128)(2,1)S(1)} %merge.2.a0), channel_id=1, source_target_pairs={{0,16},{4,20},{8,24},{12,28},{16,0},{20,4},{24,8},{28,12},{1,17},{... | collective-permute-start | bytes 39944 | tf_op jit(solution)/shard_map/ppermute | solution.py:538
  10.6 4.6 %collective-permute-start.1 = (bf16[2,2,1664]{2,1,0:T(2,128)(2,1)S(1)}, bf16[2,2,1664]{2,1,0:T(2,128)(2,1)S(1)}, u32[]{:S(2)}, u32[]{:S(2)}) collective-permute-start(bf16[2,2,1664]{2,1,0:T(2,128)(2,1)S(1)} %merge.2.a0), channel_id=1, source_target_pairs={{0,8},{4,12},{8,0},{12,4},{16,24},{20,28},{24,16},{28,20},{1,9},{5... | collective-permute-start | bytes 39944 | tf_op jit(solution)/shard_map/ppermute | solution.py:538
  15.2 11.4 %copy-start.5 = (bf16[768,384]{1,0:T(8,128)(2,1)S(1)}, bf16[768,384]{1,0:T(8,128)(2,1)}, u32[]{:S(2)}) copy-start(bf16[768,384]{1,0:T(8,128)(2,1)} %weight.2) | copy-start | bytes 1769476
  15.2 20.2 %copy-start.8 = (bf16[768]{0:T(1024)(128)(2,1)S(1)}, bf16[768]{0:T(1024)(128)(2,1)}, u32[]{:S(2)}) copy-start(bf16[768]{0:T(1024)(128)(2,1)} %param.22) | copy-start | bytes 4612
  15.3 23.3 %copy-start.3 = (bf16[768,1024]{1,0:T(8,128)(2,1)S(1)}, bf16[768,1024]{1,0:T(8,128)(2,1)}, u32[]{:S(2)}) copy-start(bf16[768,1024]{1,0:T(8,128)(2,1)} %gate.1) | copy-start | bytes 4718596
  15.3 23.2 %copy-start.4 = (bf16[768,1024]{1,0:T(8,128)(2,1)S(1)}, bf16[768,1024]{1,0:T(8,128)(2,1)}, u32[]{:S(2)}) copy-start(bf16[768,1024]{1,0:T(8,128)(2,1)} %up.1) | copy-start | bytes 4718596
  16.4 3.8 %collective-permute-start.4 = (bf16[8,768]{1,0:T(8,128)(2,1)S(1)}, bf16[8,768]{1,0:T(8,128)(2,1)S(1)}, u32[]{:S(2)}, u32[]{:S(2)}) collective-permute-start(bf16[8,768]{1,0:T(8,128)(2,1)S(1)} %get-tuple-element.18.mine), channel_id=1, source_target_pairs={{0,4},{4,0},{8,12},{12,8},{16,20},{20,16},{24,28},{28,24},{1,5},{5... | collective-permute-start | bytes 36872 | tf_op jit(solution)/shard_map/ppermute | solution.py:538
  20.2 5.6 %collective-permute-start.7 = (bf16[2,8,768]{2,1,0:T(8,128)(2,1)S(1)}, bf16[2,8,768]{2,1,0:T(8,128)(2,1)S(1)}, u32[]{:S(2)}, u32[]{:S(2)}) collective-permute-start(bf16[2,8,768]{2,1,0:T(8,128)(2,1)S(1)} %merge.3.b0), channel_id=1, source_target_pairs={{0,24},{4,28},{8,16},{12,20},{16,8},{20,12},{24,0},{28,4},{1,25},{... | collective-permute-start | bytes 73736 | tf_op jit(solution)/shard_map/ppermute | solution.py:538
  21.6 4.7 %collective-permute-start.6 = (bf16[2,8,768]{2,1,0:T(8,128)(2,1)S(1)}, bf16[2,8,768]{2,1,0:T(8,128)(2,1)S(1)}, u32[]{:S(2)}, u32[]{:S(2)}) collective-permute-start(bf16[2,8,768]{2,1,0:T(8,128)(2,1)S(1)} %merge.3.b0), channel_id=1, source_target_pairs={{0,16},{4,20},{8,24},{12,28},{16,0},{20,4},{24,8},{28,12},{1,17},{... | collective-permute-start | bytes 73736 | tf_op jit(solution)/shard_map/ppermute | solution.py:538
  22.3 4.4 %collective-permute-start.5 = (bf16[2,8,768]{2,1,0:T(8,128)(2,1)S(1)}, bf16[2,8,768]{2,1,0:T(8,128)(2,1)S(1)}, u32[]{:S(2)}, u32[]{:S(2)}) collective-permute-start(bf16[2,8,768]{2,1,0:T(8,128)(2,1)S(1)} %merge.3.b0), channel_id=1, source_target_pairs={{0,8},{4,12},{8,0},{12,4},{16,24},{20,28},{24,16},{28,20},{1,9},{5... | collective-permute-start | bytes 73736 | tf_op jit(solution)/shard_map/ppermute | solution.py:538
  27.4 3.7 %collective-permute-start.10 = (bf16[16,384]{1,0:T(8,128)(2,1)S(1)}, bf16[16,384]{1,0:T(8,128)(2,1)S(1)}, u32[]{:S(2)}, u32[]{:S(2)}) collective-permute-start(bf16[16,384]{1,0:T(8,128)(2,1)S(1)} %combine.1.p0), channel_id=1, source_target_pairs={{0,2},{1,3},{2,0},{3,1},{4,6},{5,7},{6,4},{7,5},{8,10},{9,11},{10,... | collective-permute-start | bytes 36872 | tf_op jit(solution)/shard_map/ppermute | solution.py:538
  28.9 3.1 %collective-permute-start.9 = (bf16[16,384]{1,0:T(8,128)(2,1)S(1)}, bf16[16,384]{1,0:T(8,128)(2,1)S(1)}, u32[]{:S(2)}, u32[]{:S(2)}) collective-permute-start(bf16[16,384]{1,0:T(8,128)(2,1)S(1)} %combine.1.p0), channel_id=1, source_target_pairs={{0,3},{1,2},{2,1},{3,0},{4,7},{5,6},{6,5},{7,4},{8,11},{9,10},{10,... | collective-permute-start | bytes 36872 | tf_op jit(solution)/shard_map/ppermute | solution.py:538
  28.9 3.1 %collective-permute-start.8 = (bf16[16,384]{1,0:T(8,128)(2,1)S(1)}, bf16[16,384]{1,0:T(8,128)(2,1)S(1)}, u32[]{:S(2)}, u32[]{:S(2)}) collective-permute-start(bf16[16,384]{1,0:T(8,128)(2,1)S(1)} %combine.1.p0), channel_id=1, source_target_pairs={{0,1},{1,0},{2,3},{3,2},{4,5},{5,4},{6,7},{7,6},{8,9},{9,8},{10,11... | collective-permute-start | bytes 36872 | tf_op jit(solution)/shard_map/ppermute | solution.py:538
  32.0 4.7 %collective-permute-start.12 = (bf16[16,384]{1,0:T(8,128)(2,1)S(1)}, bf16[16,384]{1,0:T(8,128)(2,1)S(1)}, u32[]{:S(2)}, u32[]{:S(2)}) collective-permute-start(bf16[16,384]{1,0:T(8,128)(2,1)S(1)} %head_sum.1), channel_id=1, source_target_pairs={{1,28},{5,24},{0,20},{4,16},{3,12},{7,8},{2,4},{6,0},{9,29},{13,25... | collective-permute-start | bytes 36872 | tf_op jit(solution)/shard_map/ppermute | solution.py:627
  34.8 3.7 %collective-permute-start.11 = (bf16[16,384]{1,0:T(8,128)(2,1)S(1)}, bf16[16,384]{1,0:T(8,128)(2,1)S(1)}, u32[]{:S(2)}, u32[]{:S(2)}) collective-permute-start(bf16[16,384]{1,0:T(8,128)(2,1)S(1)} %head_sum.1), channel_id=1, source_target_pairs={{1,24},{5,28},{0,16},{4,20},{3,8},{7,12},{2,0},{6,4},{9,25},{13,29... | collective-permute-start | bytes 36872 | tf_op jit(solution)/shard_map/ppermute | solution.py:627
  38.5 6.5 %copy-start.2 = (bf16[1024,768]{1,0:T(8,128)(2,1)S(1)}, bf16[1024,768]{1,0:T(8,128)(2,1)}, u32[]{:S(2)}) copy-start(bf16[1024,768]{1,0:T(8,128)(2,1)} %weight.3) | copy-start | bytes 4718596
  39.0 1.3 %collective-permute-start.13 = (bf16[16,2176]{1,0:T(8,128)(2,1)S(1)}, bf16[16,2176]{1,0:T(8,128)(2,1)S(1)}, u32[]{:S(2)}, u32[]{:S(2)}) collective-permute-start(bf16[16,2176]{1,0:T(8,128)(2,1)S(1)} %get-tuple-element.22.mine), channel_id=1, source_target_pairs={{0,1},{1,0},{2,3},{3,2},{4,5},{5,4},{6,7},{7,6},{8,9},{9,8},{10,11... | collective-permute-start | bytes 208904 | tf_op jit(solution)/shard_map/ppermute | solution.py:538
  40.4 4.6 %collective-permute-start.14 = (bf16[16,2176]{1,0:T(8,128)(2,1)S(1)}, bf16[16,2176]{1,0:T(8,128)(2,1)S(1)}, u32[]{:S(2)}, u32[]{:S(2)}) collective-permute-start(bf16[16,2176]{1,0:T(8,128)(2,1)S(1)} %core_sum.1.mine), channel_id=1, source_target_pairs={{0,2},{1,3},{2,0},{3,1},{4,6},{5,7},{6,4},{7,5},{8,10},{9,11},{10,... | collective-permute-start | bytes 208904 | tf_op jit(solution)/shard_map/ppermute | solution.py:538

commit v11 on v10

--- a/solution.py
+++ b/solution.py
@@ -470,19 +470,18 @@
     ).astype(BF16)
 
 
-def sum_kernel(p0, p1, p2, p3, total):
-    total[...] = (
-        (p0[...].astype(F32) + p1[...].astype(F32)) + (p2[...].astype(F32) + p3[...].astype(F32))
-    ).astype(BF16)
-
-
-def gate_up_kernel(same, flip, all_input, gain, gate, up, sums, own, scr):
+def sum_kernel(p0, p1, total):
+    total[...] = (p0[...].astype(F32) + p1[...].astype(F32)).astype(BF16)
+
+
+def gate_up_kernel(s0, s1, f0, f1, all_input, gain, gate, up, sums, own, scr):
     me = lax.axis_index("pool")
     odd = me % 2 == 1
-    part = same.shape[1]
+    part = s0.shape[1]
     ff = gate.shape[1]
     rows = own.shape[0]
-    near, far = same[...].astype(F32), flip[...].astype(F32)
+    near = round_low(s0[...].astype(F32) + s1[...].astype(F32))
+    far = round_low(f0[...].astype(F32) + f1[...].astype(F32))
     scr[:, :part] = all_input[:, :part] + jnp.where(odd, far, near)
     scr[:, part:] = all_input[:, part:] + jnp.where(odd, near, far)
     residual = scr[...]
@@ -613,18 +612,21 @@
         sum_kernel,
         "head_sum",
         [((requests, part_cols), BF16)],
-        [head_part] + [flip(head_part, "mlp", step) for step in (1, 3, 2)],
+        [head_part, flip(head_part, "mlp", 1)],
     )
     pieces = []
-    for turn in range(2):
-        route = []
-        for m in range(mlp):
-            by_distance = sorted(range(4), key=lambda z: (-abs(z - m), z))
-            for z, step in zip(by_distance, (1, 0, 3, 2) if m % 2 == 0 else (0, 1, 2, 3)):
-                for y in range(2):
-                    source = (m * 2 + y) * mlp + (m ^ step)
-                    route.append((source, (z * 2 + (y ^ turn)) * mlp + m))
-        pieces.append(lax.ppermute(head_sum, ("pool", "mlp"), route))
+    for turn_y in range(2):
+        for turn_x in range(2):
+            route = []
+            for m in range(mlp):
+                by_distance = sorted(range(4), key=lambda z: (-abs(z - m), z))
+                for place, z in enumerate(by_distance):
+                    x = m // 2 ^ turn_x ^ place // 2
+                    core = 1 - place % 2
+                    for y in range(2):
+                        source = (m * 2 + y) * mlp + x * 2 + core
+                        route.append((source, (z * 2 + (y ^ turn_y)) * mlp + m))
+            pieces.append(lax.ppermute(head_sum, ("pool", "mlp"), route))
     sums, own_residual = call(
         gate_up_kernel,
         "gate_up",

time: 54.7 us -> 56.9 us (1.040)
  starting transfers between devices: 21.4 us -> 24.8 us
  waiting for transfers between devices: 17.8 us -> 15.9 us
  blocking collectives: 8.36 us -> 9.05 us
    ppermute x2 -> x4, starting transfers between devices: 3.45 us -> 7.6 us  [per_device_small(): pieces.append(lax.ppermute(head_sum, ('pool', 'mlp'), route))]
    ppermute x13 -> x11, waiting for transfers between devices: 14.8 us -> 13.3 us  [flip(): lax.ppermute(values, axis, [(index, index ^ step) for index in range(size)])]
    ppermute x13 -> x11, starting transfers between devices: 17.9 us -> 17.2 us  [flip(): lax.ppermute(values, axis, [(index, index ^ step) for index in range(size)])]
    all_to_all x1, blocking collectives: 8.36 us -> 9.05 us  [per_device_small(): lax.all_to_all(down, 'pool', 0, 0, axis_index_groups=[backwards])]
    ppermute x2 -> x4, waiting for transfers between devices: 3.02 us -> 2.6 us  [per_device_small(): pieces.append(lax.ppermute(head_sum, ('pool', 'mlp'), route))]
  transfers between devices with their start and end apart: 15 -> 15, of which waited for: 13 -> 11; matrix products, arithmetic and copies ran while one was open for 0% -> 0% of each run, Pallas kernels for 0% -> 0%
where the time goes in v11:
time: 56.9 us; the launch traced here: 56.6 us
  starting transfers between devices  24.8 us (44%)
  waiting for transfers between devices  15.9 us (28%)
  blocking collectives  9.05 us (16%)
  Pallas kernels  5.25 us (9%)
  local copies, waits for them, and re-layouts  1.46 us (3%)
    ppermute x11, starting transfers between devices, flip(): lax.ppermute(values, axis, [(index, index ^ step) for index in range(size)])  17.2 us
    ppermute x11, waiting for transfers between devices, flip(): lax.ppermute(values, axis, [(index, index ^ step) for index in range(size)])  13.3 us
    all_to_all x1, blocking collectives, per_device_small(): lax.all_to_all(down, 'pool', 0, 0, axis_index_groups=[backwards])  9.05 us
    ppermute x4, starting transfers between devices, per_device_small(): pieces.append(lax.ppermute(head_sum, ('pool', 'mlp'), route))  7.6 us
    pallas_call x11, Pallas kernels, call(): pl.pallas_call(kernel, out_shape=[jax.ShapeDtypeStruct(shape, dtype) for...  5.25 us
    ppermute x4, waiting for transfers between devices, per_device_small(): pieces.append(lax.ppermute(head_sum, ('pool', 'mlp'), route))  2.6 us
    unnamed x18, local copies, waits for them, and re-layouts  1.45 us
  transfers between devices with their start and end apart: 15, of which 11 were waited for; matrix products, arithmetic and copies ran while one was open for 0% of the time, Pallas kernels for 0%

profile of v11, /device:TPU:0, one launch (start us, length us, event | category | flops | bytes accessed | tf_op | source)
XLA Modules:
  0.0 56.6 jit_solution(3307045341503021173)
XLA Ops:
  0.0 1.6 %rotary.1 = (bf16[2,1664]{1,0:T(2,128)(2,1)}, bf16[2,1536]{1,0:T(2,128)(2,1)}) custom-call(s32[2,8]{1,0:T(2,128)} %refs_0_.1, s32[2]{0:T(128)} %refs_1_.1, bf16[2,768]{1,0:T(2,128)(2,1)} %refs_2_.1, bf16[2,768]{1,0:T(2,128)(2,1)} %refs_3_.1, bf16[2,768]{1,0:T(2,128)(2,1)} %refs_4_.1, bf16[2,768]{1,0:T(2,128)(2,1)} %refs_5_.1, bf16[5,256,768]{2,1,0:T(8,128)(2,1)} %keys.1, ...), custom_call_target="tpu_custom_call" | custom-call | bytes 3944520 | tf_op jit(solution)/shard_map/rotary/pallas_call | solution.py:217
  1.6 3.0 %collective-permute-start = (bf16[2,1664]{1,0:T(2,128)(2,1)}, bf16[2,1664]{1,0:T(2,128)(2,1)S(1)}, u32[]{:S(2)}, u32[]{:S(2)}) collective-permute-start(bf16[2,1664]{1,0:T(2,128)(2,1)} %get-tuple-element.14.packed), channel_id=1, source_target_pairs={{0,4},{4,0},{8,12},{12,8},{16,20},{20,16},{24,28},{28,24},{1,5},{5... | collective-permute-start | bytes 19976 | tf_op jit(solution)/shard_map/ppermute | solution.py:537
  4.7 0.7 %copy-done.6 = bf16[2,1664]{1,0:T(2,128)(2,1)S(1)} copy-done((bf16[2,1664]{1,0:T(2,128)(2,1)S(1)}, bf16[2,1664]{1,0:T(2,128)(2,1)}, u32[]{:S(2)}) %copy-start.6) | copy-done | bytes 6680
  5.4 0.7 %copy-done.7 = bf16[2,1536]{1,0:T(2,128)(2,1)S(1)} copy-done((bf16[2,1536]{1,0:T(2,128)(2,1)S(1)}, bf16[2,1536]{1,0:T(2,128)(2,1)}, u32[]{:S(2)}) %copy-start.7) | copy-done | bytes 6168
  6.1 0.1 carry.1
  6.2 0.3 collective-permute-done.theirs
  6.5 4.1 %collective-permute-start.3 = (bf16[2,2,1664]{2,1,0:T(2,128)(2,1)S(1)}, bf16[2,2,1664]{2,1,0:T(2,128)(2,1)S(1)}, u32[]{:S(2)}, u32[]{:S(2)}) collective-permute-start(bf16[2,2,1664]{2,1,0:T(2,128)(2,1)S(1)} %merge.2.a0), channel_id=1, source_target_pairs={{0,24},{4,28},{8,16},{12,20},{16,8},{20,12},{24,0},{28,4},{1,25},{... | collective-permute-start | bytes 39944 | tf_op jit(solution)/shard_map/ppermute | solution.py:537
  10.6 0.0 collective-permute-start.2
  10.6 0.6 collective-permute-start.1
  11.2 1.1 %collective-permute-done.3.a3 = bf16[2,2,1664]{2,1,0:T(2,128)(2,1)S(1)} collective-permute-done((bf16[2,2,1664]{2,1,0:T(2,128)(2,1)S(1)}, bf16[2,2,1664]{2,1,0:T(2,128)(2,1)S(1)}, u32[]{:S(2)}, u32[]{:S(2)}) %collective-permute-start.3) | collective-permute-done | bytes 13344 | tf_op jit(solution)/shard_map/ppermute | solution.py:537
  12.3 2.9 %collective-permute-done.2.a2 = bf16[2,2,1664]{2,1,0:T(2,128)(2,1)S(1)} collective-permute-done((bf16[2,2,1664]{2,1,0:T(2,128)(2,1)S(1)}, bf16[2,2,1664]{2,1,0:T(2,128)(2,1)S(1)}, u32[]{:S(2)}, u32[]{:S(2)}) %collective-permute-start.2) | collective-permute-done | bytes 13344 | tf_op jit(solution)/shard_map/ppermute | solution.py:537
  15.2 0.0 collective-permute-done.1.a1
  15.2 0.0 copy-done.1
  15.2 0.0 copy-done
  15.2 0.0 copy-start.5
  15.2 0.0 copy-start.8
  15.3 0.0 copy-start.3
  15.3 0.0 copy-start.4
  15.3 1.1 %attend.1 = (bf16[8,768]{1,0:T(8,128)(2,1)S(1)}, f32[16,768]{1,0:T(8,128)S(1)}, f32[16,128]{1,0:T(8,128)S(1)}) custom-call(bf16[2,2,1664]{2,1,0:T(2,128)(2,1)S(1)} %merge.2.a0, bf16[2,2,1664]{2,1,0:T(2,128)(2,1)S(1)} %collective-permute-done.1.a1, bf16[2,2,1664]{2,1,0:T(2,128)(2,1)S(1)} %collective-permute-done.2.a2, ...), custom_call_target="tpu_custom_call" | custom-call | bytes 4014080 | tf_op jit(solution)/shard_map/attend/pallas_call | solution.py:217
  16.4 1.6 %collective-permute-start.4 = (bf16[8,768]{1,0:T(8,128)(2,1)S(1)}, bf16[8,768]{1,0:T(8,128)(2,1)S(1)}, u32[]{:S(2)}, u32[]{:S(2)}) collective-permute-start(bf16[8,768]{1,0:T(8,128)(2,1)S(1)} %get-tuple-element.18.mine), channel_id=1, source_target_pairs={{0,4},{4,0},{8,12},{12,8},{16,20},{20,16},{24,28},{28,24},{1,5},{5... | collective-permute-start | bytes 36872 | tf_op jit(solution)/shard_map/ppermute | solution.py:537
  18.0 2.2 %collective-permute-done.4.theirs = bf16[8,768]{1,0:T(8,128)(2,1)S(1)} collective-permute-done((bf16[8,768]{1,0:T(8,128)(2,1)S(1)}, bf16[8,768]{1,0:T(8,128)(2,1)S(1)}, u32[]{:S(2)}, u32[]{:S(2)}) %collective-permute-start.4) | collective-permute-done | bytes 12320 | tf_op jit(solution)/shard_map/ppermute | solution.py:537
  20.2 1.4 %collective-permute-start.7 = (bf16[2,8,768]{2,1,0:T(8,128)(2,1)S(1)}, bf16[2,8,768]{2,1,0:T(8,128)(2,1)S(1)}, u32[]{:S(2)}, u32[]{:S(2)}) collective-permute-start(bf16[2,8,768]{2,1,0:T(8,128)(2,1)S(1)} %merge.3.b0), channel_id=1, source_target_pairs={{0,24},{4,28},{8,16},{12,20},{16,8},{20,12},{24,0},{28,4},{1,25},{... | collective-permute-start | bytes 73736 | tf_op jit(solution)/shard_map/ppermute | solution.py:537
  21.6 0.6 %collective-permute-start.6 = (bf16[2,8,768]{2,1,0:T(8,128)(2,1)S(1)}, bf16[2,8,768]{2,1,0:T(8,128)(2,1)S(1)}, u32[]{:S(2)}, u32[]{:S(2)}) collective-permute-start(bf16[2,8,768]{2,1,0:T(8,128)(2,1)S(1)} %merge.3.b0), channel_id=1, source_target_pairs={{0,16},{4,20},{8,24},{12,28},{16,0},{20,4},{24,8},{28,12},{1,17},{... | collective-permute-start | bytes 73736 | tf_op jit(solution)/shard_map/ppermute | solution.py:537
  22.3 2.3 %collective-permute-start.5 = (bf16[2,8,768]{2,1,0:T(8,128)(2,1)S(1)}, bf16[2,8,768]{2,1,0:T(8,128)(2,1)S(1)}, u32[]{:S(2)}, u32[]{:S(2)}) collective-permute-start(bf16[2,8,768]{2,1,0:T(8,128)(2,1)S(1)} %merge.3.b0), channel_id=1, source_target_pairs={{0,8},{4,12},{8,0},{12,4},{16,24},{20,28},{24,16},{28,20},{1,9},{5... | collective-permute-start | bytes 73736 | tf_op jit(solution)/shard_map/ppermute | solution.py:537
  24.6 1.2 %collective-permute-done.7.b3 = bf16[2,8,768]{2,1,0:T(8,128)(2,1)S(1)} collective-permute-done((bf16[2,8,768]{2,1,0:T(8,128)(2,1)S(1)}, bf16[2,8,768]{2,1,0:T(8,128)(2,1)S(1)}, u32[]{:S(2)}, u32[]{:S(2)}) %collective-permute-start.7) | collective-permute-done | bytes 24608 | tf_op jit(solution)/shard_map/ppermute | solution.py:537
  25.8 0.6 %collective-permute-done.6.b2 = bf16[2,8,768]{2,1,0:T(8,128)(2,1)S(1)} collective-permute-done((bf16[2,8,768]{2,1,0:T(8,128)(2,1)S(1)}, bf16[2,8,768]{2,1,0:T(8,128)(2,1)S(1)}, u32[]{:S(2)}, u32[]{:S(2)}) %collective-permute-start.6) | collective-permute-done | bytes 24608 | tf_op jit(solution)/shard_map/ppermute | solution.py:537
  26.4 0.2 collective-permute-done.5.b1
  26.6 0.7 %combine.1.p0 = bf16[16,384]{1,0:T(8,128)(2,1)S(1)} custom-call(bf16[2,8,768]{2,1,0:T(8,128)(2,1)S(1)} %merge.3.b0, bf16[2,8,768]{2,1,0:T(8,128)(2,1)S(1)} %collective-permute-done.5.b1, bf16[2,8,768]{2,1,0:T(8,128)(2,1)S(1)} %collective-permute-done.6.b2, bf16[2,8,768]{2,1,0:T(8,128)(2,1)S(1)} %collective-permute-done.7.b3, ...), custom_call_target="tpu_custom_call" | custom-call | bytes 696320 | tf_op jit(solution)/shard_map/combine/pallas_call | solution.py:217
  27.4 0.1 collective-permute-start.8
  27.4 1.2 %collective-permute-done.8.p1 = bf16[16,384]{1,0:T(8,128)(2,1)S(1)} collective-permute-done((bf16[16,384]{1,0:T(8,128)(2,1)S(1)}, bf16[16,384]{1,0:T(8,128)(2,1)S(1)}, u32[]{:S(2)}, u32[]{:S(2)}) %collective-permute-start.8) | collective-permute-done | bytes 12320 | tf_op jit(solution)/shard_map/ppermute | solution.py:537
  28.6 1.5 %collective-permute-start.12 = (bf16[16,384]{1,0:T(8,128)(2,1)S(1)}, bf16[16,384]{1,0:T(8,128)(2,1)S(1)}, u32[]{:S(2)}, u32[]{:S(2)}) collective-permute-start(bf16[16,384]{1,0:T(8,128)(2,1)S(1)} %head_sum.1), channel_id=1, source_target_pairs={{3,28},{7,24},{2,20},{6,16},{1,12},{5,8},{0,4},{4,0},{11,29},{15,2... | collective-permute-start | bytes 36872 | tf_op jit(solution)/shard_map/ppermute | solution.py:629
  30.1 3.5 %collective-permute-start.11 = (bf16[16,384]{1,0:T(8,128)(2,1)S(1)}, bf16[16,384]{1,0:T(8,128)(2,1)S(1)}, u32[]{:S(2)}, u32[]{:S(2)}) collective-permute-start(bf16[16,384]{1,0:T(8,128)(2,1)S(1)} %head_sum.1), channel_id=1, source_target_pairs={{1,28},{5,24},{0,20},{4,16},{3,12},{7,8},{2,4},{6,0},{9,29},{13,25... | collective-permute-start | bytes 36872 | tf_op jit(solution)/shard_map/ppermute | solution.py:629
  33.6 0.7 %collective-permute-start.10 = (bf16[16,384]{1,0:T(8,128)(2,1)S(1)}, bf16[16,384]{1,0:T(8,128)(2,1)S(1)}, u32[]{:S(2)}, u32[]{:S(2)}) collective-permute-start(bf16[16,384]{1,0:T(8,128)(2,1)S(1)} %head_sum.1), channel_id=1, source_target_pairs={{3,24},{7,28},{2,16},{6,20},{1,8},{5,12},{0,0},{4,4},{11,25},{15,2... | collective-permute-start | bytes 36872 | tf_op jit(solution)/shard_map/ppermute | solution.py:629
  34.3 1.9 %collective-permute-start.9 = (bf16[16,384]{1,0:T(8,128)(2,1)S(1)}, bf16[16,384]{1,0:T(8,128)(2,1)S(1)}, u32[]{:S(2)}, u32[]{:S(2)}) collective-permute-start(bf16[16,384]{1,0:T(8,128)(2,1)S(1)} %head_sum.1), channel_id=1, source_target_pairs={{1,24},{5,28},{0,16},{4,20},{3,8},{7,12},{2,0},{6,4},{9,25},{13,29... | collective-permute-start | bytes 36872 | tf_op jit(solution)/shard_map/ppermute | solution.py:629
  36.2 0.0 collective-permute-done.12.f1
  36.2 0.0 collective-permute-done.11.f0
  36.2 0.0 collective-permute-done.10.s1
  36.2 2.6 %collective-permute-done.9.s0 = bf16[16,384]{1,0:T(8,128)(2,1)S(1)} collective-permute-done((bf16[16,384]{1,0:T(8,128)(2,1)S(1)}, bf16[16,384]{1,0:T(8,128)(2,1)S(1)}, u32[]{:S(2)}, u32[]{:S(2)}) %collective-permute-start.9) | collective-permute-done | bytes 12320 | tf_op jit(solution)/shard_map/ppermute | solution.py:629
  38.8 0.0 copy-done.4
  38.8 0.5 gate_up.1
  39.3 1.6 %collective-permute-start.13 = (bf16[16,2176]{1,0:T(8,128)(2,1)S(1)}, bf16[16,2176]{1,0:T(8,128)(2,1)S(1)}, u32[]{:S(2)}, u32[]{:S(2)}) collective-permute-start(bf16[16,2176]{1,0:T(8,128)(2,1)S(1)} %get-tuple-element.22.mine), channel_id=1, source_target_pairs={{0,1},{1,0},{2,3},{3,2},{4,5},{5,4},{6,7},{7,6},{8,9},{9,8},{10,11... | collective-permute-start | bytes 208904 | tf_op jit(solution)/shard_map/ppermute | solution.py:537
  40.9 0.9 %collective-permute-done.13.theirs = bf16[16,2176]{1,0:T(8,128)(2,1)S(1)} collective-permute-done((bf16[16,2176]{1,0:T(8,128)(2,1)S(1)}, bf16[16,2176]{1,0:T(8,128)(2,1)S(1)}, u32[]{:S(2)}, u32[]{:S(2)}) %collective-permute-start.13) | collective-permute-done | bytes 69664 | tf_op jit(solution)/shard_map/ppermute | solution.py:537
  41.8 0.1 core_sum.1.mine
  41.9 1.9 %collective-permute-start.14 = (bf16[16,2176]{1,0:T(8,128)(2,1)S(1)}, bf16[16,2176]{1,0:T(8,128)(2,1)S(1)}, u32[]{:S(2)}, u32[]{:S(2)}) collective-permute-start(bf16[16,2176]{1,0:T(8,128)(2,1)S(1)} %core_sum.1.mine), channel_id=1, source_target_pairs={{0,2},{1,3},{2,0},{3,1},{4,6},{5,7},{6,4},{7,5},{8,10},{9,11},{10,... | collective-permute-start | bytes 208904 | tf_op jit(solution)/shard_map/ppermute | solution.py:537
  43.8 2.7 %collective-permute-done.14.theirs = bf16[16,2176]{1,0:T(8,128)(2,1)S(1)} collective-permute-done((bf16[16,2176]{1,0:T(8,128)(2,1)S(1)}, bf16[16,2176]{1,0:T(8,128)(2,1)S(1)}, u32[]{:S(2)}, u32[]{:S(2)}) %collective-permute-start.14) | collective-permute-done | bytes 69664 | tf_op jit(solution)/shard_map/ppermute | solution.py:537
  46.5 0.4 down.1
  46.9 9.1 %all_to_all.5.parts = bf16[8,2,768]{2,1,0:T(2,128)(2,1)S(1)} all-to-all(bf16[8,2,768]{2,1,0:T(2,128)(2,1)S(1)} %down.1), channel_id=1, replica_groups={{28,24,20,16,12,8,4,0},{29,25,21,17,13,9,5,1},{30,26,22,18,14,10,6,2},{..., dimensions={0} | all-to-all | bytes 49152 | tf_op jit(solution)/shard_map/all_to_all | solution.py:655
  56.0 0.6 %final.1 = bf16[2,768]{1,0:T(2,128)(2,1)} custom-call(f32[2,768]{1,0:T(2,128)S(1)} %get-tuple-element.21.own, bf16[8,2,768]{2,1,0:T(2,128)(2,1)S(1)} %all_to_all.5.parts), custom_call_target="tpu_custom_call" | custom-call | bytes 30720 | tf_op jit(solution)/shard_map/final/pallas_call | solution.py:217
  (13 shorter events, 0.0 us)
Async XLA Ops:
  0.0 15.2 %copy-start.1 = (bf16[5,256,768]{2,1,0:T(8,128)(2,1)S(1)}, bf16[5,256,768]{2,1,0:T(8,128)(2,1)}, u32[]{:S(2)}) copy-start(bf16[5,256,768]{2,1,0:T(8,128)(2,1)} %values.1) | copy-start | bytes 5898244
  0.0 15.2 %copy-start = (bf16[5,256,768]{2,1,0:T(8,128)(2,1)S(1)}, bf16[5,256,768]{2,1,0:T(8,128)(2,1)}, u32[]{:S(2)}) copy-start(bf16[5,256,768]{2,1,0:T(8,128)(2,1)} %keys.1) | copy-start | bytes 5898244
  1.6 4.9 %collective-permute-start = (bf16[2,1664]{1,0:T(2,128)(2,1)}, bf16[2,1664]{1,0:T(2,128)(2,1)S(1)}, u32[]{:S(2)}, u32[]{:S(2)}) collective-permute-start(bf16[2,1664]{1,0:T(2,128)(2,1)} %get-tuple-element.14.packed), channel_id=1, source_target_pairs={{0,4},{4,0},{8,12},{12,8},{16,20},{20,16},{24,28},{28,24},{1,5},{5... | collective-permute-start | bytes 19976 | tf_op jit(solution)/shard_map/ppermute | solution.py:537
  4.7 0.7 %copy-start.6 = (bf16[2,1664]{1,0:T(2,128)(2,1)S(1)}, bf16[2,1664]{1,0:T(2,128)(2,1)}, u32[]{:S(2)}) copy-start(bf16[2,1664]{1,0:T(2,128)(2,1)} %get-tuple-element.14.packed) | copy-start | bytes 19972
  5.4 0.7 %copy-start.7 = (bf16[2,1536]{1,0:T(2,128)(2,1)S(1)}, bf16[2,1536]{1,0:T(2,128)(2,1)}, u32[]{:S(2)}) copy-start(bf16[2,1536]{1,0:T(2,128)(2,1)} %get-tuple-element.15.new) | copy-start | bytes 18436
  6.5 5.8 %collective-permute-start.3 = (bf16[2,2,1664]{2,1,0:T(2,128)(2,1)S(1)}, bf16[2,2,1664]{2,1,0:T(2,128)(2,1)S(1)}, u32[]{:S(2)}, u32[]{:S(2)}) collective-permute-start(bf16[2,2,1664]{2,1,0:T(2,128)(2,1)S(1)} %merge.2.a0), channel_id=1, source_target_pairs={{0,24},{4,28},{8,16},{12,20},{16,8},{20,12},{24,0},{28,4},{1,25},{... | collective-permute-start | bytes 39944 | tf_op jit(solution)/shard_map/ppermute | solution.py:537
  10.6 4.6 %collective-permute-start.2 = (bf16[2,2,1664]{2,1,0:T(2,128)(2,1)S(1)}, bf16[2,2,1664]{2,1,0:T(2,128)(2,1)S(1)}, u32[]{:S(2)}, u32[]{:S(2)}) collective-permute-start(bf16[2,2,1664]{2,1,0:T(2,128)(2,1)S(1)} %merge.2.a0), channel_id=1, source_target_pairs={{0,16},{4,20},{8,24},{12,28},{16,0},{20,4},{24,8},{28,12},{1,17},{... | collective-permute-start | bytes 39944 | tf_op jit(solution)/shard_map/ppermute | solution.py:537
  10.6 4.6 %collective-permute-start.1 = (bf16[2,2,1664]{2,1,0:T(2,128)(2,1)S(1)}, bf16[2,2,1664]{2,1,0:T(2,128)(2,1)S(1)}, u32[]{:S(2)}, u32[]{:S(2)}) collective-permute-start(bf16[2,2,1664]{2,1,0:T(2,128)(2,1)S(1)} %merge.2.a0), channel_id=1, source_target_pairs={{0,8},{4,12},{8,0},{12,4},{16,24},{20,28},{24,16},{28,20},{1,9},{5... | collective-permute-start | bytes 39944 | tf_op jit(solution)/shard_map/ppermute | solution.py:537
  15.2 11.4 %copy-start.5 = (bf16[768,384]{1,0:T(8,128)(2,1)S(1)}, bf16[768,384]{1,0:T(8,128)(2,1)}, u32[]{:S(2)}) copy-start(bf16[768,384]{1,0:T(8,128)(2,1)} %weight.2) | copy-start | bytes 1769476
  15.2 21.0 %copy-start.8 = (bf16[768]{0:T(1024)(128)(2,1)S(1)}, bf16[768]{0:T(1024)(128)(2,1)}, u32[]{:S(2)}) copy-start(bf16[768]{0:T(1024)(128)(2,1)} %param.22) | copy-start | bytes 4612
  15.3 23.6 %copy-start.3 = (bf16[768,1024]{1,0:T(8,128)(2,1)S(1)}, bf16[768,1024]{1,0:T(8,128)(2,1)}, u32[]{:S(2)}) copy-start(bf16[768,1024]{1,0:T(8,128)(2,1)} %gate.1) | copy-start | bytes 4718596
  15.3 23.6 %copy-start.4 = (bf16[768,1024]{1,0:T(8,128)(2,1)S(1)}, bf16[768,1024]{1,0:T(8,128)(2,1)}, u32[]{:S(2)}) copy-start(bf16[768,1024]{1,0:T(8,128)(2,1)} %up.1) | copy-start | bytes 4718596
  16.4 3.8 %collective-permute-start.4 = (bf16[8,768]{1,0:T(8,128)(2,1)S(1)}, bf16[8,768]{1,0:T(8,128)(2,1)S(1)}, u32[]{:S(2)}, u32[]{:S(2)}) collective-permute-start(bf16[8,768]{1,0:T(8,128)(2,1)S(1)} %get-tuple-element.18.mine), channel_id=1, source_target_pairs={{0,4},{4,0},{8,12},{12,8},{16,20},{20,16},{24,28},{28,24},{1,5},{5... | collective-permute-start | bytes 36872 | tf_op jit(solution)/shard_map/ppermute | solution.py:537
  20.2 5.6 %collective-permute-start.7 = (bf16[2,8,768]{2,1,0:T(8,128)(2,1)S(1)}, bf16[2,8,768]{2,1,0:T(8,128)(2,1)S(1)}, u32[]{:S(2)}, u32[]{:S(2)}) collective-permute-start(bf16[2,8,768]{2,1,0:T(8,128)(2,1)S(1)} %merge.3.b0), channel_id=1, source_target_pairs={{0,24},{4,28},{8,16},{12,20},{16,8},{20,12},{24,0},{28,4},{1,25},{... | collective-permute-start | bytes 73736 | tf_op jit(solution)/shard_map/ppermute | solution.py:537
  21.6 4.7 %collective-permute-start.6 = (bf16[2,8,768]{2,1,0:T(8,128)(2,1)S(1)}, bf16[2,8,768]{2,1,0:T(8,128)(2,1)S(1)}, u32[]{:S(2)}, u32[]{:S(2)}) collective-permute-start(bf16[2,8,768]{2,1,0:T(8,128)(2,1)S(1)} %merge.3.b0), channel_id=1, source_target_pairs={{0,16},{4,20},{8,24},{12,28},{16,0},{20,4},{24,8},{28,12},{1,17},{... | collective-permute-start | bytes 73736 | tf_op jit(solution)/shard_map/ppermute | solution.py:537
  22.3 4.4 %collective-permute-start.5 = (bf16[2,8,768]{2,1,0:T(8,128)(2,1)S(1)}, bf16[2,8,768]{2,1,0:T(8,128)(2,1)S(1)}, u32[]{:S(2)}, u32[]{:S(2)}) collective-permute-start(bf16[2,8,768]{2,1,0:T(8,128)(2,1)S(1)} %merge.3.b0), channel_id=1, source_target_pairs={{0,8},{4,12},{8,0},{12,4},{16,24},{20,28},{24,16},{28,20},{1,9},{5... | collective-permute-start | bytes 73736 | tf_op jit(solution)/shard_map/ppermute | solution.py:537
  27.4 1.2 %collective-permute-start.8 = (bf16[16,384]{1,0:T(8,128)(2,1)S(1)}, bf16[16,384]{1,0:T(8,128)(2,1)S(1)}, u32[]{:S(2)}, u32[]{:S(2)}) collective-permute-start(bf16[16,384]{1,0:T(8,128)(2,1)S(1)} %combine.1.p0), channel_id=1, source_target_pairs={{0,1},{1,0},{2,3},{3,2},{4,5},{5,4},{6,7},{7,6},{8,9},{9,8},{10,11... | collective-permute-start | bytes 36872 | tf_op jit(solution)/shard_map/ppermute | solution.py:537
  28.6 7.6 %collective-permute-start.12 = (bf16[16,384]{1,0:T(8,128)(2,1)S(1)}, bf16[16,384]{1,0:T(8,128)(2,1)S(1)}, u32[]{:S(2)}, u32[]{:S(2)}) collective-permute-start(bf16[16,384]{1,0:T(8,128)(2,1)S(1)} %head_sum.1), channel_id=1, source_target_pairs={{3,28},{7,24},{2,20},{6,16},{1,12},{5,8},{0,4},{4,0},{11,29},{15,2... | collective-permute-start | bytes 36872 | tf_op jit(solution)/shard_map/ppermute | solution.py:629
  30.1 6.1 %collective-permute-start.11 = (bf16[16,384]{1,0:T(8,128)(2,1)S(1)}, bf16[16,384]{1,0:T(8,128)(2,1)S(1)}, u32[]{:S(2)}, u32[]{:S(2)}) collective-permute-start(bf16[16,384]{1,0:T(8,128)(2,1)S(1)} %head_sum.1), channel_id=1, source_target_pairs={{1,28},{5,24},{0,20},{4,16},{3,12},{7,8},{2,4},{6,0},{9,29},{13,25... | collective-permute-start | bytes 36872 | tf_op jit(solution)/shard_map/ppermute | solution.py:629
  33.6 2.6 %collective-permute-start.10 = (bf16[16,384]{1,0:T(8,128)(2,1)S(1)}, bf16[16,384]{1,0:T(8,128)(2,1)S(1)}, u32[]{:S(2)}, u32[]{:S(2)}) collective-permute-start(bf16[16,384]{1,0:T(8,128)(2,1)S(1)} %head_sum.1), channel_id=1, source_target_pairs={{3,24},{7,28},{2,16},{6,20},{1,8},{5,12},{0,0},{4,4},{11,25},{15,2... | collective-permute-start | bytes 36872 | tf_op jit(solution)/shard_map/ppermute | solution.py:629
  34.3 4.5 %collective-permute-start.9 = (bf16[16,384]{1,0:T(8,128)(2,1)S(1)}, bf16[16,384]{1,0:T(8,128)(2,1)S(1)}, u32[]{:S(2)}, u32[]{:S(2)}) collective-permute-start(bf16[16,384]{1,0:T(8,128)(2,1)S(1)} %head_sum.1), channel_id=1, source_target_pairs={{1,24},{5,28},{0,16},{4,20},{3,8},{7,12},{2,0},{6,4},{9,25},{13,29... | collective-permute-start | bytes 36872 | tf_op jit(solution)/shard_map/ppermute | solution.py:629
  38.8 7.7 %copy-start.2 = (bf16[1024,768]{1,0:T(8,128)(2,1)S(1)}, bf16[1024,768]{1,0:T(8,128)(2,1)}, u32[]{:S(2)}) copy-start(bf16[1024,768]{1,0:T(8,128)(2,1)} %weight.3) | copy-start | bytes 4718596
  39.3 2.5 %collective-permute-start.13 = (bf16[16,2176]{1,0:T(8,128)(2,1)S(1)}, bf16[16,2176]{1,0:T(8,128)(2,1)S(1)}, u32[]{:S(2)}, u32[]{:S(2)}) collective-permute-start(bf16[16,2176]{1,0:T(8,128)(2,1)S(1)} %get-tuple-element.22.mine), channel_id=1, source_target_pairs={{0,1},{1,0},{2,3},{3,2},{4,5},{5,4},{6,7},{7,6},{8,9},{9,8},{10,11... | collective-permute-start | bytes 208904 | tf_op jit(solution)/shard_map/ppermute | solution.py:537
  41.9 4.6 %collective-permute-start.14 = (bf16[16,2176]{1,0:T(8,128)(2,1)S(1)}, bf16[16,2176]{1,0:T(8,128)(2,1)S(1)}, u32[]{:S(2)}, u32[]{:S(2)}) collective-permute-start(bf16[16,2176]{1,0:T(8,128)(2,1)S(1)} %core_sum.1.mine), channel_id=1, source_target_pairs={{0,2},{1,3},{2,0},{3,1},{4,6},{5,7},{6,4},{7,5},{8,10},{9,11},{10,... | collective-permute-start | bytes 208904 | tf_op jit(solution)/shard_map/ppermute | solution.py:537

commit v12 on v10

--- a/solution.py
+++ b/solution.py
@@ -613,7 +613,7 @@
         sum_kernel,
         "head_sum",
         [((requests, part_cols), BF16)],
-        [head_part] + [flip(head_part, "mlp", step) for step in (1, 3, 2)],
+        [head_part] + [flip(head_part, "mlp", step) for step in (1, 2, 3)],
     )
     pieces = []
     for turn in range(2):
@@ -642,7 +642,7 @@
         functools.partial(down_kernel, width * mlp),
         "down",
         [((pool, rows, width), BF16)],
-        [core_sums, flip(core_sums, "mlp", 2), down_weight],
+        [core_sums, flip(core_sums, "mlp", 3), down_weight],
         [pltpu.VMEM((requests, width), F32)],
     )
     backwards = list(range(pool))[::-1]

time: 54.7 us -> 53.5 us (0.978)
  waiting for transfers between devices: 17.8 us -> 16.1 us
    ppermute x13, waiting for transfers between devices: 14.8 us -> 14 us  [flip(): lax.ppermute(values, axis, [(index, index ^ step) for index in range(size)])]
    ppermute x2, waiting for transfers between devices: 3.02 us -> 2.19 us  [per_device_small(): pieces.append(lax.ppermute(head_sum, ('pool', 'mlp'), route))]
    ppermute x2, starting transfers between devices: 3.45 us -> 4.27 us  [per_device_small(): pieces.append(lax.ppermute(head_sum, ('pool', 'mlp'), route))]
where the time goes in v12:
time: 53.5 us; the launch traced here: 53.2 us
  starting transfers between devices  21.9 us (41%)
  waiting for transfers between devices  16.1 us (30%)
  blocking collectives  8.36 us (16%)
  Pallas kernels  5.26 us (10%)
  local copies, waits for them, and re-layouts  1.46 us (3%)
    ppermute x13, starting transfers between devices, flip(): lax.ppermute(values, axis, [(index, index ^ step) for index in range(size)])  17.6 us
    ppermute x13, waiting for transfers between devices, flip(): lax.ppermute(values, axis, [(index, index ^ step) for index in range(size)])  14 us
    all_to_all x1, blocking collectives, per_device_small(): lax.all_to_all(down, 'pool', 0, 0, axis_index_groups=[backwards])  8.36 us
    pallas_call x11, Pallas kernels, call(): pl.pallas_call(kernel, out_shape=[jax.ShapeDtypeStruct(shape, dtype) for...  5.26 us
    ppermute x2, starting transfers between devices, per_device_small(): pieces.append(lax.ppermute(head_sum, ('pool', 'mlp'), route))  4.27 us
    ppermute x2, waiting for transfers between devices, per_device_small(): pieces.append(lax.ppermute(head_sum, ('pool', 'mlp'), route))  2.19 us
    unnamed x18, local copies, waits for them, and re-layouts  1.45 us
  transfers between devices with their start and end apart: 15, of which 13 were waited for; matrix products, arithmetic and copies ran while one was open for 0% of the time, Pallas kernels for 0%

profile of v12, /device:TPU:0, one launch (start us, length us, event | category | flops | bytes accessed | tf_op | source)
XLA Modules:
  0.0 53.2 jit_solution(8493122879352991184)
XLA Ops:
  0.0 1.6 %rotary.1 = (bf16[2,1664]{1,0:T(2,128)(2,1)}, bf16[2,1536]{1,0:T(2,128)(2,1)}) custom-call(s32[2,8]{1,0:T(2,128)} %refs_0_.1, s32[2]{0:T(128)} %refs_1_.1, bf16[2,768]{1,0:T(2,128)(2,1)} %refs_2_.1, bf16[2,768]{1,0:T(2,128)(2,1)} %refs_3_.1, bf16[2,768]{1,0:T(2,128)(2,1)} %refs_4_.1, bf16[2,768]{1,0:T(2,128)(2,1)} %refs_5_.1, bf16[5,256,768]{2,1,0:T(8,128)(2,1)} %keys.1, ...), custom_call_target="tpu_custom_call" | custom-call | bytes 3944520 | tf_op jit(solution)/shard_map/rotary/pallas_call | solution.py:217
  1.6 3.0 %collective-permute-start = (bf16[2,1664]{1,0:T(2,128)(2,1)}, bf16[2,1664]{1,0:T(2,128)(2,1)S(1)}, u32[]{:S(2)}, u32[]{:S(2)}) collective-permute-start(bf16[2,1664]{1,0:T(2,128)(2,1)} %get-tuple-element.14.packed), channel_id=1, source_target_pairs={{0,4},{4,0},{8,12},{12,8},{16,20},{20,16},{24,28},{28,24},{1,5},{5... | collective-permute-start | bytes 19976 | tf_op jit(solution)/shard_map/ppermute | solution.py:538
  4.7 0.7 %copy-done.6 = bf16[2,1664]{1,0:T(2,128)(2,1)S(1)} copy-done((bf16[2,1664]{1,0:T(2,128)(2,1)S(1)}, bf16[2,1664]{1,0:T(2,128)(2,1)}, u32[]{:S(2)}) %copy-start.6) | copy-done | bytes 6680
  5.4 0.7 %copy-done.7 = bf16[2,1536]{1,0:T(2,128)(2,1)S(1)} copy-done((bf16[2,1536]{1,0:T(2,128)(2,1)S(1)}, bf16[2,1536]{1,0:T(2,128)(2,1)}, u32[]{:S(2)}) %copy-start.7) | copy-done | bytes 6168
  6.1 0.1 carry.1
  6.2 0.3 collective-permute-done.theirs
  6.5 4.1 %collective-permute-start.3 = (bf16[2,2,1664]{2,1,0:T(2,128)(2,1)S(1)}, bf16[2,2,1664]{2,1,0:T(2,128)(2,1)S(1)}, u32[]{:S(2)}, u32[]{:S(2)}) collective-permute-start(bf16[2,2,1664]{2,1,0:T(2,128)(2,1)S(1)} %merge.2.a0), channel_id=1, source_target_pairs={{0,24},{4,28},{8,16},{12,20},{16,8},{20,12},{24,0},{28,4},{1,25},{... | collective-permute-start | bytes 39944 | tf_op jit(solution)/shard_map/ppermute | solution.py:538
  10.6 0.0 collective-permute-start.2
  10.6 0.6 %collective-permute-start.1 = (bf16[2,2,1664]{2,1,0:T(2,128)(2,1)S(1)}, bf16[2,2,1664]{2,1,0:T(2,128)(2,1)S(1)}, u32[]{:S(2)}, u32[]{:S(2)}) collective-permute-start(bf16[2,2,1664]{2,1,0:T(2,128)(2,1)S(1)} %merge.2.a0), channel_id=1, source_target_pairs={{0,8},{4,12},{8,0},{12,4},{16,24},{20,28},{24,16},{28,20},{1,9},{5... | collective-permute-start | bytes 39944 | tf_op jit(solution)/shard_map/ppermute | solution.py:538
  11.2 1.1 %collective-permute-done.3.a3 = bf16[2,2,1664]{2,1,0:T(2,128)(2,1)S(1)} collective-permute-done((bf16[2,2,1664]{2,1,0:T(2,128)(2,1)S(1)}, bf16[2,2,1664]{2,1,0:T(2,128)(2,1)S(1)}, u32[]{:S(2)}, u32[]{:S(2)}) %collective-permute-start.3) | collective-permute-done | bytes 13344 | tf_op jit(solution)/shard_map/ppermute | solution.py:538
  12.3 2.9 %collective-permute-done.2.a2 = bf16[2,2,1664]{2,1,0:T(2,128)(2,1)S(1)} collective-permute-done((bf16[2,2,1664]{2,1,0:T(2,128)(2,1)S(1)}, bf16[2,2,1664]{2,1,0:T(2,128)(2,1)S(1)}, u32[]{:S(2)}, u32[]{:S(2)}) %collective-permute-start.2) | collective-permute-done | bytes 13344 | tf_op jit(solution)/shard_map/ppermute | solution.py:538
  15.2 0.0 collective-permute-done.1.a1
  15.2 0.0 copy-done.1
  15.2 0.0 copy-done
  15.2 0.0 copy-start.5
  15.2 0.0 copy-start.8
  15.3 0.0 copy-start.3
  15.3 0.0 copy-start.4
  15.3 1.1 %attend.1 = (bf16[8,768]{1,0:T(8,128)(2,1)S(1)}, f32[16,768]{1,0:T(8,128)S(1)}, f32[16,128]{1,0:T(8,128)S(1)}) custom-call(bf16[2,2,1664]{2,1,0:T(2,128)(2,1)S(1)} %merge.2.a0, bf16[2,2,1664]{2,1,0:T(2,128)(2,1)S(1)} %collective-permute-done.1.a1, bf16[2,2,1664]{2,1,0:T(2,128)(2,1)S(1)} %collective-permute-done.2.a2, ...), custom_call_target="tpu_custom_call" | custom-call | bytes 4014080 | tf_op jit(solution)/shard_map/attend/pallas_call | solution.py:217
  16.4 1.6 %collective-permute-start.4 = (bf16[8,768]{1,0:T(8,128)(2,1)S(1)}, bf16[8,768]{1,0:T(8,128)(2,1)S(1)}, u32[]{:S(2)}, u32[]{:S(2)}) collective-permute-start(bf16[8,768]{1,0:T(8,128)(2,1)S(1)} %get-tuple-element.18.mine), channel_id=1, source_target_pairs={{0,4},{4,0},{8,12},{12,8},{16,20},{20,16},{24,28},{28,24},{1,5},{5... | collective-permute-start | bytes 36872 | tf_op jit(solution)/shard_map/ppermute | solution.py:538
  18.0 2.2 %collective-permute-done.4.theirs = bf16[8,768]{1,0:T(8,128)(2,1)S(1)} collective-permute-done((bf16[8,768]{1,0:T(8,128)(2,1)S(1)}, bf16[8,768]{1,0:T(8,128)(2,1)S(1)}, u32[]{:S(2)}, u32[]{:S(2)}) %collective-permute-start.4) | collective-permute-done | bytes 12320 | tf_op jit(solution)/shard_map/ppermute | solution.py:538
  20.2 1.4 %collective-permute-start.7 = (bf16[2,8,768]{2,1,0:T(8,128)(2,1)S(1)}, bf16[2,8,768]{2,1,0:T(8,128)(2,1)S(1)}, u32[]{:S(2)}, u32[]{:S(2)}) collective-permute-start(bf16[2,8,768]{2,1,0:T(8,128)(2,1)S(1)} %merge.3.b0), channel_id=1, source_target_pairs={{0,24},{4,28},{8,16},{12,20},{16,8},{20,12},{24,0},{28,4},{1,25},{... | collective-permute-start | bytes 73736 | tf_op jit(solution)/shard_map/ppermute | solution.py:538
  21.6 0.6 %collective-permute-start.6 = (bf16[2,8,768]{2,1,0:T(8,128)(2,1)S(1)}, bf16[2,8,768]{2,1,0:T(8,128)(2,1)S(1)}, u32[]{:S(2)}, u32[]{:S(2)}) collective-permute-start(bf16[2,8,768]{2,1,0:T(8,128)(2,1)S(1)} %merge.3.b0), channel_id=1, source_target_pairs={{0,16},{4,20},{8,24},{12,28},{16,0},{20,4},{24,8},{28,12},{1,17},{... | collective-permute-start | bytes 73736 | tf_op jit(solution)/shard_map/ppermute | solution.py:538
  22.3 2.3 %collective-permute-start.5 = (bf16[2,8,768]{2,1,0:T(8,128)(2,1)S(1)}, bf16[2,8,768]{2,1,0:T(8,128)(2,1)S(1)}, u32[]{:S(2)}, u32[]{:S(2)}) collective-permute-start(bf16[2,8,768]{2,1,0:T(8,128)(2,1)S(1)} %merge.3.b0), channel_id=1, source_target_pairs={{0,8},{4,12},{8,0},{12,4},{16,24},{20,28},{24,16},{28,20},{1,9},{5... | collective-permute-start | bytes 73736 | tf_op jit(solution)/shard_map/ppermute | solution.py:538
  24.6 1.2 %collective-permute-done.7.b3 = bf16[2,8,768]{2,1,0:T(8,128)(2,1)S(1)} collective-permute-done((bf16[2,8,768]{2,1,0:T(8,128)(2,1)S(1)}, bf16[2,8,768]{2,1,0:T(8,128)(2,1)S(1)}, u32[]{:S(2)}, u32[]{:S(2)}) %collective-permute-start.7) | collective-permute-done | bytes 24608 | tf_op jit(solution)/shard_map/ppermute | solution.py:538
  25.8 0.6 %collective-permute-done.6.b2 = bf16[2,8,768]{2,1,0:T(8,128)(2,1)S(1)} collective-permute-done((bf16[2,8,768]{2,1,0:T(8,128)(2,1)S(1)}, bf16[2,8,768]{2,1,0:T(8,128)(2,1)S(1)}, u32[]{:S(2)}, u32[]{:S(2)}) %collective-permute-start.6) | collective-permute-done | bytes 24608 | tf_op jit(solution)/shard_map/ppermute | solution.py:538
  26.4 0.2 collective-permute-done.5.b1
  26.6 0.7 %combine.1.p0 = bf16[16,384]{1,0:T(8,128)(2,1)S(1)} custom-call(bf16[2,8,768]{2,1,0:T(8,128)(2,1)S(1)} %merge.3.b0, bf16[2,8,768]{2,1,0:T(8,128)(2,1)S(1)} %collective-permute-done.5.b1, bf16[2,8,768]{2,1,0:T(8,128)(2,1)S(1)} %collective-permute-done.6.b2, bf16[2,8,768]{2,1,0:T(8,128)(2,1)S(1)} %collective-permute-done.7.b3, ...), custom_call_target="tpu_custom_call" | custom-call | bytes 696320 | tf_op jit(solution)/shard_map/combine/pallas_call | solution.py:217
  27.4 0.1 collective-permute-start.10
  27.4 1.6 %collective-permute-start.9 = (bf16[16,384]{1,0:T(8,128)(2,1)S(1)}, bf16[16,384]{1,0:T(8,128)(2,1)S(1)}, u32[]{:S(2)}, u32[]{:S(2)}) collective-permute-start(bf16[16,384]{1,0:T(8,128)(2,1)S(1)} %combine.1.p0), channel_id=1, source_target_pairs={{0,2},{1,3},{2,0},{3,1},{4,6},{5,7},{6,4},{7,5},{8,10},{9,11},{10,... | collective-permute-start | bytes 36872 | tf_op jit(solution)/shard_map/ppermute | solution.py:538
  29.0 0.3 collective-permute-start.8
  29.3 1.3 %collective-permute-done.10.p3 = bf16[16,384]{1,0:T(8,128)(2,1)S(1)} collective-permute-done((bf16[16,384]{1,0:T(8,128)(2,1)S(1)}, bf16[16,384]{1,0:T(8,128)(2,1)S(1)}, u32[]{:S(2)}, u32[]{:S(2)}) %collective-permute-start.10) | collective-permute-done | bytes 12320 | tf_op jit(solution)/shard_map/ppermute | solution.py:538
  30.6 0.6 %collective-permute-done.9.p2 = bf16[16,384]{1,0:T(8,128)(2,1)S(1)} collective-permute-done((bf16[16,384]{1,0:T(8,128)(2,1)S(1)}, bf16[16,384]{1,0:T(8,128)(2,1)S(1)}, u32[]{:S(2)}, u32[]{:S(2)}) %collective-permute-start.9) | collective-permute-done | bytes 12320 | tf_op jit(solution)/shard_map/ppermute | solution.py:538
  31.2 0.0 collective-permute-done.8.p1
  31.2 2.8 %collective-permute-start.12 = (bf16[16,384]{1,0:T(8,128)(2,1)S(1)}, bf16[16,384]{1,0:T(8,128)(2,1)S(1)}, u32[]{:S(2)}, u32[]{:S(2)}) collective-permute-start(bf16[16,384]{1,0:T(8,128)(2,1)S(1)} %head_sum.1), channel_id=1, source_target_pairs={{1,28},{5,24},{0,20},{4,16},{3,12},{7,8},{2,4},{6,0},{9,29},{13,25... | collective-permute-start | bytes 36872 | tf_op jit(solution)/shard_map/ppermute | solution.py:627
  34.0 1.5 %collective-permute-start.11 = (bf16[16,384]{1,0:T(8,128)(2,1)S(1)}, bf16[16,384]{1,0:T(8,128)(2,1)S(1)}, u32[]{:S(2)}, u32[]{:S(2)}) collective-permute-start(bf16[16,384]{1,0:T(8,128)(2,1)S(1)} %head_sum.1), channel_id=1, source_target_pairs={{1,24},{5,28},{0,16},{4,20},{3,8},{7,12},{2,0},{6,4},{9,25},{13,29... | collective-permute-start | bytes 36872 | tf_op jit(solution)/shard_map/ppermute | solution.py:627
  35.5 0.5 collective-permute-done.12.flip
  36.0 1.7 %collective-permute-done.11.same = bf16[16,384]{1,0:T(8,128)(2,1)S(1)} collective-permute-done((bf16[16,384]{1,0:T(8,128)(2,1)S(1)}, bf16[16,384]{1,0:T(8,128)(2,1)S(1)}, u32[]{:S(2)}, u32[]{:S(2)}) %collective-permute-start.11) | collective-permute-done | bytes 12320 | tf_op jit(solution)/shard_map/ppermute | solution.py:627
  37.7 0.0 copy-done.3
  37.7 0.5 gate_up.1
  38.2 0.2 collective-permute-start.13
  38.4 1.1 %collective-permute-done.13.theirs = bf16[16,2176]{1,0:T(8,128)(2,1)S(1)} collective-permute-done((bf16[16,2176]{1,0:T(8,128)(2,1)S(1)}, bf16[16,2176]{1,0:T(8,128)(2,1)S(1)}, u32[]{:S(2)}, u32[]{:S(2)}) %collective-permute-start.13) | collective-permute-done | bytes 69664 | tf_op jit(solution)/shard_map/ppermute | solution.py:538
  39.5 0.1 core_sum.1.mine
  39.6 1.9 %collective-permute-start.14 = (bf16[16,2176]{1,0:T(8,128)(2,1)S(1)}, bf16[16,2176]{1,0:T(8,128)(2,1)S(1)}, u32[]{:S(2)}, u32[]{:S(2)}) collective-permute-start(bf16[16,2176]{1,0:T(8,128)(2,1)S(1)} %core_sum.1.mine), channel_id=1, source_target_pairs={{0,3},{1,2},{2,1},{3,0},{4,7},{5,6},{6,5},{7,4},{8,11},{9,10},{10,... | collective-permute-start | bytes 208904 | tf_op jit(solution)/shard_map/ppermute | solution.py:538
  41.4 2.4 %collective-permute-done.14.theirs = bf16[16,2176]{1,0:T(8,128)(2,1)S(1)} collective-permute-done((bf16[16,2176]{1,0:T(8,128)(2,1)S(1)}, bf16[16,2176]{1,0:T(8,128)(2,1)S(1)}, u32[]{:S(2)}, u32[]{:S(2)}) %collective-permute-start.14) | collective-permute-done | bytes 69664 | tf_op jit(solution)/shard_map/ppermute | solution.py:538
  43.8 0.4 down.1
  44.2 8.4 %all_to_all.5.parts = bf16[8,2,768]{2,1,0:T(2,128)(2,1)S(1)} all-to-all(bf16[8,2,768]{2,1,0:T(2,128)(2,1)S(1)} %down.1), channel_id=1, replica_groups={{28,24,20,16,12,8,4,0},{29,25,21,17,13,9,5,1},{30,26,22,18,14,10,6,2},{..., dimensions={0} | all-to-all | bytes 49152 | tf_op jit(solution)/shard_map/all_to_all | solution.py:653
  52.6 0.6 %final.1 = bf16[2,768]{1,0:T(2,128)(2,1)} custom-call(f32[2,768]{1,0:T(2,128)S(1)} %get-tuple-element.21.own, bf16[8,2,768]{2,1,0:T(2,128)(2,1)S(1)} %all_to_all.5.parts), custom_call_target="tpu_custom_call" | custom-call | bytes 30720 | tf_op jit(solution)/shard_map/final/pallas_call | solution.py:217
  (13 shorter events, 0.0 us)
Async XLA Ops:
  0.0 15.2 %copy-start.1 = (bf16[5,256,768]{2,1,0:T(8,128)(2,1)S(1)}, bf16[5,256,768]{2,1,0:T(8,128)(2,1)}, u32[]{:S(2)}) copy-start(bf16[5,256,768]{2,1,0:T(8,128)(2,1)} %values.1) | copy-start | bytes 5898244
  0.0 15.2 %copy-start = (bf16[5,256,768]{2,1,0:T(8,128)(2,1)S(1)}, bf16[5,256,768]{2,1,0:T(8,128)(2,1)}, u32[]{:S(2)}) copy-start(bf16[5,256,768]{2,1,0:T(8,128)(2,1)} %keys.1) | copy-start | bytes 5898244
  1.6 4.9 %collective-permute-start = (bf16[2,1664]{1,0:T(2,128)(2,1)}, bf16[2,1664]{1,0:T(2,128)(2,1)S(1)}, u32[]{:S(2)}, u32[]{:S(2)}) collective-permute-start(bf16[2,1664]{1,0:T(2,128)(2,1)} %get-tuple-element.14.packed), channel_id=1, source_target_pairs={{0,4},{4,0},{8,12},{12,8},{16,20},{20,16},{24,28},{28,24},{1,5},{5... | collective-permute-start | bytes 19976 | tf_op jit(solution)/shard_map/ppermute | solution.py:538
  4.7 0.7 %copy-start.6 = (bf16[2,1664]{1,0:T(2,128)(2,1)S(1)}, bf16[2,1664]{1,0:T(2,128)(2,1)}, u32[]{:S(2)}) copy-start(bf16[2,1664]{1,0:T(2,128)(2,1)} %get-tuple-element.14.packed) | copy-start | bytes 19972
  5.4 0.7 %copy-start.7 = (bf16[2,1536]{1,0:T(2,128)(2,1)S(1)}, bf16[2,1536]{1,0:T(2,128)(2,1)}, u32[]{:S(2)}) copy-start(bf16[2,1536]{1,0:T(2,128)(2,1)} %get-tuple-element.15.new) | copy-start | bytes 18436
  6.5 5.8 %collective-permute-start.3 = (bf16[2,2,1664]{2,1,0:T(2,128)(2,1)S(1)}, bf16[2,2,1664]{2,1,0:T(2,128)(2,1)S(1)}, u32[]{:S(2)}, u32[]{:S(2)}) collective-permute-start(bf16[2,2,1664]{2,1,0:T(2,128)(2,1)S(1)} %merge.2.a0), channel_id=1, source_target_pairs={{0,24},{4,28},{8,16},{12,20},{16,8},{20,12},{24,0},{28,4},{1,25},{... | collective-permute-start | bytes 39944 | tf_op jit(solution)/shard_map/ppermute | solution.py:538
  10.6 4.6 %collective-permute-start.2 = (bf16[2,2,1664]{2,1,0:T(2,128)(2,1)S(1)}, bf16[2,2,1664]{2,1,0:T(2,128)(2,1)S(1)}, u32[]{:S(2)}, u32[]{:S(2)}) collective-permute-start(bf16[2,2,1664]{2,1,0:T(2,128)(2,1)S(1)} %merge.2.a0), channel_id=1, source_target_pairs={{0,16},{4,20},{8,24},{12,28},{16,0},{20,4},{24,8},{28,12},{1,17},{... | collective-permute-start | bytes 39944 | tf_op jit(solution)/shard_map/ppermute | solution.py:538
  10.6 4.6 %collective-permute-start.1 = (bf16[2,2,1664]{2,1,0:T(2,128)(2,1)S(1)}, bf16[2,2,1664]{2,1,0:T(2,128)(2,1)S(1)}, u32[]{:S(2)}, u32[]{:S(2)}) collective-permute-start(bf16[2,2,1664]{2,1,0:T(2,128)(2,1)S(1)} %merge.2.a0), channel_id=1, source_target_pairs={{0,8},{4,12},{8,0},{12,4},{16,24},{20,28},{24,16},{28,20},{1,9},{5... | collective-permute-start | bytes 39944 | tf_op jit(solution)/shard_map/ppermute | solution.py:538
  15.2 11.4 %copy-start.5 = (bf16[768,384]{1,0:T(8,128)(2,1)S(1)}, bf16[768,384]{1,0:T(8,128)(2,1)}, u32[]{:S(2)}) copy-start(bf16[768,384]{1,0:T(8,128)(2,1)} %weight.2) | copy-start | bytes 1769476
  15.2 20.2 %copy-start.8 = (bf16[768]{0:T(1024)(128)(2,1)S(1)}, bf16[768]{0:T(1024)(128)(2,1)}, u32[]{:S(2)}) copy-start(bf16[768]{0:T(1024)(128)(2,1)} %param.22) | copy-start | bytes 4612
  15.3 22.4 %copy-start.3 = (bf16[768,1024]{1,0:T(8,128)(2,1)S(1)}, bf16[768,1024]{1,0:T(8,128)(2,1)}, u32[]{:S(2)}) copy-start(bf16[768,1024]{1,0:T(8,128)(2,1)} %gate.1) | copy-start | bytes 4718596
  15.3 22.4 %copy-start.4 = (bf16[768,1024]{1,0:T(8,128)(2,1)S(1)}, bf16[768,1024]{1,0:T(8,128)(2,1)}, u32[]{:S(2)}) copy-start(bf16[768,1024]{1,0:T(8,128)(2,1)} %up.1) | copy-start | bytes 4718596
  16.4 3.8 %collective-permute-start.4 = (bf16[8,768]{1,0:T(8,128)(2,1)S(1)}, bf16[8,768]{1,0:T(8,128)(2,1)S(1)}, u32[]{:S(2)}, u32[]{:S(2)}) collective-permute-start(bf16[8,768]{1,0:T(8,128)(2,1)S(1)} %get-tuple-element.18.mine), channel_id=1, source_target_pairs={{0,4},{4,0},{8,12},{12,8},{16,20},{20,16},{24,28},{28,24},{1,5},{5... | collective-permute-start | bytes 36872 | tf_op jit(solution)/shard_map/ppermute | solution.py:538
  20.2 5.6 %collective-permute-start.7 = (bf16[2,8,768]{2,1,0:T(8,128)(2,1)S(1)}, bf16[2,8,768]{2,1,0:T(8,128)(2,1)S(1)}, u32[]{:S(2)}, u32[]{:S(2)}) collective-permute-start(bf16[2,8,768]{2,1,0:T(8,128)(2,1)S(1)} %merge.3.b0), channel_id=1, source_target_pairs={{0,24},{4,28},{8,16},{12,20},{16,8},{20,12},{24,0},{28,4},{1,25},{... | collective-permute-start | bytes 73736 | tf_op jit(solution)/shard_map/ppermute | solution.py:538
  21.6 4.7 %collective-permute-start.6 = (bf16[2,8,768]{2,1,0:T(8,128)(2,1)S(1)}, bf16[2,8,768]{2,1,0:T(8,128)(2,1)S(1)}, u32[]{:S(2)}, u32[]{:S(2)}) collective-permute-start(bf16[2,8,768]{2,1,0:T(8,128)(2,1)S(1)} %merge.3.b0), channel_id=1, source_target_pairs={{0,16},{4,20},{8,24},{12,28},{16,0},{20,4},{24,8},{28,12},{1,17},{... | collective-permute-start | bytes 73736 | tf_op jit(solution)/shard_map/ppermute | solution.py:538
  22.3 4.4 %collective-permute-start.5 = (bf16[2,8,768]{2,1,0:T(8,128)(2,1)S(1)}, bf16[2,8,768]{2,1,0:T(8,128)(2,1)S(1)}, u32[]{:S(2)}, u32[]{:S(2)}) collective-permute-start(bf16[2,8,768]{2,1,0:T(8,128)(2,1)S(1)} %merge.3.b0), channel_id=1, source_target_pairs={{0,8},{4,12},{8,0},{12,4},{16,24},{20,28},{24,16},{28,20},{1,9},{5... | collective-permute-start | bytes 73736 | tf_op jit(solution)/shard_map/ppermute | solution.py:538
  27.4 3.3 %collective-permute-start.10 = (bf16[16,384]{1,0:T(8,128)(2,1)S(1)}, bf16[16,384]{1,0:T(8,128)(2,1)S(1)}, u32[]{:S(2)}, u32[]{:S(2)}) collective-permute-start(bf16[16,384]{1,0:T(8,128)(2,1)S(1)} %combine.1.p0), channel_id=1, source_target_pairs={{0,3},{1,2},{2,1},{3,0},{4,7},{5,6},{6,5},{7,4},{8,11},{9,10},{10,... | collective-permute-start | bytes 36872 | tf_op jit(solution)/shard_map/ppermute | solution.py:538
  27.4 3.8 %collective-permute-start.9 = (bf16[16,384]{1,0:T(8,128)(2,1)S(1)}, bf16[16,384]{1,0:T(8,128)(2,1)S(1)}, u32[]{:S(2)}, u32[]{:S(2)}) collective-permute-start(bf16[16,384]{1,0:T(8,128)(2,1)S(1)} %combine.1.p0), channel_id=1, source_target_pairs={{0,2},{1,3},{2,0},{3,1},{4,6},{5,7},{6,4},{7,5},{8,10},{9,11},{10,... | collective-permute-start | bytes 36872 | tf_op jit(solution)/shard_map/ppermute | solution.py:538
  29.0 2.2 %collective-permute-start.8 = (bf16[16,384]{1,0:T(8,128)(2,1)S(1)}, bf16[16,384]{1,0:T(8,128)(2,1)S(1)}, u32[]{:S(2)}, u32[]{:S(2)}) collective-permute-start(bf16[16,384]{1,0:T(8,128)(2,1)S(1)} %combine.1.p0), channel_id=1, source_target_pairs={{0,1},{1,0},{2,3},{3,2},{4,5},{5,4},{6,7},{7,6},{8,9},{9,8},{10,11... | collective-permute-start | bytes 36872 | tf_op jit(solution)/shard_map/ppermute | solution.py:538
  31.2 4.8 %collective-permute-start.12 = (bf16[16,384]{1,0:T(8,128)(2,1)S(1)}, bf16[16,384]{1,0:T(8,128)(2,1)S(1)}, u32[]{:S(2)}, u32[]{:S(2)}) collective-permute-start(bf16[16,384]{1,0:T(8,128)(2,1)S(1)} %head_sum.1), channel_id=1, source_target_pairs={{1,28},{5,24},{0,20},{4,16},{3,12},{7,8},{2,4},{6,0},{9,29},{13,25... | collective-permute-start | bytes 36872 | tf_op jit(solution)/shard_map/ppermute | solution.py:627
  34.0 3.7 %collective-permute-start.11 = (bf16[16,384]{1,0:T(8,128)(2,1)S(1)}, bf16[16,384]{1,0:T(8,128)(2,1)S(1)}, u32[]{:S(2)}, u32[]{:S(2)}) collective-permute-start(bf16[16,384]{1,0:T(8,128)(2,1)S(1)} %head_sum.1), channel_id=1, source_target_pairs={{1,24},{5,28},{0,16},{4,20},{3,8},{7,12},{2,0},{6,4},{9,25},{13,29... | collective-permute-start | bytes 36872 | tf_op jit(solution)/shard_map/ppermute | solution.py:627
  37.7 6.1 %copy-start.2 = (bf16[1024,768]{1,0:T(8,128)(2,1)S(1)}, bf16[1024,768]{1,0:T(8,128)(2,1)}, u32[]{:S(2)}) copy-start(bf16[1024,768]{1,0:T(8,128)(2,1)} %weight.3) | copy-start | bytes 4718596
  38.2 1.3 %collective-permute-start.13 = (bf16[16,2176]{1,0:T(8,128)(2,1)S(1)}, bf16[16,2176]{1,0:T(8,128)(2,1)S(1)}, u32[]{:S(2)}, u32[]{:S(2)}) collective-permute-start(bf16[16,2176]{1,0:T(8,128)(2,1)S(1)} %get-tuple-element.22.mine), channel_id=1, source_target_pairs={{0,1},{1,0},{2,3},{3,2},{4,5},{5,4},{6,7},{7,6},{8,9},{9,8},{10,11... | collective-permute-start | bytes 208904 | tf_op jit(solution)/shard_map/ppermute | solution.py:538
  39.6 4.3 %collective-permute-start.14 = (bf16[16,2176]{1,0:T(8,128)(2,1)S(1)}, bf16[16,2176]{1,0:T(8,128)(2,1)S(1)}, u32[]{:S(2)}, u32[]{:S(2)}) collective-permute-start(bf16[16,2176]{1,0:T(8,128)(2,1)S(1)} %core_sum.1.mine), channel_id=1, source_target_pairs={{0,3},{1,2},{2,1},{3,0},{4,7},{5,6},{6,5},{7,4},{8,11},{9,10},{10,... | collective-permute-start | bytes 208904 | tf_op jit(solution)/shard_map/ppermute | solution.py:538

commit v13 on v12

--- a/solution.py
+++ b/solution.py
@@ -228,13 +228,6 @@
 
 def lanes(shape):
     return lax.broadcasted_iota(jnp.int32, shape, len(shape) - 1)
-
-
-def in_order(pieces, index):
-    for bit in (1, 2):
-        odd = (index & bit) != 0
-        pieces = [jnp.where(odd, pieces[s ^ bit], pieces[s]) for s in range(4)]
-    return pieces
 
 
 def rows_of(shape):
@@ -355,20 +348,19 @@
 
 def merge_kernel(mine, theirs, both):
     y = lax.axis_index("pool") % 2
-    both[y] = mine[...]
-    both[1 - y] = theirs[...]
-
-
-def attend_kernel(a0, a1, a2, a3, own, keys, values, part, residual, tables, scr):
+    for z in range(both.shape[0]):
+        both[z, y] = mine[...]
+        both[z, 1 - y] = theirs[...]
+
+
+def attend_kernel(pieces, own, keys, values, part, residual, tables, scr):
     blocks, block_len, width = keys.shape
-    rows = a0.shape[1]
+    rows = pieces.shape[2]
     heads = width // HD
     most = 8
     me = lax.axis_index("pool")
-    for y in range(2):
-        pieces = [piece[y].astype(F32) for piece in (a0, a1, a2, a3)]
-        for z, piece in enumerate(in_order(pieces, me // 2)):
-            scr[(z * 2 + y) * rows : (z * 2 + y + 1) * rows, :] = piece
+    for p in range(8):
+        scr[p * rows : (p + 1) * rows, :] = pieces[p // 2, p % 2].astype(F32)
     queries = scr[:, :width]
     residual[...] = scr[:, width : 2 * width]
     tail = scr[:, 2 * width :]
@@ -420,20 +412,16 @@
     part[...] = numer.astype(BF16)
 
 
-def combine_kernel(b0, b1, b2, b3, tables, weight, head_part, numer, tails, mix):
+def combine_kernel(pieces, tables, weight, head_part, numer, tails, mix):
     requests = tables.shape[0]
-    slots = b0.shape[1]
+    slots = pieces.shape[2]
     width = weight.shape[0]
     heads = width // HD
     rows, blocks = 2, slots - 3
-    me = lax.axis_index("pool")
-    for step, piece in enumerate((b0, b1, b2, b3)):
-        z = (me // 2) ^ step
-        for y in range(2):
-            owner = z * 2 + y
-            values = piece[y].astype(F32)
-            numer[pl.ds(pl.multiple_of(owner * slots, 8), slots), :] = values
-            tails[owner] = unflatten(values[slots - 1 : slots], heads)
+    for owner in range(8):
+        values = pieces[owner // 2, owner % 2].astype(F32)
+        numer[owner * slots : (owner + 1) * slots, :] = values
+        tails[owner] = unflatten(values[slots - 1 : slots], heads)
     lane8 = lanes((heads, 128))
     shifts = jnp.zeros((heads, 128), F32)
     totals = jnp.zeros((heads, 128), F32)
@@ -476,7 +464,7 @@
     ).astype(BF16)
 
 
-def gate_up_kernel(same, flip, all_input, gain, gate, up, sums, own, scr):
+def gate_up_kernel(flip, same, all_input, gain, gate, up, sums, own, scr):
     me = lax.axis_index("pool")
     odd = me % 2 == 1
     part = same.shape[1]
@@ -586,10 +574,11 @@
         (both,) = call(
             merge_kernel,
             "merge",
-            [((2,) + values.shape, values.dtype)],
+            [((pool // 2, 2) + values.shape, values.dtype)],
             [near, flip(values, "pool", 1)],
         )
-        return [both] + [flip(both, "pool", step) for step in (2, 4, 6)]
+        lines = [[y + 2 * z for z in range(pool // 2)] for y in range(2)]
+        return [lax.all_to_all(both, "pool", 0, 0, axis_index_groups=lines)]
 
     part, all_input, tables = call(
         attend_kernel,
@@ -613,10 +602,10 @@
         sum_kernel,
         "head_sum",
         [((requests, part_cols), BF16)],
-        [head_part] + [flip(head_part, "mlp", step) for step in (1, 2, 3)],
+        [head_part] + [flip(head_part, "mlp", step) for step in (3, 2, 1)],
     )
     pieces = []
-    for turn in range(2):
+    for turn in (1, 0):
         route = []
         for m in range(mlp):
             by_distance = sorted(range(4), key=lambda z: (-abs(z - m), z))

time: 53.5 us -> 56.7 us (1.060)
  blocking collectives: 8.36 us -> 27.4 us
  starting transfers between devices: 21.9 us -> 12 us
  waiting for transfers between devices: 16.1 us -> 10.1 us
    all_to_all x0 -> x2, blocking collectives: none -> 19.1 us  [pool_gather(): return [lax.all_to_all(both, 'pool', 0, 0, axis_index_groups=lines)]]
    ppermute x13 -> x7, starting transfers between devices: 17.6 us -> 8.71 us  [flip(): lax.ppermute(values, axis, [(index, index ^ step) for index in range(size)])]
    ppermute x13 -> x7, waiting for transfers between devices: 14 us -> 7.95 us  [flip(): lax.ppermute(values, axis, [(index, index ^ step) for index in range(size)])]
    ppermute x2, starting transfers between devices: 4.27 us -> 3.34 us  [per_device_small(): pieces.append(lax.ppermute(head_sum, ('pool', 'mlp'), route))]
  transfers between devices with their start and end apart: 15 -> 9, of which waited for: 13 -> 8; matrix products, arithmetic and copies ran while one was open for 0% -> 0% of each run, Pallas kernels for 0% -> 0%
where the time goes in v13:
time: 56.7 us; the launch traced here: 56.4 us
  blocking collectives  27.4 us (48%)
  starting transfers between devices  12 us (21%)
  waiting for transfers between devices  10.1 us (18%)
  Pallas kernels  5.19 us (9%)
  local copies, waits for them, and re-layouts  1.45 us (3%)
    all_to_all x2, blocking collectives, pool_gather(): return [lax.all_to_all(both, 'pool', 0, 0, axis_index_groups=lines)]  19.1 us
    ppermute x7, starting transfers between devices, flip(): lax.ppermute(values, axis, [(index, index ^ step) for index in range(size)])  8.71 us
    all_to_all x1, blocking collectives, per_device_small(): lax.all_to_all(down, 'pool', 0, 0, axis_index_groups=[backwards])  8.36 us
    ppermute x7, waiting for transfers between devices, flip(): lax.ppermute(values, axis, [(index, index ^ step) for index in range(size)])  7.95 us
    pallas_call x11, Pallas kernels, call(): pl.pallas_call(kernel, out_shape=[jax.ShapeDtypeStruct(shape, dtype) for...  5.19 us
    ppermute x2, starting transfers between devices, per_device_small(): pieces.append(lax.ppermute(head_sum, ('pool', 'mlp'), route))  3.34 us
    ppermute x2, waiting for transfers between devices, per_device_small(): pieces.append(lax.ppermute(head_sum, ('pool', 'mlp'), route))  2.19 us
    unnamed x18, local copies, waits for them, and re-layouts  1.45 us
  transfers between devices with their start and end apart: 9, of which 8 were waited for; matrix products, arithmetic and copies ran while one was open for 0% of the time, Pallas kernels for 0%

profile of v13, /device:TPU:0, one launch (start us, length us, event | category | flops | bytes accessed | tf_op | source)
XLA Modules:
  0.0 56.4 jit_solution(3754753108731470470)
XLA Ops:
  0.0 0.0 copy-start
  0.0 0.0 copy-start.1
  0.0 1.6 %rotary.1 = (bf16[2,1664]{1,0:T(2,128)(2,1)}, bf16[2,1536]{1,0:T(2,128)(2,1)}) custom-call(s32[2,8]{1,0:T(2,128)} %refs_0_.1, s32[2]{0:T(128)} %refs_1_.1, bf16[2,768]{1,0:T(2,128)(2,1)} %refs_2_.1, bf16[2,768]{1,0:T(2,128)(2,1)} %refs_3_.1, bf16[2,768]{1,0:T(2,128)(2,1)} %refs_4_.1, bf16[2,768]{1,0:T(2,128)(2,1)} %refs_5_.1, bf16[5,256,768]{2,1,0:T(8,128)(2,1)} %keys.1, ...), custom_call_target="tpu_custom_call" | custom-call | bytes 3944520 | tf_op jit(solution)/shard_map/rotary/pallas_call | solution.py:217
  1.6 3.0 %collective-permute-start = (bf16[2,1664]{1,0:T(2,128)(2,1)}, bf16[2,1664]{1,0:T(2,128)(2,1)S(1)}, u32[]{:S(2)}, u32[]{:S(2)}) collective-permute-start(bf16[2,1664]{1,0:T(2,128)(2,1)} %get-tuple-element.14.packed), channel_id=1, source_target_pairs={{0,4},{4,0},{8,12},{12,8},{16,20},{20,16},{24,28},{28,24},{1,5},{5... | collective-permute-start | bytes 19976 | tf_op jit(solution)/shard_map/ppermute | solution.py:526
  4.7 0.0 copy-start.6
  4.7 0.7 %copy-done.6 = bf16[2,1664]{1,0:T(2,128)(2,1)S(1)} copy-done((bf16[2,1664]{1,0:T(2,128)(2,1)S(1)}, bf16[2,1664]{1,0:T(2,128)(2,1)}, u32[]{:S(2)}) %copy-start.6) | copy-done | bytes 6680
  5.4 0.0 copy-start.7
  5.4 0.7 %copy-done.7 = bf16[2,1536]{1,0:T(2,128)(2,1)S(1)} copy-done((bf16[2,1536]{1,0:T(2,128)(2,1)S(1)}, bf16[2,1536]{1,0:T(2,128)(2,1)}, u32[]{:S(2)}) %copy-start.7) | copy-done | bytes 6168
  6.1 0.1 carry.1
  6.2 0.3 collective-permute-done.theirs
  6.5 10.9 %all_to_all.15.pieces = bf16[4,2,2,1664]{3,2,1,0:T(2,128)(2,1)S(1)} all-to-all(bf16[4,2,2,1664]{3,2,1,0:T(2,128)(2,1)S(1)} %merge.2), channel_id=1, replica_groups={{0,8,16,24},{4,12,20,28},{1,9,17,25},{5,13,21,29},{2,10,18,26},{6,14,22..., dimensions={0} | all-to-all | bytes 106496 | tf_op jit(solution)/shard_map/all_to_all | solution.py:581
  17.4 0.0 copy-done
  17.4 0.0 copy-done.1
  17.4 0.0 copy-start.5
  17.4 0.0 copy-start.8
  17.4 0.0 copy-start.3
  17.4 0.0 copy-start.4
  17.4 1.1 %attend.1 = (bf16[8,768]{1,0:T(8,128)(2,1)S(1)}, f32[16,768]{1,0:T(8,128)S(1)}, f32[16,128]{1,0:T(8,128)S(1)}) custom-call(bf16[4,2,2,1664]{3,2,1,0:T(2,128)(2,1)S(1)} %all_to_all.15.pieces, f32[8,896]{1,0:T(8,128)S(1)} %get-tuple-element.17.own, bf16[5,256,768]{2,1,0:T(8,128)(2,1)S(1)} %copy-done, bf16[5,256,768]{2,1,0:T(8,128)(2,1)S(1)} %copy-done.1), custom_call_target="tpu_custom_call" | custom-call | bytes 4014080 | tf_op jit(solution)/shard_map/attend/pallas_call | solution.py:217
  18.5 1.6 %collective-permute-start.1 = (bf16[8,768]{1,0:T(8,128)(2,1)S(1)}, bf16[8,768]{1,0:T(8,128)(2,1)S(1)}, u32[]{:S(2)}, u32[]{:S(2)}) collective-permute-start(bf16[8,768]{1,0:T(8,128)(2,1)S(1)} %get-tuple-element.18.mine), channel_id=1, source_target_pairs={{0,4},{4,0},{8,12},{12,8},{16,20},{20,16},{24,28},{28,24},{1,5},{5... | collective-permute-start | bytes 36872 | tf_op jit(solution)/shard_map/ppermute | solution.py:526
  20.1 2.2 %collective-permute-done.1.theirs = bf16[8,768]{1,0:T(8,128)(2,1)S(1)} collective-permute-done((bf16[8,768]{1,0:T(8,128)(2,1)S(1)}, bf16[8,768]{1,0:T(8,128)(2,1)S(1)}, u32[]{:S(2)}, u32[]{:S(2)}) %collective-permute-start.1) | collective-permute-done | bytes 12320 | tf_op jit(solution)/shard_map/ppermute | solution.py:526
  22.3 8.2 %all_to_all.16.pieces = bf16[4,2,8,768]{3,2,1,0:T(8,128)(2,1)S(1)} all-to-all(bf16[4,2,8,768]{3,2,1,0:T(8,128)(2,1)S(1)} %merge.3), channel_id=1, replica_groups={{0,8,16,24},{4,12,20,28},{1,9,17,25},{5,13,21,29},{2,10,18,26},{6,14,22..., dimensions={0} | all-to-all | bytes 196608 | tf_op jit(solution)/shard_map/all_to_all | solution.py:581
  30.5 0.0 copy-done.5
  30.5 0.7 %combine.1.p0 = bf16[16,384]{1,0:T(8,128)(2,1)S(1)} custom-call(bf16[4,2,8,768]{3,2,1,0:T(8,128)(2,1)S(1)} %all_to_all.16.pieces, f32[16,128]{1,0:T(8,128)S(1)} %get-tuple-element.19.tables, bf16[768,384]{1,0:T(8,128)(2,1)S(1)} %copy-done.5), custom_call_target="tpu_custom_call" | custom-call | bytes 696320 | tf_op jit(solution)/shard_map/combine/pallas_call | solution.py:217
  31.2 0.1 collective-permute-start.2
  31.3 1.6 %collective-permute-start.3 = (bf16[16,384]{1,0:T(8,128)(2,1)S(1)}, bf16[16,384]{1,0:T(8,128)(2,1)S(1)}, u32[]{:S(2)}, u32[]{:S(2)}) collective-permute-start(bf16[16,384]{1,0:T(8,128)(2,1)S(1)} %combine.1.p0), channel_id=1, source_target_pairs={{0,2},{1,3},{2,0},{3,1},{4,6},{5,7},{6,4},{7,5},{8,10},{9,11},{10,... | collective-permute-start | bytes 36872 | tf_op jit(solution)/shard_map/ppermute | solution.py:526
  32.8 0.3 collective-permute-start.4
  33.1 1.3 %collective-permute-done.2.p1 = bf16[16,384]{1,0:T(8,128)(2,1)S(1)} collective-permute-done((bf16[16,384]{1,0:T(8,128)(2,1)S(1)}, bf16[16,384]{1,0:T(8,128)(2,1)S(1)}, u32[]{:S(2)}, u32[]{:S(2)}) %collective-permute-start.2) | collective-permute-done | bytes 12320 | tf_op jit(solution)/shard_map/ppermute | solution.py:526
  34.5 0.6 %collective-permute-done.3.p2 = bf16[16,384]{1,0:T(8,128)(2,1)S(1)} collective-permute-done((bf16[16,384]{1,0:T(8,128)(2,1)S(1)}, bf16[16,384]{1,0:T(8,128)(2,1)S(1)}, u32[]{:S(2)}, u32[]{:S(2)}) %collective-permute-start.3) | collective-permute-done | bytes 12320 | tf_op jit(solution)/shard_map/ppermute | solution.py:526
  35.0 0.0 collective-permute-done.4.p3
  35.0 1.8 %collective-permute-start.5 = (bf16[16,384]{1,0:T(8,128)(2,1)S(1)}, bf16[16,384]{1,0:T(8,128)(2,1)S(1)}, u32[]{:S(2)}, u32[]{:S(2)}) collective-permute-start(bf16[16,384]{1,0:T(8,128)(2,1)S(1)} %head_sum.1), channel_id=1, source_target_pairs={{1,28},{5,24},{0,20},{4,16},{3,12},{7,8},{2,4},{6,0},{9,29},{13,25... | collective-permute-start | bytes 36872 | tf_op jit(solution)/shard_map/ppermute | solution.py:616
  36.9 1.5 %collective-permute-start.6 = (bf16[16,384]{1,0:T(8,128)(2,1)S(1)}, bf16[16,384]{1,0:T(8,128)(2,1)S(1)}, u32[]{:S(2)}, u32[]{:S(2)}) collective-permute-start(bf16[16,384]{1,0:T(8,128)(2,1)S(1)} %head_sum.1), channel_id=1, source_target_pairs={{1,24},{5,28},{0,16},{4,20},{3,8},{7,12},{2,0},{6,4},{9,25},{13,29... | collective-permute-start | bytes 36872 | tf_op jit(solution)/shard_map/ppermute | solution.py:616
  38.4 0.0 copy-done.8
  38.4 1.4 %collective-permute-done.5.flip = bf16[16,384]{1,0:T(8,128)(2,1)S(1)} collective-permute-done((bf16[16,384]{1,0:T(8,128)(2,1)S(1)}, bf16[16,384]{1,0:T(8,128)(2,1)S(1)}, u32[]{:S(2)}, u32[]{:S(2)}) %collective-permute-start.5) | collective-permute-done | bytes 12320 | tf_op jit(solution)/shard_map/ppermute | solution.py:616
  39.8 0.8 %collective-permute-done.6.same = bf16[16,384]{1,0:T(8,128)(2,1)S(1)} collective-permute-done((bf16[16,384]{1,0:T(8,128)(2,1)S(1)}, bf16[16,384]{1,0:T(8,128)(2,1)S(1)}, u32[]{:S(2)}, u32[]{:S(2)}) %collective-permute-start.6) | collective-permute-done | bytes 12320 | tf_op jit(solution)/shard_map/ppermute | solution.py:616
  40.6 0.0 copy-done.3
  40.6 0.0 copy-done.4
  40.6 0.0 copy-start.2
  40.6 0.5 gate_up.1
  41.1 0.1 collective-permute-start.7
  41.2 1.2 %collective-permute-done.7.theirs = bf16[16,2176]{1,0:T(8,128)(2,1)S(1)} collective-permute-done((bf16[16,2176]{1,0:T(8,128)(2,1)S(1)}, bf16[16,2176]{1,0:T(8,128)(2,1)S(1)}, u32[]{:S(2)}, u32[]{:S(2)}) %collective-permute-start.7) | collective-permute-done | bytes 69664 | tf_op jit(solution)/shard_map/ppermute | solution.py:526
  42.4 0.1 core_sum.1.mine
  42.5 2.1 %collective-permute-start.8 = (bf16[16,2176]{1,0:T(8,128)(2,1)S(1)}, bf16[16,2176]{1,0:T(8,128)(2,1)S(1)}, u32[]{:S(2)}, u32[]{:S(2)}) collective-permute-start(bf16[16,2176]{1,0:T(8,128)(2,1)S(1)} %core_sum.1.mine), channel_id=1, source_target_pairs={{0,3},{1,2},{2,1},{3,0},{4,7},{5,6},{6,5},{7,4},{8,11},{9,10},{10,... | collective-permute-start | bytes 208904 | tf_op jit(solution)/shard_map/ppermute | solution.py:526
  44.6 2.4 %collective-permute-done.8.theirs = bf16[16,2176]{1,0:T(8,128)(2,1)S(1)} collective-permute-done((bf16[16,2176]{1,0:T(8,128)(2,1)S(1)}, bf16[16,2176]{1,0:T(8,128)(2,1)S(1)}, u32[]{:S(2)}, u32[]{:S(2)}) %collective-permute-start.8) | collective-permute-done | bytes 69664 | tf_op jit(solution)/shard_map/ppermute | solution.py:526
  47.0 0.0 copy-done.2
  47.0 0.4 down.1
  47.4 8.4 %all_to_all.17.parts = bf16[8,2,768]{2,1,0:T(2,128)(2,1)S(1)} all-to-all(bf16[8,2,768]{2,1,0:T(2,128)(2,1)S(1)} %down.1), channel_id=1, replica_groups={{28,24,20,16,12,8,4,0},{29,25,21,17,13,9,5,1},{30,26,22,18,14,10,6,2},{..., dimensions={0} | all-to-all | bytes 49152 | tf_op jit(solution)/shard_map/all_to_all | solution.py:642
  55.8 0.6 %final.1 = bf16[2,768]{1,0:T(2,128)(2,1)} custom-call(f32[2,768]{1,0:T(2,128)S(1)} %get-tuple-element.21.own, bf16[8,2,768]{2,1,0:T(2,128)(2,1)S(1)} %all_to_all.17.parts), custom_call_target="tpu_custom_call" | custom-call | bytes 30720 | tf_op jit(solution)/shard_map/final/pallas_call | solution.py:217
  (4 shorter events, 0.0 us)
Async XLA Ops:
  0.0 17.4 %copy-start = (bf16[5,256,768]{2,1,0:T(8,128)(2,1)S(1)}, bf16[5,256,768]{2,1,0:T(8,128)(2,1)}, u32[]{:S(2)}) copy-start(bf16[5,256,768]{2,1,0:T(8,128)(2,1)} %keys.1) | copy-start | bytes 5898244
  0.0 17.4 %copy-start.1 = (bf16[5,256,768]{2,1,0:T(8,128)(2,1)S(1)}, bf16[5,256,768]{2,1,0:T(8,128)(2,1)}, u32[]{:S(2)}) copy-start(bf16[5,256,768]{2,1,0:T(8,128)(2,1)} %values.1) | copy-start | bytes 5898244
  1.6 4.9 %collective-permute-start = (bf16[2,1664]{1,0:T(2,128)(2,1)}, bf16[2,1664]{1,0:T(2,128)(2,1)S(1)}, u32[]{:S(2)}, u32[]{:S(2)}) collective-permute-start(bf16[2,1664]{1,0:T(2,128)(2,1)} %get-tuple-element.14.packed), channel_id=1, source_target_pairs={{0,4},{4,0},{8,12},{12,8},{16,20},{20,16},{24,28},{28,24},{1,5},{5... | collective-permute-start | bytes 19976 | tf_op jit(solution)/shard_map/ppermute | solution.py:526
  4.7 0.7 %copy-start.6 = (bf16[2,1664]{1,0:T(2,128)(2,1)S(1)}, bf16[2,1664]{1,0:T(2,128)(2,1)}, u32[]{:S(2)}) copy-start(bf16[2,1664]{1,0:T(2,128)(2,1)} %get-tuple-element.14.packed) | copy-start | bytes 19972
  5.4 0.7 %copy-start.7 = (bf16[2,1536]{1,0:T(2,128)(2,1)S(1)}, bf16[2,1536]{1,0:T(2,128)(2,1)}, u32[]{:S(2)}) copy-start(bf16[2,1536]{1,0:T(2,128)(2,1)} %get-tuple-element.15.new) | copy-start | bytes 18436
  17.4 13.1 %copy-start.5 = (bf16[768,384]{1,0:T(8,128)(2,1)S(1)}, bf16[768,384]{1,0:T(8,128)(2,1)}, u32[]{:S(2)}) copy-start(bf16[768,384]{1,0:T(8,128)(2,1)} %weight.2) | copy-start | bytes 1769476
  17.4 21.0 %copy-start.8 = (bf16[768]{0:T(1024)(128)(2,1)S(1)}, bf16[768]{0:T(1024)(128)(2,1)}, u32[]{:S(2)}) copy-start(bf16[768]{0:T(1024)(128)(2,1)} %param.22) | copy-start | bytes 4612
  17.4 23.2 %copy-start.3 = (bf16[768,1024]{1,0:T(8,128)(2,1)S(1)}, bf16[768,1024]{1,0:T(8,128)(2,1)}, u32[]{:S(2)}) copy-start(bf16[768,1024]{1,0:T(8,128)(2,1)} %gate.1) | copy-start | bytes 4718596
  17.4 23.2 %copy-start.4 = (bf16[768,1024]{1,0:T(8,128)(2,1)S(1)}, bf16[768,1024]{1,0:T(8,128)(2,1)}, u32[]{:S(2)}) copy-start(bf16[768,1024]{1,0:T(8,128)(2,1)} %up.1) | copy-start | bytes 4718596
  18.5 3.8 %collective-permute-start.1 = (bf16[8,768]{1,0:T(8,128)(2,1)S(1)}, bf16[8,768]{1,0:T(8,128)(2,1)S(1)}, u32[]{:S(2)}, u32[]{:S(2)}) collective-permute-start(bf16[8,768]{1,0:T(8,128)(2,1)S(1)} %get-tuple-element.18.mine), channel_id=1, source_target_pairs={{0,4},{4,0},{8,12},{12,8},{16,20},{20,16},{24,28},{28,24},{1,5},{5... | collective-permute-start | bytes 36872 | tf_op jit(solution)/shard_map/ppermute | solution.py:526
  31.2 3.2 %collective-permute-start.2 = (bf16[16,384]{1,0:T(8,128)(2,1)S(1)}, bf16[16,384]{1,0:T(8,128)(2,1)S(1)}, u32[]{:S(2)}, u32[]{:S(2)}) collective-permute-start(bf16[16,384]{1,0:T(8,128)(2,1)S(1)} %combine.1.p0), channel_id=1, source_target_pairs={{0,3},{1,2},{2,1},{3,0},{4,7},{5,6},{6,5},{7,4},{8,11},{9,10},{10,... | collective-permute-start | bytes 36872 | tf_op jit(solution)/shard_map/ppermute | solution.py:526
  31.3 3.8 %collective-permute-start.3 = (bf16[16,384]{1,0:T(8,128)(2,1)S(1)}, bf16[16,384]{1,0:T(8,128)(2,1)S(1)}, u32[]{:S(2)}, u32[]{:S(2)}) collective-permute-start(bf16[16,384]{1,0:T(8,128)(2,1)S(1)} %combine.1.p0), channel_id=1, source_target_pairs={{0,2},{1,3},{2,0},{3,1},{4,6},{5,7},{6,4},{7,5},{8,10},{9,11},{10,... | collective-permute-start | bytes 36872 | tf_op jit(solution)/shard_map/ppermute | solution.py:526
  32.8 2.2 %collective-permute-start.4 = (bf16[16,384]{1,0:T(8,128)(2,1)S(1)}, bf16[16,384]{1,0:T(8,128)(2,1)S(1)}, u32[]{:S(2)}, u32[]{:S(2)}) collective-permute-start(bf16[16,384]{1,0:T(8,128)(2,1)S(1)} %combine.1.p0), channel_id=1, source_target_pairs={{0,1},{1,0},{2,3},{3,2},{4,5},{5,4},{6,7},{7,6},{8,9},{9,8},{10,11... | collective-permute-start | bytes 36872 | tf_op jit(solution)/shard_map/ppermute | solution.py:526
  35.0 4.8 %collective-permute-start.5 = (bf16[16,384]{1,0:T(8,128)(2,1)S(1)}, bf16[16,384]{1,0:T(8,128)(2,1)S(1)}, u32[]{:S(2)}, u32[]{:S(2)}) collective-permute-start(bf16[16,384]{1,0:T(8,128)(2,1)S(1)} %head_sum.1), channel_id=1, source_target_pairs={{1,28},{5,24},{0,20},{4,16},{3,12},{7,8},{2,4},{6,0},{9,29},{13,25... | collective-permute-start | bytes 36872 | tf_op jit(solution)/shard_map/ppermute | solution.py:616
  36.9 3.7 %collective-permute-start.6 = (bf16[16,384]{1,0:T(8,128)(2,1)S(1)}, bf16[16,384]{1,0:T(8,128)(2,1)S(1)}, u32[]{:S(2)}, u32[]{:S(2)}) collective-permute-start(bf16[16,384]{1,0:T(8,128)(2,1)S(1)} %head_sum.1), channel_id=1, source_target_pairs={{1,24},{5,28},{0,16},{4,20},{3,8},{7,12},{2,0},{6,4},{9,25},{13,29... | collective-permute-start | bytes 36872 | tf_op jit(solution)/shard_map/ppermute | solution.py:616
  40.6 6.4 %copy-start.2 = (bf16[1024,768]{1,0:T(8,128)(2,1)S(1)}, bf16[1024,768]{1,0:T(8,128)(2,1)}, u32[]{:S(2)}) copy-start(bf16[1024,768]{1,0:T(8,128)(2,1)} %weight.3) | copy-start | bytes 4718596
  41.1 1.3 %collective-permute-start.7 = (bf16[16,2176]{1,0:T(8,128)(2,1)S(1)}, bf16[16,2176]{1,0:T(8,128)(2,1)S(1)}, u32[]{:S(2)}, u32[]{:S(2)}) collective-permute-start(bf16[16,2176]{1,0:T(8,128)(2,1)S(1)} %get-tuple-element.22.mine), channel_id=1, source_target_pairs={{0,1},{1,0},{2,3},{3,2},{4,5},{5,4},{6,7},{7,6},{8,9},{9,8},{10,11... | collective-permute-start | bytes 208904 | tf_op jit(solution)/shard_map/ppermute | solution.py:526
  42.5 4.5 %collective-permute-start.8 = (bf16[16,2176]{1,0:T(8,128)(2,1)S(1)}, bf16[16,2176]{1,0:T(8,128)(2,1)S(1)}, u32[]{:S(2)}, u32[]{:S(2)}) collective-permute-start(bf16[16,2176]{1,0:T(8,128)(2,1)S(1)} %core_sum.1.mine), channel_id=1, source_target_pairs={{0,3},{1,2},{2,1},{3,0},{4,7},{5,6},{6,5},{7,4},{8,11},{9,10},{10,... | collective-permute-start | bytes 208904 | tf_op jit(solution)/shard_map/ppermute | solution.py:526

commit v14 on v12

--- a/solution.py
+++ b/solution.py
@@ -293,12 +293,8 @@
     freq = jnp.zeros((8, period), F32)
     for i in range(HD // 2):
         freq = jnp.where(turn == i, float(np.float32(10000.0 ** (-2.0 * i / HD))), freq)
-    for copy in copies:
+    for copy in copies[:2]:
         copy.wait()
-    scr[...] = jnp.zeros_like(scr)
-    scr[0:rows, :] = query[...].astype(F32)
-    scr[rows : 2 * rows, :] = key[...].astype(F32)
-    values = scr[...]
     line = rows_of((8, period))
     where_at = jnp.zeros((8, period), F32)
     for r in range(rows):
@@ -307,6 +303,12 @@
     angles = where_at * freq
     cosine = jnp.concatenate([jnp.cos(angles)] * (width // period), 1)
     sine = jnp.concatenate([jnp.sin(angles)] * (width // period), 1)
+    for copy in copies[2:]:
+        copy.wait()
+    scr[...] = jnp.zeros_like(scr)
+    scr[0:rows, :] = query[...].astype(F32)
+    scr[rows : 2 * rows, :] = key[...].astype(F32)
+    values = scr[...]
     first = lanes((8, width)) % HD < HD // 2
     ahead = pltpu.roll(values, width - HD // 2, 1)
     behind = pltpu.roll(values, HD // 2, 1)
@@ -359,7 +361,7 @@
     both[1 - y] = theirs[...]
 
 
-def attend_kernel(a0, a1, a2, a3, own, keys, values, part, residual, tables, scr):
+def attend_kernel(a0, a1, a3, a2, own, keys, values, part, residual, tables, scr):
     blocks, block_len, width = keys.shape
     rows = a0.shape[1]
     heads = width // HD
@@ -420,7 +422,7 @@
     part[...] = numer.astype(BF16)
 
 
-def combine_kernel(b0, b1, b2, b3, tables, weight, head_part, numer, tails, mix):
+def combine_kernel(b0, b1, b2, b3, tables, weight, head_part, numer, tails):
     requests = tables.shape[0]
     slots = b0.shape[1]
     width = weight.shape[0]
@@ -452,15 +454,16 @@
     belongs = (self_id == rows_of((requests, 128))) & (lane < 64)
     for k in range(8):
         belongs = belongs | (table[:, k : k + 1] == block_id)
-    for h in range(heads):
-        shift = jnp.broadcast_to(shifts[h : h + 1], (requests, 128))
-        top = jnp.max(jnp.where(belongs, shift, LOW), 1, keepdims=True)
-        scale = jnp.where(belongs, jnp.exp(shift - top), 0.0)
-        total = jnp.sum(scale * totals[h : h + 1], 1, keepdims=True)
-        mix[h * requests : (h + 1) * requests, :] = scale / total
-    full = jnp.dot(
-        mix[:, : 8 * slots].astype(BF16), numer[...].astype(BF16), preferred_element_type=F32
-    )
+    def spread(values):
+        rows_each = [jnp.broadcast_to(values[h : h + 1], (requests, 128)) for h in range(heads)]
+        return jnp.concatenate(rows_each, 0)
+
+    outside = jnp.concatenate([jnp.where(belongs, 0.0, LOW)] * heads, 0)
+    shift = spread(shifts) + outside
+    scale = jnp.exp(shift - jnp.max(shift, 1, keepdims=True))
+    total = jnp.sum(scale * spread(totals), 1, keepdims=True)
+    mix = (scale / total)[:, : 8 * slots].astype(BF16)
+    full = jnp.dot(mix, numer[...].astype(BF16), preferred_element_type=F32)
     head = lanes((requests, width)) // HD
     attended = jnp.zeros((requests, width), F32)
     for h in range(heads):
@@ -582,31 +585,31 @@
         [packed, new],
     )
 
-    def pool_gather(values, near):
+    def pool_gather(values, near, steps):
         (both,) = call(
             merge_kernel,
             "merge",
             [((2,) + values.shape, values.dtype)],
             [near, flip(values, "pool", 1)],
         )
-        return [both] + [flip(both, "pool", step) for step in (2, 4, 6)]
+        got = {step: flip(both, "pool", step) for step in steps}
+        return [both] + [got[step] for step in steps]
 
     part, all_input, tables = call(
         attend_kernel,
         "attend",
         [((slots, width), BF16), ((requests, width), F32), ((requests, 128), F32)],
-        pool_gather(packed, packed_near) + [own, key_cache, value_cache],
+        pool_gather(packed, packed_near, (2, 6, 4)) + [own, key_cache, value_cache],
         [pltpu.VMEM((requests, packed_width), F32)],
     )
     (head_part,) = call(
         combine_kernel,
         "combine",
         [((requests, part_cols), BF16)],
-        pool_gather(part, part) + [tables, out_weight],
+        pool_gather(part, part, (2, 4, 6)) + [tables, out_weight],
         [
             pltpu.VMEM((pool * slots, width), F32),
             pltpu.VMEM((pool, slots, 128), F32),
-            pltpu.VMEM((requests * width // HD, 128), F32),
         ],
     )
     (head_sum,) = call(

time: 53.5 us -> 53.9 us (level)
  waiting for transfers between devices: 16.1 us -> 17 us
    ppermute x13, waiting for transfers between devices: 14 us -> 14.8 us  [flip(): lax.ppermute(values, axis, [(index, index ^ step) for index in range(size)])]
    ppermute x13, starting transfers between devices: 17.6 us -> 16.9 us  [flip(): lax.ppermute(values, axis, [(index, index ^ step) for index in range(size)])]
  transfers between devices with their start and end apart: 15 -> 15, of which waited for: 13 -> 12; matrix products, arithmetic and copies ran while one was open for 0% -> 0% of each run, Pallas kernels for 0% -> 0%
where the time goes in v14:
time: 53.9 us; the launch traced here: 53.6 us
  starting transfers between devices  21.4 us (40%)
  waiting for transfers between devices  17 us (32%)
  blocking collectives  8.39 us (16%)
  Pallas kernels  5.28 us (10%)
  local copies, waits for them, and re-layouts  1.46 us (3%)
    ppermute x13, starting transfers between devices, flip(): lax.ppermute(values, axis, [(index, index ^ step) for index in range(size)])  16.9 us
    ppermute x13, waiting for transfers between devices, flip(): lax.ppermute(values, axis, [(index, index ^ step) for index in range(size)])  14.8 us
    all_to_all x1, blocking collectives, per_device_small(): lax.all_to_all(down, 'pool', 0, 0, axis_index_groups=[backwards])  8.39 us
    pallas_call x11, Pallas kernels, call(): pl.pallas_call(kernel, out_shape=[jax.ShapeDtypeStruct(shape, dtype) for...  5.28 us
    ppermute x2, starting transfers between devices, per_device_small(): pieces.append(lax.ppermute(head_sum, ('pool', 'mlp'), route))  4.52 us
    ppermute x2, waiting for transfers between devices, per_device_small(): pieces.append(lax.ppermute(head_sum, ('pool', 'mlp'), route))  2.2 us
    unnamed x18, local copies, waits for them, and re-layouts  1.45 us
  transfers between devices with their start and end apart: 15, of which 12 were waited for; matrix products, arithmetic and copies ran while one was open for 0% of the time, Pallas kernels for 0%

profile of v14, /device:TPU:0, one launch (start us, length us, event | category | flops | bytes accessed | tf_op | source)
XLA Modules:
  0.0 53.6 jit_solution(6516136313739573231)
XLA Ops:
  0.0 1.6 %rotary.1 = (bf16[2,1664]{1,0:T(2,128)(2,1)}, bf16[2,1536]{1,0:T(2,128)(2,1)}) custom-call(s32[2,8]{1,0:T(2,128)} %refs_0_.1, s32[2]{0:T(128)} %refs_1_.1, bf16[2,768]{1,0:T(2,128)(2,1)} %refs_2_.1, bf16[2,768]{1,0:T(2,128)(2,1)} %refs_3_.1, bf16[2,768]{1,0:T(2,128)(2,1)} %refs_4_.1, bf16[2,768]{1,0:T(2,128)(2,1)} %refs_5_.1, bf16[5,256,768]{2,1,0:T(8,128)(2,1)} %keys.1, ...), custom_call_target="tpu_custom_call" | custom-call | bytes 3944520 | tf_op jit(solution)/shard_map/rotary/pallas_call | solution.py:217
  1.7 3.0 %collective-permute-start = (bf16[2,1664]{1,0:T(2,128)(2,1)}, bf16[2,1664]{1,0:T(2,128)(2,1)S(1)}, u32[]{:S(2)}, u32[]{:S(2)}) collective-permute-start(bf16[2,1664]{1,0:T(2,128)(2,1)} %get-tuple-element.14.packed), channel_id=1, source_target_pairs={{0,4},{4,0},{8,12},{12,8},{16,20},{20,16},{24,28},{28,24},{1,5},{5... | collective-permute-start | bytes 19976 | tf_op jit(solution)/shard_map/ppermute | solution.py:541
  4.7 0.7 %copy-done.6 = bf16[2,1664]{1,0:T(2,128)(2,1)S(1)} copy-done((bf16[2,1664]{1,0:T(2,128)(2,1)S(1)}, bf16[2,1664]{1,0:T(2,128)(2,1)}, u32[]{:S(2)}) %copy-start.6) | copy-done | bytes 6680
  5.4 0.7 %copy-done.7 = bf16[2,1536]{1,0:T(2,128)(2,1)S(1)} copy-done((bf16[2,1536]{1,0:T(2,128)(2,1)S(1)}, bf16[2,1536]{1,0:T(2,128)(2,1)}, u32[]{:S(2)}) %copy-start.7) | copy-done | bytes 6168
  6.1 0.1 carry.1
  6.2 0.3 collective-permute-done.theirs
  6.5 3.1 %collective-permute-start.3 = (bf16[2,2,1664]{2,1,0:T(2,128)(2,1)S(1)}, bf16[2,2,1664]{2,1,0:T(2,128)(2,1)S(1)}, u32[]{:S(2)}, u32[]{:S(2)}) collective-permute-start(bf16[2,2,1664]{2,1,0:T(2,128)(2,1)S(1)} %merge.2.a0), channel_id=1, source_target_pairs={{0,16},{4,20},{8,24},{12,28},{16,0},{20,4},{24,8},{28,12},{1,17},{... | collective-permute-start | bytes 39944 | tf_op jit(solution)/shard_map/ppermute | solution.py:541
  9.6 1.3 %collective-permute-start.2 = (bf16[2,2,1664]{2,1,0:T(2,128)(2,1)S(1)}, bf16[2,2,1664]{2,1,0:T(2,128)(2,1)S(1)}, u32[]{:S(2)}, u32[]{:S(2)}) collective-permute-start(bf16[2,2,1664]{2,1,0:T(2,128)(2,1)S(1)} %merge.2.a0), channel_id=1, source_target_pairs={{0,24},{4,28},{8,16},{12,20},{16,8},{20,12},{24,0},{28,4},{1,25},{... | collective-permute-start | bytes 39944 | tf_op jit(solution)/shard_map/ppermute | solution.py:541
  11.0 0.2 collective-permute-start.1
  11.2 0.1 collective-permute-done.3.a2
  11.3 3.8 %collective-permute-done.2.a3 = bf16[2,2,1664]{2,1,0:T(2,128)(2,1)S(1)} collective-permute-done((bf16[2,2,1664]{2,1,0:T(2,128)(2,1)S(1)}, bf16[2,2,1664]{2,1,0:T(2,128)(2,1)S(1)}, u32[]{:S(2)}, u32[]{:S(2)}) %collective-permute-start.2) | collective-permute-done | bytes 13344 | tf_op jit(solution)/shard_map/ppermute | solution.py:541
  15.1 0.0 collective-permute-done.1.a1
  15.1 0.0 copy-done.1
  15.1 0.0 copy-done
  15.1 0.0 copy-start.5
  15.1 0.0 copy-start.8
  15.1 0.0 copy-start.3
  15.2 0.0 copy-start.4
  15.2 1.1 %attend.1 = (bf16[8,768]{1,0:T(8,128)(2,1)S(1)}, f32[16,768]{1,0:T(8,128)S(1)}, f32[16,128]{1,0:T(8,128)S(1)}) custom-call(bf16[2,2,1664]{2,1,0:T(2,128)(2,1)S(1)} %merge.2.a0, bf16[2,2,1664]{2,1,0:T(2,128)(2,1)S(1)} %collective-permute-done.1.a1, bf16[2,2,1664]{2,1,0:T(2,128)(2,1)S(1)} %collective-permute-done.2.a3, ...), custom_call_target="tpu_custom_call" | custom-call | bytes 4014080 | tf_op jit(solution)/shard_map/attend/pallas_call | solution.py:217
  16.3 1.6 %collective-permute-start.4 = (bf16[8,768]{1,0:T(8,128)(2,1)S(1)}, bf16[8,768]{1,0:T(8,128)(2,1)S(1)}, u32[]{:S(2)}, u32[]{:S(2)}) collective-permute-start(bf16[8,768]{1,0:T(8,128)(2,1)S(1)} %get-tuple-element.18.mine), channel_id=1, source_target_pairs={{0,4},{4,0},{8,12},{12,8},{16,20},{20,16},{24,28},{28,24},{1,5},{5... | collective-permute-start | bytes 36872 | tf_op jit(solution)/shard_map/ppermute | solution.py:541
  17.9 2.2 %collective-permute-done.4.theirs = bf16[8,768]{1,0:T(8,128)(2,1)S(1)} collective-permute-done((bf16[8,768]{1,0:T(8,128)(2,1)S(1)}, bf16[8,768]{1,0:T(8,128)(2,1)S(1)}, u32[]{:S(2)}, u32[]{:S(2)}) %collective-permute-start.4) | collective-permute-done | bytes 12320 | tf_op jit(solution)/shard_map/ppermute | solution.py:541
  20.1 2.0 %collective-permute-start.7 = (bf16[2,8,768]{2,1,0:T(8,128)(2,1)S(1)}, bf16[2,8,768]{2,1,0:T(8,128)(2,1)S(1)}, u32[]{:S(2)}, u32[]{:S(2)}) collective-permute-start(bf16[2,8,768]{2,1,0:T(8,128)(2,1)S(1)} %merge.3.b0), channel_id=1, source_target_pairs={{0,24},{4,28},{8,16},{12,20},{16,8},{20,12},{24,0},{28,4},{1,25},{... | collective-permute-start | bytes 73736 | tf_op jit(solution)/shard_map/ppermute | solution.py:541
  22.1 0.0 collective-permute-start.6
  22.1 2.4 %collective-permute-start.5 = (bf16[2,8,768]{2,1,0:T(8,128)(2,1)S(1)}, bf16[2,8,768]{2,1,0:T(8,128)(2,1)S(1)}, u32[]{:S(2)}, u32[]{:S(2)}) collective-permute-start(bf16[2,8,768]{2,1,0:T(8,128)(2,1)S(1)} %merge.3.b0), channel_id=1, source_target_pairs={{0,8},{4,12},{8,0},{12,4},{16,24},{20,28},{24,16},{28,20},{1,9},{5... | collective-permute-start | bytes 73736 | tf_op jit(solution)/shard_map/ppermute | solution.py:541
  24.5 1.2 %collective-permute-done.7.b3 = bf16[2,8,768]{2,1,0:T(8,128)(2,1)S(1)} collective-permute-done((bf16[2,8,768]{2,1,0:T(8,128)(2,1)S(1)}, bf16[2,8,768]{2,1,0:T(8,128)(2,1)S(1)}, u32[]{:S(2)}, u32[]{:S(2)}) %collective-permute-start.7) | collective-permute-done | bytes 24608 | tf_op jit(solution)/shard_map/ppermute | solution.py:541
  25.7 1.1 %collective-permute-done.6.b2 = bf16[2,8,768]{2,1,0:T(8,128)(2,1)S(1)} collective-permute-done((bf16[2,8,768]{2,1,0:T(8,128)(2,1)S(1)}, bf16[2,8,768]{2,1,0:T(8,128)(2,1)S(1)}, u32[]{:S(2)}, u32[]{:S(2)}) %collective-permute-start.6) | collective-permute-done | bytes 24608 | tf_op jit(solution)/shard_map/ppermute | solution.py:541
  26.8 0.0 collective-permute-done.5.b1
  26.8 0.7 %combine.1.p0 = bf16[16,384]{1,0:T(8,128)(2,1)S(1)} custom-call(bf16[2,8,768]{2,1,0:T(8,128)(2,1)S(1)} %merge.3.b0, bf16[2,8,768]{2,1,0:T(8,128)(2,1)S(1)} %collective-permute-done.5.b1, bf16[2,8,768]{2,1,0:T(8,128)(2,1)S(1)} %collective-permute-done.6.b2, bf16[2,8,768]{2,1,0:T(8,128)(2,1)S(1)} %collective-permute-done.7.b3, ...), custom_call_target="tpu_custom_call" | custom-call | bytes 696320 | tf_op jit(solution)/shard_map/combine/pallas_call | solution.py:217
  27.6 0.1 collective-permute-start.10
  27.6 1.6 %collective-permute-start.9 = (bf16[16,384]{1,0:T(8,128)(2,1)S(1)}, bf16[16,384]{1,0:T(8,128)(2,1)S(1)}, u32[]{:S(2)}, u32[]{:S(2)}) collective-permute-start(bf16[16,384]{1,0:T(8,128)(2,1)S(1)} %combine.1.p0), channel_id=1, source_target_pairs={{0,2},{1,3},{2,0},{3,1},{4,6},{5,7},{6,4},{7,5},{8,10},{9,11},{10,... | collective-permute-start | bytes 36872 | tf_op jit(solution)/shard_map/ppermute | solution.py:541
  29.2 0.3 collective-permute-start.8
  29.5 1.3 %collective-permute-done.10.p3 = bf16[16,384]{1,0:T(8,128)(2,1)S(1)} collective-permute-done((bf16[16,384]{1,0:T(8,128)(2,1)S(1)}, bf16[16,384]{1,0:T(8,128)(2,1)S(1)}, u32[]{:S(2)}, u32[]{:S(2)}) %collective-permute-start.10) | collective-permute-done | bytes 12320 | tf_op jit(solution)/shard_map/ppermute | solution.py:541
  30.8 0.6 %collective-permute-done.9.p2 = bf16[16,384]{1,0:T(8,128)(2,1)S(1)} collective-permute-done((bf16[16,384]{1,0:T(8,128)(2,1)S(1)}, bf16[16,384]{1,0:T(8,128)(2,1)S(1)}, u32[]{:S(2)}, u32[]{:S(2)}) %collective-permute-start.9) | collective-permute-done | bytes 12320 | tf_op jit(solution)/shard_map/ppermute | solution.py:541
  31.4 0.0 collective-permute-done.8.p1
  31.4 3.0 %collective-permute-start.12 = (bf16[16,384]{1,0:T(8,128)(2,1)S(1)}, bf16[16,384]{1,0:T(8,128)(2,1)S(1)}, u32[]{:S(2)}, u32[]{:S(2)}) collective-permute-start(bf16[16,384]{1,0:T(8,128)(2,1)S(1)} %head_sum.1), channel_id=1, source_target_pairs={{1,28},{5,24},{0,20},{4,16},{3,12},{7,8},{2,4},{6,0},{9,29},{13,25... | collective-permute-start | bytes 36872 | tf_op jit(solution)/shard_map/ppermute | solution.py:630
  34.4 1.5 %collective-permute-start.11 = (bf16[16,384]{1,0:T(8,128)(2,1)S(1)}, bf16[16,384]{1,0:T(8,128)(2,1)S(1)}, u32[]{:S(2)}, u32[]{:S(2)}) collective-permute-start(bf16[16,384]{1,0:T(8,128)(2,1)S(1)} %head_sum.1), channel_id=1, source_target_pairs={{1,24},{5,28},{0,16},{4,20},{3,8},{7,12},{2,0},{6,4},{9,25},{13,29... | collective-permute-start | bytes 36872 | tf_op jit(solution)/shard_map/ppermute | solution.py:630
  35.9 0.0 copy-done.8
  35.9 0.2 collective-permute-done.12.flip
  36.2 2.0 %collective-permute-done.11.same = bf16[16,384]{1,0:T(8,128)(2,1)S(1)} collective-permute-done((bf16[16,384]{1,0:T(8,128)(2,1)S(1)}, bf16[16,384]{1,0:T(8,128)(2,1)S(1)}, u32[]{:S(2)}, u32[]{:S(2)}) %collective-permute-start.11) | collective-permute-done | bytes 12320 | tf_op jit(solution)/shard_map/ppermute | solution.py:630
  38.1 0.5 gate_up.1
  38.7 0.0 collective-permute-start.13
  38.7 1.3 %collective-permute-done.13.theirs = bf16[16,2176]{1,0:T(8,128)(2,1)S(1)} collective-permute-done((bf16[16,2176]{1,0:T(8,128)(2,1)S(1)}, bf16[16,2176]{1,0:T(8,128)(2,1)S(1)}, u32[]{:S(2)}, u32[]{:S(2)}) %collective-permute-start.13) | collective-permute-done | bytes 69664 | tf_op jit(solution)/shard_map/ppermute | solution.py:541
  39.9 0.1 core_sum.1.mine
  40.0 1.3 %collective-permute-start.14 = (bf16[16,2176]{1,0:T(8,128)(2,1)S(1)}, bf16[16,2176]{1,0:T(8,128)(2,1)S(1)}, u32[]{:S(2)}, u32[]{:S(2)}) collective-permute-start(bf16[16,2176]{1,0:T(8,128)(2,1)S(1)} %core_sum.1.mine), channel_id=1, source_target_pairs={{0,3},{1,2},{2,1},{3,0},{4,7},{5,6},{6,5},{7,4},{8,11},{9,10},{10,... | collective-permute-start | bytes 208904 | tf_op jit(solution)/shard_map/ppermute | solution.py:541
  41.3 2.8 %collective-permute-done.14.theirs = bf16[16,2176]{1,0:T(8,128)(2,1)S(1)} collective-permute-done((bf16[16,2176]{1,0:T(8,128)(2,1)S(1)}, bf16[16,2176]{1,0:T(8,128)(2,1)S(1)}, u32[]{:S(2)}, u32[]{:S(2)}) %collective-permute-start.14) | collective-permute-done | bytes 69664 | tf_op jit(solution)/shard_map/ppermute | solution.py:541
  44.2 0.4 down.1
  44.6 8.4 %all_to_all.5.parts = bf16[8,2,768]{2,1,0:T(2,128)(2,1)S(1)} all-to-all(bf16[8,2,768]{2,1,0:T(2,128)(2,1)S(1)} %down.1), channel_id=1, replica_groups={{28,24,20,16,12,8,4,0},{29,25,21,17,13,9,5,1},{30,26,22,18,14,10,6,2},{..., dimensions={0} | all-to-all | bytes 49152 | tf_op jit(solution)/shard_map/all_to_all | solution.py:656
  53.0 0.6 %final.1 = bf16[2,768]{1,0:T(2,128)(2,1)} custom-call(f32[2,768]{1,0:T(2,128)S(1)} %get-tuple-element.21.own, bf16[8,2,768]{2,1,0:T(2,128)(2,1)S(1)} %all_to_all.5.parts), custom_call_target="tpu_custom_call" | custom-call | bytes 30720 | tf_op jit(solution)/shard_map/final/pallas_call | solution.py:217
  (13 shorter events, 0.0 us)
Async XLA Ops:
  0.0 15.1 %copy-start.1 = (bf16[5,256,768]{2,1,0:T(8,128)(2,1)S(1)}, bf16[5,256,768]{2,1,0:T(8,128)(2,1)}, u32[]{:S(2)}) copy-start(bf16[5,256,768]{2,1,0:T(8,128)(2,1)} %values.1) | copy-start | bytes 5898244
  0.0 15.1 %copy-start = (bf16[5,256,768]{2,1,0:T(8,128)(2,1)S(1)}, bf16[5,256,768]{2,1,0:T(8,128)(2,1)}, u32[]{:S(2)}) copy-start(bf16[5,256,768]{2,1,0:T(8,128)(2,1)} %keys.1) | copy-start | bytes 5898244
  1.7 4.9 %collective-permute-start = (bf16[2,1664]{1,0:T(2,128)(2,1)}, bf16[2,1664]{1,0:T(2,128)(2,1)S(1)}, u32[]{:S(2)}, u32[]{:S(2)}) collective-permute-start(bf16[2,1664]{1,0:T(2,128)(2,1)} %get-tuple-element.14.packed), channel_id=1, source_target_pairs={{0,4},{4,0},{8,12},{12,8},{16,20},{20,16},{24,28},{28,24},{1,5},{5... | collective-permute-start | bytes 19976 | tf_op jit(solution)/shard_map/ppermute | solution.py:541
  4.7 0.7 %copy-start.6 = (bf16[2,1664]{1,0:T(2,128)(2,1)S(1)}, bf16[2,1664]{1,0:T(2,128)(2,1)}, u32[]{:S(2)}) copy-start(bf16[2,1664]{1,0:T(2,128)(2,1)} %get-tuple-element.14.packed) | copy-start | bytes 19972
  5.4 0.7 %copy-start.7 = (bf16[2,1536]{1,0:T(2,128)(2,1)S(1)}, bf16[2,1536]{1,0:T(2,128)(2,1)}, u32[]{:S(2)}) copy-start(bf16[2,1536]{1,0:T(2,128)(2,1)} %get-tuple-element.15.new) | copy-start | bytes 18436
  6.5 4.8 %collective-permute-start.3 = (bf16[2,2,1664]{2,1,0:T(2,128)(2,1)S(1)}, bf16[2,2,1664]{2,1,0:T(2,128)(2,1)S(1)}, u32[]{:S(2)}, u32[]{:S(2)}) collective-permute-start(bf16[2,2,1664]{2,1,0:T(2,128)(2,1)S(1)} %merge.2.a0), channel_id=1, source_target_pairs={{0,16},{4,20},{8,24},{12,28},{16,0},{20,4},{24,8},{28,12},{1,17},{... | collective-permute-start | bytes 39944 | tf_op jit(solution)/shard_map/ppermute | solution.py:541
  9.6 5.5 %collective-permute-start.2 = (bf16[2,2,1664]{2,1,0:T(2,128)(2,1)S(1)}, bf16[2,2,1664]{2,1,0:T(2,128)(2,1)S(1)}, u32[]{:S(2)}, u32[]{:S(2)}) collective-permute-start(bf16[2,2,1664]{2,1,0:T(2,128)(2,1)S(1)} %merge.2.a0), channel_id=1, source_target_pairs={{0,24},{4,28},{8,16},{12,20},{16,8},{20,12},{24,0},{28,4},{1,25},{... | collective-permute-start | bytes 39944 | tf_op jit(solution)/shard_map/ppermute | solution.py:541
  11.0 4.2 %collective-permute-start.1 = (bf16[2,2,1664]{2,1,0:T(2,128)(2,1)S(1)}, bf16[2,2,1664]{2,1,0:T(2,128)(2,1)S(1)}, u32[]{:S(2)}, u32[]{:S(2)}) collective-permute-start(bf16[2,2,1664]{2,1,0:T(2,128)(2,1)S(1)} %merge.2.a0), channel_id=1, source_target_pairs={{0,8},{4,12},{8,0},{12,4},{16,24},{20,28},{24,16},{28,20},{1,9},{5... | collective-permute-start | bytes 39944 | tf_op jit(solution)/shard_map/ppermute | solution.py:541
  15.1 11.7 %copy-start.5 = (bf16[768,384]{1,0:T(8,128)(2,1)S(1)}, bf16[768,384]{1,0:T(8,128)(2,1)}, u32[]{:S(2)}) copy-start(bf16[768,384]{1,0:T(8,128)(2,1)} %weight.2) | copy-start | bytes 1769476
  15.1 20.8 %copy-start.8 = (bf16[768]{0:T(1024)(128)(2,1)S(1)}, bf16[768]{0:T(1024)(128)(2,1)}, u32[]{:S(2)}) copy-start(bf16[768]{0:T(1024)(128)(2,1)} %param.22) | copy-start | bytes 4612
  15.1 23.0 %copy-start.3 = (bf16[768,1024]{1,0:T(8,128)(2,1)S(1)}, bf16[768,1024]{1,0:T(8,128)(2,1)}, u32[]{:S(2)}) copy-start(bf16[768,1024]{1,0:T(8,128)(2,1)} %gate.1) | copy-start | bytes 4718596
  15.2 23.0 %copy-start.4 = (bf16[768,1024]{1,0:T(8,128)(2,1)S(1)}, bf16[768,1024]{1,0:T(8,128)(2,1)}, u32[]{:S(2)}) copy-start(bf16[768,1024]{1,0:T(8,128)(2,1)} %up.1) | copy-start | bytes 4718596
  16.3 3.8 %collective-permute-start.4 = (bf16[8,768]{1,0:T(8,128)(2,1)S(1)}, bf16[8,768]{1,0:T(8,128)(2,1)S(1)}, u32[]{:S(2)}, u32[]{:S(2)}) collective-permute-start(bf16[8,768]{1,0:T(8,128)(2,1)S(1)} %get-tuple-element.18.mine), channel_id=1, source_target_pairs={{0,4},{4,0},{8,12},{12,8},{16,20},{20,16},{24,28},{28,24},{1,5},{5... | collective-permute-start | bytes 36872 | tf_op jit(solution)/shard_map/ppermute | solution.py:541
  20.1 5.6 %collective-permute-start.7 = (bf16[2,8,768]{2,1,0:T(8,128)(2,1)S(1)}, bf16[2,8,768]{2,1,0:T(8,128)(2,1)S(1)}, u32[]{:S(2)}, u32[]{:S(2)}) collective-permute-start(bf16[2,8,768]{2,1,0:T(8,128)(2,1)S(1)} %merge.3.b0), channel_id=1, source_target_pairs={{0,24},{4,28},{8,16},{12,20},{16,8},{20,12},{24,0},{28,4},{1,25},{... | collective-permute-start | bytes 73736 | tf_op jit(solution)/shard_map/ppermute | solution.py:541
  22.1 4.7 %collective-permute-start.6 = (bf16[2,8,768]{2,1,0:T(8,128)(2,1)S(1)}, bf16[2,8,768]{2,1,0:T(8,128)(2,1)S(1)}, u32[]{:S(2)}, u32[]{:S(2)}) collective-permute-start(bf16[2,8,768]{2,1,0:T(8,128)(2,1)S(1)} %merge.3.b0), channel_id=1, source_target_pairs={{0,16},{4,20},{8,24},{12,28},{16,0},{20,4},{24,8},{28,12},{1,17},{... | collective-permute-start | bytes 73736 | tf_op jit(solution)/shard_map/ppermute | solution.py:541
  22.1 4.7 %collective-permute-start.5 = (bf16[2,8,768]{2,1,0:T(8,128)(2,1)S(1)}, bf16[2,8,768]{2,1,0:T(8,128)(2,1)S(1)}, u32[]{:S(2)}, u32[]{:S(2)}) collective-permute-start(bf16[2,8,768]{2,1,0:T(8,128)(2,1)S(1)} %merge.3.b0), channel_id=1, source_target_pairs={{0,8},{4,12},{8,0},{12,4},{16,24},{20,28},{24,16},{28,20},{1,9},{5... | collective-permute-start | bytes 73736 | tf_op jit(solution)/shard_map/ppermute | solution.py:541
  27.6 3.2 %collective-permute-start.10 = (bf16[16,384]{1,0:T(8,128)(2,1)S(1)}, bf16[16,384]{1,0:T(8,128)(2,1)S(1)}, u32[]{:S(2)}, u32[]{:S(2)}) collective-permute-start(bf16[16,384]{1,0:T(8,128)(2,1)S(1)} %combine.1.p0), channel_id=1, source_target_pairs={{0,3},{1,2},{2,1},{3,0},{4,7},{5,6},{6,5},{7,4},{8,11},{9,10},{10,... | collective-permute-start | bytes 36872 | tf_op jit(solution)/shard_map/ppermute | solution.py:541
  27.6 3.8 %collective-permute-start.9 = (bf16[16,384]{1,0:T(8,128)(2,1)S(1)}, bf16[16,384]{1,0:T(8,128)(2,1)S(1)}, u32[]{:S(2)}, u32[]{:S(2)}) collective-permute-start(bf16[16,384]{1,0:T(8,128)(2,1)S(1)} %combine.1.p0), channel_id=1, source_target_pairs={{0,2},{1,3},{2,0},{3,1},{4,6},{5,7},{6,4},{7,5},{8,10},{9,11},{10,... | collective-permute-start | bytes 36872 | tf_op jit(solution)/shard_map/ppermute | solution.py:541
  29.2 2.2 %collective-permute-start.8 = (bf16[16,384]{1,0:T(8,128)(2,1)S(1)}, bf16[16,384]{1,0:T(8,128)(2,1)S(1)}, u32[]{:S(2)}, u32[]{:S(2)}) collective-permute-start(bf16[16,384]{1,0:T(8,128)(2,1)S(1)} %combine.1.p0), channel_id=1, source_target_pairs={{0,1},{1,0},{2,3},{3,2},{4,5},{5,4},{6,7},{7,6},{8,9},{9,8},{10,11... | collective-permute-start | bytes 36872 | tf_op jit(solution)/shard_map/ppermute | solution.py:541
  31.4 4.8 %collective-permute-start.12 = (bf16[16,384]{1,0:T(8,128)(2,1)S(1)}, bf16[16,384]{1,0:T(8,128)(2,1)S(1)}, u32[]{:S(2)}, u32[]{:S(2)}) collective-permute-start(bf16[16,384]{1,0:T(8,128)(2,1)S(1)} %head_sum.1), channel_id=1, source_target_pairs={{1,28},{5,24},{0,20},{4,16},{3,12},{7,8},{2,4},{6,0},{9,29},{13,25... | collective-permute-start | bytes 36872 | tf_op jit(solution)/shard_map/ppermute | solution.py:630
  34.4 3.7 %collective-permute-start.11 = (bf16[16,384]{1,0:T(8,128)(2,1)S(1)}, bf16[16,384]{1,0:T(8,128)(2,1)S(1)}, u32[]{:S(2)}, u32[]{:S(2)}) collective-permute-start(bf16[16,384]{1,0:T(8,128)(2,1)S(1)} %head_sum.1), channel_id=1, source_target_pairs={{1,24},{5,28},{0,16},{4,20},{3,8},{7,12},{2,0},{6,4},{9,25},{13,29... | collective-permute-start | bytes 36872 | tf_op jit(solution)/shard_map/ppermute | solution.py:630
  38.1 6.0 %copy-start.2 = (bf16[1024,768]{1,0:T(8,128)(2,1)S(1)}, bf16[1024,768]{1,0:T(8,128)(2,1)}, u32[]{:S(2)}) copy-start(bf16[1024,768]{1,0:T(8,128)(2,1)} %weight.3) | copy-start | bytes 4718596
  38.7 1.3 %collective-permute-start.13 = (bf16[16,2176]{1,0:T(8,128)(2,1)S(1)}, bf16[16,2176]{1,0:T(8,128)(2,1)S(1)}, u32[]{:S(2)}, u32[]{:S(2)}) collective-permute-start(bf16[16,2176]{1,0:T(8,128)(2,1)S(1)} %get-tuple-element.22.mine), channel_id=1, source_target_pairs={{0,1},{1,0},{2,3},{3,2},{4,5},{5,4},{6,7},{7,6},{8,9},{9,8},{10,11... | collective-permute-start | bytes 208904 | tf_op jit(solution)/shard_map/ppermute | solution.py:541
  40.0 4.2 %collective-permute-start.14 = (bf16[16,2176]{1,0:T(8,128)(2,1)S(1)}, bf16[16,2176]{1,0:T(8,128)(2,1)S(1)}, u32[]{:S(2)}, u32[]{:S(2)}) collective-permute-start(bf16[16,2176]{1,0:T(8,128)(2,1)S(1)} %core_sum.1.mine), channel_id=1, source_target_pairs={{0,3},{1,2},{2,1},{3,0},{4,7},{5,6},{6,5},{7,4},{8,11},{9,10},{10,... | collective-permute-start | bytes 208904 | tf_op jit(solution)/shard_map/ppermute | solution.py:541

commit v15 on v12

--- a/solution.py
+++ b/solution.py
@@ -208,6 +208,13 @@
 
 
 F32, BF16 = jnp.float32, jnp.bfloat16
+
+ROUTES = (
+    ((1, 1, 1, 1), (2, 0, 3, 1), (2, 3, 0, 1)),
+    ((0, 0, 0, 1), (2, 0, 3, 1), (0, 3, 1, 2)),
+    ((1, 1, 0, 1), (2, 3, 0, 1), (3, 1, 2, 0)),
+    ((1, 1, 1, 1), (2, 3, 1, 0), (3, 2, 1, 0)),
+)
 VMEM = pl.BlockSpec(memory_space=pltpu.VMEM)
 HBM = pl.BlockSpec(memory_space=pl.ANY)
 
@@ -476,15 +483,21 @@
     ).astype(BF16)
 
 
-def gate_up_kernel(same, flip, all_input, gain, gate, up, sums, own, scr):
+def gate_up_kernel(second, first, all_input, gain, gate, up, sums, own, scr):
     me = lax.axis_index("pool")
-    odd = me % 2 == 1
-    part = same.shape[1]
+    place = lax.axis_index("mlp") * 4 + me // 2
+    crossed = functools.reduce(
+        lambda found, at: jnp.where(place == at, 1, found),
+        [m * 4 + z for m in range(4) for z in range(4) if ROUTES[m][0][z]],
+        0,
+    )
+    swapped = (me % 2) ^ crossed == 1
+    part = first.shape[1]
     ff = gate.shape[1]
     rows = own.shape[0]
-    near, far = same[...].astype(F32), flip[...].astype(F32)
-    scr[:, :part] = all_input[:, :part] + jnp.where(odd, far, near)
-    scr[:, part:] = all_input[:, part:] + jnp.where(odd, near, far)
+    one, other = first[...].astype(F32), second[...].astype(F32)
+    scr[:, :part] = all_input[:, :part] + jnp.where(swapped, other, one)
+    scr[:, part:] = all_input[:, part:] + jnp.where(swapped, one, other)
     residual = scr[...]
     mine = scr[0:rows, :]
     for p in range(1, residual.shape[0] // rows):
@@ -616,14 +629,13 @@
         [head_part] + [flip(head_part, "mlp", step) for step in (1, 2, 3)],
     )
     pieces = []
-    for turn in range(2):
+    for turn in (1, 0):
         route = []
-        for m in range(mlp):
-            by_distance = sorted(range(4), key=lambda z: (-abs(z - m), z))
-            for z, step in zip(by_distance, (1, 0, 3, 2) if m % 2 == 0 else (0, 1, 2, 3)):
+        for m, (crossing, *members) in enumerate(ROUTES):
+            for z in range(4):
                 for y in range(2):
-                    source = (m * 2 + y) * mlp + (m ^ step)
-                    route.append((source, (z * 2 + (y ^ turn)) * mlp + m))
+                    source = (m * 2 + (y ^ crossing[z] ^ turn)) * mlp + members[turn][z]
+                    route.append((source, (z * 2 + y) * mlp + m))
         pieces.append(lax.ppermute(head_sum, ("pool", "mlp"), route))
     sums, own_residual = call(
         gate_up_kernel,

time: 53.5 us -> 54 us (level)
  waiting for transfers between devices: 16.1 us -> 17.4 us
  starting transfers between devices: 21.9 us -> 21.1 us
    ppermute x2, waiting for transfers between devices: 2.19 us -> 3.16 us  [per_device_small(): pieces.append(lax.ppermute(head_sum, ('pool', 'mlp'), route))]
    ppermute x2, starting transfers between devices: 4.27 us -> 3.31 us  [per_device_small(): pieces.append(lax.ppermute(head_sum, ('pool', 'mlp'), route))]
where the time goes in v15:
time: 54 us; the launch traced here: 53.7 us
  starting transfers between devices  21.1 us (39%)
  waiting for transfers between devices  17.4 us (32%)
  blocking collectives  8.36 us (15%)
  Pallas kernels  5.25 us (10%)
  local copies, waits for them, and re-layouts  1.46 us (3%)
    ppermute x13, starting transfers between devices, flip(): lax.ppermute(values, axis, [(index, index ^ step) for index in range(size)])  17.8 us
    ppermute x13, waiting for transfers between devices, flip(): lax.ppermute(values, axis, [(index, index ^ step) for index in range(size)])  14.2 us
    all_to_all x1, blocking collectives, per_device_small(): lax.all_to_all(down, 'pool', 0, 0, axis_index_groups=[backwards])  8.36 us
    pallas_call x11, Pallas kernels, call(): pl.pallas_call(kernel, out_shape=[jax.ShapeDtypeStruct(shape, dtype) for...  5.25 us
    ppermute x2, starting transfers between devices, per_device_small(): pieces.append(lax.ppermute(head_sum, ('pool', 'mlp'), route))  3.31 us
    ppermute x2, waiting for transfers between devices, per_device_small(): pieces.append(lax.ppermute(head_sum, ('pool', 'mlp'), route))  3.16 us
    unnamed x18, local copies, waits for them, and re-layouts  1.45 us
  transfers between devices with their start and end apart: 15, of which 13 were waited for; matrix products, arithmetic and copies ran while one was open for 0% of the time, Pallas kernels for 0%

profile of v15, /device:TPU:0, one launch (start us, length us, event | category | flops | bytes accessed | tf_op | source)
XLA Modules:
  0.0 53.7 jit_solution(10786009233711753962)
XLA Ops:
  0.0 1.6 %rotary.1 = (bf16[2,1664]{1,0:T(2,128)(2,1)}, bf16[2,1536]{1,0:T(2,128)(2,1)}) custom-call(s32[2,8]{1,0:T(2,128)} %refs_0_.1, s32[2]{0:T(128)} %refs_1_.1, bf16[2,768]{1,0:T(2,128)(2,1)} %refs_2_.1, bf16[2,768]{1,0:T(2,128)(2,1)} %refs_3_.1, bf16[2,768]{1,0:T(2,128)(2,1)} %refs_4_.1, bf16[2,768]{1,0:T(2,128)(2,1)} %refs_5_.1, bf16[5,256,768]{2,1,0:T(8,128)(2,1)} %keys.1, ...), custom_call_target="tpu_custom_call" | custom-call | bytes 3944520 | tf_op jit(solution)/shard_map/rotary/pallas_call | solution.py:224
  1.6 3.0 %collective-permute-start = (bf16[2,1664]{1,0:T(2,128)(2,1)}, bf16[2,1664]{1,0:T(2,128)(2,1)S(1)}, u32[]{:S(2)}, u32[]{:S(2)}) collective-permute-start(bf16[2,1664]{1,0:T(2,128)(2,1)} %get-tuple-element.14.packed), channel_id=1, source_target_pairs={{0,4},{4,0},{8,12},{12,8},{16,20},{20,16},{24,28},{28,24},{1,5},{5... | collective-permute-start | bytes 19976 | tf_op jit(solution)/shard_map/ppermute | solution.py:551
  4.7 0.7 %copy-done.6 = bf16[2,1664]{1,0:T(2,128)(2,1)S(1)} copy-done((bf16[2,1664]{1,0:T(2,128)(2,1)S(1)}, bf16[2,1664]{1,0:T(2,128)(2,1)}, u32[]{:S(2)}) %copy-start.6) | copy-done | bytes 6680
  5.4 0.7 %copy-done.7 = bf16[2,1536]{1,0:T(2,128)(2,1)S(1)} copy-done((bf16[2,1536]{1,0:T(2,128)(2,1)S(1)}, bf16[2,1536]{1,0:T(2,128)(2,1)}, u32[]{:S(2)}) %copy-start.7) | copy-done | bytes 6168
  6.1 0.1 carry.1
  6.2 0.3 collective-permute-done.theirs
  6.5 4.1 %collective-permute-start.3 = (bf16[2,2,1664]{2,1,0:T(2,128)(2,1)S(1)}, bf16[2,2,1664]{2,1,0:T(2,128)(2,1)S(1)}, u32[]{:S(2)}, u32[]{:S(2)}) collective-permute-start(bf16[2,2,1664]{2,1,0:T(2,128)(2,1)S(1)} %merge.2.a0), channel_id=1, source_target_pairs={{0,24},{4,28},{8,16},{12,20},{16,8},{20,12},{24,0},{28,4},{1,25},{... | collective-permute-start | bytes 39944 | tf_op jit(solution)/shard_map/ppermute | solution.py:551
  10.6 0.0 collective-permute-start.2
  10.6 0.6 %collective-permute-start.1 = (bf16[2,2,1664]{2,1,0:T(2,128)(2,1)S(1)}, bf16[2,2,1664]{2,1,0:T(2,128)(2,1)S(1)}, u32[]{:S(2)}, u32[]{:S(2)}) collective-permute-start(bf16[2,2,1664]{2,1,0:T(2,128)(2,1)S(1)} %merge.2.a0), channel_id=1, source_target_pairs={{0,8},{4,12},{8,0},{12,4},{16,24},{20,28},{24,16},{28,20},{1,9},{5... | collective-permute-start | bytes 39944 | tf_op jit(solution)/shard_map/ppermute | solution.py:551
  11.2 1.1 %collective-permute-done.3.a3 = bf16[2,2,1664]{2,1,0:T(2,128)(2,1)S(1)} collective-permute-done((bf16[2,2,1664]{2,1,0:T(2,128)(2,1)S(1)}, bf16[2,2,1664]{2,1,0:T(2,128)(2,1)S(1)}, u32[]{:S(2)}, u32[]{:S(2)}) %collective-permute-start.3) | collective-permute-done | bytes 13344 | tf_op jit(solution)/shard_map/ppermute | solution.py:551
  12.3 2.9 %collective-permute-done.2.a2 = bf16[2,2,1664]{2,1,0:T(2,128)(2,1)S(1)} collective-permute-done((bf16[2,2,1664]{2,1,0:T(2,128)(2,1)S(1)}, bf16[2,2,1664]{2,1,0:T(2,128)(2,1)S(1)}, u32[]{:S(2)}, u32[]{:S(2)}) %collective-permute-start.2) | collective-permute-done | bytes 13344 | tf_op jit(solution)/shard_map/ppermute | solution.py:551
  15.2 0.0 collective-permute-done.1.a1
  15.2 0.0 copy-done.1
  15.2 0.0 copy-done
  15.2 0.0 copy-start.5
  15.2 0.0 copy-start.8
  15.3 0.0 copy-start.3
  15.3 0.0 copy-start.4
  15.3 1.1 %attend.1 = (bf16[8,768]{1,0:T(8,128)(2,1)S(1)}, f32[16,768]{1,0:T(8,128)S(1)}, f32[16,128]{1,0:T(8,128)S(1)}) custom-call(bf16[2,2,1664]{2,1,0:T(2,128)(2,1)S(1)} %merge.2.a0, bf16[2,2,1664]{2,1,0:T(2,128)(2,1)S(1)} %collective-permute-done.1.a1, bf16[2,2,1664]{2,1,0:T(2,128)(2,1)S(1)} %collective-permute-done.2.a2, ...), custom_call_target="tpu_custom_call" | custom-call | bytes 4014080 | tf_op jit(solution)/shard_map/attend/pallas_call | solution.py:224
  16.4 1.6 %collective-permute-start.4 = (bf16[8,768]{1,0:T(8,128)(2,1)S(1)}, bf16[8,768]{1,0:T(8,128)(2,1)S(1)}, u32[]{:S(2)}, u32[]{:S(2)}) collective-permute-start(bf16[8,768]{1,0:T(8,128)(2,1)S(1)} %get-tuple-element.18.mine), channel_id=1, source_target_pairs={{0,4},{4,0},{8,12},{12,8},{16,20},{20,16},{24,28},{28,24},{1,5},{5... | collective-permute-start | bytes 36872 | tf_op jit(solution)/shard_map/ppermute | solution.py:551
  18.0 2.2 %collective-permute-done.4.theirs = bf16[8,768]{1,0:T(8,128)(2,1)S(1)} collective-permute-done((bf16[8,768]{1,0:T(8,128)(2,1)S(1)}, bf16[8,768]{1,0:T(8,128)(2,1)S(1)}, u32[]{:S(2)}, u32[]{:S(2)}) %collective-permute-start.4) | collective-permute-done | bytes 12320 | tf_op jit(solution)/shard_map/ppermute | solution.py:551
  20.2 1.4 %collective-permute-start.7 = (bf16[2,8,768]{2,1,0:T(8,128)(2,1)S(1)}, bf16[2,8,768]{2,1,0:T(8,128)(2,1)S(1)}, u32[]{:S(2)}, u32[]{:S(2)}) collective-permute-start(bf16[2,8,768]{2,1,0:T(8,128)(2,1)S(1)} %merge.3.b0), channel_id=1, source_target_pairs={{0,24},{4,28},{8,16},{12,20},{16,8},{20,12},{24,0},{28,4},{1,25},{... | collective-permute-start | bytes 73736 | tf_op jit(solution)/shard_map/ppermute | solution.py:551
  21.6 0.6 %collective-permute-start.6 = (bf16[2,8,768]{2,1,0:T(8,128)(2,1)S(1)}, bf16[2,8,768]{2,1,0:T(8,128)(2,1)S(1)}, u32[]{:S(2)}, u32[]{:S(2)}) collective-permute-start(bf16[2,8,768]{2,1,0:T(8,128)(2,1)S(1)} %merge.3.b0), channel_id=1, source_target_pairs={{0,16},{4,20},{8,24},{12,28},{16,0},{20,4},{24,8},{28,12},{1,17},{... | collective-permute-start | bytes 73736 | tf_op jit(solution)/shard_map/ppermute | solution.py:551
  22.3 2.3 %collective-permute-start.5 = (bf16[2,8,768]{2,1,0:T(8,128)(2,1)S(1)}, bf16[2,8,768]{2,1,0:T(8,128)(2,1)S(1)}, u32[]{:S(2)}, u32[]{:S(2)}) collective-permute-start(bf16[2,8,768]{2,1,0:T(8,128)(2,1)S(1)} %merge.3.b0), channel_id=1, source_target_pairs={{0,8},{4,12},{8,0},{12,4},{16,24},{20,28},{24,16},{28,20},{1,9},{5... | collective-permute-start | bytes 73736 | tf_op jit(solution)/shard_map/ppermute | solution.py:551
  24.6 1.2 %collective-permute-done.7.b3 = bf16[2,8,768]{2,1,0:T(8,128)(2,1)S(1)} collective-permute-done((bf16[2,8,768]{2,1,0:T(8,128)(2,1)S(1)}, bf16[2,8,768]{2,1,0:T(8,128)(2,1)S(1)}, u32[]{:S(2)}, u32[]{:S(2)}) %collective-permute-start.7) | collective-permute-done | bytes 24608 | tf_op jit(solution)/shard_map/ppermute | solution.py:551
  25.8 0.6 %collective-permute-done.6.b2 = bf16[2,8,768]{2,1,0:T(8,128)(2,1)S(1)} collective-permute-done((bf16[2,8,768]{2,1,0:T(8,128)(2,1)S(1)}, bf16[2,8,768]{2,1,0:T(8,128)(2,1)S(1)}, u32[]{:S(2)}, u32[]{:S(2)}) %collective-permute-start.6) | collective-permute-done | bytes 24608 | tf_op jit(solution)/shard_map/ppermute | solution.py:551
  26.4 0.2 collective-permute-done.5.b1
  26.6 0.0 copy-done.5
  26.6 0.7 %combine.1.p0 = bf16[16,384]{1,0:T(8,128)(2,1)S(1)} custom-call(bf16[2,8,768]{2,1,0:T(8,128)(2,1)S(1)} %merge.3.b0, bf16[2,8,768]{2,1,0:T(8,128)(2,1)S(1)} %collective-permute-done.5.b1, bf16[2,8,768]{2,1,0:T(8,128)(2,1)S(1)} %collective-permute-done.6.b2, bf16[2,8,768]{2,1,0:T(8,128)(2,1)S(1)} %collective-permute-done.7.b3, ...), custom_call_target="tpu_custom_call" | custom-call | bytes 696320 | tf_op jit(solution)/shard_map/combine/pallas_call | solution.py:224
  27.4 0.1 collective-permute-start.10
  27.4 1.6 %collective-permute-start.9 = (bf16[16,384]{1,0:T(8,128)(2,1)S(1)}, bf16[16,384]{1,0:T(8,128)(2,1)S(1)}, u32[]{:S(2)}, u32[]{:S(2)}) collective-permute-start(bf16[16,384]{1,0:T(8,128)(2,1)S(1)} %combine.1.p0), channel_id=1, source_target_pairs={{0,2},{1,3},{2,0},{3,1},{4,6},{5,7},{6,4},{7,5},{8,10},{9,11},{10,... | collective-permute-start | bytes 36872 | tf_op jit(solution)/shard_map/ppermute | solution.py:551
  29.0 0.3 collective-permute-start.8
  29.3 1.3 %collective-permute-done.10.p3 = bf16[16,384]{1,0:T(8,128)(2,1)S(1)} collective-permute-done((bf16[16,384]{1,0:T(8,128)(2,1)S(1)}, bf16[16,384]{1,0:T(8,128)(2,1)S(1)}, u32[]{:S(2)}, u32[]{:S(2)}) %collective-permute-start.10) | collective-permute-done | bytes 12320 | tf_op jit(solution)/shard_map/ppermute | solution.py:551
  30.6 0.6 %collective-permute-done.9.p2 = bf16[16,384]{1,0:T(8,128)(2,1)S(1)} collective-permute-done((bf16[16,384]{1,0:T(8,128)(2,1)S(1)}, bf16[16,384]{1,0:T(8,128)(2,1)S(1)}, u32[]{:S(2)}, u32[]{:S(2)}) %collective-permute-start.9) | collective-permute-done | bytes 12320 | tf_op jit(solution)/shard_map/ppermute | solution.py:551
  31.2 0.0 collective-permute-done.8.p1
  31.2 2.8 %collective-permute-start.12 = (bf16[16,384]{1,0:T(8,128)(2,1)S(1)}, bf16[16,384]{1,0:T(8,128)(2,1)S(1)}, u32[]{:S(2)}, u32[]{:S(2)}) collective-permute-start(bf16[16,384]{1,0:T(8,128)(2,1)S(1)} %head_sum.1), channel_id=1, source_target_pairs={{6,0},{2,4},{4,8},{0,12},{7,16},{3,20},{5,24},{1,28},{10,1},{14,5}... | collective-permute-start | bytes 36872 | tf_op jit(solution)/shard_map/ppermute | solution.py:639
  34.0 0.5 collective-permute-start.11
  34.5 1.3 %collective-permute-done.12.first = bf16[16,384]{1,0:T(8,128)(2,1)S(1)} collective-permute-done((bf16[16,384]{1,0:T(8,128)(2,1)S(1)}, bf16[16,384]{1,0:T(8,128)(2,1)S(1)}, u32[]{:S(2)}, u32[]{:S(2)}) %collective-permute-start.12) | collective-permute-done | bytes 12320 | tf_op jit(solution)/shard_map/ppermute | solution.py:639
  35.8 1.8 %collective-permute-done.11.second = bf16[16,384]{1,0:T(8,128)(2,1)S(1)} collective-permute-done((bf16[16,384]{1,0:T(8,128)(2,1)S(1)}, bf16[16,384]{1,0:T(8,128)(2,1)S(1)}, u32[]{:S(2)}, u32[]{:S(2)}) %collective-permute-start.11) | collective-permute-done | bytes 12320 | tf_op jit(solution)/shard_map/ppermute | solution.py:639
  37.7 0.5 gate_up.1
  38.2 1.0 %collective-permute-start.13 = (bf16[16,2176]{1,0:T(8,128)(2,1)S(1)}, bf16[16,2176]{1,0:T(8,128)(2,1)S(1)}, u32[]{:S(2)}, u32[]{:S(2)}) collective-permute-start(bf16[16,2176]{1,0:T(8,128)(2,1)S(1)} %get-tuple-element.22.mine), channel_id=1, source_target_pairs={{0,1},{1,0},{2,3},{3,2},{4,5},{5,4},{6,7},{7,6},{8,9},{9,8},{10,11... | collective-permute-start | bytes 208904 | tf_op jit(solution)/shard_map/ppermute | solution.py:551
  39.3 0.9 %collective-permute-done.13.theirs = bf16[16,2176]{1,0:T(8,128)(2,1)S(1)} collective-permute-done((bf16[16,2176]{1,0:T(8,128)(2,1)S(1)}, bf16[16,2176]{1,0:T(8,128)(2,1)S(1)}, u32[]{:S(2)}, u32[]{:S(2)}) %collective-permute-start.13) | collective-permute-done | bytes 69664 | tf_op jit(solution)/shard_map/ppermute | solution.py:551
  40.2 0.1 core_sum.1.mine
  40.3 1.1 %collective-permute-start.14 = (bf16[16,2176]{1,0:T(8,128)(2,1)S(1)}, bf16[16,2176]{1,0:T(8,128)(2,1)S(1)}, u32[]{:S(2)}, u32[]{:S(2)}) collective-permute-start(bf16[16,2176]{1,0:T(8,128)(2,1)S(1)} %core_sum.1.mine), channel_id=1, source_target_pairs={{0,3},{1,2},{2,1},{3,0},{4,7},{5,6},{6,5},{7,4},{8,11},{9,10},{10,... | collective-permute-start | bytes 208904 | tf_op jit(solution)/shard_map/ppermute | solution.py:551
  41.4 2.9 %collective-permute-done.14.theirs = bf16[16,2176]{1,0:T(8,128)(2,1)S(1)} collective-permute-done((bf16[16,2176]{1,0:T(8,128)(2,1)S(1)}, bf16[16,2176]{1,0:T(8,128)(2,1)S(1)}, u32[]{:S(2)}, u32[]{:S(2)}) %collective-permute-start.14) | collective-permute-done | bytes 69664 | tf_op jit(solution)/shard_map/ppermute | solution.py:551
  44.3 0.4 down.1
  44.7 8.4 %all_to_all.5.parts = bf16[8,2,768]{2,1,0:T(2,128)(2,1)S(1)} all-to-all(bf16[8,2,768]{2,1,0:T(2,128)(2,1)S(1)} %down.1), channel_id=1, replica_groups={{28,24,20,16,12,8,4,0},{29,25,21,17,13,9,5,1},{30,26,22,18,14,10,6,2},{..., dimensions={0} | all-to-all | bytes 49152 | tf_op jit(solution)/shard_map/all_to_all | solution.py:665
  53.1 0.6 %final.1 = bf16[2,768]{1,0:T(2,128)(2,1)} custom-call(f32[2,768]{1,0:T(2,128)S(1)} %get-tuple-element.21.own, bf16[8,2,768]{2,1,0:T(2,128)(2,1)S(1)} %all_to_all.5.parts), custom_call_target="tpu_custom_call" | custom-call | bytes 30720 | tf_op jit(solution)/shard_map/final/pallas_call | solution.py:224
  (13 shorter events, 0.0 us)
Async XLA Ops:
  0.0 15.2 %copy-start.1 = (bf16[5,256,768]{2,1,0:T(8,128)(2,1)S(1)}, bf16[5,256,768]{2,1,0:T(8,128)(2,1)}, u32[]{:S(2)}) copy-start(bf16[5,256,768]{2,1,0:T(8,128)(2,1)} %values.1) | copy-start | bytes 5898244
  0.0 15.2 %copy-start = (bf16[5,256,768]{2,1,0:T(8,128)(2,1)S(1)}, bf16[5,256,768]{2,1,0:T(8,128)(2,1)}, u32[]{:S(2)}) copy-start(bf16[5,256,768]{2,1,0:T(8,128)(2,1)} %keys.1) | copy-start | bytes 5898244
  1.6 4.9 %collective-permute-start = (bf16[2,1664]{1,0:T(2,128)(2,1)}, bf16[2,1664]{1,0:T(2,128)(2,1)S(1)}, u32[]{:S(2)}, u32[]{:S(2)}) collective-permute-start(bf16[2,1664]{1,0:T(2,128)(2,1)} %get-tuple-element.14.packed), channel_id=1, source_target_pairs={{0,4},{4,0},{8,12},{12,8},{16,20},{20,16},{24,28},{28,24},{1,5},{5... | collective-permute-start | bytes 19976 | tf_op jit(solution)/shard_map/ppermute | solution.py:551
  4.7 0.7 %copy-start.6 = (bf16[2,1664]{1,0:T(2,128)(2,1)S(1)}, bf16[2,1664]{1,0:T(2,128)(2,1)}, u32[]{:S(2)}) copy-start(bf16[2,1664]{1,0:T(2,128)(2,1)} %get-tuple-element.14.packed) | copy-start | bytes 19972
  5.4 0.7 %copy-start.7 = (bf16[2,1536]{1,0:T(2,128)(2,1)S(1)}, bf16[2,1536]{1,0:T(2,128)(2,1)}, u32[]{:S(2)}) copy-start(bf16[2,1536]{1,0:T(2,128)(2,1)} %get-tuple-element.15.new) | copy-start | bytes 18436
  6.5 5.8 %collective-permute-start.3 = (bf16[2,2,1664]{2,1,0:T(2,128)(2,1)S(1)}, bf16[2,2,1664]{2,1,0:T(2,128)(2,1)S(1)}, u32[]{:S(2)}, u32[]{:S(2)}) collective-permute-start(bf16[2,2,1664]{2,1,0:T(2,128)(2,1)S(1)} %merge.2.a0), channel_id=1, source_target_pairs={{0,24},{4,28},{8,16},{12,20},{16,8},{20,12},{24,0},{28,4},{1,25},{... | collective-permute-start | bytes 39944 | tf_op jit(solution)/shard_map/ppermute | solution.py:551
  10.6 4.6 %collective-permute-start.2 = (bf16[2,2,1664]{2,1,0:T(2,128)(2,1)S(1)}, bf16[2,2,1664]{2,1,0:T(2,128)(2,1)S(1)}, u32[]{:S(2)}, u32[]{:S(2)}) collective-permute-start(bf16[2,2,1664]{2,1,0:T(2,128)(2,1)S(1)} %merge.2.a0), channel_id=1, source_target_pairs={{0,16},{4,20},{8,24},{12,28},{16,0},{20,4},{24,8},{28,12},{1,17},{... | collective-permute-start | bytes 39944 | tf_op jit(solution)/shard_map/ppermute | solution.py:551
  10.6 4.6 %collective-permute-start.1 = (bf16[2,2,1664]{2,1,0:T(2,128)(2,1)S(1)}, bf16[2,2,1664]{2,1,0:T(2,128)(2,1)S(1)}, u32[]{:S(2)}, u32[]{:S(2)}) collective-permute-start(bf16[2,2,1664]{2,1,0:T(2,128)(2,1)S(1)} %merge.2.a0), channel_id=1, source_target_pairs={{0,8},{4,12},{8,0},{12,4},{16,24},{20,28},{24,16},{28,20},{1,9},{5... | collective-permute-start | bytes 39944 | tf_op jit(solution)/shard_map/ppermute | solution.py:551
  15.2 11.4 %copy-start.5 = (bf16[768,384]{1,0:T(8,128)(2,1)S(1)}, bf16[768,384]{1,0:T(8,128)(2,1)}, u32[]{:S(2)}) copy-start(bf16[768,384]{1,0:T(8,128)(2,1)} %weight.2) | copy-start | bytes 1769476
  15.2 19.3 %copy-start.8 = (bf16[768]{0:T(1024)(128)(2,1)S(1)}, bf16[768]{0:T(1024)(128)(2,1)}, u32[]{:S(2)}) copy-start(bf16[768]{0:T(1024)(128)(2,1)} %param.22) | copy-start | bytes 4612
  15.3 22.4 %copy-start.3 = (bf16[768,1024]{1,0:T(8,128)(2,1)S(1)}, bf16[768,1024]{1,0:T(8,128)(2,1)}, u32[]{:S(2)}) copy-start(bf16[768,1024]{1,0:T(8,128)(2,1)} %gate.1) | copy-start | bytes 4718596
  15.3 22.4 %copy-start.4 = (bf16[768,1024]{1,0:T(8,128)(2,1)S(1)}, bf16[768,1024]{1,0:T(8,128)(2,1)}, u32[]{:S(2)}) copy-start(bf16[768,1024]{1,0:T(8,128)(2,1)} %up.1) | copy-start | bytes 4718596
  16.4 3.8 %collective-permute-start.4 = (bf16[8,768]{1,0:T(8,128)(2,1)S(1)}, bf16[8,768]{1,0:T(8,128)(2,1)S(1)}, u32[]{:S(2)}, u32[]{:S(2)}) collective-permute-start(bf16[8,768]{1,0:T(8,128)(2,1)S(1)} %get-tuple-element.18.mine), channel_id=1, source_target_pairs={{0,4},{4,0},{8,12},{12,8},{16,20},{20,16},{24,28},{28,24},{1,5},{5... | collective-permute-start | bytes 36872 | tf_op jit(solution)/shard_map/ppermute | solution.py:551
  20.2 5.6 %collective-permute-start.7 = (bf16[2,8,768]{2,1,0:T(8,128)(2,1)S(1)}, bf16[2,8,768]{2,1,0:T(8,128)(2,1)S(1)}, u32[]{:S(2)}, u32[]{:S(2)}) collective-permute-start(bf16[2,8,768]{2,1,0:T(8,128)(2,1)S(1)} %merge.3.b0), channel_id=1, source_target_pairs={{0,24},{4,28},{8,16},{12,20},{16,8},{20,12},{24,0},{28,4},{1,25},{... | collective-permute-start | bytes 73736 | tf_op jit(solution)/shard_map/ppermute | solution.py:551
  21.6 4.7 %collective-permute-start.6 = (bf16[2,8,768]{2,1,0:T(8,128)(2,1)S(1)}, bf16[2,8,768]{2,1,0:T(8,128)(2,1)S(1)}, u32[]{:S(2)}, u32[]{:S(2)}) collective-permute-start(bf16[2,8,768]{2,1,0:T(8,128)(2,1)S(1)} %merge.3.b0), channel_id=1, source_target_pairs={{0,16},{4,20},{8,24},{12,28},{16,0},{20,4},{24,8},{28,12},{1,17},{... | collective-permute-start | bytes 73736 | tf_op jit(solution)/shard_map/ppermute | solution.py:551
  22.3 4.4 %collective-permute-start.5 = (bf16[2,8,768]{2,1,0:T(8,128)(2,1)S(1)}, bf16[2,8,768]{2,1,0:T(8,128)(2,1)S(1)}, u32[]{:S(2)}, u32[]{:S(2)}) collective-permute-start(bf16[2,8,768]{2,1,0:T(8,128)(2,1)S(1)} %merge.3.b0), channel_id=1, source_target_pairs={{0,8},{4,12},{8,0},{12,4},{16,24},{20,28},{24,16},{28,20},{1,9},{5... | collective-permute-start | bytes 73736 | tf_op jit(solution)/shard_map/ppermute | solution.py:551
  27.4 3.3 %collective-permute-start.10 = (bf16[16,384]{1,0:T(8,128)(2,1)S(1)}, bf16[16,384]{1,0:T(8,128)(2,1)S(1)}, u32[]{:S(2)}, u32[]{:S(2)}) collective-permute-start(bf16[16,384]{1,0:T(8,128)(2,1)S(1)} %combine.1.p0), channel_id=1, source_target_pairs={{0,3},{1,2},{2,1},{3,0},{4,7},{5,6},{6,5},{7,4},{8,11},{9,10},{10,... | collective-permute-start | bytes 36872 | tf_op jit(solution)/shard_map/ppermute | solution.py:551
  27.4 3.8 %collective-permute-start.9 = (bf16[16,384]{1,0:T(8,128)(2,1)S(1)}, bf16[16,384]{1,0:T(8,128)(2,1)S(1)}, u32[]{:S(2)}, u32[]{:S(2)}) collective-permute-start(bf16[16,384]{1,0:T(8,128)(2,1)S(1)} %combine.1.p0), channel_id=1, source_target_pairs={{0,2},{1,3},{2,0},{3,1},{4,6},{5,7},{6,4},{7,5},{8,10},{9,11},{10,... | collective-permute-start | bytes 36872 | tf_op jit(solution)/shard_map/ppermute | solution.py:551
  29.0 2.2 %collective-permute-start.8 = (bf16[16,384]{1,0:T(8,128)(2,1)S(1)}, bf16[16,384]{1,0:T(8,128)(2,1)S(1)}, u32[]{:S(2)}, u32[]{:S(2)}) collective-permute-start(bf16[16,384]{1,0:T(8,128)(2,1)S(1)} %combine.1.p0), channel_id=1, source_target_pairs={{0,1},{1,0},{2,3},{3,2},{4,5},{5,4},{6,7},{7,6},{8,9},{9,8},{10,11... | collective-permute-start | bytes 36872 | tf_op jit(solution)/shard_map/ppermute | solution.py:551
  31.2 4.7 %collective-permute-start.12 = (bf16[16,384]{1,0:T(8,128)(2,1)S(1)}, bf16[16,384]{1,0:T(8,128)(2,1)S(1)}, u32[]{:S(2)}, u32[]{:S(2)}) collective-permute-start(bf16[16,384]{1,0:T(8,128)(2,1)S(1)} %head_sum.1), channel_id=1, source_target_pairs={{6,0},{2,4},{4,8},{0,12},{7,16},{3,20},{5,24},{1,28},{10,1},{14,5}... | collective-permute-start | bytes 36872 | tf_op jit(solution)/shard_map/ppermute | solution.py:639
  34.0 3.7 %collective-permute-start.11 = (bf16[16,384]{1,0:T(8,128)(2,1)S(1)}, bf16[16,384]{1,0:T(8,128)(2,1)S(1)}, u32[]{:S(2)}, u32[]{:S(2)}) collective-permute-start(bf16[16,384]{1,0:T(8,128)(2,1)S(1)} %head_sum.1), channel_id=1, source_target_pairs={{2,0},{6,4},{3,8},{7,12},{0,16},{4,20},{1,24},{5,28},{12,1},{8,5},... | collective-permute-start | bytes 36872 | tf_op jit(solution)/shard_map/ppermute | solution.py:639
  37.7 6.6 %copy-start.2 = (bf16[1024,768]{1,0:T(8,128)(2,1)S(1)}, bf16[1024,768]{1,0:T(8,128)(2,1)}, u32[]{:S(2)}) copy-start(bf16[1024,768]{1,0:T(8,128)(2,1)} %weight.3) | copy-start | bytes 4718596
  38.2 2.0 %collective-permute-start.13 = (bf16[16,2176]{1,0:T(8,128)(2,1)S(1)}, bf16[16,2176]{1,0:T(8,128)(2,1)S(1)}, u32[]{:S(2)}, u32[]{:S(2)}) collective-permute-start(bf16[16,2176]{1,0:T(8,128)(2,1)S(1)} %get-tuple-element.22.mine), channel_id=1, source_target_pairs={{0,1},{1,0},{2,3},{3,2},{4,5},{5,4},{6,7},{7,6},{8,9},{9,8},{10,11... | collective-permute-start | bytes 208904 | tf_op jit(solution)/shard_map/ppermute | solution.py:551
  40.3 4.0 %collective-permute-start.14 = (bf16[16,2176]{1,0:T(8,128)(2,1)S(1)}, bf16[16,2176]{1,0:T(8,128)(2,1)S(1)}, u32[]{:S(2)}, u32[]{:S(2)}) collective-permute-start(bf16[16,2176]{1,0:T(8,128)(2,1)S(1)} %core_sum.1.mine), channel_id=1, source_target_pairs={{0,3},{1,2},{2,1},{3,0},{4,7},{5,6},{6,5},{7,4},{8,11},{9,10},{10,... | collective-permute-start | bytes 208904 | tf_op jit(solution)/shard_map/ppermute | solution.py:551

commit v16 on v12

--- a/solution.py
+++ b/solution.py
@@ -500,24 +500,17 @@
     sums[:, 2 * ff :] = tail.astype(BF16)
 
 
-def core_sum_kernel(mine, theirs, total):
-    ff2 = mine.shape[1] - 128
-    total[:, :ff2] = (mine[:, :ff2].astype(F32) + theirs[:, :ff2].astype(F32)).astype(BF16)
-    tail = mine[:, ff2:].astype(F32) + theirs[:, ff2:].astype(F32)
-    square = jnp.sum(tail, 1, keepdims=True)
-    lane = lanes(tail.shape)
-    high = round_low(square)
-    tail = jnp.where(lane == 0, high, jnp.where(lane == 1, square - high, 0.0))
-    total[:, ff2:] = tail.astype(BF16)
-
-
-def down_kernel(features, mine, theirs, weight, parts, scr):
+def down_kernel(features, p0, p1, p2, p3, weight, parts, scr):
     ff = weight.shape[0]
-    tail = mine[:, 2 * ff :].astype(F32) + theirs[:, 2 * ff :].astype(F32)
-    square = jnp.sum(tail, 1, keepdims=True)
+
+    def total(columns):
+        a, b, c, d = (p[:, columns].astype(F32) for p in (p0, p1, p2, p3))
+        return (a + b) + (c + d)
+
+    square = jnp.sum(total(slice(2 * ff, None)), 1, keepdims=True)
     factor = lax.rsqrt(square * (1.0 / features) + 1e-05)
-    gate = (mine[:, :ff].astype(F32) + theirs[:, :ff].astype(F32)) * factor
-    up = (mine[:, ff : 2 * ff].astype(F32) + theirs[:, ff : 2 * ff].astype(F32)) * factor
+    gate = total(slice(0, ff)) * factor
+    up = total(slice(ff, 2 * ff)) * factor
     hidden = (gate / (1.0 + jnp.exp(-gate)) * up).astype(BF16)
     scr[...] = jnp.dot(hidden, weight[...], preferred_element_type=F32)
     rows = parts.shape[1]
@@ -632,17 +625,11 @@
         pieces + [all_input, norm_gain.reshape(1, width), gate_weight, up_weight],
         [pltpu.VMEM((requests, width), F32)],
     )
-    (core_sums,) = call(
-        core_sum_kernel,
-        "core_sum",
-        [((requests, 2 * ff + 128), BF16)],
-        [sums, flip(sums, "mlp", 1)],
-    )
     (down,) = call(
         functools.partial(down_kernel, width * mlp),
         "down",
         [((pool, rows, width), BF16)],
-        [core_sums, flip(core_sums, "mlp", 3), down_weight],
+        [sums] + [flip(sums, "mlp", step) for step in (1, 2, 3)] + [down_weight],
         [pltpu.VMEM((requests, width), F32)],
     )
     backwards = list(range(pool))[::-1]

time: 53.5 us -> 54 us (level)
  waiting for transfers between devices: 16.1 us -> 16.8 us
    ppermute x13 -> x14, waiting for transfers between devices: 14 us -> 14.6 us  [flip(): lax.ppermute(values, axis, [(index, index ^ step) for index in range(size)])]
    pallas_call x11 -> x10, Pallas kernels: 5.26 us -> 5.17 us  [call(): pl.pallas_call(kernel, out_shape=[jax.ShapeDtypeStruct(shape, dtype) for...]
    ppermute x13 -> x14, starting transfers between devices: 17.6 us -> 17.6 us  [flip(): lax.ppermute(values, axis, [(index, index ^ step) for index in range(size)])]
  transfers between devices with their start and end apart: 15 -> 16, of which waited for: 13 -> 13; matrix products, arithmetic and copies ran while one was open for 0% -> 0% of each run, Pallas kernels for 0% -> 0%
where the time goes in v16:
time: 54 us; the launch traced here: 53.8 us
  starting transfers between devices  21.9 us (41%)
  waiting for transfers between devices  16.8 us (31%)
  blocking collectives  8.36 us (15%)
  Pallas kernels  5.17 us (10%)
  local copies, waits for them, and re-layouts  1.46 us (3%)
    ppermute x14, starting transfers between devices, flip(): lax.ppermute(values, axis, [(index, index ^ step) for index in range(size)])  17.6 us
    ppermute x14, waiting for transfers between devices, flip(): lax.ppermute(values, axis, [(index, index ^ step) for index in range(size)])  14.6 us
    all_to_all x1, blocking collectives, per_device_small(): lax.all_to_all(down, 'pool', 0, 0, axis_index_groups=[backwards])  8.36 us
    pallas_call x10, Pallas kernels, call(): pl.pallas_call(kernel, out_shape=[jax.ShapeDtypeStruct(shape, dtype) for...  5.17 us
    ppermute x2, starting transfers between devices, per_device_small(): pieces.append(lax.ppermute(head_sum, ('pool', 'mlp'), route))  4.27 us
    ppermute x2, waiting for transfers between devices, per_device_small(): pieces.append(lax.ppermute(head_sum, ('pool', 'mlp'), route))  2.2 us
    unnamed x18, local copies, waits for them, and re-layouts  1.45 us
  transfers between devices with their start and end apart: 16, of which 13 were waited for; matrix products, arithmetic and copies ran while one was open for 0% of the time, Pallas kernels for 0%

profile of v16, /device:TPU:0, one launch (start us, length us, event | category | flops | bytes accessed | tf_op | source)
XLA Modules:
  0.0 53.8 jit_solution(3273599673909501626)
XLA Ops:
  0.0 1.6 %rotary.1 = (bf16[2,1664]{1,0:T(2,128)(2,1)}, bf16[2,1536]{1,0:T(2,128)(2,1)}) custom-call(s32[2,8]{1,0:T(2,128)} %refs_0_.1, s32[2]{0:T(128)} %refs_1_.1, bf16[2,768]{1,0:T(2,128)(2,1)} %refs_2_.1, bf16[2,768]{1,0:T(2,128)(2,1)} %refs_3_.1, bf16[2,768]{1,0:T(2,128)(2,1)} %refs_4_.1, bf16[2,768]{1,0:T(2,128)(2,1)} %refs_5_.1, bf16[5,256,768]{2,1,0:T(8,128)(2,1)} %keys.1, ...), custom_call_target="tpu_custom_call" | custom-call | bytes 3944520 | tf_op jit(solution)/shard_map/rotary/pallas_call | solution.py:217
  1.6 3.0 %collective-permute-start = (bf16[2,1664]{1,0:T(2,128)(2,1)}, bf16[2,1664]{1,0:T(2,128)(2,1)S(1)}, u32[]{:S(2)}, u32[]{:S(2)}) collective-permute-start(bf16[2,1664]{1,0:T(2,128)(2,1)} %get-tuple-element.14.packed), channel_id=1, source_target_pairs={{0,4},{4,0},{8,12},{12,8},{16,20},{20,16},{24,28},{28,24},{1,5},{5... | collective-permute-start | bytes 19976 | tf_op jit(solution)/shard_map/ppermute | solution.py:531
  4.7 0.7 %copy-done.6 = bf16[2,1664]{1,0:T(2,128)(2,1)S(1)} copy-done((bf16[2,1664]{1,0:T(2,128)(2,1)S(1)}, bf16[2,1664]{1,0:T(2,128)(2,1)}, u32[]{:S(2)}) %copy-start.6) | copy-done | bytes 6680
  5.4 0.7 %copy-done.7 = bf16[2,1536]{1,0:T(2,128)(2,1)S(1)} copy-done((bf16[2,1536]{1,0:T(2,128)(2,1)S(1)}, bf16[2,1536]{1,0:T(2,128)(2,1)}, u32[]{:S(2)}) %copy-start.7) | copy-done | bytes 6168
  6.1 0.1 carry.1
  6.2 0.3 collective-permute-done.theirs
  6.5 4.1 %collective-permute-start.3 = (bf16[2,2,1664]{2,1,0:T(2,128)(2,1)S(1)}, bf16[2,2,1664]{2,1,0:T(2,128)(2,1)S(1)}, u32[]{:S(2)}, u32[]{:S(2)}) collective-permute-start(bf16[2,2,1664]{2,1,0:T(2,128)(2,1)S(1)} %merge.2.a0), channel_id=1, source_target_pairs={{0,24},{4,28},{8,16},{12,20},{16,8},{20,12},{24,0},{28,4},{1,25},{... | collective-permute-start | bytes 39944 | tf_op jit(solution)/shard_map/ppermute | solution.py:531
  10.6 0.0 collective-permute-start.2
  10.6 0.6 %collective-permute-start.1 = (bf16[2,2,1664]{2,1,0:T(2,128)(2,1)S(1)}, bf16[2,2,1664]{2,1,0:T(2,128)(2,1)S(1)}, u32[]{:S(2)}, u32[]{:S(2)}) collective-permute-start(bf16[2,2,1664]{2,1,0:T(2,128)(2,1)S(1)} %merge.2.a0), channel_id=1, source_target_pairs={{0,8},{4,12},{8,0},{12,4},{16,24},{20,28},{24,16},{28,20},{1,9},{5... | collective-permute-start | bytes 39944 | tf_op jit(solution)/shard_map/ppermute | solution.py:531
  11.2 1.1 %collective-permute-done.3.a3 = bf16[2,2,1664]{2,1,0:T(2,128)(2,1)S(1)} collective-permute-done((bf16[2,2,1664]{2,1,0:T(2,128)(2,1)S(1)}, bf16[2,2,1664]{2,1,0:T(2,128)(2,1)S(1)}, u32[]{:S(2)}, u32[]{:S(2)}) %collective-permute-start.3) | collective-permute-done | bytes 13344 | tf_op jit(solution)/shard_map/ppermute | solution.py:531
  12.3 2.9 %collective-permute-done.2.a2 = bf16[2,2,1664]{2,1,0:T(2,128)(2,1)S(1)} collective-permute-done((bf16[2,2,1664]{2,1,0:T(2,128)(2,1)S(1)}, bf16[2,2,1664]{2,1,0:T(2,128)(2,1)S(1)}, u32[]{:S(2)}, u32[]{:S(2)}) %collective-permute-start.2) | collective-permute-done | bytes 13344 | tf_op jit(solution)/shard_map/ppermute | solution.py:531
  15.2 0.0 collective-permute-done.1.a1
  15.2 0.0 copy-done.1
  15.2 0.0 copy-start.5
  15.2 0.0 copy-start.8
  15.3 0.0 copy-start.3
  15.3 0.0 copy-start.4
  15.3 1.1 %attend.1 = (bf16[8,768]{1,0:T(8,128)(2,1)S(1)}, f32[16,768]{1,0:T(8,128)S(1)}, f32[16,128]{1,0:T(8,128)S(1)}) custom-call(bf16[2,2,1664]{2,1,0:T(2,128)(2,1)S(1)} %merge.2.a0, bf16[2,2,1664]{2,1,0:T(2,128)(2,1)S(1)} %collective-permute-done.1.a1, bf16[2,2,1664]{2,1,0:T(2,128)(2,1)S(1)} %collective-permute-done.2.a2, ...), custom_call_target="tpu_custom_call" | custom-call | bytes 4014080 | tf_op jit(solution)/shard_map/attend/pallas_call | solution.py:217
  16.4 1.6 %collective-permute-start.4 = (bf16[8,768]{1,0:T(8,128)(2,1)S(1)}, bf16[8,768]{1,0:T(8,128)(2,1)S(1)}, u32[]{:S(2)}, u32[]{:S(2)}) collective-permute-start(bf16[8,768]{1,0:T(8,128)(2,1)S(1)} %get-tuple-element.18.mine), channel_id=1, source_target_pairs={{0,4},{4,0},{8,12},{12,8},{16,20},{20,16},{24,28},{28,24},{1,5},{5... | collective-permute-start | bytes 36872 | tf_op jit(solution)/shard_map/ppermute | solution.py:531
  18.0 2.2 %collective-permute-done.4.theirs = bf16[8,768]{1,0:T(8,128)(2,1)S(1)} collective-permute-done((bf16[8,768]{1,0:T(8,128)(2,1)S(1)}, bf16[8,768]{1,0:T(8,128)(2,1)S(1)}, u32[]{:S(2)}, u32[]{:S(2)}) %collective-permute-start.4) | collective-permute-done | bytes 12320 | tf_op jit(solution)/shard_map/ppermute | solution.py:531
  20.2 1.4 %collective-permute-start.7 = (bf16[2,8,768]{2,1,0:T(8,128)(2,1)S(1)}, bf16[2,8,768]{2,1,0:T(8,128)(2,1)S(1)}, u32[]{:S(2)}, u32[]{:S(2)}) collective-permute-start(bf16[2,8,768]{2,1,0:T(8,128)(2,1)S(1)} %merge.3.b0), channel_id=1, source_target_pairs={{0,24},{4,28},{8,16},{12,20},{16,8},{20,12},{24,0},{28,4},{1,25},{... | collective-permute-start | bytes 73736 | tf_op jit(solution)/shard_map/ppermute | solution.py:531
  21.6 0.6 %collective-permute-start.6 = (bf16[2,8,768]{2,1,0:T(8,128)(2,1)S(1)}, bf16[2,8,768]{2,1,0:T(8,128)(2,1)S(1)}, u32[]{:S(2)}, u32[]{:S(2)}) collective-permute-start(bf16[2,8,768]{2,1,0:T(8,128)(2,1)S(1)} %merge.3.b0), channel_id=1, source_target_pairs={{0,16},{4,20},{8,24},{12,28},{16,0},{20,4},{24,8},{28,12},{1,17},{... | collective-permute-start | bytes 73736 | tf_op jit(solution)/shard_map/ppermute | solution.py:531
  22.3 2.3 %collective-permute-start.5 = (bf16[2,8,768]{2,1,0:T(8,128)(2,1)S(1)}, bf16[2,8,768]{2,1,0:T(8,128)(2,1)S(1)}, u32[]{:S(2)}, u32[]{:S(2)}) collective-permute-start(bf16[2,8,768]{2,1,0:T(8,128)(2,1)S(1)} %merge.3.b0), channel_id=1, source_target_pairs={{0,8},{4,12},{8,0},{12,4},{16,24},{20,28},{24,16},{28,20},{1,9},{5... | collective-permute-start | bytes 73736 | tf_op jit(solution)/shard_map/ppermute | solution.py:531
  24.6 1.2 %collective-permute-done.7.b3 = bf16[2,8,768]{2,1,0:T(8,128)(2,1)S(1)} collective-permute-done((bf16[2,8,768]{2,1,0:T(8,128)(2,1)S(1)}, bf16[2,8,768]{2,1,0:T(8,128)(2,1)S(1)}, u32[]{:S(2)}, u32[]{:S(2)}) %collective-permute-start.7) | collective-permute-done | bytes 24608 | tf_op jit(solution)/shard_map/ppermute | solution.py:531
  25.8 0.6 %collective-permute-done.6.b2 = bf16[2,8,768]{2,1,0:T(8,128)(2,1)S(1)} collective-permute-done((bf16[2,8,768]{2,1,0:T(8,128)(2,1)S(1)}, bf16[2,8,768]{2,1,0:T(8,128)(2,1)S(1)}, u32[]{:S(2)}, u32[]{:S(2)}) %collective-permute-start.6) | collective-permute-done | bytes 24608 | tf_op jit(solution)/shard_map/ppermute | solution.py:531
  26.4 0.2 collective-permute-done.5.b1
  26.6 0.7 %combine.1.p0 = bf16[16,384]{1,0:T(8,128)(2,1)S(1)} custom-call(bf16[2,8,768]{2,1,0:T(8,128)(2,1)S(1)} %merge.3.b0, bf16[2,8,768]{2,1,0:T(8,128)(2,1)S(1)} %collective-permute-done.5.b1, bf16[2,8,768]{2,1,0:T(8,128)(2,1)S(1)} %collective-permute-done.6.b2, bf16[2,8,768]{2,1,0:T(8,128)(2,1)S(1)} %collective-permute-done.7.b3, ...), custom_call_target="tpu_custom_call" | custom-call | bytes 696320 | tf_op jit(solution)/shard_map/combine/pallas_call | solution.py:217
  27.4 0.1 collective-permute-start.10
  27.4 1.6 %collective-permute-start.9 = (bf16[16,384]{1,0:T(8,128)(2,1)S(1)}, bf16[16,384]{1,0:T(8,128)(2,1)S(1)}, u32[]{:S(2)}, u32[]{:S(2)}) collective-permute-start(bf16[16,384]{1,0:T(8,128)(2,1)S(1)} %combine.1.p0), channel_id=1, source_target_pairs={{0,2},{1,3},{2,0},{3,1},{4,6},{5,7},{6,4},{7,5},{8,10},{9,11},{10,... | collective-permute-start | bytes 36872 | tf_op jit(solution)/shard_map/ppermute | solution.py:531
  29.0 0.3 collective-permute-start.8
  29.3 1.3 %collective-permute-done.10.p3 = bf16[16,384]{1,0:T(8,128)(2,1)S(1)} collective-permute-done((bf16[16,384]{1,0:T(8,128)(2,1)S(1)}, bf16[16,384]{1,0:T(8,128)(2,1)S(1)}, u32[]{:S(2)}, u32[]{:S(2)}) %collective-permute-start.10) | collective-permute-done | bytes 12320 | tf_op jit(solution)/shard_map/ppermute | solution.py:531
  30.6 0.6 %collective-permute-done.9.p2 = bf16[16,384]{1,0:T(8,128)(2,1)S(1)} collective-permute-done((bf16[16,384]{1,0:T(8,128)(2,1)S(1)}, bf16[16,384]{1,0:T(8,128)(2,1)S(1)}, u32[]{:S(2)}, u32[]{:S(2)}) %collective-permute-start.9) | collective-permute-done | bytes 12320 | tf_op jit(solution)/shard_map/ppermute | solution.py:531
  31.2 0.0 collective-permute-done.8.p1
  31.2 2.8 %collective-permute-start.12 = (bf16[16,384]{1,0:T(8,128)(2,1)S(1)}, bf16[16,384]{1,0:T(8,128)(2,1)S(1)}, u32[]{:S(2)}, u32[]{:S(2)}) collective-permute-start(bf16[16,384]{1,0:T(8,128)(2,1)S(1)} %head_sum.1), channel_id=1, source_target_pairs={{1,28},{5,24},{0,20},{4,16},{3,12},{7,8},{2,4},{6,0},{9,29},{13,25... | collective-permute-start | bytes 36872 | tf_op jit(solution)/shard_map/ppermute | solution.py:620
  34.0 1.5 %collective-permute-start.11 = (bf16[16,384]{1,0:T(8,128)(2,1)S(1)}, bf16[16,384]{1,0:T(8,128)(2,1)S(1)}, u32[]{:S(2)}, u32[]{:S(2)}) collective-permute-start(bf16[16,384]{1,0:T(8,128)(2,1)S(1)} %head_sum.1), channel_id=1, source_target_pairs={{1,24},{5,28},{0,16},{4,20},{3,8},{7,12},{2,0},{6,4},{9,25},{13,29... | collective-permute-start | bytes 36872 | tf_op jit(solution)/shard_map/ppermute | solution.py:620
  35.5 0.5 collective-permute-done.12.flip
  36.0 1.7 %collective-permute-done.11.same = bf16[16,384]{1,0:T(8,128)(2,1)S(1)} collective-permute-done((bf16[16,384]{1,0:T(8,128)(2,1)S(1)}, bf16[16,384]{1,0:T(8,128)(2,1)S(1)}, u32[]{:S(2)}, u32[]{:S(2)}) %collective-permute-start.11) | collective-permute-done | bytes 12320 | tf_op jit(solution)/shard_map/ppermute | solution.py:620
  37.7 0.0 copy-done.4
  37.7 0.5 gate_up.1
  38.2 1.9 %collective-permute-start.15 = (bf16[16,2176]{1,0:T(8,128)(2,1)S(1)}, bf16[16,2176]{1,0:T(8,128)(2,1)S(1)}, u32[]{:S(2)}, u32[]{:S(2)}) collective-permute-start(bf16[16,2176]{1,0:T(8,128)(2,1)S(1)} %get-tuple-element.22.p0), channel_id=1, source_target_pairs={{0,3},{1,2},{2,1},{3,0},{4,7},{5,6},{6,5},{7,4},{8,11},{9,10},{10,... | collective-permute-start | bytes 208904 | tf_op jit(solution)/shard_map/ppermute | solution.py:531
  40.1 0.0 collective-permute-start.14
  40.1 0.2 collective-permute-start.13
  40.2 2.3 %collective-permute-done.15.p3 = bf16[16,2176]{1,0:T(8,128)(2,1)S(1)} collective-permute-done((bf16[16,2176]{1,0:T(8,128)(2,1)S(1)}, bf16[16,2176]{1,0:T(8,128)(2,1)S(1)}, u32[]{:S(2)}, u32[]{:S(2)}) %collective-permute-start.15) | collective-permute-done | bytes 69664 | tf_op jit(solution)/shard_map/ppermute | solution.py:531
  42.6 1.8 %collective-permute-done.14.p2 = bf16[16,2176]{1,0:T(8,128)(2,1)S(1)} collective-permute-done((bf16[16,2176]{1,0:T(8,128)(2,1)S(1)}, bf16[16,2176]{1,0:T(8,128)(2,1)S(1)}, u32[]{:S(2)}, u32[]{:S(2)}) %collective-permute-start.14) | collective-permute-done | bytes 69664 | tf_op jit(solution)/shard_map/ppermute | solution.py:531
  44.4 0.0 collective-permute-done.13.p1
  44.4 0.4 down.1
  44.8 8.4 %all_to_all.5.parts = bf16[8,2,768]{2,1,0:T(2,128)(2,1)S(1)} all-to-all(bf16[8,2,768]{2,1,0:T(2,128)(2,1)S(1)} %down.1), channel_id=1, replica_groups={{28,24,20,16,12,8,4,0},{29,25,21,17,13,9,5,1},{30,26,22,18,14,10,6,2},{..., dimensions={0} | all-to-all | bytes 49152 | tf_op jit(solution)/shard_map/all_to_all | solution.py:640
  53.2 0.6 %final.1 = bf16[2,768]{1,0:T(2,128)(2,1)} custom-call(f32[2,768]{1,0:T(2,128)S(1)} %get-tuple-element.21.own, bf16[8,2,768]{2,1,0:T(2,128)(2,1)S(1)} %all_to_all.5.parts), custom_call_target="tpu_custom_call" | custom-call | bytes 30720 | tf_op jit(solution)/shard_map/final/pallas_call | solution.py:217
  (14 shorter events, 0.0 us)
Async XLA Ops:
  0.0 15.2 %copy-start.1 = (bf16[5,256,768]{2,1,0:T(8,128)(2,1)S(1)}, bf16[5,256,768]{2,1,0:T(8,128)(2,1)}, u32[]{:S(2)}) copy-start(bf16[5,256,768]{2,1,0:T(8,128)(2,1)} %values.1) | copy-start | bytes 5898244
  0.0 15.2 %copy-start = (bf16[5,256,768]{2,1,0:T(8,128)(2,1)S(1)}, bf16[5,256,768]{2,1,0:T(8,128)(2,1)}, u32[]{:S(2)}) copy-start(bf16[5,256,768]{2,1,0:T(8,128)(2,1)} %keys.1) | copy-start | bytes 5898244
  1.6 4.9 %collective-permute-start = (bf16[2,1664]{1,0:T(2,128)(2,1)}, bf16[2,1664]{1,0:T(2,128)(2,1)S(1)}, u32[]{:S(2)}, u32[]{:S(2)}) collective-permute-start(bf16[2,1664]{1,0:T(2,128)(2,1)} %get-tuple-element.14.packed), channel_id=1, source_target_pairs={{0,4},{4,0},{8,12},{12,8},{16,20},{20,16},{24,28},{28,24},{1,5},{5... | collective-permute-start | bytes 19976 | tf_op jit(solution)/shard_map/ppermute | solution.py:531
  4.7 0.7 %copy-start.6 = (bf16[2,1664]{1,0:T(2,128)(2,1)S(1)}, bf16[2,1664]{1,0:T(2,128)(2,1)}, u32[]{:S(2)}) copy-start(bf16[2,1664]{1,0:T(2,128)(2,1)} %get-tuple-element.14.packed) | copy-start | bytes 19972
  5.4 0.7 %copy-start.7 = (bf16[2,1536]{1,0:T(2,128)(2,1)S(1)}, bf16[2,1536]{1,0:T(2,128)(2,1)}, u32[]{:S(2)}) copy-start(bf16[2,1536]{1,0:T(2,128)(2,1)} %get-tuple-element.15.new) | copy-start | bytes 18436
  6.5 5.8 %collective-permute-start.3 = (bf16[2,2,1664]{2,1,0:T(2,128)(2,1)S(1)}, bf16[2,2,1664]{2,1,0:T(2,128)(2,1)S(1)}, u32[]{:S(2)}, u32[]{:S(2)}) collective-permute-start(bf16[2,2,1664]{2,1,0:T(2,128)(2,1)S(1)} %merge.2.a0), channel_id=1, source_target_pairs={{0,24},{4,28},{8,16},{12,20},{16,8},{20,12},{24,0},{28,4},{1,25},{... | collective-permute-start | bytes 39944 | tf_op jit(solution)/shard_map/ppermute | solution.py:531
  10.6 4.6 %collective-permute-start.2 = (bf16[2,2,1664]{2,1,0:T(2,128)(2,1)S(1)}, bf16[2,2,1664]{2,1,0:T(2,128)(2,1)S(1)}, u32[]{:S(2)}, u32[]{:S(2)}) collective-permute-start(bf16[2,2,1664]{2,1,0:T(2,128)(2,1)S(1)} %merge.2.a0), channel_id=1, source_target_pairs={{0,16},{4,20},{8,24},{12,28},{16,0},{20,4},{24,8},{28,12},{1,17},{... | collective-permute-start | bytes 39944 | tf_op jit(solution)/shard_map/ppermute | solution.py:531
  10.6 4.6 %collective-permute-start.1 = (bf16[2,2,1664]{2,1,0:T(2,128)(2,1)S(1)}, bf16[2,2,1664]{2,1,0:T(2,128)(2,1)S(1)}, u32[]{:S(2)}, u32[]{:S(2)}) collective-permute-start(bf16[2,2,1664]{2,1,0:T(2,128)(2,1)S(1)} %merge.2.a0), channel_id=1, source_target_pairs={{0,8},{4,12},{8,0},{12,4},{16,24},{20,28},{24,16},{28,20},{1,9},{5... | collective-permute-start | bytes 39944 | tf_op jit(solution)/shard_map/ppermute | solution.py:531
  15.2 11.4 %copy-start.5 = (bf16[768,384]{1,0:T(8,128)(2,1)S(1)}, bf16[768,384]{1,0:T(8,128)(2,1)}, u32[]{:S(2)}) copy-start(bf16[768,384]{1,0:T(8,128)(2,1)} %weight.2) | copy-start | bytes 1769476
  15.2 20.2 %copy-start.8 = (bf16[768]{0:T(1024)(128)(2,1)S(1)}, bf16[768]{0:T(1024)(128)(2,1)}, u32[]{:S(2)}) copy-start(bf16[768]{0:T(1024)(128)(2,1)} %param.22) | copy-start | bytes 4612
  15.3 22.4 %copy-start.3 = (bf16[768,1024]{1,0:T(8,128)(2,1)S(1)}, bf16[768,1024]{1,0:T(8,128)(2,1)}, u32[]{:S(2)}) copy-start(bf16[768,1024]{1,0:T(8,128)(2,1)} %gate.1) | copy-start | bytes 4718596
  15.3 22.4 %copy-start.4 = (bf16[768,1024]{1,0:T(8,128)(2,1)S(1)}, bf16[768,1024]{1,0:T(8,128)(2,1)}, u32[]{:S(2)}) copy-start(bf16[768,1024]{1,0:T(8,128)(2,1)} %up.1) | copy-start | bytes 4718596
  16.4 3.8 %collective-permute-start.4 = (bf16[8,768]{1,0:T(8,128)(2,1)S(1)}, bf16[8,768]{1,0:T(8,128)(2,1)S(1)}, u32[]{:S(2)}, u32[]{:S(2)}) collective-permute-start(bf16[8,768]{1,0:T(8,128)(2,1)S(1)} %get-tuple-element.18.mine), channel_id=1, source_target_pairs={{0,4},{4,0},{8,12},{12,8},{16,20},{20,16},{24,28},{28,24},{1,5},{5... | collective-permute-start | bytes 36872 | tf_op jit(solution)/shard_map/ppermute | solution.py:531
  20.2 5.6 %collective-permute-start.7 = (bf16[2,8,768]{2,1,0:T(8,128)(2,1)S(1)}, bf16[2,8,768]{2,1,0:T(8,128)(2,1)S(1)}, u32[]{:S(2)}, u32[]{:S(2)}) collective-permute-start(bf16[2,8,768]{2,1,0:T(8,128)(2,1)S(1)} %merge.3.b0), channel_id=1, source_target_pairs={{0,24},{4,28},{8,16},{12,20},{16,8},{20,12},{24,0},{28,4},{1,25},{... | collective-permute-start | bytes 73736 | tf_op jit(solution)/shard_map/ppermute | solution.py:531
  21.6 4.7 %collective-permute-start.6 = (bf16[2,8,768]{2,1,0:T(8,128)(2,1)S(1)}, bf16[2,8,768]{2,1,0:T(8,128)(2,1)S(1)}, u32[]{:S(2)}, u32[]{:S(2)}) collective-permute-start(bf16[2,8,768]{2,1,0:T(8,128)(2,1)S(1)} %merge.3.b0), channel_id=1, source_target_pairs={{0,16},{4,20},{8,24},{12,28},{16,0},{20,4},{24,8},{28,12},{1,17},{... | collective-permute-start | bytes 73736 | tf_op jit(solution)/shard_map/ppermute | solution.py:531
  22.3 4.4 %collective-permute-start.5 = (bf16[2,8,768]{2,1,0:T(8,128)(2,1)S(1)}, bf16[2,8,768]{2,1,0:T(8,128)(2,1)S(1)}, u32[]{:S(2)}, u32[]{:S(2)}) collective-permute-start(bf16[2,8,768]{2,1,0:T(8,128)(2,1)S(1)} %merge.3.b0), channel_id=1, source_target_pairs={{0,8},{4,12},{8,0},{12,4},{16,24},{20,28},{24,16},{28,20},{1,9},{5... | collective-permute-start | bytes 73736 | tf_op jit(solution)/shard_map/ppermute | solution.py:531
  27.4 3.2 %collective-permute-start.10 = (bf16[16,384]{1,0:T(8,128)(2,1)S(1)}, bf16[16,384]{1,0:T(8,128)(2,1)S(1)}, u32[]{:S(2)}, u32[]{:S(2)}) collective-permute-start(bf16[16,384]{1,0:T(8,128)(2,1)S(1)} %combine.1.p0), channel_id=1, source_target_pairs={{0,3},{1,2},{2,1},{3,0},{4,7},{5,6},{6,5},{7,4},{8,11},{9,10},{10,... | collective-permute-start | bytes 36872 | tf_op jit(solution)/shard_map/ppermute | solution.py:531
  27.4 3.8 %collective-permute-start.9 = (bf16[16,384]{1,0:T(8,128)(2,1)S(1)}, bf16[16,384]{1,0:T(8,128)(2,1)S(1)}, u32[]{:S(2)}, u32[]{:S(2)}) collective-permute-start(bf16[16,384]{1,0:T(8,128)(2,1)S(1)} %combine.1.p0), channel_id=1, source_target_pairs={{0,2},{1,3},{2,0},{3,1},{4,6},{5,7},{6,4},{7,5},{8,10},{9,11},{10,... | collective-permute-start | bytes 36872 | tf_op jit(solution)/shard_map/ppermute | solution.py:531
  29.0 2.2 %collective-permute-start.8 = (bf16[16,384]{1,0:T(8,128)(2,1)S(1)}, bf16[16,384]{1,0:T(8,128)(2,1)S(1)}, u32[]{:S(2)}, u32[]{:S(2)}) collective-permute-start(bf16[16,384]{1,0:T(8,128)(2,1)S(1)} %combine.1.p0), channel_id=1, source_target_pairs={{0,1},{1,0},{2,3},{3,2},{4,5},{5,4},{6,7},{7,6},{8,9},{9,8},{10,11... | collective-permute-start | bytes 36872 | tf_op jit(solution)/shard_map/ppermute | solution.py:531
  31.2 4.8 %collective-permute-start.12 = (bf16[16,384]{1,0:T(8,128)(2,1)S(1)}, bf16[16,384]{1,0:T(8,128)(2,1)S(1)}, u32[]{:S(2)}, u32[]{:S(2)}) collective-permute-start(bf16[16,384]{1,0:T(8,128)(2,1)S(1)} %head_sum.1), channel_id=1, source_target_pairs={{1,28},{5,24},{0,20},{4,16},{3,12},{7,8},{2,4},{6,0},{9,29},{13,25... | collective-permute-start | bytes 36872 | tf_op jit(solution)/shard_map/ppermute | solution.py:620
  34.0 3.7 %collective-permute-start.11 = (bf16[16,384]{1,0:T(8,128)(2,1)S(1)}, bf16[16,384]{1,0:T(8,128)(2,1)S(1)}, u32[]{:S(2)}, u32[]{:S(2)}) collective-permute-start(bf16[16,384]{1,0:T(8,128)(2,1)S(1)} %head_sum.1), channel_id=1, source_target_pairs={{1,24},{5,28},{0,16},{4,20},{3,8},{7,12},{2,0},{6,4},{9,25},{13,29... | collective-permute-start | bytes 36872 | tf_op jit(solution)/shard_map/ppermute | solution.py:620
  37.7 6.7 %copy-start.2 = (bf16[1024,768]{1,0:T(8,128)(2,1)S(1)}, bf16[1024,768]{1,0:T(8,128)(2,1)}, u32[]{:S(2)}) copy-start(bf16[1024,768]{1,0:T(8,128)(2,1)} %weight.3) | copy-start | bytes 4718596
  38.2 4.4 %collective-permute-start.15 = (bf16[16,2176]{1,0:T(8,128)(2,1)S(1)}, bf16[16,2176]{1,0:T(8,128)(2,1)S(1)}, u32[]{:S(2)}, u32[]{:S(2)}) collective-permute-start(bf16[16,2176]{1,0:T(8,128)(2,1)S(1)} %get-tuple-element.22.p0), channel_id=1, source_target_pairs={{0,3},{1,2},{2,1},{3,0},{4,7},{5,6},{6,5},{7,4},{8,11},{9,10},{10,... | collective-permute-start | bytes 208904 | tf_op jit(solution)/shard_map/ppermute | solution.py:531
  40.1 4.3 %collective-permute-start.14 = (bf16[16,2176]{1,0:T(8,128)(2,1)S(1)}, bf16[16,2176]{1,0:T(8,128)(2,1)S(1)}, u32[]{:S(2)}, u32[]{:S(2)}) collective-permute-start(bf16[16,2176]{1,0:T(8,128)(2,1)S(1)} %get-tuple-element.22.p0), channel_id=1, source_target_pairs={{0,2},{1,3},{2,0},{3,1},{4,6},{5,7},{6,4},{7,5},{8,10},{9,11},{10,... | collective-permute-start | bytes 208904 | tf_op jit(solution)/shard_map/ppermute | solution.py:531
  40.1 4.3 %collective-permute-start.13 = (bf16[16,2176]{1,0:T(8,128)(2,1)S(1)}, bf16[16,2176]{1,0:T(8,128)(2,1)S(1)}, u32[]{:S(2)}, u32[]{:S(2)}) collective-permute-start(bf16[16,2176]{1,0:T(8,128)(2,1)S(1)} %get-tuple-element.22.p0), channel_id=1, source_target_pairs={{0,1},{1,0},{2,3},{3,2},{4,5},{5,4},{6,7},{7,6},{8,9},{9,8},{10,11... | collective-permute-start | bytes 208904 | tf_op jit(solution)/shard_map/ppermute | solution.py:531

commit v17 on v12

--- a/solution.py
+++ b/solution.py
@@ -389,12 +389,19 @@
         limit = jnp.sum(holder * length, 0, keepdims=True) - place * block_len
         limits.append(jnp.broadcast_to(limit, (heads, block_len)))
         query = jnp.sum(holder * queries, 0, keepdims=True)
-        spread = jnp.where(head_mask, query, 0.0).astype(BF16)
-        scores.append(
-            lax.dot_general(
-                spread, keys[b], (((1,), (1,)), ((), ())), preferred_element_type=F32
-            )
-        )
+        scores.append(jnp.where(head_mask, query, 0.0))
+    filler = jnp.zeros((128 - blocks * heads, width), F32)
+    stacked = jnp.concatenate(scores + [filler], 0).astype(BF16)
+    every = lax.dot_general(
+        keys[...].reshape(blocks * block_len, width),
+        stacked,
+        (((1,), (1,)), ((), ())),
+        preferred_element_type=F32,
+    )
+    scores = []
+    for b in range(blocks):
+        turned = jnp.transpose(every[b * block_len : (b + 1) * block_len])
+        scores.append(turned[b * heads : (b + 1) * heads])
     scores = jnp.concatenate(scores, 0) * (1.0 / math.sqrt(HD))
     token = lanes((blocks * heads, block_len)).astype(F32)
     valid = token < jnp.concatenate(limits, 0)

time: 53.5 us -> 54.1 us (1.011)
  Pallas kernels: 5.26 us -> 5.82 us
    pallas_call x11, Pallas kernels: 5.26 us -> 5.82 us  [call(): pl.pallas_call(kernel, out_shape=[jax.ShapeDtypeStruct(shape, dtype) for...]
where the time goes in v17:
time: 54.1 us; the launch traced here: 53.8 us
  starting transfers between devices  21.9 us (40%)
  waiting for transfers between devices  16.1 us (30%)
  blocking collectives  8.36 us (15%)
  Pallas kernels  5.82 us (11%)
  local copies, waits for them, and re-layouts  1.46 us (3%)
    ppermute x13, starting transfers between devices, flip(): lax.ppermute(values, axis, [(index, index ^ step) for index in range(size)])  17.6 us
    ppermute x13, waiting for transfers between devices, flip(): lax.ppermute(values, axis, [(index, index ^ step) for index in range(size)])  13.9 us
    all_to_all x1, blocking collectives, per_device_small(): lax.all_to_all(down, 'pool', 0, 0, axis_index_groups=[backwards])  8.36 us
    pallas_call x11, Pallas kernels, call(): pl.pallas_call(kernel, out_shape=[jax.ShapeDtypeStruct(shape, dtype) for...  5.82 us
    ppermute x2, starting transfers between devices, per_device_small(): pieces.append(lax.ppermute(head_sum, ('pool', 'mlp'), route))  4.27 us
    ppermute x2, waiting for transfers between devices, per_device_small(): pieces.append(lax.ppermute(head_sum, ('pool', 'mlp'), route))  2.2 us
    unnamed x18, local copies, waits for them, and re-layouts  1.45 us
  transfers between devices with their start and end apart: 15, of which 13 were waited for; matrix products, arithmetic and copies ran while one was open for 0% of the time, Pallas kernels for 0%

profile of v17, /device:TPU:0, one launch (start us, length us, event | category | flops | bytes accessed | tf_op | source)
XLA Modules:
  0.0 53.8 jit_solution(16662994230391150193)
XLA Ops:
  0.0 1.6 %rotary.1 = (bf16[2,1664]{1,0:T(2,128)(2,1)}, bf16[2,1536]{1,0:T(2,128)(2,1)}) custom-call(s32[2,8]{1,0:T(2,128)} %refs_0_.1, s32[2]{0:T(128)} %refs_1_.1, bf16[2,768]{1,0:T(2,128)(2,1)} %refs_2_.1, bf16[2,768]{1,0:T(2,128)(2,1)} %refs_3_.1, bf16[2,768]{1,0:T(2,128)(2,1)} %refs_4_.1, bf16[2,768]{1,0:T(2,128)(2,1)} %refs_5_.1, bf16[5,256,768]{2,1,0:T(8,128)(2,1)} %keys.1, ...), custom_call_target="tpu_custom_call" | custom-call | bytes 3944520 | tf_op jit(solution)/shard_map/rotary/pallas_call | solution.py:217
  1.6 3.0 %collective-permute-start = (bf16[2,1664]{1,0:T(2,128)(2,1)}, bf16[2,1664]{1,0:T(2,128)(2,1)S(1)}, u32[]{:S(2)}, u32[]{:S(2)}) collective-permute-start(bf16[2,1664]{1,0:T(2,128)(2,1)} %get-tuple-element.14.packed), channel_id=1, source_target_pairs={{0,4},{4,0},{8,12},{12,8},{16,20},{20,16},{24,28},{28,24},{1,5},{5... | collective-permute-start | bytes 19976 | tf_op jit(solution)/shard_map/ppermute | solution.py:545
  4.7 0.7 %copy-done.6 = bf16[2,1664]{1,0:T(2,128)(2,1)S(1)} copy-done((bf16[2,1664]{1,0:T(2,128)(2,1)S(1)}, bf16[2,1664]{1,0:T(2,128)(2,1)}, u32[]{:S(2)}) %copy-start.6) | copy-done | bytes 6680
  5.4 0.7 %copy-done.7 = bf16[2,1536]{1,0:T(2,128)(2,1)S(1)} copy-done((bf16[2,1536]{1,0:T(2,128)(2,1)S(1)}, bf16[2,1536]{1,0:T(2,128)(2,1)}, u32[]{:S(2)}) %copy-start.7) | copy-done | bytes 6168
  6.1 0.1 carry.1
  6.2 0.3 collective-permute-done.theirs
  6.5 4.1 %collective-permute-start.3 = (bf16[2,2,1664]{2,1,0:T(2,128)(2,1)S(1)}, bf16[2,2,1664]{2,1,0:T(2,128)(2,1)S(1)}, u32[]{:S(2)}, u32[]{:S(2)}) collective-permute-start(bf16[2,2,1664]{2,1,0:T(2,128)(2,1)S(1)} %merge.2.a0), channel_id=1, source_target_pairs={{0,24},{4,28},{8,16},{12,20},{16,8},{20,12},{24,0},{28,4},{1,25},{... | collective-permute-start | bytes 39944 | tf_op jit(solution)/shard_map/ppermute | solution.py:545
  10.6 0.0 collective-permute-start.2
  10.6 0.6 %collective-permute-start.1 = (bf16[2,2,1664]{2,1,0:T(2,128)(2,1)S(1)}, bf16[2,2,1664]{2,1,0:T(2,128)(2,1)S(1)}, u32[]{:S(2)}, u32[]{:S(2)}) collective-permute-start(bf16[2,2,1664]{2,1,0:T(2,128)(2,1)S(1)} %merge.2.a0), channel_id=1, source_target_pairs={{0,8},{4,12},{8,0},{12,4},{16,24},{20,28},{24,16},{28,20},{1,9},{5... | collective-permute-start | bytes 39944 | tf_op jit(solution)/shard_map/ppermute | solution.py:545
  11.2 1.1 %collective-permute-done.3.a3 = bf16[2,2,1664]{2,1,0:T(2,128)(2,1)S(1)} collective-permute-done((bf16[2,2,1664]{2,1,0:T(2,128)(2,1)S(1)}, bf16[2,2,1664]{2,1,0:T(2,128)(2,1)S(1)}, u32[]{:S(2)}, u32[]{:S(2)}) %collective-permute-start.3) | collective-permute-done | bytes 13344 | tf_op jit(solution)/shard_map/ppermute | solution.py:545
  12.3 2.9 %collective-permute-done.2.a2 = bf16[2,2,1664]{2,1,0:T(2,128)(2,1)S(1)} collective-permute-done((bf16[2,2,1664]{2,1,0:T(2,128)(2,1)S(1)}, bf16[2,2,1664]{2,1,0:T(2,128)(2,1)S(1)}, u32[]{:S(2)}, u32[]{:S(2)}) %collective-permute-start.2) | collective-permute-done | bytes 13344 | tf_op jit(solution)/shard_map/ppermute | solution.py:545
  15.2 0.0 collective-permute-done.1.a1
  15.2 0.0 copy-start.5
  15.2 0.0 copy-start.8
  15.3 0.0 copy-start.3
  15.3 0.0 copy-start.4
  15.3 1.7 %attend.1 = (bf16[8,768]{1,0:T(8,128)(2,1)S(1)}, f32[16,768]{1,0:T(8,128)S(1)}, f32[16,128]{1,0:T(8,128)S(1)}) custom-call(bf16[2,2,1664]{2,1,0:T(2,128)(2,1)S(1)} %merge.2.a0, bf16[2,2,1664]{2,1,0:T(2,128)(2,1)S(1)} %collective-permute-done.1.a1, bf16[2,2,1664]{2,1,0:T(2,128)(2,1)S(1)} %collective-permute-done.2.a2, ...), custom_call_target="tpu_custom_call" | custom-call | bytes 4014080 | tf_op jit(solution)/shard_map/attend/pallas_call | solution.py:217
  17.0 1.6 %collective-permute-start.4 = (bf16[8,768]{1,0:T(8,128)(2,1)S(1)}, bf16[8,768]{1,0:T(8,128)(2,1)S(1)}, u32[]{:S(2)}, u32[]{:S(2)}) collective-permute-start(bf16[8,768]{1,0:T(8,128)(2,1)S(1)} %get-tuple-element.18.mine), channel_id=1, source_target_pairs={{0,4},{4,0},{8,12},{12,8},{16,20},{20,16},{24,28},{28,24},{1,5},{5... | collective-permute-start | bytes 36872 | tf_op jit(solution)/shard_map/ppermute | solution.py:545
  18.6 2.2 %collective-permute-done.4.theirs = bf16[8,768]{1,0:T(8,128)(2,1)S(1)} collective-permute-done((bf16[8,768]{1,0:T(8,128)(2,1)S(1)}, bf16[8,768]{1,0:T(8,128)(2,1)S(1)}, u32[]{:S(2)}, u32[]{:S(2)}) %collective-permute-start.4) | collective-permute-done | bytes 12320 | tf_op jit(solution)/shard_map/ppermute | solution.py:545
  20.7 1.4 %collective-permute-start.7 = (bf16[2,8,768]{2,1,0:T(8,128)(2,1)S(1)}, bf16[2,8,768]{2,1,0:T(8,128)(2,1)S(1)}, u32[]{:S(2)}, u32[]{:S(2)}) collective-permute-start(bf16[2,8,768]{2,1,0:T(8,128)(2,1)S(1)} %merge.3.b0), channel_id=1, source_target_pairs={{0,24},{4,28},{8,16},{12,20},{16,8},{20,12},{24,0},{28,4},{1,25},{... | collective-permute-start | bytes 73736 | tf_op jit(solution)/shard_map/ppermute | solution.py:545
  22.2 0.6 %collective-permute-start.6 = (bf16[2,8,768]{2,1,0:T(8,128)(2,1)S(1)}, bf16[2,8,768]{2,1,0:T(8,128)(2,1)S(1)}, u32[]{:S(2)}, u32[]{:S(2)}) collective-permute-start(bf16[2,8,768]{2,1,0:T(8,128)(2,1)S(1)} %merge.3.b0), channel_id=1, source_target_pairs={{0,16},{4,20},{8,24},{12,28},{16,0},{20,4},{24,8},{28,12},{1,17},{... | collective-permute-start | bytes 73736 | tf_op jit(solution)/shard_map/ppermute | solution.py:545
  22.8 2.3 %collective-permute-start.5 = (bf16[2,8,768]{2,1,0:T(8,128)(2,1)S(1)}, bf16[2,8,768]{2,1,0:T(8,128)(2,1)S(1)}, u32[]{:S(2)}, u32[]{:S(2)}) collective-permute-start(bf16[2,8,768]{2,1,0:T(8,128)(2,1)S(1)} %merge.3.b0), channel_id=1, source_target_pairs={{0,8},{4,12},{8,0},{12,4},{16,24},{20,28},{24,16},{28,20},{1,9},{5... | collective-permute-start | bytes 73736 | tf_op jit(solution)/shard_map/ppermute | solution.py:545
  25.1 1.2 %collective-permute-done.7.b3 = bf16[2,8,768]{2,1,0:T(8,128)(2,1)S(1)} collective-permute-done((bf16[2,8,768]{2,1,0:T(8,128)(2,1)S(1)}, bf16[2,8,768]{2,1,0:T(8,128)(2,1)S(1)}, u32[]{:S(2)}, u32[]{:S(2)}) %collective-permute-start.7) | collective-permute-done | bytes 24608 | tf_op jit(solution)/shard_map/ppermute | solution.py:545
  26.4 0.6 %collective-permute-done.6.b2 = bf16[2,8,768]{2,1,0:T(8,128)(2,1)S(1)} collective-permute-done((bf16[2,8,768]{2,1,0:T(8,128)(2,1)S(1)}, bf16[2,8,768]{2,1,0:T(8,128)(2,1)S(1)}, u32[]{:S(2)}, u32[]{:S(2)}) %collective-permute-start.6) | collective-permute-done | bytes 24608 | tf_op jit(solution)/shard_map/ppermute | solution.py:545
  26.9 0.2 collective-permute-done.5.b1
  27.2 0.0 copy-done.5
  27.2 0.7 %combine.1.p0 = bf16[16,384]{1,0:T(8,128)(2,1)S(1)} custom-call(bf16[2,8,768]{2,1,0:T(8,128)(2,1)S(1)} %merge.3.b0, bf16[2,8,768]{2,1,0:T(8,128)(2,1)S(1)} %collective-permute-done.5.b1, bf16[2,8,768]{2,1,0:T(8,128)(2,1)S(1)} %collective-permute-done.6.b2, bf16[2,8,768]{2,1,0:T(8,128)(2,1)S(1)} %collective-permute-done.7.b3, ...), custom_call_target="tpu_custom_call" | custom-call | bytes 696320 | tf_op jit(solution)/shard_map/combine/pallas_call | solution.py:217
  27.9 0.1 collective-permute-start.10
  28.0 1.6 %collective-permute-start.9 = (bf16[16,384]{1,0:T(8,128)(2,1)S(1)}, bf16[16,384]{1,0:T(8,128)(2,1)S(1)}, u32[]{:S(2)}, u32[]{:S(2)}) collective-permute-start(bf16[16,384]{1,0:T(8,128)(2,1)S(1)} %combine.1.p0), channel_id=1, source_target_pairs={{0,2},{1,3},{2,0},{3,1},{4,6},{5,7},{6,4},{7,5},{8,10},{9,11},{10,... | collective-permute-start | bytes 36872 | tf_op jit(solution)/shard_map/ppermute | solution.py:545
  29.5 0.3 collective-permute-start.8
  29.8 1.3 %collective-permute-done.10.p3 = bf16[16,384]{1,0:T(8,128)(2,1)S(1)} collective-permute-done((bf16[16,384]{1,0:T(8,128)(2,1)S(1)}, bf16[16,384]{1,0:T(8,128)(2,1)S(1)}, u32[]{:S(2)}, u32[]{:S(2)}) %collective-permute-start.10) | collective-permute-done | bytes 12320 | tf_op jit(solution)/shard_map/ppermute | solution.py:545
  31.2 0.6 %collective-permute-done.9.p2 = bf16[16,384]{1,0:T(8,128)(2,1)S(1)} collective-permute-done((bf16[16,384]{1,0:T(8,128)(2,1)S(1)}, bf16[16,384]{1,0:T(8,128)(2,1)S(1)}, u32[]{:S(2)}, u32[]{:S(2)}) %collective-permute-start.9) | collective-permute-done | bytes 12320 | tf_op jit(solution)/shard_map/ppermute | solution.py:545
  31.7 0.0 collective-permute-done.8.p1
  31.7 2.8 %collective-permute-start.12 = (bf16[16,384]{1,0:T(8,128)(2,1)S(1)}, bf16[16,384]{1,0:T(8,128)(2,1)S(1)}, u32[]{:S(2)}, u32[]{:S(2)}) collective-permute-start(bf16[16,384]{1,0:T(8,128)(2,1)S(1)} %head_sum.1), channel_id=1, source_target_pairs={{1,28},{5,24},{0,20},{4,16},{3,12},{7,8},{2,4},{6,0},{9,29},{13,25... | collective-permute-start | bytes 36872 | tf_op jit(solution)/shard_map/ppermute | solution.py:634
  34.5 1.5 %collective-permute-start.11 = (bf16[16,384]{1,0:T(8,128)(2,1)S(1)}, bf16[16,384]{1,0:T(8,128)(2,1)S(1)}, u32[]{:S(2)}, u32[]{:S(2)}) collective-permute-start(bf16[16,384]{1,0:T(8,128)(2,1)S(1)} %head_sum.1), channel_id=1, source_target_pairs={{1,24},{5,28},{0,16},{4,20},{3,8},{7,12},{2,0},{6,4},{9,25},{13,29... | collective-permute-start | bytes 36872 | tf_op jit(solution)/shard_map/ppermute | solution.py:634
  36.0 0.0 copy-done.8
  36.0 0.5 collective-permute-done.12.flip
  36.5 1.7 %collective-permute-done.11.same = bf16[16,384]{1,0:T(8,128)(2,1)S(1)} collective-permute-done((bf16[16,384]{1,0:T(8,128)(2,1)S(1)}, bf16[16,384]{1,0:T(8,128)(2,1)S(1)}, u32[]{:S(2)}, u32[]{:S(2)}) %collective-permute-start.11) | collective-permute-done | bytes 12320 | tf_op jit(solution)/shard_map/ppermute | solution.py:634
  38.2 0.0 copy-done.4
  38.2 0.5 gate_up.1
  38.8 0.2 collective-permute-start.13
  38.9 1.1 %collective-permute-done.13.theirs = bf16[16,2176]{1,0:T(8,128)(2,1)S(1)} collective-permute-done((bf16[16,2176]{1,0:T(8,128)(2,1)S(1)}, bf16[16,2176]{1,0:T(8,128)(2,1)S(1)}, u32[]{:S(2)}, u32[]{:S(2)}) %collective-permute-start.13) | collective-permute-done | bytes 69664 | tf_op jit(solution)/shard_map/ppermute | solution.py:545
  40.0 0.1 core_sum.1.mine
  40.1 1.9 %collective-permute-start.14 = (bf16[16,2176]{1,0:T(8,128)(2,1)S(1)}, bf16[16,2176]{1,0:T(8,128)(2,1)S(1)}, u32[]{:S(2)}, u32[]{:S(2)}) collective-permute-start(bf16[16,2176]{1,0:T(8,128)(2,1)S(1)} %core_sum.1.mine), channel_id=1, source_target_pairs={{0,3},{1,2},{2,1},{3,0},{4,7},{5,6},{6,5},{7,4},{8,11},{9,10},{10,... | collective-permute-start | bytes 208904 | tf_op jit(solution)/shard_map/ppermute | solution.py:545
  42.0 2.4 %collective-permute-done.14.theirs = bf16[16,2176]{1,0:T(8,128)(2,1)S(1)} collective-permute-done((bf16[16,2176]{1,0:T(8,128)(2,1)S(1)}, bf16[16,2176]{1,0:T(8,128)(2,1)S(1)}, u32[]{:S(2)}, u32[]{:S(2)}) %collective-permute-start.14) | collective-permute-done | bytes 69664 | tf_op jit(solution)/shard_map/ppermute | solution.py:545
  44.4 0.4 down.1
  44.8 8.4 %all_to_all.5.parts = bf16[8,2,768]{2,1,0:T(2,128)(2,1)S(1)} all-to-all(bf16[8,2,768]{2,1,0:T(2,128)(2,1)S(1)} %down.1), channel_id=1, replica_groups={{28,24,20,16,12,8,4,0},{29,25,21,17,13,9,5,1},{30,26,22,18,14,10,6,2},{..., dimensions={0} | all-to-all | bytes 49152 | tf_op jit(solution)/shard_map/all_to_all | solution.py:660
  53.2 0.6 %final.1 = bf16[2,768]{1,0:T(2,128)(2,1)} custom-call(f32[2,768]{1,0:T(2,128)S(1)} %get-tuple-element.21.own, bf16[8,2,768]{2,1,0:T(2,128)(2,1)S(1)} %all_to_all.5.parts), custom_call_target="tpu_custom_call" | custom-call | bytes 30720 | tf_op jit(solution)/shard_map/final/pallas_call | solution.py:217
  (13 shorter events, 0.0 us)
Async XLA Ops:
  0.0 15.2 %copy-start.1 = (bf16[5,256,768]{2,1,0:T(8,128)(2,1)S(1)}, bf16[5,256,768]{2,1,0:T(8,128)(2,1)}, u32[]{:S(2)}) copy-start(bf16[5,256,768]{2,1,0:T(8,128)(2,1)} %values.1) | copy-start | bytes 5898244
  0.0 15.2 %copy-start = (bf16[5,256,768]{2,1,0:T(8,128)(2,1)S(1)}, bf16[5,256,768]{2,1,0:T(8,128)(2,1)}, u32[]{:S(2)}) copy-start(bf16[5,256,768]{2,1,0:T(8,128)(2,1)} %keys.1) | copy-start | bytes 5898244
  1.6 4.9 %collective-permute-start = (bf16[2,1664]{1,0:T(2,128)(2,1)}, bf16[2,1664]{1,0:T(2,128)(2,1)S(1)}, u32[]{:S(2)}, u32[]{:S(2)}) collective-permute-start(bf16[2,1664]{1,0:T(2,128)(2,1)} %get-tuple-element.14.packed), channel_id=1, source_target_pairs={{0,4},{4,0},{8,12},{12,8},{16,20},{20,16},{24,28},{28,24},{1,5},{5... | collective-permute-start | bytes 19976 | tf_op jit(solution)/shard_map/ppermute | solution.py:545
  4.7 0.7 %copy-start.6 = (bf16[2,1664]{1,0:T(2,128)(2,1)S(1)}, bf16[2,1664]{1,0:T(2,128)(2,1)}, u32[]{:S(2)}) copy-start(bf16[2,1664]{1,0:T(2,128)(2,1)} %get-tuple-element.14.packed) | copy-start | bytes 19972
  5.4 0.7 %copy-start.7 = (bf16[2,1536]{1,0:T(2,128)(2,1)S(1)}, bf16[2,1536]{1,0:T(2,128)(2,1)}, u32[]{:S(2)}) copy-start(bf16[2,1536]{1,0:T(2,128)(2,1)} %get-tuple-element.15.new) | copy-start | bytes 18436
  6.5 5.8 %collective-permute-start.3 = (bf16[2,2,1664]{2,1,0:T(2,128)(2,1)S(1)}, bf16[2,2,1664]{2,1,0:T(2,128)(2,1)S(1)}, u32[]{:S(2)}, u32[]{:S(2)}) collective-permute-start(bf16[2,2,1664]{2,1,0:T(2,128)(2,1)S(1)} %merge.2.a0), channel_id=1, source_target_pairs={{0,24},{4,28},{8,16},{12,20},{16,8},{20,12},{24,0},{28,4},{1,25},{... | collective-permute-start | bytes 39944 | tf_op jit(solution)/shard_map/ppermute | solution.py:545
  10.6 4.6 %collective-permute-start.2 = (bf16[2,2,1664]{2,1,0:T(2,128)(2,1)S(1)}, bf16[2,2,1664]{2,1,0:T(2,128)(2,1)S(1)}, u32[]{:S(2)}, u32[]{:S(2)}) collective-permute-start(bf16[2,2,1664]{2,1,0:T(2,128)(2,1)S(1)} %merge.2.a0), channel_id=1, source_target_pairs={{0,16},{4,20},{8,24},{12,28},{16,0},{20,4},{24,8},{28,12},{1,17},{... | collective-permute-start | bytes 39944 | tf_op jit(solution)/shard_map/ppermute | solution.py:545
  10.6 4.6 %collective-permute-start.1 = (bf16[2,2,1664]{2,1,0:T(2,128)(2,1)S(1)}, bf16[2,2,1664]{2,1,0:T(2,128)(2,1)S(1)}, u32[]{:S(2)}, u32[]{:S(2)}) collective-permute-start(bf16[2,2,1664]{2,1,0:T(2,128)(2,1)S(1)} %merge.2.a0), channel_id=1, source_target_pairs={{0,8},{4,12},{8,0},{12,4},{16,24},{20,28},{24,16},{28,20},{1,9},{5... | collective-permute-start | bytes 39944 | tf_op jit(solution)/shard_map/ppermute | solution.py:545
  15.2 12.0 %copy-start.5 = (bf16[768,384]{1,0:T(8,128)(2,1)S(1)}, bf16[768,384]{1,0:T(8,128)(2,1)}, u32[]{:S(2)}) copy-start(bf16[768,384]{1,0:T(8,128)(2,1)} %weight.2) | copy-start | bytes 1769476
  15.2 20.8 %copy-start.8 = (bf16[768]{0:T(1024)(128)(2,1)S(1)}, bf16[768]{0:T(1024)(128)(2,1)}, u32[]{:S(2)}) copy-start(bf16[768]{0:T(1024)(128)(2,1)} %param.22) | copy-start | bytes 4612
  15.3 23.0 %copy-start.3 = (bf16[768,1024]{1,0:T(8,128)(2,1)S(1)}, bf16[768,1024]{1,0:T(8,128)(2,1)}, u32[]{:S(2)}) copy-start(bf16[768,1024]{1,0:T(8,128)(2,1)} %gate.1) | copy-start | bytes 4718596
  15.3 23.0 %copy-start.4 = (bf16[768,1024]{1,0:T(8,128)(2,1)S(1)}, bf16[768,1024]{1,0:T(8,128)(2,1)}, u32[]{:S(2)}) copy-start(bf16[768,1024]{1,0:T(8,128)(2,1)} %up.1) | copy-start | bytes 4718596
  17.0 3.8 %collective-permute-start.4 = (bf16[8,768]{1,0:T(8,128)(2,1)S(1)}, bf16[8,768]{1,0:T(8,128)(2,1)S(1)}, u32[]{:S(2)}, u32[]{:S(2)}) collective-permute-start(bf16[8,768]{1,0:T(8,128)(2,1)S(1)} %get-tuple-element.18.mine), channel_id=1, source_target_pairs={{0,4},{4,0},{8,12},{12,8},{16,20},{20,16},{24,28},{28,24},{1,5},{5... | collective-permute-start | bytes 36872 | tf_op jit(solution)/shard_map/ppermute | solution.py:545
  20.7 5.6 %collective-permute-start.7 = (bf16[2,8,768]{2,1,0:T(8,128)(2,1)S(1)}, bf16[2,8,768]{2,1,0:T(8,128)(2,1)S(1)}, u32[]{:S(2)}, u32[]{:S(2)}) collective-permute-start(bf16[2,8,768]{2,1,0:T(8,128)(2,1)S(1)} %merge.3.b0), channel_id=1, source_target_pairs={{0,24},{4,28},{8,16},{12,20},{16,8},{20,12},{24,0},{28,4},{1,25},{... | collective-permute-start | bytes 73736 | tf_op jit(solution)/shard_map/ppermute | solution.py:545
  22.2 4.7 %collective-permute-start.6 = (bf16[2,8,768]{2,1,0:T(8,128)(2,1)S(1)}, bf16[2,8,768]{2,1,0:T(8,128)(2,1)S(1)}, u32[]{:S(2)}, u32[]{:S(2)}) collective-permute-start(bf16[2,8,768]{2,1,0:T(8,128)(2,1)S(1)} %merge.3.b0), channel_id=1, source_target_pairs={{0,16},{4,20},{8,24},{12,28},{16,0},{20,4},{24,8},{28,12},{1,17},{... | collective-permute-start | bytes 73736 | tf_op jit(solution)/shard_map/ppermute | solution.py:545
  22.8 4.4 %collective-permute-start.5 = (bf16[2,8,768]{2,1,0:T(8,128)(2,1)S(1)}, bf16[2,8,768]{2,1,0:T(8,128)(2,1)S(1)}, u32[]{:S(2)}, u32[]{:S(2)}) collective-permute-start(bf16[2,8,768]{2,1,0:T(8,128)(2,1)S(1)} %merge.3.b0), channel_id=1, source_target_pairs={{0,8},{4,12},{8,0},{12,4},{16,24},{20,28},{24,16},{28,20},{1,9},{5... | collective-permute-start | bytes 73736 | tf_op jit(solution)/shard_map/ppermute | solution.py:545
  27.9 3.3 %collective-permute-start.10 = (bf16[16,384]{1,0:T(8,128)(2,1)S(1)}, bf16[16,384]{1,0:T(8,128)(2,1)S(1)}, u32[]{:S(2)}, u32[]{:S(2)}) collective-permute-start(bf16[16,384]{1,0:T(8,128)(2,1)S(1)} %combine.1.p0), channel_id=1, source_target_pairs={{0,3},{1,2},{2,1},{3,0},{4,7},{5,6},{6,5},{7,4},{8,11},{9,10},{10,... | collective-permute-start | bytes 36872 | tf_op jit(solution)/shard_map/ppermute | solution.py:545
  28.0 3.8 %collective-permute-start.9 = (bf16[16,384]{1,0:T(8,128)(2,1)S(1)}, bf16[16,384]{1,0:T(8,128)(2,1)S(1)}, u32[]{:S(2)}, u32[]{:S(2)}) collective-permute-start(bf16[16,384]{1,0:T(8,128)(2,1)S(1)} %combine.1.p0), channel_id=1, source_target_pairs={{0,2},{1,3},{2,0},{3,1},{4,6},{5,7},{6,4},{7,5},{8,10},{9,11},{10,... | collective-permute-start | bytes 36872 | tf_op jit(solution)/shard_map/ppermute | solution.py:545
  29.5 2.2 %collective-permute-start.8 = (bf16[16,384]{1,0:T(8,128)(2,1)S(1)}, bf16[16,384]{1,0:T(8,128)(2,1)S(1)}, u32[]{:S(2)}, u32[]{:S(2)}) collective-permute-start(bf16[16,384]{1,0:T(8,128)(2,1)S(1)} %combine.1.p0), channel_id=1, source_target_pairs={{0,1},{1,0},{2,3},{3,2},{4,5},{5,4},{6,7},{7,6},{8,9},{9,8},{10,11... | collective-permute-start | bytes 36872 | tf_op jit(solution)/shard_map/ppermute | solution.py:545
  31.7 4.8 %collective-permute-start.12 = (bf16[16,384]{1,0:T(8,128)(2,1)S(1)}, bf16[16,384]{1,0:T(8,128)(2,1)S(1)}, u32[]{:S(2)}, u32[]{:S(2)}) collective-permute-start(bf16[16,384]{1,0:T(8,128)(2,1)S(1)} %head_sum.1), channel_id=1, source_target_pairs={{1,28},{5,24},{0,20},{4,16},{3,12},{7,8},{2,4},{6,0},{9,29},{13,25... | collective-permute-start | bytes 36872 | tf_op jit(solution)/shard_map/ppermute | solution.py:634
  34.5 3.7 %collective-permute-start.11 = (bf16[16,384]{1,0:T(8,128)(2,1)S(1)}, bf16[16,384]{1,0:T(8,128)(2,1)S(1)}, u32[]{:S(2)}, u32[]{:S(2)}) collective-permute-start(bf16[16,384]{1,0:T(8,128)(2,1)S(1)} %head_sum.1), channel_id=1, source_target_pairs={{1,24},{5,28},{0,16},{4,20},{3,8},{7,12},{2,0},{6,4},{9,25},{13,29... | collective-permute-start | bytes 36872 | tf_op jit(solution)/shard_map/ppermute | solution.py:634
  38.2 6.1 %copy-start.2 = (bf16[1024,768]{1,0:T(8,128)(2,1)S(1)}, bf16[1024,768]{1,0:T(8,128)(2,1)}, u32[]{:S(2)}) copy-start(bf16[1024,768]{1,0:T(8,128)(2,1)} %weight.3) | copy-start | bytes 4718596
  38.8 1.3 %collective-permute-start.13 = (bf16[16,2176]{1,0:T(8,128)(2,1)S(1)}, bf16[16,2176]{1,0:T(8,128)(2,1)S(1)}, u32[]{:S(2)}, u32[]{:S(2)}) collective-permute-start(bf16[16,2176]{1,0:T(8,128)(2,1)S(1)} %get-tuple-element.22.mine), channel_id=1, source_target_pairs={{0,1},{1,0},{2,3},{3,2},{4,5},{5,4},{6,7},{7,6},{8,9},{9,8},{10,11... | collective-permute-start | bytes 208904 | tf_op jit(solution)/shard_map/ppermute | solution.py:545
  40.1 4.3 %collective-permute-start.14 = (bf16[16,2176]{1,0:T(8,128)(2,1)S(1)}, bf16[16,2176]{1,0:T(8,128)(2,1)S(1)}, u32[]{:S(2)}, u32[]{:S(2)}) collective-permute-start(bf16[16,2176]{1,0:T(8,128)(2,1)S(1)} %core_sum.1.mine), channel_id=1, source_target_pairs={{0,3},{1,2},{2,1},{3,0},{4,7},{5,6},{6,5},{7,4},{8,11},{9,10},{10,... | collective-permute-start | bytes 208904 | tf_op jit(solution)/shard_map/ppermute | solution.py:545

commit v18 on v16

--- a/solution.py
+++ b/solution.py
@@ -629,7 +629,7 @@
         functools.partial(down_kernel, width * mlp),
         "down",
         [((pool, rows, width), BF16)],
-        [sums] + [flip(sums, "mlp", step) for step in (1, 2, 3)] + [down_weight],
+        [sums] + [flip(sums, "mlp", step) for step in (1, 3, 2)] + [down_weight],
         [pltpu.VMEM((requests, width), F32)],
     )
     backwards = list(range(pool))[::-1]

time: 54 us -> 53.3 us (0.987)
  waiting for transfers between devices: 16.8 us -> 16 us
    ppermute x14, waiting for transfers between devices: 14.6 us -> 13.8 us  [flip(): lax.ppermute(values, axis, [(index, index ^ step) for index in range(size)])]
where the time goes in v18:
time: 53.3 us; the launch traced here: 53.1 us
  starting transfers between devices  22 us (41%)
  waiting for transfers between devices  16 us (30%)
  blocking collectives  8.36 us (16%)
  Pallas kernels  5.17 us (10%)
  local copies, waits for them, and re-layouts  1.46 us (3%)
    ppermute x14, starting transfers between devices, flip(): lax.ppermute(values, axis, [(index, index ^ step) for index in range(size)])  17.7 us
    ppermute x14, waiting for transfers between devices, flip(): lax.ppermute(values, axis, [(index, index ^ step) for index in range(size)])  13.8 us
    all_to_all x1, blocking collectives, per_device_small(): lax.all_to_all(down, 'pool', 0, 0, axis_index_groups=[backwards])  8.36 us
    pallas_call x10, Pallas kernels, call(): pl.pallas_call(kernel, out_shape=[jax.ShapeDtypeStruct(shape, dtype) for...  5.17 us
    ppermute x2, starting transfers between devices, per_device_small(): pieces.append(lax.ppermute(head_sum, ('pool', 'mlp'), route))  4.27 us
    ppermute x2, waiting for transfers between devices, per_device_small(): pieces.append(lax.ppermute(head_sum, ('pool', 'mlp'), route))  2.2 us
    unnamed x18, local copies, waits for them, and re-layouts  1.45 us
  transfers between devices with their start and end apart: 16, of which 13 were waited for; matrix products, arithmetic and copies ran while one was open for 0% of the time, Pallas kernels for 0%

profile of v18, /device:TPU:0, one launch (start us, length us, event | category | flops | bytes accessed | tf_op | source)
XLA Modules:
  0.0 53.1 jit_solution(9284682872422852767)
XLA Ops:
  0.0 1.6 %rotary.1 = (bf16[2,1664]{1,0:T(2,128)(2,1)}, bf16[2,1536]{1,0:T(2,128)(2,1)}) custom-call(s32[2,8]{1,0:T(2,128)} %refs_0_.1, s32[2]{0:T(128)} %refs_1_.1, bf16[2,768]{1,0:T(2,128)(2,1)} %refs_2_.1, bf16[2,768]{1,0:T(2,128)(2,1)} %refs_3_.1, bf16[2,768]{1,0:T(2,128)(2,1)} %refs_4_.1, bf16[2,768]{1,0:T(2,128)(2,1)} %refs_5_.1, bf16[5,256,768]{2,1,0:T(8,128)(2,1)} %keys.1, ...), custom_call_target="tpu_custom_call" | custom-call | bytes 3944520 | tf_op jit(solution)/shard_map/rotary/pallas_call | solution.py:217
  1.6 3.0 %collective-permute-start = (bf16[2,1664]{1,0:T(2,128)(2,1)}, bf16[2,1664]{1,0:T(2,128)(2,1)S(1)}, u32[]{:S(2)}, u32[]{:S(2)}) collective-permute-start(bf16[2,1664]{1,0:T(2,128)(2,1)} %get-tuple-element.14.packed), channel_id=1, source_target_pairs={{0,4},{4,0},{8,12},{12,8},{16,20},{20,16},{24,28},{28,24},{1,5},{5... | collective-permute-start | bytes 19976 | tf_op jit(solution)/shard_map/ppermute | solution.py:531
  4.7 0.7 %copy-done.6 = bf16[2,1664]{1,0:T(2,128)(2,1)S(1)} copy-done((bf16[2,1664]{1,0:T(2,128)(2,1)S(1)}, bf16[2,1664]{1,0:T(2,128)(2,1)}, u32[]{:S(2)}) %copy-start.6) | copy-done | bytes 6680
  5.4 0.7 %copy-done.7 = bf16[2,1536]{1,0:T(2,128)(2,1)S(1)} copy-done((bf16[2,1536]{1,0:T(2,128)(2,1)S(1)}, bf16[2,1536]{1,0:T(2,128)(2,1)}, u32[]{:S(2)}) %copy-start.7) | copy-done | bytes 6168
  6.1 0.1 carry.1
  6.2 0.3 collective-permute-done.theirs
  6.5 4.1 %collective-permute-start.3 = (bf16[2,2,1664]{2,1,0:T(2,128)(2,1)S(1)}, bf16[2,2,1664]{2,1,0:T(2,128)(2,1)S(1)}, u32[]{:S(2)}, u32[]{:S(2)}) collective-permute-start(bf16[2,2,1664]{2,1,0:T(2,128)(2,1)S(1)} %merge.2.a0), channel_id=1, source_target_pairs={{0,24},{4,28},{8,16},{12,20},{16,8},{20,12},{24,0},{28,4},{1,25},{... | collective-permute-start | bytes 39944 | tf_op jit(solution)/shard_map/ppermute | solution.py:531
  10.6 0.0 collective-permute-start.2
  10.6 0.6 %collective-permute-start.1 = (bf16[2,2,1664]{2,1,0:T(2,128)(2,1)S(1)}, bf16[2,2,1664]{2,1,0:T(2,128)(2,1)S(1)}, u32[]{:S(2)}, u32[]{:S(2)}) collective-permute-start(bf16[2,2,1664]{2,1,0:T(2,128)(2,1)S(1)} %merge.2.a0), channel_id=1, source_target_pairs={{0,8},{4,12},{8,0},{12,4},{16,24},{20,28},{24,16},{28,20},{1,9},{5... | collective-permute-start | bytes 39944 | tf_op jit(solution)/shard_map/ppermute | solution.py:531
  11.2 1.1 %collective-permute-done.3.a3 = bf16[2,2,1664]{2,1,0:T(2,128)(2,1)S(1)} collective-permute-done((bf16[2,2,1664]{2,1,0:T(2,128)(2,1)S(1)}, bf16[2,2,1664]{2,1,0:T(2,128)(2,1)S(1)}, u32[]{:S(2)}, u32[]{:S(2)}) %collective-permute-start.3) | collective-permute-done | bytes 13344 | tf_op jit(solution)/shard_map/ppermute | solution.py:531
  12.3 2.9 %collective-permute-done.2.a2 = bf16[2,2,1664]{2,1,0:T(2,128)(2,1)S(1)} collective-permute-done((bf16[2,2,1664]{2,1,0:T(2,128)(2,1)S(1)}, bf16[2,2,1664]{2,1,0:T(2,128)(2,1)S(1)}, u32[]{:S(2)}, u32[]{:S(2)}) %collective-permute-start.2) | collective-permute-done | bytes 13344 | tf_op jit(solution)/shard_map/ppermute | solution.py:531
  15.2 0.0 collective-permute-done.1.a1
  15.2 0.0 copy-done.1
  15.2 0.0 copy-done
  15.2 0.0 copy-start.5
  15.2 0.0 copy-start.8
  15.3 0.0 copy-start.3
  15.3 0.0 copy-start.4
  15.3 1.1 %attend.1 = (bf16[8,768]{1,0:T(8,128)(2,1)S(1)}, f32[16,768]{1,0:T(8,128)S(1)}, f32[16,128]{1,0:T(8,128)S(1)}) custom-call(bf16[2,2,1664]{2,1,0:T(2,128)(2,1)S(1)} %merge.2.a0, bf16[2,2,1664]{2,1,0:T(2,128)(2,1)S(1)} %collective-permute-done.1.a1, bf16[2,2,1664]{2,1,0:T(2,128)(2,1)S(1)} %collective-permute-done.2.a2, ...), custom_call_target="tpu_custom_call" | custom-call | bytes 4014080 | tf_op jit(solution)/shard_map/attend/pallas_call | solution.py:217
  16.4 1.6 %collective-permute-start.4 = (bf16[8,768]{1,0:T(8,128)(2,1)S(1)}, bf16[8,768]{1,0:T(8,128)(2,1)S(1)}, u32[]{:S(2)}, u32[]{:S(2)}) collective-permute-start(bf16[8,768]{1,0:T(8,128)(2,1)S(1)} %get-tuple-element.18.mine), channel_id=1, source_target_pairs={{0,4},{4,0},{8,12},{12,8},{16,20},{20,16},{24,28},{28,24},{1,5},{5... | collective-permute-start | bytes 36872 | tf_op jit(solution)/shard_map/ppermute | solution.py:531
  18.0 2.2 %collective-permute-done.4.theirs = bf16[8,768]{1,0:T(8,128)(2,1)S(1)} collective-permute-done((bf16[8,768]{1,0:T(8,128)(2,1)S(1)}, bf16[8,768]{1,0:T(8,128)(2,1)S(1)}, u32[]{:S(2)}, u32[]{:S(2)}) %collective-permute-start.4) | collective-permute-done | bytes 12320 | tf_op jit(solution)/shard_map/ppermute | solution.py:531
  20.2 1.4 %collective-permute-start.7 = (bf16[2,8,768]{2,1,0:T(8,128)(2,1)S(1)}, bf16[2,8,768]{2,1,0:T(8,128)(2,1)S(1)}, u32[]{:S(2)}, u32[]{:S(2)}) collective-permute-start(bf16[2,8,768]{2,1,0:T(8,128)(2,1)S(1)} %merge.3.b0), channel_id=1, source_target_pairs={{0,24},{4,28},{8,16},{12,20},{16,8},{20,12},{24,0},{28,4},{1,25},{... | collective-permute-start | bytes 73736 | tf_op jit(solution)/shard_map/ppermute | solution.py:531
  21.6 0.6 %collective-permute-start.6 = (bf16[2,8,768]{2,1,0:T(8,128)(2,1)S(1)}, bf16[2,8,768]{2,1,0:T(8,128)(2,1)S(1)}, u32[]{:S(2)}, u32[]{:S(2)}) collective-permute-start(bf16[2,8,768]{2,1,0:T(8,128)(2,1)S(1)} %merge.3.b0), channel_id=1, source_target_pairs={{0,16},{4,20},{8,24},{12,28},{16,0},{20,4},{24,8},{28,12},{1,17},{... | collective-permute-start | bytes 73736 | tf_op jit(solution)/shard_map/ppermute | solution.py:531
  22.3 2.3 %collective-permute-start.5 = (bf16[2,8,768]{2,1,0:T(8,128)(2,1)S(1)}, bf16[2,8,768]{2,1,0:T(8,128)(2,1)S(1)}, u32[]{:S(2)}, u32[]{:S(2)}) collective-permute-start(bf16[2,8,768]{2,1,0:T(8,128)(2,1)S(1)} %merge.3.b0), channel_id=1, source_target_pairs={{0,8},{4,12},{8,0},{12,4},{16,24},{20,28},{24,16},{28,20},{1,9},{5... | collective-permute-start | bytes 73736 | tf_op jit(solution)/shard_map/ppermute | solution.py:531
  24.6 1.2 %collective-permute-done.7.b3 = bf16[2,8,768]{2,1,0:T(8,128)(2,1)S(1)} collective-permute-done((bf16[2,8,768]{2,1,0:T(8,128)(2,1)S(1)}, bf16[2,8,768]{2,1,0:T(8,128)(2,1)S(1)}, u32[]{:S(2)}, u32[]{:S(2)}) %collective-permute-start.7) | collective-permute-done | bytes 24608 | tf_op jit(solution)/shard_map/ppermute | solution.py:531
  25.8 0.6 %collective-permute-done.6.b2 = bf16[2,8,768]{2,1,0:T(8,128)(2,1)S(1)} collective-permute-done((bf16[2,8,768]{2,1,0:T(8,128)(2,1)S(1)}, bf16[2,8,768]{2,1,0:T(8,128)(2,1)S(1)}, u32[]{:S(2)}, u32[]{:S(2)}) %collective-permute-start.6) | collective-permute-done | bytes 24608 | tf_op jit(solution)/shard_map/ppermute | solution.py:531
  26.4 0.2 collective-permute-done.5.b1
  26.6 0.7 %combine.1.p0 = bf16[16,384]{1,0:T(8,128)(2,1)S(1)} custom-call(bf16[2,8,768]{2,1,0:T(8,128)(2,1)S(1)} %merge.3.b0, bf16[2,8,768]{2,1,0:T(8,128)(2,1)S(1)} %collective-permute-done.5.b1, bf16[2,8,768]{2,1,0:T(8,128)(2,1)S(1)} %collective-permute-done.6.b2, bf16[2,8,768]{2,1,0:T(8,128)(2,1)S(1)} %collective-permute-done.7.b3, ...), custom_call_target="tpu_custom_call" | custom-call | bytes 696320 | tf_op jit(solution)/shard_map/combine/pallas_call | solution.py:217
  27.4 0.1 collective-permute-start.10
  27.4 1.6 %collective-permute-start.9 = (bf16[16,384]{1,0:T(8,128)(2,1)S(1)}, bf16[16,384]{1,0:T(8,128)(2,1)S(1)}, u32[]{:S(2)}, u32[]{:S(2)}) collective-permute-start(bf16[16,384]{1,0:T(8,128)(2,1)S(1)} %combine.1.p0), channel_id=1, source_target_pairs={{0,2},{1,3},{2,0},{3,1},{4,6},{5,7},{6,4},{7,5},{8,10},{9,11},{10,... | collective-permute-start | bytes 36872 | tf_op jit(solution)/shard_map/ppermute | solution.py:531
  29.0 0.3 collective-permute-start.8
  29.3 1.3 %collective-permute-done.10.p3 = bf16[16,384]{1,0:T(8,128)(2,1)S(1)} collective-permute-done((bf16[16,384]{1,0:T(8,128)(2,1)S(1)}, bf16[16,384]{1,0:T(8,128)(2,1)S(1)}, u32[]{:S(2)}, u32[]{:S(2)}) %collective-permute-start.10) | collective-permute-done | bytes 12320 | tf_op jit(solution)/shard_map/ppermute | solution.py:531
  30.6 0.6 %collective-permute-done.9.p2 = bf16[16,384]{1,0:T(8,128)(2,1)S(1)} collective-permute-done((bf16[16,384]{1,0:T(8,128)(2,1)S(1)}, bf16[16,384]{1,0:T(8,128)(2,1)S(1)}, u32[]{:S(2)}, u32[]{:S(2)}) %collective-permute-start.9) | collective-permute-done | bytes 12320 | tf_op jit(solution)/shard_map/ppermute | solution.py:531
  31.2 0.0 collective-permute-done.8.p1
  31.2 2.8 %collective-permute-start.12 = (bf16[16,384]{1,0:T(8,128)(2,1)S(1)}, bf16[16,384]{1,0:T(8,128)(2,1)S(1)}, u32[]{:S(2)}, u32[]{:S(2)}) collective-permute-start(bf16[16,384]{1,0:T(8,128)(2,1)S(1)} %head_sum.1), channel_id=1, source_target_pairs={{1,28},{5,24},{0,20},{4,16},{3,12},{7,8},{2,4},{6,0},{9,29},{13,25... | collective-permute-start | bytes 36872 | tf_op jit(solution)/shard_map/ppermute | solution.py:620
  34.0 1.5 %collective-permute-start.11 = (bf16[16,384]{1,0:T(8,128)(2,1)S(1)}, bf16[16,384]{1,0:T(8,128)(2,1)S(1)}, u32[]{:S(2)}, u32[]{:S(2)}) collective-permute-start(bf16[16,384]{1,0:T(8,128)(2,1)S(1)} %head_sum.1), channel_id=1, source_target_pairs={{1,24},{5,28},{0,16},{4,20},{3,8},{7,12},{2,0},{6,4},{9,25},{13,29... | collective-permute-start | bytes 36872 | tf_op jit(solution)/shard_map/ppermute | solution.py:620
  35.5 0.5 collective-permute-done.12.flip
  36.0 1.7 %collective-permute-done.11.same = bf16[16,384]{1,0:T(8,128)(2,1)S(1)} collective-permute-done((bf16[16,384]{1,0:T(8,128)(2,1)S(1)}, bf16[16,384]{1,0:T(8,128)(2,1)S(1)}, u32[]{:S(2)}, u32[]{:S(2)}) %collective-permute-start.11) | collective-permute-done | bytes 12320 | tf_op jit(solution)/shard_map/ppermute | solution.py:620
  37.7 0.5 gate_up.1
  38.2 0.6 %collective-permute-start.15 = (bf16[16,2176]{1,0:T(8,128)(2,1)S(1)}, bf16[16,2176]{1,0:T(8,128)(2,1)S(1)}, u32[]{:S(2)}, u32[]{:S(2)}) collective-permute-start(bf16[16,2176]{1,0:T(8,128)(2,1)S(1)} %get-tuple-element.22.p0), channel_id=1, source_target_pairs={{0,2},{1,3},{2,0},{3,1},{4,6},{5,7},{6,4},{7,5},{8,10},{9,11},{10,... | collective-permute-start | bytes 208904 | tf_op jit(solution)/shard_map/ppermute | solution.py:531
  38.8 1.3 %collective-permute-start.14 = (bf16[16,2176]{1,0:T(8,128)(2,1)S(1)}, bf16[16,2176]{1,0:T(8,128)(2,1)S(1)}, u32[]{:S(2)}, u32[]{:S(2)}) collective-permute-start(bf16[16,2176]{1,0:T(8,128)(2,1)S(1)} %get-tuple-element.22.p0), channel_id=1, source_target_pairs={{0,3},{1,2},{2,1},{3,0},{4,7},{5,6},{6,5},{7,4},{8,11},{9,10},{10,... | collective-permute-start | bytes 208904 | tf_op jit(solution)/shard_map/ppermute | solution.py:531
  40.1 0.2 collective-permute-start.13
  40.3 2.8 %collective-permute-done.15.p3 = bf16[16,2176]{1,0:T(8,128)(2,1)S(1)} collective-permute-done((bf16[16,2176]{1,0:T(8,128)(2,1)S(1)}, bf16[16,2176]{1,0:T(8,128)(2,1)S(1)}, u32[]{:S(2)}, u32[]{:S(2)}) %collective-permute-start.15) | collective-permute-done | bytes 69664 | tf_op jit(solution)/shard_map/ppermute | solution.py:531
  43.2 0.5 collective-permute-done.14.p2
  43.7 0.0 collective-permute-done.13.p1
  43.7 0.4 down.1
  44.1 8.4 %all_to_all.5.parts = bf16[8,2,768]{2,1,0:T(2,128)(2,1)S(1)} all-to-all(bf16[8,2,768]{2,1,0:T(2,128)(2,1)S(1)} %down.1), channel_id=1, replica_groups={{28,24,20,16,12,8,4,0},{29,25,21,17,13,9,5,1},{30,26,22,18,14,10,6,2},{..., dimensions={0} | all-to-all | bytes 49152 | tf_op jit(solution)/shard_map/all_to_all | solution.py:640
  52.5 0.6 %final.1 = bf16[2,768]{1,0:T(2,128)(2,1)} custom-call(f32[2,768]{1,0:T(2,128)S(1)} %get-tuple-element.21.own, bf16[8,2,768]{2,1,0:T(2,128)(2,1)S(1)} %all_to_all.5.parts), custom_call_target="tpu_custom_call" | custom-call | bytes 30720 | tf_op jit(solution)/shard_map/final/pallas_call | solution.py:217
  (14 shorter events, 0.0 us)
Async XLA Ops:
  0.0 15.2 %copy-start.1 = (bf16[5,256,768]{2,1,0:T(8,128)(2,1)S(1)}, bf16[5,256,768]{2,1,0:T(8,128)(2,1)}, u32[]{:S(2)}) copy-start(bf16[5,256,768]{2,1,0:T(8,128)(2,1)} %values.1) | copy-start | bytes 5898244
  0.0 15.2 %copy-start = (bf16[5,256,768]{2,1,0:T(8,128)(2,1)S(1)}, bf16[5,256,768]{2,1,0:T(8,128)(2,1)}, u32[]{:S(2)}) copy-start(bf16[5,256,768]{2,1,0:T(8,128)(2,1)} %keys.1) | copy-start | bytes 5898244
  1.6 4.9 %collective-permute-start = (bf16[2,1664]{1,0:T(2,128)(2,1)}, bf16[2,1664]{1,0:T(2,128)(2,1)S(1)}, u32[]{:S(2)}, u32[]{:S(2)}) collective-permute-start(bf16[2,1664]{1,0:T(2,128)(2,1)} %get-tuple-element.14.packed), channel_id=1, source_target_pairs={{0,4},{4,0},{8,12},{12,8},{16,20},{20,16},{24,28},{28,24},{1,5},{5... | collective-permute-start | bytes 19976 | tf_op jit(solution)/shard_map/ppermute | solution.py:531
  4.7 0.7 %copy-start.6 = (bf16[2,1664]{1,0:T(2,128)(2,1)S(1)}, bf16[2,1664]{1,0:T(2,128)(2,1)}, u32[]{:S(2)}) copy-start(bf16[2,1664]{1,0:T(2,128)(2,1)} %get-tuple-element.14.packed) | copy-start | bytes 19972
  5.4 0.7 %copy-start.7 = (bf16[2,1536]{1,0:T(2,128)(2,1)S(1)}, bf16[2,1536]{1,0:T(2,128)(2,1)}, u32[]{:S(2)}) copy-start(bf16[2,1536]{1,0:T(2,128)(2,1)} %get-tuple-element.15.new) | copy-start | bytes 18436
  6.5 5.8 %collective-permute-start.3 = (bf16[2,2,1664]{2,1,0:T(2,128)(2,1)S(1)}, bf16[2,2,1664]{2,1,0:T(2,128)(2,1)S(1)}, u32[]{:S(2)}, u32[]{:S(2)}) collective-permute-start(bf16[2,2,1664]{2,1,0:T(2,128)(2,1)S(1)} %merge.2.a0), channel_id=1, source_target_pairs={{0,24},{4,28},{8,16},{12,20},{16,8},{20,12},{24,0},{28,4},{1,25},{... | collective-permute-start | bytes 39944 | tf_op jit(solution)/shard_map/ppermute | solution.py:531
  10.6 4.6 %collective-permute-start.2 = (bf16[2,2,1664]{2,1,0:T(2,128)(2,1)S(1)}, bf16[2,2,1664]{2,1,0:T(2,128)(2,1)S(1)}, u32[]{:S(2)}, u32[]{:S(2)}) collective-permute-start(bf16[2,2,1664]{2,1,0:T(2,128)(2,1)S(1)} %merge.2.a0), channel_id=1, source_target_pairs={{0,16},{4,20},{8,24},{12,28},{16,0},{20,4},{24,8},{28,12},{1,17},{... | collective-permute-start | bytes 39944 | tf_op jit(solution)/shard_map/ppermute | solution.py:531
  10.6 4.6 %collective-permute-start.1 = (bf16[2,2,1664]{2,1,0:T(2,128)(2,1)S(1)}, bf16[2,2,1664]{2,1,0:T(2,128)(2,1)S(1)}, u32[]{:S(2)}, u32[]{:S(2)}) collective-permute-start(bf16[2,2,1664]{2,1,0:T(2,128)(2,1)S(1)} %merge.2.a0), channel_id=1, source_target_pairs={{0,8},{4,12},{8,0},{12,4},{16,24},{20,28},{24,16},{28,20},{1,9},{5... | collective-permute-start | bytes 39944 | tf_op jit(solution)/shard_map/ppermute | solution.py:531
  15.2 11.4 %copy-start.5 = (bf16[768,384]{1,0:T(8,128)(2,1)S(1)}, bf16[768,384]{1,0:T(8,128)(2,1)}, u32[]{:S(2)}) copy-start(bf16[768,384]{1,0:T(8,128)(2,1)} %weight.2) | copy-start | bytes 1769476
  15.2 20.2 %copy-start.8 = (bf16[768]{0:T(1024)(128)(2,1)S(1)}, bf16[768]{0:T(1024)(128)(2,1)}, u32[]{:S(2)}) copy-start(bf16[768]{0:T(1024)(128)(2,1)} %param.22) | copy-start | bytes 4612
  15.3 22.4 %copy-start.3 = (bf16[768,1024]{1,0:T(8,128)(2,1)S(1)}, bf16[768,1024]{1,0:T(8,128)(2,1)}, u32[]{:S(2)}) copy-start(bf16[768,1024]{1,0:T(8,128)(2,1)} %gate.1) | copy-start | bytes 4718596
  15.3 22.4 %copy-start.4 = (bf16[768,1024]{1,0:T(8,128)(2,1)S(1)}, bf16[768,1024]{1,0:T(8,128)(2,1)}, u32[]{:S(2)}) copy-start(bf16[768,1024]{1,0:T(8,128)(2,1)} %up.1) | copy-start | bytes 4718596
  16.4 3.8 %collective-permute-start.4 = (bf16[8,768]{1,0:T(8,128)(2,1)S(1)}, bf16[8,768]{1,0:T(8,128)(2,1)S(1)}, u32[]{:S(2)}, u32[]{:S(2)}) collective-permute-start(bf16[8,768]{1,0:T(8,128)(2,1)S(1)} %get-tuple-element.18.mine), channel_id=1, source_target_pairs={{0,4},{4,0},{8,12},{12,8},{16,20},{20,16},{24,28},{28,24},{1,5},{5... | collective-permute-start | bytes 36872 | tf_op jit(solution)/shard_map/ppermute | solution.py:531
  20.2 5.6 %collective-permute-start.7 = (bf16[2,8,768]{2,1,0:T(8,128)(2,1)S(1)}, bf16[2,8,768]{2,1,0:T(8,128)(2,1)S(1)}, u32[]{:S(2)}, u32[]{:S(2)}) collective-permute-start(bf16[2,8,768]{2,1,0:T(8,128)(2,1)S(1)} %merge.3.b0), channel_id=1, source_target_pairs={{0,24},{4,28},{8,16},{12,20},{16,8},{20,12},{24,0},{28,4},{1,25},{... | collective-permute-start | bytes 73736 | tf_op jit(solution)/shard_map/ppermute | solution.py:531
  21.6 4.7 %collective-permute-start.6 = (bf16[2,8,768]{2,1,0:T(8,128)(2,1)S(1)}, bf16[2,8,768]{2,1,0:T(8,128)(2,1)S(1)}, u32[]{:S(2)}, u32[]{:S(2)}) collective-permute-start(bf16[2,8,768]{2,1,0:T(8,128)(2,1)S(1)} %merge.3.b0), channel_id=1, source_target_pairs={{0,16},{4,20},{8,24},{12,28},{16,0},{20,4},{24,8},{28,12},{1,17},{... | collective-permute-start | bytes 73736 | tf_op jit(solution)/shard_map/ppermute | solution.py:531
  22.3 4.4 %collective-permute-start.5 = (bf16[2,8,768]{2,1,0:T(8,128)(2,1)S(1)}, bf16[2,8,768]{2,1,0:T(8,128)(2,1)S(1)}, u32[]{:S(2)}, u32[]{:S(2)}) collective-permute-start(bf16[2,8,768]{2,1,0:T(8,128)(2,1)S(1)} %merge.3.b0), channel_id=1, source_target_pairs={{0,8},{4,12},{8,0},{12,4},{16,24},{20,28},{24,16},{28,20},{1,9},{5... | collective-permute-start | bytes 73736 | tf_op jit(solution)/shard_map/ppermute | solution.py:531
  27.4 3.2 %collective-permute-start.10 = (bf16[16,384]{1,0:T(8,128)(2,1)S(1)}, bf16[16,384]{1,0:T(8,128)(2,1)S(1)}, u32[]{:S(2)}, u32[]{:S(2)}) collective-permute-start(bf16[16,384]{1,0:T(8,128)(2,1)S(1)} %combine.1.p0), channel_id=1, source_target_pairs={{0,3},{1,2},{2,1},{3,0},{4,7},{5,6},{6,5},{7,4},{8,11},{9,10},{10,... | collective-permute-start | bytes 36872 | tf_op jit(solution)/shard_map/ppermute | solution.py:531
  27.4 3.8 %collective-permute-start.9 = (bf16[16,384]{1,0:T(8,128)(2,1)S(1)}, bf16[16,384]{1,0:T(8,128)(2,1)S(1)}, u32[]{:S(2)}, u32[]{:S(2)}) collective-permute-start(bf16[16,384]{1,0:T(8,128)(2,1)S(1)} %combine.1.p0), channel_id=1, source_target_pairs={{0,2},{1,3},{2,0},{3,1},{4,6},{5,7},{6,4},{7,5},{8,10},{9,11},{10,... | collective-permute-start | bytes 36872 | tf_op jit(solution)/shard_map/ppermute | solution.py:531
  29.0 2.2 %collective-permute-start.8 = (bf16[16,384]{1,0:T(8,128)(2,1)S(1)}, bf16[16,384]{1,0:T(8,128)(2,1)S(1)}, u32[]{:S(2)}, u32[]{:S(2)}) collective-permute-start(bf16[16,384]{1,0:T(8,128)(2,1)S(1)} %combine.1.p0), channel_id=1, source_target_pairs={{0,1},{1,0},{2,3},{3,2},{4,5},{5,4},{6,7},{7,6},{8,9},{9,8},{10,11... | collective-permute-start | bytes 36872 | tf_op jit(solution)/shard_map/ppermute | solution.py:531
  31.2 4.8 %collective-permute-start.12 = (bf16[16,384]{1,0:T(8,128)(2,1)S(1)}, bf16[16,384]{1,0:T(8,128)(2,1)S(1)}, u32[]{:S(2)}, u32[]{:S(2)}) collective-permute-start(bf16[16,384]{1,0:T(8,128)(2,1)S(1)} %head_sum.1), channel_id=1, source_target_pairs={{1,28},{5,24},{0,20},{4,16},{3,12},{7,8},{2,4},{6,0},{9,29},{13,25... | collective-permute-start | bytes 36872 | tf_op jit(solution)/shard_map/ppermute | solution.py:620
  34.0 3.7 %collective-permute-start.11 = (bf16[16,384]{1,0:T(8,128)(2,1)S(1)}, bf16[16,384]{1,0:T(8,128)(2,1)S(1)}, u32[]{:S(2)}, u32[]{:S(2)}) collective-permute-start(bf16[16,384]{1,0:T(8,128)(2,1)S(1)} %head_sum.1), channel_id=1, source_target_pairs={{1,24},{5,28},{0,16},{4,20},{3,8},{7,12},{2,0},{6,4},{9,25},{13,29... | collective-permute-start | bytes 36872 | tf_op jit(solution)/shard_map/ppermute | solution.py:620
  37.7 6.0 %copy-start.2 = (bf16[1024,768]{1,0:T(8,128)(2,1)S(1)}, bf16[1024,768]{1,0:T(8,128)(2,1)}, u32[]{:S(2)}) copy-start(bf16[1024,768]{1,0:T(8,128)(2,1)} %weight.3) | copy-start | bytes 4718596
  38.2 5.0 %collective-permute-start.15 = (bf16[16,2176]{1,0:T(8,128)(2,1)S(1)}, bf16[16,2176]{1,0:T(8,128)(2,1)S(1)}, u32[]{:S(2)}, u32[]{:S(2)}) collective-permute-start(bf16[16,2176]{1,0:T(8,128)(2,1)S(1)} %get-tuple-element.22.p0), channel_id=1, source_target_pairs={{0,2},{1,3},{2,0},{3,1},{4,6},{5,7},{6,4},{7,5},{8,10},{9,11},{10,... | collective-permute-start | bytes 208904 | tf_op jit(solution)/shard_map/ppermute | solution.py:531
  38.8 4.9 %collective-permute-start.14 = (bf16[16,2176]{1,0:T(8,128)(2,1)S(1)}, bf16[16,2176]{1,0:T(8,128)(2,1)S(1)}, u32[]{:S(2)}, u32[]{:S(2)}) collective-permute-start(bf16[16,2176]{1,0:T(8,128)(2,1)S(1)} %get-tuple-element.22.p0), channel_id=1, source_target_pairs={{0,3},{1,2},{2,1},{3,0},{4,7},{5,6},{6,5},{7,4},{8,11},{9,10},{10,... | collective-permute-start | bytes 208904 | tf_op jit(solution)/shard_map/ppermute | solution.py:531
  40.1 3.6 %collective-permute-start.13 = (bf16[16,2176]{1,0:T(8,128)(2,1)S(1)}, bf16[16,2176]{1,0:T(8,128)(2,1)S(1)}, u32[]{:S(2)}, u32[]{:S(2)}) collective-permute-start(bf16[16,2176]{1,0:T(8,128)(2,1)S(1)} %get-tuple-element.22.p0), channel_id=1, source_target_pairs={{0,1},{1,0},{2,3},{3,2},{4,5},{5,4},{6,7},{7,6},{8,9},{9,8},{10,11... | collective-permute-start | bytes 208904 | tf_op jit(solution)/shard_map/ppermute | solution.py:531

commit v19 on v18

--- a/solution.py
+++ b/solution.py
@@ -629,7 +629,7 @@
         functools.partial(down_kernel, width * mlp),
         "down",
         [((pool, rows, width), BF16)],
-        [sums] + [flip(sums, "mlp", step) for step in (1, 3, 2)] + [down_weight],
+        [sums] + [flip(sums, "mlp", step) for step in (3, 1, 2)] + [down_weight],
         [pltpu.VMEM((requests, width), F32)],
     )
     backwards = list(range(pool))[::-1]

time: 53.3 us -> 54.1 us (1.015)
  waiting for transfers between devices: 16 us -> 16.8 us
    ppermute x14, waiting for transfers between devices: 13.8 us -> 14.6 us  [flip(): lax.ppermute(values, axis, [(index, index ^ step) for index in range(size)])]
where the time goes in v19:
time: 54.1 us; the launch traced here: 53.9 us
  starting transfers between devices  22 us (41%)
  waiting for transfers between devices  16.8 us (31%)
  blocking collectives  8.36 us (15%)
  Pallas kernels  5.17 us (10%)
  local copies, waits for them, and re-layouts  1.46 us (3%)
    ppermute x14, starting transfers between devices, flip(): lax.ppermute(values, axis, [(index, index ^ step) for index in range(size)])  17.7 us
    ppermute x14, waiting for transfers between devices, flip(): lax.ppermute(values, axis, [(index, index ^ step) for index in range(size)])  14.6 us
    all_to_all x1, blocking collectives, per_device_small(): lax.all_to_all(down, 'pool', 0, 0, axis_index_groups=[backwards])  8.36 us
    pallas_call x10, Pallas kernels, call(): pl.pallas_call(kernel, out_shape=[jax.ShapeDtypeStruct(shape, dtype) for...  5.17 us
    ppermute x2, starting transfers between devices, per_device_small(): pieces.append(lax.ppermute(head_sum, ('pool', 'mlp'), route))  4.27 us
    ppermute x2, waiting for transfers between devices, per_device_small(): pieces.append(lax.ppermute(head_sum, ('pool', 'mlp'), route))  2.2 us
    unnamed x18, local copies, waits for them, and re-layouts  1.45 us
  transfers between devices with their start and end apart: 16, of which 13 were waited for; matrix products, arithmetic and copies ran while one was open for 0% of the time, Pallas kernels for 0%

profile of v19, /device:TPU:0, one launch (start us, length us, event | category | flops | bytes accessed | tf_op | source)
XLA Modules:
  0.0 53.9 jit_solution(2515560887065524095)
XLA Ops:
  0.0 1.6 %rotary.1 = (bf16[2,1664]{1,0:T(2,128)(2,1)}, bf16[2,1536]{1,0:T(2,128)(2,1)}) custom-call(s32[2,8]{1,0:T(2,128)} %refs_0_.1, s32[2]{0:T(128)} %refs_1_.1, bf16[2,768]{1,0:T(2,128)(2,1)} %refs_2_.1, bf16[2,768]{1,0:T(2,128)(2,1)} %refs_3_.1, bf16[2,768]{1,0:T(2,128)(2,1)} %refs_4_.1, bf16[2,768]{1,0:T(2,128)(2,1)} %refs_5_.1, bf16[5,256,768]{2,1,0:T(8,128)(2,1)} %keys.1, ...), custom_call_target="tpu_custom_call" | custom-call | bytes 3944520 | tf_op jit(solution)/shard_map/rotary/pallas_call | solution.py:217
  1.6 3.0 %collective-permute-start = (bf16[2,1664]{1,0:T(2,128)(2,1)}, bf16[2,1664]{1,0:T(2,128)(2,1)S(1)}, u32[]{:S(2)}, u32[]{:S(2)}) collective-permute-start(bf16[2,1664]{1,0:T(2,128)(2,1)} %get-tuple-element.14.packed), channel_id=1, source_target_pairs={{0,4},{4,0},{8,12},{12,8},{16,20},{20,16},{24,28},{28,24},{1,5},{5... | collective-permute-start | bytes 19976 | tf_op jit(solution)/shard_map/ppermute | solution.py:531
  4.7 0.7 %copy-done.6 = bf16[2,1664]{1,0:T(2,128)(2,1)S(1)} copy-done((bf16[2,1664]{1,0:T(2,128)(2,1)S(1)}, bf16[2,1664]{1,0:T(2,128)(2,1)}, u32[]{:S(2)}) %copy-start.6) | copy-done | bytes 6680
  5.4 0.7 %copy-done.7 = bf16[2,1536]{1,0:T(2,128)(2,1)S(1)} copy-done((bf16[2,1536]{1,0:T(2,128)(2,1)S(1)}, bf16[2,1536]{1,0:T(2,128)(2,1)}, u32[]{:S(2)}) %copy-start.7) | copy-done | bytes 6168
  6.1 0.1 carry.1
  6.2 0.3 collective-permute-done.theirs
  6.5 4.1 %collective-permute-start.3 = (bf16[2,2,1664]{2,1,0:T(2,128)(2,1)S(1)}, bf16[2,2,1664]{2,1,0:T(2,128)(2,1)S(1)}, u32[]{:S(2)}, u32[]{:S(2)}) collective-permute-start(bf16[2,2,1664]{2,1,0:T(2,128)(2,1)S(1)} %merge.2.a0), channel_id=1, source_target_pairs={{0,24},{4,28},{8,16},{12,20},{16,8},{20,12},{24,0},{28,4},{1,25},{... | collective-permute-start | bytes 39944 | tf_op jit(solution)/shard_map/ppermute | solution.py:531
  10.6 0.0 collective-permute-start.2
  10.6 0.6 %collective-permute-start.1 = (bf16[2,2,1664]{2,1,0:T(2,128)(2,1)S(1)}, bf16[2,2,1664]{2,1,0:T(2,128)(2,1)S(1)}, u32[]{:S(2)}, u32[]{:S(2)}) collective-permute-start(bf16[2,2,1664]{2,1,0:T(2,128)(2,1)S(1)} %merge.2.a0), channel_id=1, source_target_pairs={{0,8},{4,12},{8,0},{12,4},{16,24},{20,28},{24,16},{28,20},{1,9},{5... | collective-permute-start | bytes 39944 | tf_op jit(solution)/shard_map/ppermute | solution.py:531
  11.2 1.1 %collective-permute-done.3.a3 = bf16[2,2,1664]{2,1,0:T(2,128)(2,1)S(1)} collective-permute-done((bf16[2,2,1664]{2,1,0:T(2,128)(2,1)S(1)}, bf16[2,2,1664]{2,1,0:T(2,128)(2,1)S(1)}, u32[]{:S(2)}, u32[]{:S(2)}) %collective-permute-start.3) | collective-permute-done | bytes 13344 | tf_op jit(solution)/shard_map/ppermute | solution.py:531
  12.3 2.9 %collective-permute-done.2.a2 = bf16[2,2,1664]{2,1,0:T(2,128)(2,1)S(1)} collective-permute-done((bf16[2,2,1664]{2,1,0:T(2,128)(2,1)S(1)}, bf16[2,2,1664]{2,1,0:T(2,128)(2,1)S(1)}, u32[]{:S(2)}, u32[]{:S(2)}) %collective-permute-start.2) | collective-permute-done | bytes 13344 | tf_op jit(solution)/shard_map/ppermute | solution.py:531
  15.2 0.0 collective-permute-done.1.a1
  15.2 0.0 copy-done.1
  15.2 0.0 copy-start.5
  15.2 0.0 copy-start.8
  15.3 0.0 copy-start.3
  15.3 0.0 copy-start.4
  15.3 1.1 %attend.1 = (bf16[8,768]{1,0:T(8,128)(2,1)S(1)}, f32[16,768]{1,0:T(8,128)S(1)}, f32[16,128]{1,0:T(8,128)S(1)}) custom-call(bf16[2,2,1664]{2,1,0:T(2,128)(2,1)S(1)} %merge.2.a0, bf16[2,2,1664]{2,1,0:T(2,128)(2,1)S(1)} %collective-permute-done.1.a1, bf16[2,2,1664]{2,1,0:T(2,128)(2,1)S(1)} %collective-permute-done.2.a2, ...), custom_call_target="tpu_custom_call" | custom-call | bytes 4014080 | tf_op jit(solution)/shard_map/attend/pallas_call | solution.py:217
  16.4 1.6 %collective-permute-start.4 = (bf16[8,768]{1,0:T(8,128)(2,1)S(1)}, bf16[8,768]{1,0:T(8,128)(2,1)S(1)}, u32[]{:S(2)}, u32[]{:S(2)}) collective-permute-start(bf16[8,768]{1,0:T(8,128)(2,1)S(1)} %get-tuple-element.18.mine), channel_id=1, source_target_pairs={{0,4},{4,0},{8,12},{12,8},{16,20},{20,16},{24,28},{28,24},{1,5},{5... | collective-permute-start | bytes 36872 | tf_op jit(solution)/shard_map/ppermute | solution.py:531
  18.0 2.2 %collective-permute-done.4.theirs = bf16[8,768]{1,0:T(8,128)(2,1)S(1)} collective-permute-done((bf16[8,768]{1,0:T(8,128)(2,1)S(1)}, bf16[8,768]{1,0:T(8,128)(2,1)S(1)}, u32[]{:S(2)}, u32[]{:S(2)}) %collective-permute-start.4) | collective-permute-done | bytes 12320 | tf_op jit(solution)/shard_map/ppermute | solution.py:531
  20.2 1.4 %collective-permute-start.7 = (bf16[2,8,768]{2,1,0:T(8,128)(2,1)S(1)}, bf16[2,8,768]{2,1,0:T(8,128)(2,1)S(1)}, u32[]{:S(2)}, u32[]{:S(2)}) collective-permute-start(bf16[2,8,768]{2,1,0:T(8,128)(2,1)S(1)} %merge.3.b0), channel_id=1, source_target_pairs={{0,24},{4,28},{8,16},{12,20},{16,8},{20,12},{24,0},{28,4},{1,25},{... | collective-permute-start | bytes 73736 | tf_op jit(solution)/shard_map/ppermute | solution.py:531
  21.6 0.6 %collective-permute-start.6 = (bf16[2,8,768]{2,1,0:T(8,128)(2,1)S(1)}, bf16[2,8,768]{2,1,0:T(8,128)(2,1)S(1)}, u32[]{:S(2)}, u32[]{:S(2)}) collective-permute-start(bf16[2,8,768]{2,1,0:T(8,128)(2,1)S(1)} %merge.3.b0), channel_id=1, source_target_pairs={{0,16},{4,20},{8,24},{12,28},{16,0},{20,4},{24,8},{28,12},{1,17},{... | collective-permute-start | bytes 73736 | tf_op jit(solution)/shard_map/ppermute | solution.py:531
  22.3 2.3 %collective-permute-start.5 = (bf16[2,8,768]{2,1,0:T(8,128)(2,1)S(1)}, bf16[2,8,768]{2,1,0:T(8,128)(2,1)S(1)}, u32[]{:S(2)}, u32[]{:S(2)}) collective-permute-start(bf16[2,8,768]{2,1,0:T(8,128)(2,1)S(1)} %merge.3.b0), channel_id=1, source_target_pairs={{0,8},{4,12},{8,0},{12,4},{16,24},{20,28},{24,16},{28,20},{1,9},{5... | collective-permute-start | bytes 73736 | tf_op jit(solution)/shard_map/ppermute | solution.py:531
  24.6 1.2 %collective-permute-done.7.b3 = bf16[2,8,768]{2,1,0:T(8,128)(2,1)S(1)} collective-permute-done((bf16[2,8,768]{2,1,0:T(8,128)(2,1)S(1)}, bf16[2,8,768]{2,1,0:T(8,128)(2,1)S(1)}, u32[]{:S(2)}, u32[]{:S(2)}) %collective-permute-start.7) | collective-permute-done | bytes 24608 | tf_op jit(solution)/shard_map/ppermute | solution.py:531
  25.8 0.6 %collective-permute-done.6.b2 = bf16[2,8,768]{2,1,0:T(8,128)(2,1)S(1)} collective-permute-done((bf16[2,8,768]{2,1,0:T(8,128)(2,1)S(1)}, bf16[2,8,768]{2,1,0:T(8,128)(2,1)S(1)}, u32[]{:S(2)}, u32[]{:S(2)}) %collective-permute-start.6) | collective-permute-done | bytes 24608 | tf_op jit(solution)/shard_map/ppermute | solution.py:531
  26.4 0.2 collective-permute-done.5.b1
  26.6 0.7 %combine.1.p0 = bf16[16,384]{1,0:T(8,128)(2,1)S(1)} custom-call(bf16[2,8,768]{2,1,0:T(8,128)(2,1)S(1)} %merge.3.b0, bf16[2,8,768]{2,1,0:T(8,128)(2,1)S(1)} %collective-permute-done.5.b1, bf16[2,8,768]{2,1,0:T(8,128)(2,1)S(1)} %collective-permute-done.6.b2, bf16[2,8,768]{2,1,0:T(8,128)(2,1)S(1)} %collective-permute-done.7.b3, ...), custom_call_target="tpu_custom_call" | custom-call | bytes 696320 | tf_op jit(solution)/shard_map/combine/pallas_call | solution.py:217
  27.4 0.1 collective-permute-start.10
  27.4 1.6 %collective-permute-start.9 = (bf16[16,384]{1,0:T(8,128)(2,1)S(1)}, bf16[16,384]{1,0:T(8,128)(2,1)S(1)}, u32[]{:S(2)}, u32[]{:S(2)}) collective-permute-start(bf16[16,384]{1,0:T(8,128)(2,1)S(1)} %combine.1.p0), channel_id=1, source_target_pairs={{0,2},{1,3},{2,0},{3,1},{4,6},{5,7},{6,4},{7,5},{8,10},{9,11},{10,... | collective-permute-start | bytes 36872 | tf_op jit(solution)/shard_map/ppermute | solution.py:531
  29.0 0.3 collective-permute-start.8
  29.3 1.3 %collective-permute-done.10.p3 = bf16[16,384]{1,0:T(8,128)(2,1)S(1)} collective-permute-done((bf16[16,384]{1,0:T(8,128)(2,1)S(1)}, bf16[16,384]{1,0:T(8,128)(2,1)S(1)}, u32[]{:S(2)}, u32[]{:S(2)}) %collective-permute-start.10) | collective-permute-done | bytes 12320 | tf_op jit(solution)/shard_map/ppermute | solution.py:531
  30.6 0.6 %collective-permute-done.9.p2 = bf16[16,384]{1,0:T(8,128)(2,1)S(1)} collective-permute-done((bf16[16,384]{1,0:T(8,128)(2,1)S(1)}, bf16[16,384]{1,0:T(8,128)(2,1)S(1)}, u32[]{:S(2)}, u32[]{:S(2)}) %collective-permute-start.9) | collective-permute-done | bytes 12320 | tf_op jit(solution)/shard_map/ppermute | solution.py:531
  31.2 0.0 collective-permute-done.8.p1
  31.2 2.8 %collective-permute-start.12 = (bf16[16,384]{1,0:T(8,128)(2,1)S(1)}, bf16[16,384]{1,0:T(8,128)(2,1)S(1)}, u32[]{:S(2)}, u32[]{:S(2)}) collective-permute-start(bf16[16,384]{1,0:T(8,128)(2,1)S(1)} %head_sum.1), channel_id=1, source_target_pairs={{1,28},{5,24},{0,20},{4,16},{3,12},{7,8},{2,4},{6,0},{9,29},{13,25... | collective-permute-start | bytes 36872 | tf_op jit(solution)/shard_map/ppermute | solution.py:620
  34.0 1.5 %collective-permute-start.11 = (bf16[16,384]{1,0:T(8,128)(2,1)S(1)}, bf16[16,384]{1,0:T(8,128)(2,1)S(1)}, u32[]{:S(2)}, u32[]{:S(2)}) collective-permute-start(bf16[16,384]{1,0:T(8,128)(2,1)S(1)} %head_sum.1), channel_id=1, source_target_pairs={{1,24},{5,28},{0,16},{4,20},{3,8},{7,12},{2,0},{6,4},{9,25},{13,29... | collective-permute-start | bytes 36872 | tf_op jit(solution)/shard_map/ppermute | solution.py:620
  35.5 0.5 collective-permute-done.12.flip
  36.0 1.7 %collective-permute-done.11.same = bf16[16,384]{1,0:T(8,128)(2,1)S(1)} collective-permute-done((bf16[16,384]{1,0:T(8,128)(2,1)S(1)}, bf16[16,384]{1,0:T(8,128)(2,1)S(1)}, u32[]{:S(2)}, u32[]{:S(2)}) %collective-permute-start.11) | collective-permute-done | bytes 12320 | tf_op jit(solution)/shard_map/ppermute | solution.py:620
  37.7 0.0 copy-done.4
  37.7 0.5 gate_up.1
  38.2 0.6 %collective-permute-start.15 = (bf16[16,2176]{1,0:T(8,128)(2,1)S(1)}, bf16[16,2176]{1,0:T(8,128)(2,1)S(1)}, u32[]{:S(2)}, u32[]{:S(2)}) collective-permute-start(bf16[16,2176]{1,0:T(8,128)(2,1)S(1)} %get-tuple-element.22.p0), channel_id=1, source_target_pairs={{0,2},{1,3},{2,0},{3,1},{4,6},{5,7},{6,4},{7,5},{8,10},{9,11},{10,... | collective-permute-start | bytes 208904 | tf_op jit(solution)/shard_map/ppermute | solution.py:531
  38.8 1.4 %collective-permute-start.14 = (bf16[16,2176]{1,0:T(8,128)(2,1)S(1)}, bf16[16,2176]{1,0:T(8,128)(2,1)S(1)}, u32[]{:S(2)}, u32[]{:S(2)}) collective-permute-start(bf16[16,2176]{1,0:T(8,128)(2,1)S(1)} %get-tuple-element.22.p0), channel_id=1, source_target_pairs={{0,1},{1,0},{2,3},{3,2},{4,5},{5,4},{6,7},{7,6},{8,9},{9,8},{10,11... | collective-permute-start | bytes 208904 | tf_op jit(solution)/shard_map/ppermute | solution.py:531
  40.2 0.2 collective-permute-start.13
  40.3 2.4 %collective-permute-done.15.p3 = bf16[16,2176]{1,0:T(8,128)(2,1)S(1)} collective-permute-done((bf16[16,2176]{1,0:T(8,128)(2,1)S(1)}, bf16[16,2176]{1,0:T(8,128)(2,1)S(1)}, u32[]{:S(2)}, u32[]{:S(2)}) %collective-permute-start.15) | collective-permute-done | bytes 69664 | tf_op jit(solution)/shard_map/ppermute | solution.py:531
  42.8 0.0 collective-permute-done.14.p2
  42.8 1.7 %collective-permute-done.13.p1 = bf16[16,2176]{1,0:T(8,128)(2,1)S(1)} collective-permute-done((bf16[16,2176]{1,0:T(8,128)(2,1)S(1)}, bf16[16,2176]{1,0:T(8,128)(2,1)S(1)}, u32[]{:S(2)}, u32[]{:S(2)}) %collective-permute-start.13) | collective-permute-done | bytes 69664 | tf_op jit(solution)/shard_map/ppermute | solution.py:531
  44.5 0.4 down.1
  44.9 8.4 %all_to_all.5.parts = bf16[8,2,768]{2,1,0:T(2,128)(2,1)S(1)} all-to-all(bf16[8,2,768]{2,1,0:T(2,128)(2,1)S(1)} %down.1), channel_id=1, replica_groups={{28,24,20,16,12,8,4,0},{29,25,21,17,13,9,5,1},{30,26,22,18,14,10,6,2},{..., dimensions={0} | all-to-all | bytes 49152 | tf_op jit(solution)/shard_map/all_to_all | solution.py:640
  53.3 0.6 %final.1 = bf16[2,768]{1,0:T(2,128)(2,1)} custom-call(f32[2,768]{1,0:T(2,128)S(1)} %get-tuple-element.21.own, bf16[8,2,768]{2,1,0:T(2,128)(2,1)S(1)} %all_to_all.5.parts), custom_call_target="tpu_custom_call" | custom-call | bytes 30720 | tf_op jit(solution)/shard_map/final/pallas_call | solution.py:217
  (14 shorter events, 0.0 us)
Async XLA Ops:
  0.0 15.2 %copy-start.1 = (bf16[5,256,768]{2,1,0:T(8,128)(2,1)S(1)}, bf16[5,256,768]{2,1,0:T(8,128)(2,1)}, u32[]{:S(2)}) copy-start(bf16[5,256,768]{2,1,0:T(8,128)(2,1)} %values.1) | copy-start | bytes 5898244
  0.0 15.2 %copy-start = (bf16[5,256,768]{2,1,0:T(8,128)(2,1)S(1)}, bf16[5,256,768]{2,1,0:T(8,128)(2,1)}, u32[]{:S(2)}) copy-start(bf16[5,256,768]{2,1,0:T(8,128)(2,1)} %keys.1) | copy-start | bytes 5898244
  1.6 4.9 %collective-permute-start = (bf16[2,1664]{1,0:T(2,128)(2,1)}, bf16[2,1664]{1,0:T(2,128)(2,1)S(1)}, u32[]{:S(2)}, u32[]{:S(2)}) collective-permute-start(bf16[2,1664]{1,0:T(2,128)(2,1)} %get-tuple-element.14.packed), channel_id=1, source_target_pairs={{0,4},{4,0},{8,12},{12,8},{16,20},{20,16},{24,28},{28,24},{1,5},{5... | collective-permute-start | bytes 19976 | tf_op jit(solution)/shard_map/ppermute | solution.py:531
  4.7 0.7 %copy-start.6 = (bf16[2,1664]{1,0:T(2,128)(2,1)S(1)}, bf16[2,1664]{1,0:T(2,128)(2,1)}, u32[]{:S(2)}) copy-start(bf16[2,1664]{1,0:T(2,128)(2,1)} %get-tuple-element.14.packed) | copy-start | bytes 19972
  5.4 0.7 %copy-start.7 = (bf16[2,1536]{1,0:T(2,128)(2,1)S(1)}, bf16[2,1536]{1,0:T(2,128)(2,1)}, u32[]{:S(2)}) copy-start(bf16[2,1536]{1,0:T(2,128)(2,1)} %get-tuple-element.15.new) | copy-start | bytes 18436
  6.5 5.8 %collective-permute-start.3 = (bf16[2,2,1664]{2,1,0:T(2,128)(2,1)S(1)}, bf16[2,2,1664]{2,1,0:T(2,128)(2,1)S(1)}, u32[]{:S(2)}, u32[]{:S(2)}) collective-permute-start(bf16[2,2,1664]{2,1,0:T(2,128)(2,1)S(1)} %merge.2.a0), channel_id=1, source_target_pairs={{0,24},{4,28},{8,16},{12,20},{16,8},{20,12},{24,0},{28,4},{1,25},{... | collective-permute-start | bytes 39944 | tf_op jit(solution)/shard_map/ppermute | solution.py:531
  10.6 4.6 %collective-permute-start.2 = (bf16[2,2,1664]{2,1,0:T(2,128)(2,1)S(1)}, bf16[2,2,1664]{2,1,0:T(2,128)(2,1)S(1)}, u32[]{:S(2)}, u32[]{:S(2)}) collective-permute-start(bf16[2,2,1664]{2,1,0:T(2,128)(2,1)S(1)} %merge.2.a0), channel_id=1, source_target_pairs={{0,16},{4,20},{8,24},{12,28},{16,0},{20,4},{24,8},{28,12},{1,17},{... | collective-permute-start | bytes 39944 | tf_op jit(solution)/shard_map/ppermute | solution.py:531
  10.6 4.6 %collective-permute-start.1 = (bf16[2,2,1664]{2,1,0:T(2,128)(2,1)S(1)}, bf16[2,2,1664]{2,1,0:T(2,128)(2,1)S(1)}, u32[]{:S(2)}, u32[]{:S(2)}) collective-permute-start(bf16[2,2,1664]{2,1,0:T(2,128)(2,1)S(1)} %merge.2.a0), channel_id=1, source_target_pairs={{0,8},{4,12},{8,0},{12,4},{16,24},{20,28},{24,16},{28,20},{1,9},{5... | collective-permute-start | bytes 39944 | tf_op jit(solution)/shard_map/ppermute | solution.py:531
  15.2 11.4 %copy-start.5 = (bf16[768,384]{1,0:T(8,128)(2,1)S(1)}, bf16[768,384]{1,0:T(8,128)(2,1)}, u32[]{:S(2)}) copy-start(bf16[768,384]{1,0:T(8,128)(2,1)} %weight.2) | copy-start | bytes 1769476
  15.2 20.2 %copy-start.8 = (bf16[768]{0:T(1024)(128)(2,1)S(1)}, bf16[768]{0:T(1024)(128)(2,1)}, u32[]{:S(2)}) copy-start(bf16[768]{0:T(1024)(128)(2,1)} %param.22) | copy-start | bytes 4612
  15.3 22.4 %copy-start.3 = (bf16[768,1024]{1,0:T(8,128)(2,1)S(1)}, bf16[768,1024]{1,0:T(8,128)(2,1)}, u32[]{:S(2)}) copy-start(bf16[768,1024]{1,0:T(8,128)(2,1)} %gate.1) | copy-start | bytes 4718596
  15.3 22.4 %copy-start.4 = (bf16[768,1024]{1,0:T(8,128)(2,1)S(1)}, bf16[768,1024]{1,0:T(8,128)(2,1)}, u32[]{:S(2)}) copy-start(bf16[768,1024]{1,0:T(8,128)(2,1)} %up.1) | copy-start | bytes 4718596
  16.4 3.8 %collective-permute-start.4 = (bf16[8,768]{1,0:T(8,128)(2,1)S(1)}, bf16[8,768]{1,0:T(8,128)(2,1)S(1)}, u32[]{:S(2)}, u32[]{:S(2)}) collective-permute-start(bf16[8,768]{1,0:T(8,128)(2,1)S(1)} %get-tuple-element.18.mine), channel_id=1, source_target_pairs={{0,4},{4,0},{8,12},{12,8},{16,20},{20,16},{24,28},{28,24},{1,5},{5... | collective-permute-start | bytes 36872 | tf_op jit(solution)/shard_map/ppermute | solution.py:531
  20.2 5.6 %collective-permute-start.7 = (bf16[2,8,768]{2,1,0:T(8,128)(2,1)S(1)}, bf16[2,8,768]{2,1,0:T(8,128)(2,1)S(1)}, u32[]{:S(2)}, u32[]{:S(2)}) collective-permute-start(bf16[2,8,768]{2,1,0:T(8,128)(2,1)S(1)} %merge.3.b0), channel_id=1, source_target_pairs={{0,24},{4,28},{8,16},{12,20},{16,8},{20,12},{24,0},{28,4},{1,25},{... | collective-permute-start | bytes 73736 | tf_op jit(solution)/shard_map/ppermute | solution.py:531
  21.6 4.7 %collective-permute-start.6 = (bf16[2,8,768]{2,1,0:T(8,128)(2,1)S(1)}, bf16[2,8,768]{2,1,0:T(8,128)(2,1)S(1)}, u32[]{:S(2)}, u32[]{:S(2)}) collective-permute-start(bf16[2,8,768]{2,1,0:T(8,128)(2,1)S(1)} %merge.3.b0), channel_id=1, source_target_pairs={{0,16},{4,20},{8,24},{12,28},{16,0},{20,4},{24,8},{28,12},{1,17},{... | collective-permute-start | bytes 73736 | tf_op jit(solution)/shard_map/ppermute | solution.py:531
  22.3 4.4 %collective-permute-start.5 = (bf16[2,8,768]{2,1,0:T(8,128)(2,1)S(1)}, bf16[2,8,768]{2,1,0:T(8,128)(2,1)S(1)}, u32[]{:S(2)}, u32[]{:S(2)}) collective-permute-start(bf16[2,8,768]{2,1,0:T(8,128)(2,1)S(1)} %merge.3.b0), channel_id=1, source_target_pairs={{0,8},{4,12},{8,0},{12,4},{16,24},{20,28},{24,16},{28,20},{1,9},{5... | collective-permute-start | bytes 73736 | tf_op jit(solution)/shard_map/ppermute | solution.py:531
  27.4 3.2 %collective-permute-start.10 = (bf16[16,384]{1,0:T(8,128)(2,1)S(1)}, bf16[16,384]{1,0:T(8,128)(2,1)S(1)}, u32[]{:S(2)}, u32[]{:S(2)}) collective-permute-start(bf16[16,384]{1,0:T(8,128)(2,1)S(1)} %combine.1.p0), channel_id=1, source_target_pairs={{0,3},{1,2},{2,1},{3,0},{4,7},{5,6},{6,5},{7,4},{8,11},{9,10},{10,... | collective-permute-start | bytes 36872 | tf_op jit(solution)/shard_map/ppermute | solution.py:531
  27.4 3.8 %collective-permute-start.9 = (bf16[16,384]{1,0:T(8,128)(2,1)S(1)}, bf16[16,384]{1,0:T(8,128)(2,1)S(1)}, u32[]{:S(2)}, u32[]{:S(2)}) collective-permute-start(bf16[16,384]{1,0:T(8,128)(2,1)S(1)} %combine.1.p0), channel_id=1, source_target_pairs={{0,2},{1,3},{2,0},{3,1},{4,6},{5,7},{6,4},{7,5},{8,10},{9,11},{10,... | collective-permute-start | bytes 36872 | tf_op jit(solution)/shard_map/ppermute | solution.py:531
  29.0 2.2 %collective-permute-start.8 = (bf16[16,384]{1,0:T(8,128)(2,1)S(1)}, bf16[16,384]{1,0:T(8,128)(2,1)S(1)}, u32[]{:S(2)}, u32[]{:S(2)}) collective-permute-start(bf16[16,384]{1,0:T(8,128)(2,1)S(1)} %combine.1.p0), channel_id=1, source_target_pairs={{0,1},{1,0},{2,3},{3,2},{4,5},{5,4},{6,7},{7,6},{8,9},{9,8},{10,11... | collective-permute-start | bytes 36872 | tf_op jit(solution)/shard_map/ppermute | solution.py:531
  31.2 4.8 %collective-permute-start.12 = (bf16[16,384]{1,0:T(8,128)(2,1)S(1)}, bf16[16,384]{1,0:T(8,128)(2,1)S(1)}, u32[]{:S(2)}, u32[]{:S(2)}) collective-permute-start(bf16[16,384]{1,0:T(8,128)(2,1)S(1)} %head_sum.1), channel_id=1, source_target_pairs={{1,28},{5,24},{0,20},{4,16},{3,12},{7,8},{2,4},{6,0},{9,29},{13,25... | collective-permute-start | bytes 36872 | tf_op jit(solution)/shard_map/ppermute | solution.py:620
  34.0 3.7 %collective-permute-start.11 = (bf16[16,384]{1,0:T(8,128)(2,1)S(1)}, bf16[16,384]{1,0:T(8,128)(2,1)S(1)}, u32[]{:S(2)}, u32[]{:S(2)}) collective-permute-start(bf16[16,384]{1,0:T(8,128)(2,1)S(1)} %head_sum.1), channel_id=1, source_target_pairs={{1,24},{5,28},{0,16},{4,20},{3,8},{7,12},{2,0},{6,4},{9,25},{13,29... | collective-permute-start | bytes 36872 | tf_op jit(solution)/shard_map/ppermute | solution.py:620
  37.7 6.8 %copy-start.2 = (bf16[1024,768]{1,0:T(8,128)(2,1)S(1)}, bf16[1024,768]{1,0:T(8,128)(2,1)}, u32[]{:S(2)}) copy-start(bf16[1024,768]{1,0:T(8,128)(2,1)} %weight.3) | copy-start | bytes 4718596
  38.2 4.6 %collective-permute-start.15 = (bf16[16,2176]{1,0:T(8,128)(2,1)S(1)}, bf16[16,2176]{1,0:T(8,128)(2,1)S(1)}, u32[]{:S(2)}, u32[]{:S(2)}) collective-permute-start(bf16[16,2176]{1,0:T(8,128)(2,1)S(1)} %get-tuple-element.22.p0), channel_id=1, source_target_pairs={{0,2},{1,3},{2,0},{3,1},{4,6},{5,7},{6,4},{7,5},{8,10},{9,11},{10,... | collective-permute-start | bytes 208904 | tf_op jit(solution)/shard_map/ppermute | solution.py:531
  38.8 4.0 %collective-permute-start.14 = (bf16[16,2176]{1,0:T(8,128)(2,1)S(1)}, bf16[16,2176]{1,0:T(8,128)(2,1)S(1)}, u32[]{:S(2)}, u32[]{:S(2)}) collective-permute-start(bf16[16,2176]{1,0:T(8,128)(2,1)S(1)} %get-tuple-element.22.p0), channel_id=1, source_target_pairs={{0,1},{1,0},{2,3},{3,2},{4,5},{5,4},{6,7},{7,6},{8,9},{9,8},{10,11... | collective-permute-start | bytes 208904 | tf_op jit(solution)/shard_map/ppermute | solution.py:531
  40.2 4.3 %collective-permute-start.13 = (bf16[16,2176]{1,0:T(8,128)(2,1)S(1)}, bf16[16,2176]{1,0:T(8,128)(2,1)S(1)}, u32[]{:S(2)}, u32[]{:S(2)}) collective-permute-start(bf16[16,2176]{1,0:T(8,128)(2,1)S(1)} %get-tuple-element.22.p0), channel_id=1, source_target_pairs={{0,3},{1,2},{2,1},{3,0},{4,7},{5,6},{6,5},{7,4},{8,11},{9,10},{10,... | collective-permute-start | bytes 208904 | tf_op jit(solution)/shard_map/ppermute | solution.py:531
